TPU v7x, 128 devices: a whole 4x4x4 slice. The times are simulated.
128 devices in a mesh: section: 4 (over x), dp: 32 (over y, z, core).
Axes of the slice: x: 4, y: 4, z: 4, core: 2. Of those that a mesh axis runs over, the one named last changes fastest.
Arguments:
- tokens: bfloat16 [24576, 768], P('dp'), may hold values from -6 to 6
- cotangent: bfloat16 [24576, 768], P('dp'), may hold values from -6 to 6
- lengths: int32 [64, 3], P('dp'), may hold values from 0 to 361, as said below
- proj_in: bfloat16 [4, 768, 5376], P('section', 'dp'), may hold values from -0.21875 to 0.21875
- proj_attn: bfloat16 [4, 768, 768], P('section', 'dp'), may hold values from -1.5 to 1.5
- proj_down: bfloat16 [4, 3072, 768], P('section', 'dp'), may hold values from -0.109375 to 0.109375
- norm_gain: bfloat16 [4, 768], P('section', 'dp'), may hold values from 0.75 to 1.25
- query_gain: bfloat16 [4, 64], P('section', 'dp'), may hold values from 0.75 to 1.25
- key_gain: bfloat16 [4, 64], P('section', 'dp'), may hold values from 0.75 to 1.25
- up_bias: bfloat16 [4, 3072], P('section', 'dp'), may hold values from -2.5 to 2.5
- out_bias: bfloat16 [4, 768], P('section', 'dp'), may hold values from -2.5 to 2.5
Outputs:
- section_outputs: float32 [4, 24576, 768], P('section', 'dp')
- section_grads: float32 [4, 24576, 768], P('section', 'dp')
- grad_proj_in: float32 [4, 768, 5376], P('section', 'dp')
- grad_proj_attn: float32 [4, 768, 768], P('section', 'dp')
- grad_proj_down: float32 [4, 3072, 768], P('section', 'dp')
- grad_norm_gain: float32 [4, 768], P('section', 'dp')
- grad_query_gain: float32 [4, 64], P('section', 'dp')
- grad_key_gain: float32 [4, 64], P('section', 'dp')
- grad_up_bias: float32 [4, 3072], P('section', 'dp')
- grad_out_bias: float32 [4, 768], P('section', 'dp')
Inputs may be any that keep to these rules, and one draw needn't show every extreme that they name: `lengths`: each slot holds one image of 361 tokens, one of 256 tokens, or three of 100 tokens; unused entries are zero. The first slot holds one of 361.
All inputs are finite; a program needn't handle non-finite values.
Results may differ from a plain program's by a relative error of at most 0.035.
Values may be sent and summed in bfloat16 or wider, within the bound.
No kernel may reach another device: no remote copies, remote signals or barrier semaphores. Data moves between devices by JAX's collectives and lax.ppermute only.
A program may use at most 256 MiB of HBM per device.

v0:
```python
from functools import partial
import math

import jax
import jax.numpy as jnp
from jax import lax
from jax.sharding import PartitionSpec as P


def shifted(x, axis, by):
    devices = lax.axis_size(axis)
    pairs = [(i, i + by) for i in range(devices) if 0 <= i + by < devices]
    return lax.ppermute(x, axis, pairs)


def normalize(values):
    centered = values - jnp.mean(values, axis=-1, keepdims=True)
    return centered * lax.rsqrt(jnp.mean(centered * centered, axis=-1, keepdims=True) + 1e-06)


def scaled_norm(values, gain):
    return normalize(values) * gain


def slot_layout(lengths, slot_size):
    boundary = jnp.cumsum(lengths, axis=-1)
    position = jnp.arange(slot_size, dtype=jnp.int32)
    image_of = jnp.sum((position[None, :, None] >= boundary[:, None, :]).astype(jnp.int32), axis=-1)
    present = position[None, :] < boundary[:, 2:3]
    image_ids = jnp.where(present, image_of, 16 + position[None, :])
    return (image_ids, present)


def project(layer_in, weights, present):
    proj_in, proj_attn, proj_down, norm_gain, query_gain, key_gain, up_bias, out_bias = weights
    model_width = proj_attn.shape[0]
    head_dim = query_gain.shape[0]
    heads_count = model_width // head_dim
    row_count = layer_in.shape[0]
    keep_rows = present[:, None].astype(jnp.float32)
    masked = keep_rows * layer_in
    hidden = scaled_norm(masked, norm_gain.astype(jnp.float32)).astype(jnp.bfloat16)
    joined = jnp.dot(hidden, proj_in, preferred_element_type=jnp.float32)
    query_raw = joined[:, :model_width].reshape(row_count, heads_count, head_dim)
    key_raw = joined[:, model_width : 2 * model_width].reshape(row_count, heads_count, head_dim)
    values = (
        joined[:, 2 * model_width : 3 * model_width]
        .reshape(row_count, heads_count, head_dim)
        .astype(jnp.bfloat16)
    )
    pre_act = joined[:, 3 * model_width :] + up_bias.astype(jnp.float32)
    queries = scaled_norm(query_raw, query_gain.astype(jnp.float32)).astype(jnp.bfloat16)
    key_rows = scaled_norm(key_raw, key_gain.astype(jnp.float32)).astype(jnp.bfloat16)
    activated = jax.nn.gelu(pre_act, approximate=False).astype(jnp.bfloat16)
    return (
        keep_rows,
        masked,
        hidden,
        query_raw,
        key_raw,
        values,
        pre_act,
        queries,
        key_rows,
        activated,
    )


def score_block(queries, key_rows, image_ids):
    head_dim = queries.shape[2]
    scores = jnp.einsum("qhd,khd->hqk", queries, key_rows, preferred_element_type=jnp.float32) * (
        1.0 / math.sqrt(head_dim)
    )
    allowed = image_ids[:, None] == image_ids[None, :]
    return jnp.where(allowed[None], scores, -1000000000.0)


def run_forward(layer_in, weights, image_ids, present):
    keep_rows, masked, hidden, query_raw, key_raw, values, pre_act, queries, key_rows, activated = (
        project(layer_in, weights, present)
    )
    scores = score_block(queries, key_rows, image_ids)
    row_peak = jnp.max(scores, axis=-1, keepdims=True)
    log_total = row_peak[..., 0] + jnp.log(jnp.sum(jnp.exp(scores - row_peak), axis=-1))
    attn_probs = jnp.exp(scores - log_total[..., None]).astype(jnp.bfloat16)
    attended = jnp.einsum(
        "hqk,khd->qhd", attn_probs, values, preferred_element_type=jnp.float32
    ).astype(jnp.bfloat16)
    attended = attended.reshape(layer_in.shape[0], -1)
    branch = jnp.dot(attended, weights[1], preferred_element_type=jnp.float32) + jnp.dot(
        activated, weights[2], preferred_element_type=jnp.float32
    )
    layer_out = keep_rows * (masked + branch + weights[7].astype(jnp.float32))
    return (layer_out, log_total)


def run_backward(layer_in, log_total, grad_out, weights, image_ids, present):
    proj_in, proj_attn, proj_down, norm_gain, query_gain, key_gain, up_bias, out_bias = weights
    keep_rows, masked, hidden, query_raw, key_raw, values, pre_act, queries, key_rows, activated = (
        project(layer_in, weights, present)
    )
    row_count = layer_in.shape[0]
    head_dim = queries.shape[2]
    score_scale = 1.0 / math.sqrt(head_dim)
    scores = score_block(queries, key_rows, image_ids)
    exact_probs = jnp.exp(scores - log_total[..., None])
    attn_probs = exact_probs.astype(jnp.bfloat16)
    attended = jnp.einsum(
        "hqk,khd->qhd", attn_probs, values, preferred_element_type=jnp.float32
    ).astype(jnp.bfloat16)
    attended = attended.reshape(row_count, -1)
    grad_res = keep_rows * grad_out
    grad_out_bias = jnp.sum(grad_res, axis=0)
    grad_branch = grad_res.astype(jnp.bfloat16)
    grad_attn = jnp.einsum("sd,sj->dj", attended, grad_branch, preferred_element_type=jnp.float32)
    grad_down = jnp.einsum("sf,sj->fj", activated, grad_branch, preferred_element_type=jnp.float32)
    grad_attended = jnp.einsum(
        "sj,dj->sd", grad_branch, proj_attn, preferred_element_type=jnp.float32
    ).astype(jnp.bfloat16)
    grad_attended = grad_attended.reshape(queries.shape)
    grad_act = jnp.einsum("sj,fj->sf", grad_branch, proj_down, preferred_element_type=jnp.float32)
    unused, gelu_back = jax.vjp(partial(jax.nn.gelu, approximate=False), pre_act)
    grad_pre = gelu_back(grad_act)[0]
    grad_up_bias = jnp.sum(grad_pre, axis=0)
    grad_probs = jnp.einsum(
        "qhd,khd->hqk", grad_attended, values, preferred_element_type=jnp.float32
    )
    grad_values = jnp.einsum(
        "hqk,qhd->khd", attn_probs, grad_attended, preferred_element_type=jnp.float32
    )
    grad_scores = exact_probs * (
        grad_probs - jnp.sum(grad_probs * exact_probs, axis=-1, keepdims=True)
    )
    grad_scores = grad_scores.astype(jnp.bfloat16)
    grad_queries = (
        jnp.einsum("hqk,khd->qhd", grad_scores, key_rows, preferred_element_type=jnp.float32)
        * score_scale
    )
    grad_keys = (
        jnp.einsum("hqk,qhd->khd", grad_scores, queries, preferred_element_type=jnp.float32)
        * score_scale
    )
    unused, query_back = jax.vjp(scaled_norm, query_raw, query_gain.astype(jnp.float32))
    grad_query_raw, grad_query_gain = query_back(grad_queries)
    unused, key_back = jax.vjp(scaled_norm, key_raw, key_gain.astype(jnp.float32))
    grad_key_raw, grad_key_gain = key_back(grad_keys)
    grad_joined = jnp.concatenate(
        [
            grad_query_raw.reshape(row_count, -1),
            grad_key_raw.reshape(row_count, -1),
            grad_values.reshape(row_count, -1),
            grad_pre,
        ],
        axis=1,
    ).astype(jnp.bfloat16)
    grad_in_proj = jnp.einsum("sd,sj->dj", hidden, grad_joined, preferred_element_type=jnp.float32)
    grad_hidden = jnp.einsum("sj,dj->sd", grad_joined, proj_in, preferred_element_type=jnp.float32)
    unused, norm_back = jax.vjp(scaled_norm, masked, norm_gain.astype(jnp.float32))
    grad_masked, grad_norm_gain = norm_back(grad_hidden)
    grad_in = keep_rows * (grad_res + grad_masked)
    return (
        grad_in,
        (
            grad_in_proj,
            grad_attn,
            grad_down,
            grad_norm_gain,
            grad_query_gain,
            grad_key_gain,
            grad_up_bias,
            grad_out_bias,
        ),
    )


def store(buffer, chosen, active, fresh):
    previous = lax.dynamic_index_in_dim(buffer, chosen, 0, keepdims=False)
    return lax.dynamic_update_index_in_dim(buffer, jnp.where(active, fresh, previous), chosen, 0)


def body(
    tokens,
    cotangent,
    lengths,
    proj_in,
    proj_attn,
    proj_down,
    norm_gain,
    query_gain,
    key_gain,
    up_bias,
    out_bias,
):
    section_count = lax.axis_size("section")
    section_index = lax.axis_index("section")
    micro_count = lengths.shape[0]
    slot_size = tokens.shape[0] // micro_count
    model_width = tokens.shape[1]
    image_ids, present = slot_layout(lengths, slot_size)
    inputs = tokens.astype(jnp.float32).reshape(micro_count, slot_size, model_width)
    grad_seeds = cotangent.astype(jnp.float32).reshape(micro_count, slot_size, model_width)
    weights = (
        lax.all_gather(proj_in[0], "dp", axis=0, tiled=True),
        lax.all_gather(proj_attn[0], "dp", axis=0, tiled=True),
        lax.all_gather(proj_down[0], "dp", axis=0, tiled=True),
        lax.all_gather(norm_gain[0], "dp", axis=0, tiled=True),
        lax.all_gather(query_gain[0], "dp", axis=0, tiled=True),
        lax.all_gather(key_gain[0], "dp", axis=0, tiled=True),
        lax.all_gather(up_bias[0], "dp", axis=0, tiled=True),
        lax.all_gather(out_bias[0], "dp", axis=0, tiled=True),
    )
    heads_count = model_width // weights[4].shape[0]

    def forward_tick(moment, carried):
        outgoing, kept_in, kept_out, kept_lse = carried
        arrived = shifted(outgoing, "section", 1)
        which_micro = moment - section_index
        active = (which_micro >= 0) & (which_micro < micro_count)
        chosen = jnp.clip(which_micro, 0, micro_count - 1)
        source_rows = lax.dynamic_index_in_dim(inputs, chosen, 0, keepdims=False)
        layer_in = jnp.where(section_index == 0, source_rows, arrived)
        ids_now = lax.dynamic_index_in_dim(image_ids, chosen, 0, keepdims=False)
        present_now = lax.dynamic_index_in_dim(present, chosen, 0, keepdims=False)

        def forward_work(operand):
            return run_forward(operand, weights, ids_now, present_now)

        def forward_skip(operand):
            return (jnp.zeros_like(operand), jnp.zeros((heads_count, slot_size), jnp.float32))

        layer_out, log_total = lax.cond(active, forward_work, forward_skip, layer_in)
        kept_in = store(kept_in, chosen, active, layer_in)
        kept_out = store(kept_out, chosen, active, layer_out)
        kept_lse = store(kept_lse, chosen, active, log_total)
        return (layer_out, kept_in, kept_out, kept_lse)

    blank_rows = jnp.zeros((slot_size, model_width), jnp.float32)
    blank_acts = jnp.zeros((micro_count, slot_size, model_width), jnp.float32)
    blank_lse = jnp.zeros((micro_count, heads_count, slot_size), jnp.float32)
    carried = lax.fori_loop(
        0,
        micro_count + section_count - 1,
        forward_tick,
        (blank_rows, blank_acts, blank_acts, blank_lse),
    )
    kept_in, kept_out, kept_lse = (carried[1], carried[2], carried[3])
    weights = (
        lax.all_gather(proj_in[0], "dp", axis=0, tiled=True),
        lax.all_gather(proj_attn[0], "dp", axis=0, tiled=True),
        lax.all_gather(proj_down[0], "dp", axis=0, tiled=True),
        lax.all_gather(norm_gain[0], "dp", axis=0, tiled=True),
        lax.all_gather(query_gain[0], "dp", axis=0, tiled=True),
        lax.all_gather(key_gain[0], "dp", axis=0, tiled=True),
        lax.all_gather(up_bias[0], "dp", axis=0, tiled=True),
        lax.all_gather(out_bias[0], "dp", axis=0, tiled=True),
    )
    blank_grads = tuple((jnp.zeros(piece.shape, jnp.float32) for piece in weights))

    def backward_tick(moment, carried):
        outgoing, kept_grad, totals = carried
        arrived = shifted(outgoing, "section", -1)
        which_micro = moment - (section_count - 1 - section_index)
        active = (which_micro >= 0) & (which_micro < micro_count)
        chosen = jnp.clip(which_micro, 0, micro_count - 1)
        seed_rows = lax.dynamic_index_in_dim(grad_seeds, chosen, 0, keepdims=False)
        grad_out = jnp.where(section_index == section_count - 1, seed_rows, arrived)
        layer_in = lax.dynamic_index_in_dim(kept_in, chosen, 0, keepdims=False)
        log_total = lax.dynamic_index_in_dim(kept_lse, chosen, 0, keepdims=False)
        ids_now = lax.dynamic_index_in_dim(image_ids, chosen, 0, keepdims=False)
        present_now = lax.dynamic_index_in_dim(present, chosen, 0, keepdims=False)

        def backward_work(operand):
            return run_backward(layer_in, log_total, operand, weights, ids_now, present_now)

        def backward_skip(operand):
            return (jnp.zeros_like(operand), blank_grads)

        grad_in, grads = lax.cond(active, backward_work, backward_skip, grad_out)
        totals = tuple((total + piece for total, piece in zip(totals, grads)))
        kept_grad = store(kept_grad, chosen, active, grad_in)
        return (grad_in, kept_grad, totals)

    carried = lax.fori_loop(
        0, micro_count + section_count - 1, backward_tick, (blank_rows, blank_acts, blank_grads)
    )
    kept_grad, totals = (carried[1], carried[2])
    summed = (
        lax.psum_scatter(totals[0], "dp", scatter_dimension=0, tiled=True),
        lax.psum_scatter(totals[1], "dp", scatter_dimension=0, tiled=True),
        lax.psum_scatter(totals[2], "dp", scatter_dimension=0, tiled=True),
        lax.psum_scatter(totals[3], "dp", scatter_dimension=0, tiled=True),
        lax.psum_scatter(totals[4], "dp", scatter_dimension=0, tiled=True),
        lax.psum_scatter(totals[5], "dp", scatter_dimension=0, tiled=True),
        lax.psum_scatter(totals[6], "dp", scatter_dimension=0, tiled=True),
        lax.psum_scatter(totals[7], "dp", scatter_dimension=0, tiled=True),
    )
    grads_out = tuple((piece[None] for piece in summed))
    return (kept_out.reshape(1, -1, model_width), kept_grad.reshape(1, -1, model_width)) + grads_out


def solution(mesh):
    in_specs = (
        P("dp", None),
        P("dp", None),
        P("dp", None),
        P("section", "dp", None),
        P("section", "dp", None),
        P("section", "dp", None),
        P("section", "dp"),
        P("section", "dp"),
        P("section", "dp"),
        P("section", "dp"),
        P("section", "dp"),
    )
    out_specs = (
        P("section", "dp", None),
        P("section", "dp", None),
        P("section", "dp", None),
        P("section", "dp", None),
        P("section", "dp", None),
        P("section", "dp"),
        P("section", "dp"),
        P("section", "dp"),
        P("section", "dp"),
        P("section", "dp"),
    )
    return jax.shard_map(body, mesh=mesh, in_specs=in_specs, out_specs=out_specs, check_vma=False)
```

profile of v0, /device:TPU:1, one launch (start us, length us, event | category | flops | bytes accessed | tf_op | source)
XLA Modules:
  0.0 1821.1 jit_solution(4373425751466127973)
XLA Ops:
  19.4 126.2 %all-reduce.11 = (bf16[768]{0:T(1024)(128)(2,1)}, bf16[64]{0:T(256)(128)(2,1)}, bf16[64]{0:T(256)(128)(2,1)}, bf16[3072]{0:T(1024)(128)(2,1)}, bf16[768]{0:T(1024)(128)(2,1)S(1)}) all-reduce(bf16[768]{0:T(1024)(128)(2,1)S(1)} %dynamic-update-slice, bf16[64]{0:T(256)(128)(2,1)S(1)} %dynamic-update-slice.1, ...), channel_id=2, replica_groups=mesh['section'=4,'dp'=32] {'dp'}, use_global_device_ids=true, to_apply=%add | all-reduce | flops 4736 | bytes 18944 | tf_op jit(solution)/shard_map/all_gather | solution.py:206
  163.6 354.1 %while.55 = (s32[]{:T(128)}, f32[384,768]{1,0:T(8,128)}, f32[2,384,768]{2,1,0:T(8,128)S(1)}, f32[2,384,768]{2,1,0:T(8,128)}, f32[2,12,384]{2,1,0:T(8,128)}, /*in...) while((s32[]{:T(128)}, f32[384,768]{1,0:T(8,128)}, ...), condition=%wide.region_13.14_spmd.clone, body=%wide.region_2.13_spmd.clone.sunk | while | flops 5996902912 | bytes 211654256 | solution.py:240
  171.3 21.2 %collective-permute-done = f32[384,768]{1,0:T(8,128)S(1)} collective-permute-done((f32[384,768]{1,0:T(8,128)}, f32[384,768]{1,0:T(8,128)S(1)}, u32[]{:S(2)}, u32[]{:S(2)}) %collective-permute-start) | collective-permute-done | bytes 1179680 | tf_op jit(solution)/shard_map/while/body/eval_jaxpr/ppermute | solution.py:13
  193.8 61.8 %conditional.6 = (f32[384,768]{1,0:T(8,128)}, f32[12,384]{1,0:T(8,128)}) conditional(s32[]{:T(128)} %convert_element_type.240, () %tuple.136, (s32[2,384]{1,0:T(2,128)S(1)}, s32[]{:T(128)}, f32[384,768]{1,0:T(8,128)S(1)}, bf16[768]{0:T(1024)(128)(2,1)}, bf16[768,5376]{1,0:T(8,128)(2,1)S(1)}, /*index=5*/s32[2,384]{1,0:T(2,128)S(1)}, ...), branch_computations={%region_3.3_spmd, %region_4.12_spmd} | conditional | flops 5996013568 | bytes 145116592 | solution.py:231
  239.7 14.2 fusion.17
  265.4 20.6 %collective-permute-done = f32[384,768]{1,0:T(8,128)S(1)} collective-permute-done((f32[384,768]{1,0:T(8,128)}, f32[384,768]{1,0:T(8,128)S(1)}, u32[]{:S(2)}, u32[]{:S(2)}) %collective-permute-start) | collective-permute-done | bytes 1179680 | tf_op jit(solution)/shard_map/while/body/eval_jaxpr/ppermute | solution.py:13
  287.3 61.8 %conditional.6 = (f32[384,768]{1,0:T(8,128)}, f32[12,384]{1,0:T(8,128)}) conditional(s32[]{:T(128)} %convert_element_type.240, () %tuple.136, (s32[2,384]{1,0:T(2,128)S(1)}, s32[]{:T(128)}, f32[384,768]{1,0:T(8,128)S(1)}, bf16[768]{0:T(1024)(128)(2,1)}, bf16[768,5376]{1,0:T(8,128)(2,1)S(1)}, /*index=5*/s32[2,384]{1,0:T(2,128)S(1)}, ...), branch_computations={%region_3.3_spmd, %region_4.12_spmd} | conditional | flops 5996013568 | bytes 145116592 | solution.py:231
  362.8 19.7 %collective-permute-done = f32[384,768]{1,0:T(8,128)S(1)} collective-permute-done((f32[384,768]{1,0:T(8,128)}, f32[384,768]{1,0:T(8,128)S(1)}, u32[]{:S(2)}, u32[]{:S(2)}) %collective-permute-start) | collective-permute-done | bytes 1179680 | tf_op jit(solution)/shard_map/while/body/eval_jaxpr/ppermute | solution.py:13
  388.6 66.5 %collective-permute-start = (f32[384,768]{1,0:T(8,128)}, f32[384,768]{1,0:T(8,128)S(1)}, u32[]{:S(2)}, u32[]{:S(2)}) collective-permute-start(f32[384,768]{1,0:T(8,128)} %get-tuple-element.1782), channel_id=1, source_target_pairs={{0,32},{32,64},{64,96},{1,33},{33,65},{65,97},{2,34},{34,66},{66,9... | collective-permute-start | bytes 3538952 | tf_op jit(solution)/shard_map/while/body/eval_jaxpr/ppermute | solution.py:13
  459.3 18.7 %collective-permute-done = f32[384,768]{1,0:T(8,128)S(1)} collective-permute-done((f32[384,768]{1,0:T(8,128)}, f32[384,768]{1,0:T(8,128)S(1)}, u32[]{:S(2)}, u32[]{:S(2)}) %collective-permute-start) | collective-permute-done | bytes 1179680 | tf_op jit(solution)/shard_map/while/body/eval_jaxpr/ppermute | solution.py:13
  493.7 17.8 collective-permute-done
  520.3 993.9 %while.56 = (s32[]{:T(128)}, f32[384,768]{1,0:T(8,128)}, f32[2,384,768]{2,1,0:T(8,128)}, f32[768,5376]{1,0:T(8,128)}, f32[768,768]{1,0:T(8,128)}, /*index=5*/f32...) while((s32[]{:T(128)}, f32[384,768]{1,0:T(8,128)}, ...), condition=%wide.region_35.36_spmd.clone, body=%wide.region_14.35_spmd.clone.sunk | while | flops 15609911296 | bytes 495828608 | solution.py:283
  547.4 83.7 %collective-permute-done.1 = f32[384,768]{1,0:T(8,128)S(1)} collective-permute-done((f32[384,768]{1,0:T(8,128)}, f32[384,768]{1,0:T(8,128)S(1)}, u32[]{:S(2)}, u32[]{:S(2)}) %collective-permute-start.1) | collective-permute-done | bytes 1179680 | tf_op jit(solution)/shard_map/while/body/eval_jaxpr/ppermute | solution.py:13
  669.3 21.9 %collective-permute-done.1 = f32[384,768]{1,0:T(8,128)S(1)} collective-permute-done((f32[384,768]{1,0:T(8,128)}, f32[384,768]{1,0:T(8,128)S(1)}, u32[]{:S(2)}, u32[]{:S(2)}) %collective-permute-start.1) | collective-permute-done | bytes 1179680 | tf_op jit(solution)/shard_map/while/body/eval_jaxpr/ppermute | solution.py:13
  738.1 81.1 %collective-permute-done.1 = f32[384,768]{1,0:T(8,128)S(1)} collective-permute-done((f32[384,768]{1,0:T(8,128)}, f32[384,768]{1,0:T(8,128)S(1)}, u32[]{:S(2)}, u32[]{:S(2)}) %collective-permute-start.1) | collective-permute-done | bytes 1179680 | tf_op jit(solution)/shard_map/while/body/eval_jaxpr/ppermute | solution.py:13
  866.3 328.6 %collective-permute-done.1 = f32[384,768]{1,0:T(8,128)S(1)} collective-permute-done((f32[384,768]{1,0:T(8,128)}, f32[384,768]{1,0:T(8,128)S(1)}, u32[]{:S(2)}, u32[]{:S(2)}) %collective-permute-start.1) | collective-permute-done | bytes 1179680 | tf_op jit(solution)/shard_map/while/body/eval_jaxpr/ppermute | solution.py:13
  1194.9 114.5 %conditional.7 = (f32[384,768]{1,0:T(8,128)}, f32[768,5376]{1,0:T(8,128)S(1)}, f32[768,768]{1,0:T(8,128)}, f32[3072,768]{1,0:T(8,128)}, f32[768]{0:T(1024)}, /*i...) conditional(s32[]{:T(128)} %convert_element_type.241, () %tuple.141, (s32[2,384]{1,0:T(2,128)S(1)}, ...), branch_computations={%region_15.15_spmd, %region_16.34_spmd} | conditional | flops 15595451392 | bytes 371727968 | solution.py:278
  1261.2 16.2 fusion.114
  1346.0 19.3 %collective-permute-done.1 = f32[384,768]{1,0:T(8,128)S(1)} collective-permute-done((f32[384,768]{1,0:T(8,128)}, f32[384,768]{1,0:T(8,128)S(1)}, u32[]{:S(2)}, u32[]{:S(2)}) %collective-permute-start.1) | collective-permute-done | bytes 1179680 | tf_op jit(solution)/shard_map/while/body/eval_jaxpr/ppermute | solution.py:13
  1365.3 114.6 %conditional.7 = (f32[384,768]{1,0:T(8,128)}, f32[768,5376]{1,0:T(8,128)S(1)}, f32[768,768]{1,0:T(8,128)}, f32[3072,768]{1,0:T(8,128)}, f32[768]{0:T(1024)}, /*i...) conditional(s32[]{:T(128)} %convert_element_type.241, () %tuple.141, (s32[2,384]{1,0:T(2,128)S(1)}, ...), branch_computations={%region_15.15_spmd, %region_16.34_spmd} | conditional | flops 15595451392 | bytes 371727968 | solution.py:278
  1431.7 16.2 fusion.114
  1517.4 125.7 %all-reduce.10 = (f32[768]{0:T(1024)S(1)}, f32[64]{0:T(128)S(1)}, f32[64]{0:T(128)S(1)}, f32[3072]{0:T(1024)S(1)}, f32[768]{0:T(1024)S(1)}) all-reduce(f32[768]{0:T(1024)S(1)} %copy-done.51, f32[64]{0:T(128)S(1)} %copy-done.65, f32[64]{0:T(128)S(1)} %copy-done.68, ...), channel_id=13, replica_groups=mesh['section'=4,'dp'=32] {'dp'}, use_global_device_ids=true, to_apply=%region_39.40.clone | all-reduce | flops 4736 | bytes 37888
  1644.9 50.3 %reduce-scatter.8.cloned.1.call-done = f32[96,768]{1,0:T(8,128)} async-done(((f32[3072,768]{1,0:T(8,128)}), f32[96,768]{1,0:T(8,128)}) %reduce-scatter.8.cloned.1.call-update) | async-done | bytes 294928 | tf_op jit(solution)/shard_map/reduce_scatter | solution.py:290
  1695.2 118.9 %reduce-scatter.4.cloned.1.call-done = f32[24,5376]{1,0:T(8,128)} async-done(((f32[768,5376]{1,0:T(8,128)}), f32[24,5376]{1,0:T(8,128)}) %reduce-scatter.4.cloned.1.call-update) | async-done | bytes 516112 | tf_op jit(solution)/shard_map/reduce_scatter | solution.py:288
  (848 shorter events, 645.5 us)
Async XLA Ops:
  7.2 138.8 %all-gather.14.cloned.1.call-start = ((), (), s32[]{:S(2)}) async-start(), calls=%async_computation.7 | async-start | bytes 1216512 | tf_op jit(solution)/shard_map/all_gather | solution.py:204
  7.9 138.1 %all-gather.16.cloned.1.call-start = ((), (), s32[]{:S(2)}) async-start(), calls=%async_computation.8 | async-start | bytes 4866048 | tf_op jit(solution)/shard_map/all_gather | solution.py:205
  8.7 151.5 %all-gather.12.cloned.1.call-start = ((), (), s32[]{:S(2)}) async-start(), calls=%async_computation.6 | async-start | bytes 8515584 | tf_op jit(solution)/shard_map/all_gather | solution.py:203
  9.4 1635.5 %reduce-scatter.6.cloned.1.call-start = ((), (), s32[]{:S(2)}) async-start(), calls=%async_computation.4 | async-start | bytes 2433024 | tf_op jit(solution)/shard_map/reduce_scatter | solution.py:289
  164.0 28.5 %collective-permute-start = (f32[384,768]{1,0:T(8,128)}, f32[384,768]{1,0:T(8,128)S(1)}, u32[]{:S(2)}, u32[]{:S(2)}) collective-permute-start(f32[384,768]{1,0:T(8,128)} %get-tuple-element.1782), channel_id=1, source_target_pairs={{0,32},{32,64},{64,96},{1,33},{33,65},{65,97},{2,34},{34,66},{66,9... | collective-permute-start | bytes 3538952 | tf_op jit(solution)/shard_map/while/body/eval_jaxpr/ppermute | solution.py:13
  259.8 26.1 %collective-permute-start = (f32[384,768]{1,0:T(8,128)}, f32[384,768]{1,0:T(8,128)S(1)}, u32[]{:S(2)}, u32[]{:S(2)}) collective-permute-start(f32[384,768]{1,0:T(8,128)} %get-tuple-element.1782), channel_id=1, source_target_pairs={{0,32},{32,64},{64,96},{1,33},{33,65},{65,97},{2,34},{34,66},{66,9... | collective-permute-start | bytes 3538952 | tf_op jit(solution)/shard_map/while/body/eval_jaxpr/ppermute | solution.py:13
  353.3 29.2 %collective-permute-start = (f32[384,768]{1,0:T(8,128)}, f32[384,768]{1,0:T(8,128)S(1)}, u32[]{:S(2)}, u32[]{:S(2)}) collective-permute-start(f32[384,768]{1,0:T(8,128)} %get-tuple-element.1782), channel_id=1, source_target_pairs={{0,32},{32,64},{64,96},{1,33},{33,65},{65,97},{2,34},{34,66},{66,9... | collective-permute-start | bytes 3538952 | tf_op jit(solution)/shard_map/while/body/eval_jaxpr/ppermute | solution.py:13
  388.6 90.7 %copy-start.69 = (s32[2]{0:T(128)}, s32[2]{0:T(128)S(1)}, u32[]{:S(2)}) copy-start(s32[2]{0:T(128)S(1)} %get-tuple-element.1819) | copy-start | bytes 28 | tf_op jit(solution)/shard_map/while
  388.6 89.4 %collective-permute-start = (f32[384,768]{1,0:T(8,128)}, f32[384,768]{1,0:T(8,128)S(1)}, u32[]{:S(2)}, u32[]{:S(2)}) collective-permute-start(f32[384,768]{1,0:T(8,128)} %get-tuple-element.1782), channel_id=1, source_target_pairs={{0,32},{32,64},{64,96},{1,33},{33,65},{65,97},{2,34},{34,66},{66,9... | collective-permute-start | bytes 3538952 | tf_op jit(solution)/shard_map/while/body/eval_jaxpr/ppermute | solution.py:13
  484.2 27.3 %collective-permute-start = (f32[384,768]{1,0:T(8,128)}, f32[384,768]{1,0:T(8,128)S(1)}, u32[]{:S(2)}, u32[]{:S(2)}) collective-permute-start(f32[384,768]{1,0:T(8,128)} %get-tuple-element.1782), channel_id=1, source_target_pairs={{0,32},{32,64},{64,96},{1,33},{33,65},{65,97},{2,34},{34,66},{66,9... | collective-permute-start | bytes 3538952 | tf_op jit(solution)/shard_map/while/body/eval_jaxpr/ppermute | solution.py:13
  543.6 87.5 %copy-start.71 = (s32[2]{0:T(128)}, s32[2]{0:T(128)S(1)}, u32[]{:S(2)}) copy-start(s32[2]{0:T(128)S(1)} %get-tuple-element.1903) | copy-start | bytes 28 | tf_op jit(solution)/shard_map/while
  543.6 87.5 %copy-start.1 = (f32[2,384,768]{2,1,0:T(8,128)}, f32[2,384,768]{2,1,0:T(8,128)S(1)}, u32[]{:S(2)}) copy-start(f32[2,384,768]{2,1,0:T(8,128)S(1)} %get-tuple-element.1893) | copy-start | bytes 7077892 | tf_op jit(solution)/shard_map/while
  543.6 87.5 %copy-start.56 = (s32[2,384]{1,0:T(2,128)}, s32[2,384]{1,0:T(2,128)S(1)}, u32[]{:S(2)}) copy-start(s32[2,384]{1,0:T(2,128)S(1)} %get-tuple-element.1897) | copy-start | bytes 9220 | tf_op jit(solution)/shard_map/while
  543.6 87.5 %collective-permute-start.1 = (f32[384,768]{1,0:T(8,128)}, f32[384,768]{1,0:T(8,128)S(1)}, u32[]{:S(2)}, u32[]{:S(2)}) collective-permute-start(f32[384,768]{1,0:T(8,128)} %get-tuple-element.1852), channel_id=1, source_target_pairs={{32,0},{64,32},{96,64},{33,1},{65,33},{97,65},{34,2},{66,34},{98,6... | collective-permute-start | bytes 3538952 | tf_op jit(solution)/shard_map/while/body/eval_jaxpr/ppermute | solution.py:13
  665.4 25.7 %collective-permute-start.1 = (f32[384,768]{1,0:T(8,128)}, f32[384,768]{1,0:T(8,128)S(1)}, u32[]{:S(2)}, u32[]{:S(2)}) collective-permute-start(f32[384,768]{1,0:T(8,128)} %get-tuple-element.1852), channel_id=1, source_target_pairs={{32,0},{64,32},{96,64},{33,1},{65,33},{97,65},{34,2},{66,34},{98,6... | collective-permute-start | bytes 3538952 | tf_op jit(solution)/shard_map/while/body/eval_jaxpr/ppermute | solution.py:13
  734.3 84.9 %collective-permute-start.1 = (f32[384,768]{1,0:T(8,128)}, f32[384,768]{1,0:T(8,128)S(1)}, u32[]{:S(2)}, u32[]{:S(2)}) collective-permute-start(f32[384,768]{1,0:T(8,128)} %get-tuple-element.1852), channel_id=1, source_target_pairs={{32,0},{64,32},{96,64},{33,1},{65,33},{97,65},{34,2},{66,34},{98,6... | collective-permute-start | bytes 3538952 | tf_op jit(solution)/shard_map/while/body/eval_jaxpr/ppermute | solution.py:13
  862.4 332.4 %copy-start.71 = (s32[2]{0:T(128)}, s32[2]{0:T(128)S(1)}, u32[]{:S(2)}) copy-start(s32[2]{0:T(128)S(1)} %get-tuple-element.1903) | copy-start | bytes 28 | tf_op jit(solution)/shard_map/while
  862.4 332.4 %copy-start.1 = (f32[2,384,768]{2,1,0:T(8,128)}, f32[2,384,768]{2,1,0:T(8,128)S(1)}, u32[]{:S(2)}) copy-start(f32[2,384,768]{2,1,0:T(8,128)S(1)} %get-tuple-element.1893) | copy-start | bytes 7077892 | tf_op jit(solution)/shard_map/while
  862.5 332.4 %copy-start.56 = (s32[2,384]{1,0:T(2,128)}, s32[2,384]{1,0:T(2,128)S(1)}, u32[]{:S(2)}) copy-start(s32[2,384]{1,0:T(2,128)S(1)} %get-tuple-element.1897) | copy-start | bytes 9220 | tf_op jit(solution)/shard_map/while
  862.5 332.4 %collective-permute-start.1 = (f32[384,768]{1,0:T(8,128)}, f32[384,768]{1,0:T(8,128)S(1)}, u32[]{:S(2)}, u32[]{:S(2)}) collective-permute-start(f32[384,768]{1,0:T(8,128)} %get-tuple-element.1852), channel_id=1, source_target_pairs={{32,0},{64,32},{96,64},{33,1},{65,33},{97,65},{34,2},{66,34},{98,6... | collective-permute-start | bytes 3538952 | tf_op jit(solution)/shard_map/while/body/eval_jaxpr/ppermute | solution.py:13
  863.8 331.1 %copy-start.26 = (f32[2,384,768]{2,1,0:T(8,128)S(1)}, f32[2,384,768]{2,1,0:T(8,128)}, u32[]{:S(2)}) copy-start(f32[2,384,768]{2,1,0:T(8,128)} %get-tuple-element.1892) | copy-start | bytes 7077892 | tf_op jit(solution)/shard_map/while
  1342.2 23.1 %collective-permute-start.1 = (f32[384,768]{1,0:T(8,128)}, f32[384,768]{1,0:T(8,128)S(1)}, u32[]{:S(2)}, u32[]{:S(2)}) collective-permute-start(f32[384,768]{1,0:T(8,128)} %get-tuple-element.1852), channel_id=1, source_target_pairs={{32,0},{64,32},{96,64},{33,1},{65,33},{97,65},{34,2},{66,34},{98,6... | collective-permute-start | bytes 3538952 | tf_op jit(solution)/shard_map/while/body/eval_jaxpr/ppermute | solution.py:13
  1514.2 181.0 %reduce-scatter.8.cloned.1.call-start = ((), (), s32[]{:S(2)}) async-start(), calls=%async_computation.5 | async-start | bytes 9732096 | tf_op jit(solution)/shard_map/reduce_scatter | solution.py:290
  1514.8 299.3 %reduce-scatter.4.cloned.1.call-start = ((), (), s32[]{:S(2)}) async-start(), calls=%async_computation.3 | async-start | bytes 17031168 | tf_op jit(solution)/shard_map/reduce_scatter | solution.py:288
  (236 other events, 1857.0 us)
Sparse Core Ops, SparseCore 0:
  10.3 46.7 all-gather.13
  59.4 46.3 all-gather.15
  108.1 52.0 all-gather.11
  1514.3 81.4 reduce-scatter.5
  1600.5 94.6 reduce-scatter.7
  1699.6 114.4 reduce-scatter.3
where the time goes:
time: 1830 us; the launch traced here: 1820 us
  waiting for transfers between devices  819 us (45%)
  blocking collectives  252 us (14%)
  other arithmetic  238 us (13%)
  matrix products  206 us (11%)
  local copies, waits for them, and re-layouts  171 us (9%)
  starting transfers between devices  88.4 us (5%)
  loops' own time  28.2 us (2%)
  between operations  18.4 us (1%)
    ppermute x10, waiting for transfers between devices, shifted(): return lax.ppermute(x, axis, pairs)  632 us
    add x30, other arithmetic, backward_tick(): totals = tuple((total + piece for total, piece in zip(totals, grads)))  137 us
    all_gather x1, blocking collectives, body(): lax.all_gather(norm_gain[0], 'dp', axis=0, tiled=True)  126 us
    unnamed x1, blocking collectives  126 us
    reduce_scatter x1, waiting for transfers between devices, body(): lax.psum_scatter(totals[0], 'dp', scatter_dimension=0, tiled=True)  119 us
    ppermute x10, starting transfers between devices, shifted(): return lax.ppermute(x, axis, pairs)  88.1 us
    reduce_scatter x1, waiting for transfers between devices, body(): lax.psum_scatter(totals[2], 'dp', scatter_dimension=0, tiled=True)  50.3 us
  transfers between devices with their start and end apart: 16, of which 13 were waited for; matrix products, arithmetic and copies ran while one was open for 2% of the time, Pallas kernels for 0%

commit v1 on v0

v1 whole, which is shorter than its diff:
```python
from functools import partial
import math

import jax
import jax.numpy as jnp
from jax import lax
from jax.experimental import pallas as pl
from jax.experimental.pallas import tpu as pltpu
from jax.sharding import PartitionSpec as P

BF = jnp.bfloat16
F32 = jnp.float32
VMEM_LIMIT = 60 * 1024 * 1024
EPS = 1e-06
NN = (((1,), (0,)), ((), ()))
NT = (((1,), (1,)), ((), ()))
LANES = 128
WIDE = 256
ABSENT = 16


def mm(a, b, dims=NN):
    return lax.dot_general(a, b, dims, preferred_element_type=F32)


def head_mean(x, spread, exact):
    parts = []
    for at in range(0, x.shape[1], WIDE):
        piece = x[:, at : at + WIDE]
        top = piece.astype(BF)
        total = mm(top, spread)
        if exact:
            total = total + mm((piece - top.astype(F32)).astype(BF), spread)
        parts.append(total)
    return jnp.concatenate(parts, axis=1)


def row_norm(x):
    centered = x - jnp.mean(x, axis=-1, keepdims=True)
    rstd = lax.rsqrt(jnp.mean(centered * centered, axis=-1, keepdims=True) + EPS)
    return centered * rstd, rstd


def norm_back(grad, normal, rstd, spread):
    return rstd * (grad - head_mean(grad, spread, False) - normal * head_mean(grad * normal, spread, False))


def lane_half(x, second):
    lane = lax.broadcasted_iota(jnp.int32, x.shape, 1)
    return jnp.where((lane >= LANES // 2) if second else (lane < LANES // 2), x, jnp.zeros_like(x))


class Copies:
    def __init__(self, sems):
        self.sems, self.used = sems, 0

    def start(self, src, dst):
        copy = pltpu.make_async_copy(src, dst, self.sems.at[self.used])
        self.used += 1
        copy.start()
        return copy


def forward_kernel(d, ff, chunks, idx, tok, recv, g, g3, ids_col, ids_row, ngain, gains, ubias, obias, spread, *refs):
    refs = refs[13:]
    ybf, refs = refs[0], refs[1:]
    xs, hs, qs, ks, vs, ns, nrs, acts, gps, es, small = refs[:11]
    at_out, y_out = refs[11:13]
    (x_v, h_v, w_v, u_v, d_v, a_v, q_v, k_v, v_v, n_v, r_v, act_v, gp_v, e_v, rs_v, at_v, att_v, acc_v, y_v, ins, outs) = refs[13:]
    rows = x_v.shape[0]
    fc = ff // chunks
    which, st = idx[0], idx[1]
    cin, cout = Copies(ins), Copies(outs)

    @pl.when(idx[2] == 1)
    def _():
        pltpu.make_async_copy(tok.at[which], x_v, ins.at[0]).start()

    @pl.when(idx[2] != 1)
    def _():
        pltpu.make_async_copy(recv, x_v, ins.at[0]).start()

    cin.used = 1
    wq = [cin.start(g.at[:, pl.ds(ff + d * i, d)], w_v.at[:, pl.ds(d * i, d)]) for i in range(3)]
    groups = fc // WIDE
    wff = []
    for c in range(chunks):
        wff.append([cin.start(g.at[:, pl.ds(fc * c, fc)], u_v.at[c])] + [
            cin.start(g3.at[pl.ds(groups * c, groups), :, pl.ds(ff + 4 * d + d * j, d)], d_v.at[pl.ds(groups * c, groups), j])
            for j in range(4)
        ])
    wa = cin.start(g.at[:, pl.ds(ff + 3 * d, d)], a_v)

    pending = []
    pltpu.make_async_copy(recv, x_v, ins.at[0]).wait()
    keep = jnp.where(ids_col[0] < ABSENT, 1.0, 0.0)
    masked = keep * x_v[...].astype(F32)
    h_v[...] = (row_norm(masked)[0] * ngain[...]).astype(BF)
    pending += [cout.start(x_v, xs.at[st]), cout.start(h_v, hs.at[st])]
    bias_mask = jnp.where(ids_col[0] == ids_row[0], 0.0, -1e9)
    for i in range(3):
        wq[i].wait()
        raw = mm(h_v[...], w_v[:, d * i : d * i + d])
        if i == 2:
            v_v[...] = raw.astype(BF)
            pending.append(cout.start(v_v, vs.at[st]))
        else:
            centered = raw - head_mean(raw, spread[...], True)
            rstd = lax.rsqrt(head_mean(centered * centered, spread[...], True) + EPS)
            normal = centered * rstd
            scaled = (normal * gains[i]).astype(BF)
            n_v[:, d * i : d * i + d] = normal.astype(BF)
            r_v[:, d * i : d * i + d] = rstd.astype(BF)
            if i == 0:
                q_v[...] = scaled * jnp.asarray(0.125, BF)
                pending.append(cout.start(q_v, qs.at[st]))
            else:
                k_v[...] = scaled
                pending.append(cout.start(k_v, ks.at[st]))
    pending += [cout.start(n_v, ns.at[st]), cout.start(r_v, nrs.at[st])]
    ones = jnp.ones((16, rows), BF)
    pairs = d // LANES // chunks
    for c in range(chunks):
        for copy in wff[c]:
            copy.wait()
        pre = mm(h_v[...], u_v[c]) + ubias[:, fc * c : fc * c + fc]
        cdf = 0.5 * (1.0 + lax.erf(pre * (1.0 / math.sqrt(2.0))))
        density = jnp.exp(-0.5 * pre * pre) * (1.0 / math.sqrt(2.0 * math.pi))
        act = (pre * cdf).astype(BF)
        act_v[c] = act
        gp_v[c] = (cdf + pre * density).astype(BF)
        total = mm(act, d_v[groups * c : groups * c + groups].reshape(fc, d))
        if c == 0:
            acc_v[...] = total
        else:
            acc_v[...] += total
        for p in range(pairs * c, pairs * c + pairs):
            cols = slice(LANES * p, LANES * p + LANES)
            vals_t = v_v[:, cols].T
            pair = q_v[:, cols]
            both = []
            for half in range(2):
                h = 2 * p + half
                e = jnp.exp(mm(k_v[:, cols], lane_half(pair, half), NT) + bias_mask).astype(BF)
                e_v[h] = e
                got = mm(jnp.concatenate([vals_t[64 * half : 64 * half + 64], ones], axis=0), e)
                inv = 1.0 / got[64:65]
                rs_v[h : h + 1, :] = inv
                both.append((got[:64] * inv).astype(BF))
            both = jnp.concatenate(both, axis=0)
            at_v[cols, :] = both
            att_v[:, cols] = both.T
        pending += [cout.start(act_v.at[c], acts.at[st, c]), cout.start(gp_v.at[c], gps.at[st, c]),
                    cout.start(e_v.at[pl.ds(2 * pairs * c, 2 * pairs)], es.at[st, pl.ds(2 * pairs * c, 2 * pairs)])]
    pending += [cout.start(rs_v, small.at[st]), cout.start(at_v, at_out.at[st])]
    wa.wait()
    y = keep * (keep * x_v[...].astype(F32) + acc_v[...] + mm(att_v[...], a_v[...]) + obias[...])
    y_v[...] = y
    ybf[...] = y.astype(BF)
    pending.append(cout.start(y_v, y_out.at[st]))
    for copy in pending:
        copy.wait()


def backward_kernel(d, ff, chunks, idx, seed, recv, g, g3, ids_col, ngain, gains, spread, *refs):
    xs, qs, ks, vs, ns, nrs, gps, es, small, ats = refs[:10]
    refs = refs[10:]
    refs = refs[5 + 5 :]
    gbf, refs = refs[0], refs[1:]
    gbs, gjs, gqs, gks, gvs, refs = refs[0], refs[1], refs[2], refs[3], refs[4], refs[5:]
    grs, obs, ngs, qkgs, ubs, refs = refs[0], refs[1], refs[2], refs[3], refs[4], refs[5:]
    (g_v, gb_v, w_v, u_v, d_v, a_v, x_v, q_v, k_v, v_v, n_v, r_v, gp_v, e_v, rs_v, at_v, gat_v, gqt_v, gk_v,
     gq_b, gk_b, gv_b, gj_v, acc_v, out_v, ob_v, ng_v, qk_v, ub_v, ins, outs) = refs
    rows = x_v.shape[0]
    fc = ff // chunks
    groups = fc // WIDE
    which, st = idx[0], idx[1]
    cin, cout = Copies(ins), Copies(outs)

    @pl.when(idx[2] == 1)
    def _():
        pltpu.make_async_copy(seed.at[which], g_v, ins.at[0]).start()

    @pl.when(idx[2] != 1)
    def _():
        pltpu.make_async_copy(recv, g_v, ins.at[0]).start()

    cin.used = 1
    wa = cin.start(g.at[:, pl.ds(ff + 3 * d, d)], a_v)
    heads = [cin.start(s.at[which], v) for s, v in ((small, rs_v), (ats, at_v), (ks, k_v), (vs, v_v), (qs, q_v))]
    pairs = d // LANES // chunks
    wff = []
    for c in range(chunks):
        wff.append(
            [cin.start(g3.at[pl.ds(groups * c, groups), :, pl.ds(ff + 4 * d + d * j, d)], d_v.at[pl.ds(groups * c, groups), j])
             for j in range(4)]
            + [cin.start(gps.at[which, c], gp_v.at[c]), cin.start(g.at[:, pl.ds(fc * c, fc)], u_v.at[c]),
               cin.start(es.at[which, pl.ds(2 * pairs * c, 2 * pairs)], e_v.at[pl.ds(2 * pairs * c, 2 * pairs)])]
        )
    norms = [cin.start(ns.at[which], n_v), cin.start(nrs.at[which], r_v)]
    wq = [cin.start(g.at[:, pl.ds(ff + d * i, d)], w_v.at[:, pl.ds(d * i, d)]) for i in range(3)]
    rows_in = cin.start(xs.at[which], x_v)

    pending = []
    pltpu.make_async_copy(recv, g_v, ins.at[0]).wait()
    keep = jnp.where(ids_col[0] < ABSENT, 1.0, 0.0)
    gres = keep * g_v[...].astype(F32)
    ob_v[...] = jnp.sum(gres, axis=0, keepdims=True)
    gb_v[...] = gres.astype(BF)
    pending += [cout.start(gb_v, gbs.at[st]), cout.start(ob_v, obs.at[st])]
    wa.wait()
    gat_v[...] = mm(a_v[...], gb_v[...], NT).astype(BF)
    for copy in heads:
        copy.wait()
    zeros = jnp.zeros((LANES // 2, rows), BF)
    for c in range(chunks):
        for copy in wff[c]:
            copy.wait()
        gup = mm(gb_v[...], d_v[groups * c : groups * c + groups].reshape(fc, d), NT) * gp_v[c].astype(F32)
        ub_v[:, fc * c : fc * c + fc] = jnp.sum(gup, axis=0, keepdims=True)
        gup = gup.astype(BF)
        gj_v[c] = gup
        pending.append(cout.start(gj_v.at[c], gjs.at[st, c]))
        total = mm(gup, u_v[c], NT)
        if c == 0:
            acc_v[...] = total
        else:
            acc_v[...] += total
        for p in range(pairs * c, pairs * c + pairs):
            cols = slice(LANES * p, LANES * p + LANES)
            keys, vals, pair = k_v[:, cols], v_v[:, cols], q_v[:, cols]
            keys_t = keys.T
            gk, gv = None, None
            for half in range(2):
                h = 2 * p + half
                at_rows = slice(64 * h, 64 * h + 64)
                inv = rs_v[h : h + 1, :]
                ga = (gat_v[at_rows, :].astype(F32) * inv).astype(BF)
                ga = jnp.concatenate([zeros, ga] if half else [ga, zeros], axis=0)
                e = e_v[h]
                ef = e.astype(F32)
                gp = ef * mm(vals, ga)
                dot = jnp.sum(gp, axis=0, keepdims=True) * inv
                gs = (gp - ef * dot).astype(BF)
                gk_h = mm(gs, lane_half(pair, half))
                gv_h = mm(e, ga, NT)
                gk = gk_h if gk is None else gk + gk_h
                gv = gv_h if gv is None else gv + gv_h
                gqt_v[at_rows, :] = mm(keys_t[64 * half : 64 * half + 64], gs) * 0.125
            gk_v[:, cols] = gk
            gv_b[:, cols] = gv.astype(BF)
    pending += [cout.start(ub_v, ubs.at[st]), cout.start(gv_b, gvs.at[st])]
    for copy in norms:
        copy.wait()
    for i, (grad, out, stack) in enumerate(((gqt_v[...].T, gq_b, gqs), (gk_v[...], gk_b, gks))):
        normal = n_v[:, d * i : d * i + d].astype(F32)
        qk_v[:, d * i : d * i + d] = jnp.sum(grad * normal, axis=0, keepdims=True)
        out[...] = norm_back(grad * gains[i], normal, r_v[:, d * i : d * i + d].astype(F32), spread[...]).astype(BF)
        pending.append(cout.start(out, stack.at[st]))
    pending.append(cout.start(qk_v, qkgs.at[st]))
    for copy in wq:
        copy.wait()
    ghid = acc_v[...]
    for i, part in enumerate((gq_b, gk_b, gv_b)):
        ghid = ghid + mm(part[...], w_v[:, d * i : d * i + d], NT)
    rows_in.wait()
    xhat, rstd = row_norm(keep * x_v[...].astype(F32))
    ng_v[...] = jnp.sum(ghid * xhat, axis=0, keepdims=True)
    gx = ghid * ngain[...]
    gmask = rstd * (gx - jnp.mean(gx, axis=-1, keepdims=True) - xhat * jnp.mean(gx * xhat, axis=-1, keepdims=True))
    out = keep * (keep * g_v[...].astype(F32) + gmask)
    out_v[...] = out
    gbf[...] = out.astype(BF)
    pending += [cout.start(out_v, grs.at[st]), cout.start(ng_v, ngs.at[st])]
    for copy in pending:
        copy.wait()


ANY = pl.BlockSpec(memory_space=pl.ANY)


def whole(shape):
    return pl.BlockSpec(shape, lambda i, idx: (0,) * len(shape))


def pick(shape):
    return pl.BlockSpec((1,) + shape, lambda i, idx: (idx[0],) + (0,) * len(shape))


def call(kernel, idx, ins, fresh, stashes, scratch, flops):
    outs = pl.pallas_call(
        kernel,
        grid_spec=pltpu.PrefetchScalarGridSpec(
            num_scalar_prefetch=1,
            grid=(1,),
            in_specs=[s for _, s in ins] + [ANY] * len(stashes),
            out_specs=[whole(fresh[0])] + [ANY] * len(stashes),
            scratch_shapes=scratch,
        ),
        out_shape=[jax.ShapeDtypeStruct(*fresh)] + [jax.ShapeDtypeStruct(a.shape, a.dtype) for a in stashes],
        input_output_aliases={1 + len(ins) + i: 1 + i for i in range(len(stashes))},
        compiler_params=pltpu.CompilerParams(dimension_semantics=("arbitrary",), vmem_limit_bytes=VMEM_LIMIT),
        cost_estimate=pl.CostEstimate(flops=flops, bytes_accessed=30 << 20, transcendentals=0),
    )(idx, *[a for a, _ in ins], *stashes)
    return outs[0], outs[1:]


def shifted(x, by):
    devices = lax.axis_size("section")
    return lax.ppermute(x, "section", [(i, i + by) for i in range(devices) if 0 <= i + by < devices])


def summed_everywhere(x):
    devices = lax.axis_size("dp")
    step = 1
    while step < devices:
        x = x + lax.ppermute(x, "dp", [(i, i ^ step) for i in range(devices)])
        step *= 2
    return x


def body(tokens, cotangent, lengths, proj_in, proj_attn, proj_down, norm_gain, query_gain, key_gain, up_bias, out_bias):
    sections = lax.axis_size("section")
    ranks = lax.axis_size("dp")
    section = lax.axis_index("section")
    rank = lax.axis_index("dp")
    slots = lengths.shape[0]
    rows = tokens.shape[0] // slots
    d = tokens.shape[1]
    joined = proj_in.shape[2]
    ff = proj_down.shape[1] * ranks
    head = query_gain.shape[1] * ranks
    heads = d // head
    dshare = proj_in.shape[1]
    fshare = proj_down.shape[1] // dshare
    hshare = query_gain.shape[1]
    chunks = 3
    ticks = slots + sections - 1
    wide = joined + d + ff

    place = jnp.arange(WIDE, dtype=jnp.int32)
    source = (place % (WIDE // fshare)) * fshare + place // (WIDE // fshare)
    shuffle = (place[:, None] == source[None, :]).astype(BF)

    def shuffled(x, back=False):
        flat = x.reshape(-1, WIDE)
        out = lax.dot_general(flat, shuffle, NT if back else NN, preferred_element_type=F32)
        return out.reshape(x.shape)

    small = jnp.concatenate(
        [
            norm_gain[0][:, None],
            out_bias[0][:, None],
            up_bias[0].reshape(dshare, fshare),
            jnp.pad(query_gain[0], (0, dshare - hshare))[:, None],
            jnp.pad(key_gain[0], (0, dshare - hshare))[:, None],
            jnp.zeros((dshare, LANES - 4 - fshare), BF),
        ],
        axis=1,
    )
    heads_part = joined - ff
    local = jnp.concatenate(
        [shuffled(proj_in[0][:, heads_part:]).astype(BF), proj_in[0][:, :heads_part], proj_attn[0],
         proj_down[0].reshape(dshare, fshare * d), small],
        axis=1,
    )
    g = lax.all_gather(local, "dp", axis=0, tiled=True)
    g3 = g.reshape(ff // WIDE, WIDE // fshare, g.shape[1])
    tail = g[:, wide : wide + LANES].astype(F32)
    ngain = tail[:, 0].reshape(1, d)
    obias = tail[:, 1].reshape(1, d)
    ubias = shuffled(tail[:, 2 : 2 + fshare].reshape(1, ff).astype(BF))
    qk_gain = tail[:, 2 + fshare : 4 + fshare].reshape(ranks, dshare, 2)[:, :hshare].reshape(head, 2).T
    gains = jnp.tile(qk_gain, (1, heads)).reshape(2, 1, d)
    column = jnp.arange(WIDE, dtype=jnp.int32) // head
    spread = jnp.where(column[:, None] == column[None, :], 1.0 / head, 0.0).astype(BF)

    toks = tokens.reshape(slots, rows, d)
    seeds = cotangent.reshape(slots, rows, d)
    ends = jnp.cumsum(lengths, axis=-1)
    position = jnp.arange(rows, dtype=jnp.int32)
    image = jnp.sum((position[None, :, None] >= ends[:, None, :]).astype(jnp.int32), axis=-1)
    image = jnp.where(position[None, :] < ends[:, 2:3], image, ABSENT + position[None, :])
    ids_col, ids_row = image[:, :, None], image[:, None, :]

    def stash(*shape, dtype=BF):
        return pl.pallas_call(
            lambda out: None,
            out_shape=jax.ShapeDtypeStruct((slots + 1,) + shape, dtype),
            out_specs=pl.BlockSpec(memory_space=pl.ANY),
        )()

    fc = ff // chunks
    groups = ff // WIDE
    kept = [stash(rows, d), stash(rows, d), stash(rows, d), stash(rows, d), stash(rows, d), stash(rows, 2 * d), stash(rows, 2 * d),
            stash(chunks, rows, fc), stash(chunks, rows, fc), stash(heads, rows, rows), stash(16, rows, dtype=F32),
            stash(d, rows), stash(rows, d, dtype=F32)]

    def index_of(tick, distance, first):
        which = tick - distance
        active = (which >= 0) & (which < slots)
        return jnp.stack(
            [jnp.clip(which, 0, slots - 1), jnp.where(active, which, slots), first.astype(jnp.int32)]
        ).astype(jnp.int32)

    V = pltpu.VMEM
    weights_v = [V((d, heads_part), BF), V((chunks, d, fc), BF), V((groups, fshare, WIDE // fshare, d), BF), V((d, d), BF)]
    sems = [pltpu.SemaphoreType.DMA((48,)), pltpu.SemaphoreType.DMA((48,))]
    smalls = [(ngain, whole((1, d))), (gains, whole((2, 1, d)))]
    nothing = jnp.zeros((rows, d), BF)
    recv = nothing
    for t in range(ticks):
        ybf, kept = call(
            partial(forward_kernel, d, ff, chunks),
            index_of(t, section, section == 0),
            [(toks, ANY), (recv, ANY), (g, ANY), (g3, ANY), (ids_col, pick((rows, 1))), (ids_row, pick((1, rows)))] + smalls
            + [(ubias, whole((1, ff))), (obias, whole((1, d))), (spread, whole((WIDE, WIDE)))],
            ((rows, d), BF),
            kept,
            [V((rows, d), BF), V((rows, d), BF)] + weights_v
            + [V((rows, d), BF)] * 3 + [V((rows, 2 * d), BF)] * 2 + [V((chunks, rows, fc), BF)] * 2
            + [V((heads, rows, rows), BF), V((16, rows), F32), V((d, rows), BF), V((rows, d), BF), V((rows, d), F32), V((rows, d), F32)]
            + sems,
            2 * rows * (d * wide + 2 * rows * d),
        )
        if t < ticks - 1:
            recv = shifted(ybf, 1)

    xs, hs, qs, ks, vs, ns, nrs, acts, gps, es, rsums, ats, ys = kept
    back = [stash(rows, d), stash(chunks, rows, fc), stash(rows, d), stash(rows, d), stash(rows, d),
            stash(rows, d, dtype=F32), stash(1, d, dtype=F32), stash(1, d, dtype=F32), stash(1, 2 * d, dtype=F32), stash(1, ff, dtype=F32)]
    recv = nothing
    for t in range(ticks):
        gbf, back = call(
            partial(backward_kernel, d, ff, chunks),
            index_of(t, sections - 1 - section, section == sections - 1),
            [(seeds, ANY), (recv, ANY), (g, ANY), (g3, ANY), (ids_col, pick((rows, 1)))] + smalls + [(spread, whole((WIDE, WIDE)))]
            + [(a, ANY) for a in (xs, qs, ks, vs, ns, nrs, gps, es, rsums, ats)],
            ((rows, d), BF),
            back,
            [V((rows, d), BF), V((rows, d), BF)] + weights_v
            + [V((rows, d), BF)] * 4 + [V((rows, 2 * d), BF)] * 2
            + [V((chunks, rows, fc), BF), V((heads, rows, rows), BF), V((16, rows), F32), V((d, rows), BF)]
            + [V((d, rows), BF), V((d, rows), F32), V((rows, d), F32)]
            + [V((rows, d), BF)] * 3 + [V((chunks, rows, fc), BF), V((rows, d), F32), V((rows, d), F32)]
            + [V((1, d), F32), V((1, d), F32), V((1, 2 * d), F32), V((1, ff), F32)]
            + sems,
            2 * rows * (d * wide + 4 * rows * d),
        )
        if t < ticks - 1:
            recv = shifted(gbf, -1)

    gbs, gjs, gqs, gks, gvs, grs, obs, ngs, qkgs, ubs = back

    def over_rows(left, right):
        return jnp.einsum("md,mj->dj", left[:slots].reshape(-1, left.shape[-1]), right[:slots].reshape(-1, right.shape[-1]),
                          preferred_element_type=F32).astype(BF)

    g_up = [jnp.einsum("smd,smj->dj", hs[:slots], gjs[:slots, c], preferred_element_type=F32).astype(BF) for c in range(chunks)]
    g_heads = [over_rows(hs, v) for v in (gqs, gks, gvs)]
    g_attn = jnp.einsum("sdm,smj->dj", ats[:slots], gbs[:slots], preferred_element_type=F32).astype(BF)
    g_down = [jnp.einsum("smf,smj->fj", acts[:slots, c], gbs[:slots], preferred_element_type=F32).astype(BF) for c in range(chunks)]
    g_down = jnp.concatenate(g_down).reshape(groups, fshare, WIDE // fshare, d).transpose(0, 2, 1, 3).reshape(d, fshare * d)
    flat = jnp.concatenate([jnp.sum(v[:slots], axis=0)[0] for v in (ngs, obs, qkgs, ubs)]).reshape(-1, LANES)
    flat = summed_everywhere(flat).reshape(-1)
    g_ng, g_ob, g_q, g_k, g_ub = (flat[:d], flat[d : 2 * d], flat[2 * d : 3 * d], flat[3 * d : 4 * d], flat[4 * d :])
    g_q, g_k = (jnp.sum(v.reshape(heads, head), axis=0) for v in (g_q, g_k))
    g_ub = g_ub.reshape(-1, fshare, WIDE // fshare).transpose(0, 2, 1).reshape(-1)

    def share(v):
        size = v.shape[0] // ranks
        return lax.dynamic_slice_in_dim(v, rank * size, size)[None]

    total = lax.optimization_barrier(
        lax.psum_scatter(jnp.concatenate(g_up + g_heads + [g_attn, g_down], axis=1), "dp", scatter_dimension=0, tiled=True)
    )
    g_in = jnp.concatenate([total[:, ff:joined].astype(F32), shuffled(total[:, :ff], back=True)], axis=1)
    return (
        ys[:slots].reshape(1, slots * rows, d),
        grs[:slots].reshape(1, slots * rows, d),
        g_in[None],
        total[None, :, joined : joined + d].astype(F32),
        total[:, joined + d : wide].astype(F32).reshape(1, dshare * fshare, d),
        share(g_ng),
        share(g_q),
        share(g_k),
        share(g_ub),
        share(g_ob),
    )


def solution(mesh):
    in_specs = (P("dp", None),) * 3 + (P("section", "dp", None),) * 3 + (P("section", "dp"),) * 5
    out_specs = (P("section", "dp", None),) * 5 + (P("section", "dp"),) * 5
    return jax.shard_map(body, mesh=mesh, in_specs=in_specs, out_specs=out_specs, check_vma=False)
```

time: 1830 us -> 606 us (0.33)
  waiting for transfers between devices: 819 us -> 235 us
  blocking collectives: 252 us -> 0 us
  other arithmetic: 238 us -> 19.4 us
  Pallas kernels: 0 us -> 203 us
  matrix products: 206 us -> 30.6 us
  local copies, waits for them, and re-layouts: 171 us -> 55.1 us
  starting transfers between devices: 88.4 us -> 36.7 us
  loops' own time: 28.2 us -> 0 us
    ppermute x10 -> x13, waiting for transfers between devices: 632 us -> 88.3 us  [the longest x8 82.4 us: shifted(): lax.ppermute(x, 'section', [(i, i + by) for i in range(devices) if 0 <= i...]
    pallas_call x0 -> x33, Pallas kernels: none -> 203 us  [the longest x10 203 us: call(): pl.pallas_call(kernel, grid_spec=pltpu.PrefetchScalarGridSpec(num_scalar_...]
    dot_general x36 -> x13, matrix products: 206 us -> 30.6 us  [the longest x3 12.3 us: body(): jnp.einsum('smd,smj->dj', hs[:slots], gjs[:slots, c], preferred_element_t...]
    add x33 -> x7, other arithmetic: 138 us -> 1.43 us  [the longest x5 1.42 us: summed_everywhere(): x = x + lax.ppermute(x, 'dp', [(i, i ^ step) for i in range(devices)])]
    all_gather x1 -> x0, blocking collectives: 126 us -> none  [body(): lax.all_gather(norm_gain[0], 'dp', axis=0, tiled=True)]
    unnamed x1 -> x0, blocking collectives: 126 us -> none
    reduce_scatter x3 -> x1, waiting for transfers between devices: 169 us -> 80.2 us  [body(): lax.psum_scatter(jnp.concatenate(g_up + g_heads + [g_attn, g_down], axis=...]
    all_gather x3 -> x1, waiting for transfers between devices: 14.2 us -> 66.5 us  [body(): g = lax.all_gather(local, 'dp', axis=0, tiled=True)]
  transfers between devices with their start and end apart: 16 -> 15, of which waited for: 13 -> 14; matrix products, arithmetic and copies ran while one was open for 2% -> 3% of each run, Pallas kernels for 0% -> 0%
where the time goes in v1:
time: 606 us; the launch traced here: 596 us
  waiting for transfers between devices  235 us (39%)
  Pallas kernels  203 us (33%)
  local copies, waits for them, and re-layouts  55.1 us (9%)
  starting transfers between devices  36.7 us (6%)
  matrix products  30.6 us (5%)
  other arithmetic  19.4 us (3%)
  between operations  15.2 us (3%)
    pallas_call x10, Pallas kernels, call(): pl.pallas_call(kernel, grid_spec=pltpu.PrefetchScalarGridSpec(num_scalar_...  203 us
    ppermute x8, waiting for transfers between devices, shifted(): lax.ppermute(x, 'section', [(i, i + by) for i in range(devices) if 0 <= i...  82.4 us
    reduce_scatter x1, waiting for transfers between devices, body(): lax.psum_scatter(jnp.concatenate(g_up + g_heads + [g_attn, g_down], axis=...  80.2 us
    all_gather x1, waiting for transfers between devices, body(): g = lax.all_gather(local, 'dp', axis=0, tiled=True)  66.5 us
    ppermute x8, starting transfers between devices, shifted(): lax.ppermute(x, 'section', [(i, i + by) for i in range(devices) if 0 <= i...  21.6 us
    unnamed x59, local copies, waits for them, and re-layouts  19.6 us
    ppermute x5, starting transfers between devices, summed_everywhere(): x = x + lax.ppermute(x, 'dp', [(i, i ^ step) for i in range(devices)])  15 us
    dot_general x3, matrix products, body(): jnp.einsum('smd,smj->dj', hs[:slots], gjs[:slots, c], preferred_element_t...  12.3 us
  transfers between devices with their start and end apart: 15, of which 14 were waited for; matrix products, arithmetic and copies ran while one was open for 3% of the time, Pallas kernels for 0%

profile of v1, /device:TPU:1, one launch (start us, length us, event | category | flops | bytes accessed | tf_op | source)
XLA Modules:
  0.0 595.6 jit_solution(4315291592124974276)
XLA Ops:
  21.0 66.5 %all-gather.2.cloned.1.call-done.g = bf16[768,9344]{1,0:T(8,128)(2,1)} async-done(((bf16[24,9344]{1,0:T(8,128)(2,1)}), bf16[768,9344]{1,0:T(8,128)(2,1)}) %all-gather.2.cloned.1.call-update) | async-done | bytes 14352400 | tf_op jit(solution)/shard_map/all_gather | solution.py:367
  94.0 18.0 %shard_map.199 = (bf16[384,768]{1,0:T(8,128)(2,1)}, bf16[3,384,768]{2,1,0:T(8,128)(2,1)}, bf16[3,384,768]{2,1,0:T(8,128)(2,1)}, bf16[3,384,768]{2,1,0:T(8,128)(2...) custom-call(s32[3]{0:T(128)} %add_add_fusion.4.idx, ...), custom_call_target="tpu_custom_call", output_to_operand_aliasing={{1}: (12, {}), {2}: (13, {}), {3}: (14, {}), {4}: (15, {}),... | custom-call | flops 5888802816 | bytes 31457280 | tf_op jit(solution)/shard_map/pallas_call | solution.py:291
  116.0 11.9 %collective-permute-done.recv = bf16[384,768]{1,0:T(8,128)(2,1)S(1)} collective-permute-done((bf16[384,768]{1,0:T(8,128)(2,1)}, bf16[384,768]{1,0:T(8,128)(2,1)S(1)}, u32[]{:S(2)}, u32[]{:S(2)}) %collective-permute-start) | collective-permute-done | bytes 589856 | tf_op jit(solution)/shard_map/ppermute | solution.py:310
  128.8 18.1 %shard_map.200 = (bf16[384,768]{1,0:T(8,128)(2,1)}, bf16[3,384,768]{2,1,0:T(8,128)(2,1)}, bf16[3,384,768]{2,1,0:T(8,128)(2,1)}, bf16[3,384,768]{2,1,0:T(8,128)(2...) custom-call(s32[3]{0:T(128)} %add_add_fusion.3.idx, ...), custom_call_target="tpu_custom_call", output_to_operand_aliasing={{1}: (12, {}), {2}: (13, {}), {3}: (14, {}), {4}: (15, {}),... | custom-call | flops 5888802816 | bytes 31457280 | tf_op jit(solution)/shard_map/pallas_call | solution.py:291
  146.9 4.4 collective-permute-start.1
  151.9 10.8 %collective-permute-done.1.recv = bf16[384,768]{1,0:T(8,128)(2,1)S(1)} collective-permute-done((bf16[384,768]{1,0:T(8,128)(2,1)}, bf16[384,768]{1,0:T(8,128)(2,1)S(1)}, u32[]{:S(2)}, u32[]{:S(2)}) %collective-permute-start.1) | collective-permute-done | bytes 589856 | tf_op jit(solution)/shard_map/ppermute | solution.py:310
  163.5 18.1 %shard_map.201 = (bf16[384,768]{1,0:T(8,128)(2,1)}, bf16[3,384,768]{2,1,0:T(8,128)(2,1)}, bf16[3,384,768]{2,1,0:T(8,128)(2,1)}, bf16[3,384,768]{2,1,0:T(8,128)(2...) custom-call(s32[3]{0:T(128)} %add_add_fusion.2.idx, ...), custom_call_target="tpu_custom_call", output_to_operand_aliasing={{1}: (12, {}), {2}: (13, {}), {3}: (14, {}), {4}: (15, {}),... | custom-call | flops 5888802816 | bytes 31457280 | tf_op jit(solution)/shard_map/pallas_call | solution.py:291
  181.6 4.2 collective-permute-start.2
  186.4 10.1 %collective-permute-done.2.recv = bf16[384,768]{1,0:T(8,128)(2,1)S(1)} collective-permute-done((bf16[384,768]{1,0:T(8,128)(2,1)}, bf16[384,768]{1,0:T(8,128)(2,1)S(1)}, u32[]{:S(2)}, u32[]{:S(2)}) %collective-permute-start.2) | collective-permute-done | bytes 589856 | tf_op jit(solution)/shard_map/ppermute | solution.py:310
  197.3 18.1 %shard_map.202 = (bf16[384,768]{1,0:T(8,128)(2,1)}, bf16[3,384,768]{2,1,0:T(8,128)(2,1)}, bf16[3,384,768]{2,1,0:T(8,128)(2,1)}, bf16[3,384,768]{2,1,0:T(8,128)(2...) custom-call(s32[3]{0:T(128)} %add_add_fusion.1.idx, ...), custom_call_target="tpu_custom_call", output_to_operand_aliasing={{1}: (12, {}), {2}: (13, {}), {3}: (14, {}), {4}: (15, {}),... | custom-call | flops 5888802816 | bytes 31457280 | tf_op jit(solution)/shard_map/pallas_call | solution.py:291
  215.5 4.2 collective-permute-start.3
  221.0 8.4 %collective-permute-done.3.recv = bf16[384,768]{1,0:T(8,128)(2,1)S(1)} collective-permute-done((bf16[384,768]{1,0:T(8,128)(2,1)}, bf16[384,768]{1,0:T(8,128)(2,1)S(1)}, u32[]{:S(2)}, u32[]{:S(2)}) %collective-permute-start.3) | collective-permute-done | bytes 589856 | tf_op jit(solution)/shard_map/ppermute | solution.py:310
  230.3 18.1 %shard_map.203 = (bf16[384,768]{1,0:T(8,128)(2,1)}, bf16[3,384,768]{2,1,0:T(8,128)(2,1)}, bf16[3,384,768]{2,1,0:T(8,128)(2,1)}, bf16[3,384,768]{2,1,0:T(8,128)(2...) custom-call(s32[3]{0:T(128)} %add_add_fusion.idx, ...), custom_call_target="tpu_custom_call", output_to_operand_aliasing={{1}: (12, {}), {2}: (13, {}), {3}: (14, {}), {4}: (15, {}),... | custom-call | flops 5888802816 | bytes 31457280 | tf_op jit(solution)/shard_map/pallas_call | solution.py:291
  248.4 22.8 %shard_map.214 = (bf16[384,768]{1,0:T(8,128)(2,1)}, bf16[3,384,768]{2,1,0:T(8,128)(2,1)}, bf16[3,3,384,1024]{3,2,1,0:T(8,128)(2,1)}, bf16[3,384,768]{2,1,0:T(8,1...) custom-call(s32[3]{0:T(128)} %add_add_fusion.9.idx, ...), custom_call_target="tpu_custom_call", output_to_operand_aliasing={{1}: (19, {}), {2}: (20, {}), {3}: (21, {}), {4}: (22, {}),... | custom-call | flops 6341787648 | bytes 31457280 | tf_op jit(solution)/shard_map/pallas_call | solution.py:291
  273.3 11.9 %collective-permute-done.4.recv = bf16[384,768]{1,0:T(8,128)(2,1)S(1)} collective-permute-done((bf16[384,768]{1,0:T(8,128)(2,1)}, bf16[384,768]{1,0:T(8,128)(2,1)S(1)}, u32[]{:S(2)}, u32[]{:S(2)}) %collective-permute-start.4) | collective-permute-done | bytes 589856 | tf_op jit(solution)/shard_map/ppermute | solution.py:310
  286.0 22.7 %shard_map.215 = (bf16[384,768]{1,0:T(8,128)(2,1)}, bf16[3,384,768]{2,1,0:T(8,128)(2,1)}, bf16[3,3,384,1024]{3,2,1,0:T(8,128)(2,1)}, bf16[3,384,768]{2,1,0:T(8,1...) custom-call(s32[3]{0:T(128)} %add_add_fusion.8.idx, ...), custom_call_target="tpu_custom_call", output_to_operand_aliasing={{1}: (19, {}), {2}: (20, {}), {3}: (21, {}), {4}: (22, {}),... | custom-call | flops 6341787648 | bytes 31457280 | tf_op jit(solution)/shard_map/pallas_call | solution.py:291
  310.6 10.6 %collective-permute-done.5.recv = bf16[384,768]{1,0:T(8,128)(2,1)S(1)} collective-permute-done((bf16[384,768]{1,0:T(8,128)(2,1)}, bf16[384,768]{1,0:T(8,128)(2,1)S(1)}, u32[]{:S(2)}, u32[]{:S(2)}) %collective-permute-start.5) | collective-permute-done | bytes 589856 | tf_op jit(solution)/shard_map/ppermute | solution.py:310
  322.0 22.5 %shard_map.216 = (bf16[384,768]{1,0:T(8,128)(2,1)}, bf16[3,384,768]{2,1,0:T(8,128)(2,1)}, bf16[3,3,384,1024]{3,2,1,0:T(8,128)(2,1)}, bf16[3,384,768]{2,1,0:T(8,1...) custom-call(s32[3]{0:T(128)} %add_add_fusion.7.idx, ...), custom_call_target="tpu_custom_call", output_to_operand_aliasing={{1}: (19, {}), {2}: (20, {}), {3}: (21, {}), {4}: (22, {}),... | custom-call | flops 6341787648 | bytes 31457280 | tf_op jit(solution)/shard_map/pallas_call | solution.py:291
  346.4 9.6 %collective-permute-done.6.recv = bf16[384,768]{1,0:T(8,128)(2,1)S(1)} collective-permute-done((bf16[384,768]{1,0:T(8,128)(2,1)}, bf16[384,768]{1,0:T(8,128)(2,1)S(1)}, u32[]{:S(2)}, u32[]{:S(2)}) %collective-permute-start.6) | collective-permute-done | bytes 589856 | tf_op jit(solution)/shard_map/ppermute | solution.py:310
  356.9 22.7 %shard_map.217 = (bf16[384,768]{1,0:T(8,128)(2,1)}, bf16[3,384,768]{2,1,0:T(8,128)(2,1)}, bf16[3,3,384,1024]{3,2,1,0:T(8,128)(2,1)}, bf16[3,384,768]{2,1,0:T(8,1...) custom-call(s32[3]{0:T(128)} %add_add_fusion.6.idx, ...), custom_call_target="tpu_custom_call", output_to_operand_aliasing={{1}: (19, {}), {2}: (20, {}), {3}: (21, {}), {4}: (22, {}),... | custom-call | flops 6341787648 | bytes 31457280 | tf_op jit(solution)/shard_map/pallas_call | solution.py:291
  381.5 8.9 %collective-permute-done.7.recv = bf16[384,768]{1,0:T(8,128)(2,1)S(1)} collective-permute-done((bf16[384,768]{1,0:T(8,128)(2,1)}, bf16[384,768]{1,0:T(8,128)(2,1)S(1)}, u32[]{:S(2)}, u32[]{:S(2)}) %collective-permute-start.7) | collective-permute-done | bytes 589856 | tf_op jit(solution)/shard_map/ppermute | solution.py:310
  391.2 22.4 %shard_map.218 = (bf16[384,768]{1,0:T(8,128)(2,1)}, bf16[3,384,768]{2,1,0:T(8,128)(2,1)}, bf16[3,3,384,1024]{3,2,1,0:T(8,128)(2,1)}, bf16[3,384,768]{2,1,0:T(8,1...) custom-call(s32[3]{0:T(128)} %add_add_fusion.5.idx, ...), custom_call_target="tpu_custom_call", output_to_operand_aliasing={{1}: (19, {}), {2}: (20, {}), {3}: (21, {}), {4}: (22, {}),... | custom-call | flops 6341787648 | bytes 31457280 | tf_op jit(solution)/shard_map/pallas_call | solution.py:291
  471.9 7.5 %collective-permute-start.8 = (f32[48,128]{1,0:T(8,128)S(1)}, f32[48,128]{1,0:T(8,128)S(1)}, u32[]{:S(2)}, u32[]{:S(2)}) collective-permute-start(f32[48,128]{1,0:T(8,128)S(1)} %maximum_bitcast_fusion.1), channel_id=1, source_target_pairs={{0,1},{1,0},{2,3},{3,2},{4,5},{5,4},{6,7},{7,6},{8,9},{9,8},{10,11... | collective-permute-start | bytes 73736 | tf_op jit(solution)/shard_map/ppermute | solution.py:317
  502.6 80.2 %reduce-scatter.2.cloned.1.call-done = bf16[24,9216]{1,0:T(8,128)(2,1)} async-done(((bf16[768,9216]{1,0:T(8,128)(2,1)}), bf16[24,9216]{1,0:T(8,128)(2,1)}) %reduce-scatter.2.cloned.1.call-update) | async-done | bytes 442384 | tf_op jit(solution)/shard_map/reduce_scatter | solution.py:475
  (201 shorter events, 127.5 us)
Async XLA Ops:
  7.2 8.5 %copy-start.20 = (bf16[1,24,768]{2,1,0:T(8,128)(2,1)S(1)}, bf16[1,24,768]{2,1,0:T(8,128)(2,1)}, u32[]{:S(2)}) copy-start(bf16[1,24,768]{2,1,0:T(8,128)(2,1)} %param.15) | copy-start | bytes 110596
  7.2 80.4 %all-gather.2.cloned.1.call-start = ((), (), s32[]{:S(2)}) async-start(), calls=%async_computation.1 | async-start | bytes 14800896 | tf_op jit(solution)/shard_map/all_gather | solution.py:367
  7.2 85.1 %copy-start.21 = (s32[256]{0:T(256)}, s32[256]{0:T(256)S(1)}, u32[]{:S(2)}) copy-start(s32[256]{0:T(256)S(1)} %fusion.33) | copy-start | bytes 3076
  16.6 566.3 %reduce-scatter.2.cloned.1.call-start = ((), (), s32[]{:S(2)}) async-start(), calls=%async_computation.2 | async-start | bytes 14598144 | tf_op jit(solution)/shard_map/reduce_scatter | solution.py:475
  112.0 15.9 %collective-permute-start = (bf16[384,768]{1,0:T(8,128)(2,1)}, bf16[384,768]{1,0:T(8,128)(2,1)S(1)}, u32[]{:S(2)}, u32[]{:S(2)}) collective-permute-start(bf16[384,768]{1,0:T(8,128)(2,1)} %get-tuple-element.133), channel_id=1, source_target_pairs={{0,32},{32,64},{64,96},{1,33},{33,65},{65,97},{2,34},{34,66},{66,9... | collective-permute-start | bytes 1769480 | tf_op jit(solution)/shard_map/ppermute | solution.py:310
  146.9 15.8 %collective-permute-start.1 = (bf16[384,768]{1,0:T(8,128)(2,1)}, bf16[384,768]{1,0:T(8,128)(2,1)S(1)}, u32[]{:S(2)}, u32[]{:S(2)}) collective-permute-start(bf16[384,768]{1,0:T(8,128)(2,1)} %get-tuple-element.147), channel_id=1, source_target_pairs={{0,32},{32,64},{64,96},{1,33},{33,65},{65,97},{2,34},{34,66},{66,9... | collective-permute-start | bytes 1769480 | tf_op jit(solution)/shard_map/ppermute | solution.py:310
  181.6 14.9 %collective-permute-start.2 = (bf16[384,768]{1,0:T(8,128)(2,1)}, bf16[384,768]{1,0:T(8,128)(2,1)S(1)}, u32[]{:S(2)}, u32[]{:S(2)}) collective-permute-start(bf16[384,768]{1,0:T(8,128)(2,1)} %get-tuple-element.161), channel_id=1, source_target_pairs={{0,32},{32,64},{64,96},{1,33},{33,65},{65,97},{2,34},{34,66},{66,9... | collective-permute-start | bytes 1769480 | tf_op jit(solution)/shard_map/ppermute | solution.py:310
  215.5 14.0 %collective-permute-start.3 = (bf16[384,768]{1,0:T(8,128)(2,1)}, bf16[384,768]{1,0:T(8,128)(2,1)S(1)}, u32[]{:S(2)}, u32[]{:S(2)}) collective-permute-start(bf16[384,768]{1,0:T(8,128)(2,1)} %get-tuple-element.175), channel_id=1, source_target_pairs={{0,32},{32,64},{64,96},{1,33},{33,65},{65,97},{2,34},{34,66},{66,9... | collective-permute-start | bytes 1769480 | tf_op jit(solution)/shard_map/ppermute | solution.py:310
  271.2 14.0 %collective-permute-start.4 = (bf16[384,768]{1,0:T(8,128)(2,1)}, bf16[384,768]{1,0:T(8,128)(2,1)S(1)}, u32[]{:S(2)}, u32[]{:S(2)}) collective-permute-start(bf16[384,768]{1,0:T(8,128)(2,1)} %get-tuple-element.200), channel_id=1, source_target_pairs={{32,0},{64,32},{96,64},{33,1},{65,33},{97,65},{34,2},{66,34},{98,6... | collective-permute-start | bytes 1769480 | tf_op jit(solution)/shard_map/ppermute | solution.py:310
  308.7 12.5 %collective-permute-start.5 = (bf16[384,768]{1,0:T(8,128)(2,1)}, bf16[384,768]{1,0:T(8,128)(2,1)S(1)}, u32[]{:S(2)}, u32[]{:S(2)}) collective-permute-start(bf16[384,768]{1,0:T(8,128)(2,1)} %get-tuple-element.211), channel_id=1, source_target_pairs={{32,0},{64,32},{96,64},{33,1},{65,33},{97,65},{34,2},{66,34},{98,6... | collective-permute-start | bytes 1769480 | tf_op jit(solution)/shard_map/ppermute | solution.py:310
  344.5 11.5 %collective-permute-start.6 = (bf16[384,768]{1,0:T(8,128)(2,1)}, bf16[384,768]{1,0:T(8,128)(2,1)S(1)}, u32[]{:S(2)}, u32[]{:S(2)}) collective-permute-start(bf16[384,768]{1,0:T(8,128)(2,1)} %get-tuple-element.222), channel_id=1, source_target_pairs={{32,0},{64,32},{96,64},{33,1},{65,33},{97,65},{34,2},{66,34},{98,6... | collective-permute-start | bytes 1769480 | tf_op jit(solution)/shard_map/ppermute | solution.py:310
  379.6 10.8 %collective-permute-start.7 = (bf16[384,768]{1,0:T(8,128)(2,1)}, bf16[384,768]{1,0:T(8,128)(2,1)S(1)}, u32[]{:S(2)}, u32[]{:S(2)}) collective-permute-start(bf16[384,768]{1,0:T(8,128)(2,1)} %get-tuple-element.233), channel_id=1, source_target_pairs={{32,0},{64,32},{96,64},{33,1},{65,33},{97,65},{34,2},{66,34},{98,6... | collective-permute-start | bytes 1769480 | tf_op jit(solution)/shard_map/ppermute | solution.py:310
  413.7 3.3 copy-start.4
  429.2 5.7 copy-start.7
  452.2 14.6 %slice-start = ((s8[4718592]{0:T(1024)(128)(4,1)}), s8[4194304]{0:T(1024)(128)(4,1)S(1)}, s32[]{:S(2)}) async-start(s8[4718592]{0:T(1024)(128)(4,1)} %bitcast.155), calls=%async_computation.3 | async-start | bytes 8388608
  456.3 10.4 %slice-start.1 = ((s8[4718592]{0:T(1024)(128)(4,1)}), s8[524288]{0:T(1024)(128)(4,1)S(1)}, s32[]{:S(2)}) async-start(s8[4718592]{0:T(1024)(128)(4,1)} %bitcast.155), calls=%async_computation.4 | async-start | bytes 1048576
  469.3 24.2 %copy-start.1 = (f32[3,384,768]{2,1,0:T(8,128)S(1)}, f32[3,384,768]{2,1,0:T(8,128)}, u32[]{:S(2)}) copy-start(f32[3,384,768]{2,1,0:T(8,128)} %get-tuple-element.189) | copy-start | bytes 10616836
  471.9 8.4 %collective-permute-start.8 = (f32[48,128]{1,0:T(8,128)S(1)}, f32[48,128]{1,0:T(8,128)S(1)}, u32[]{:S(2)}, u32[]{:S(2)}) collective-permute-start(f32[48,128]{1,0:T(8,128)S(1)} %maximum_bitcast_fusion.1), channel_id=1, source_target_pairs={{0,1},{1,0},{2,3},{3,2},{4,5},{5,4},{6,7},{7,6},{8,9},{9,8},{10,11... | collective-permute-start | bytes 73736 | tf_op jit(solution)/shard_map/ppermute | solution.py:317
  480.2 2.7 collective-permute-start.9
  482.9 4.3 collective-permute-start.10
  487.2 2.7 collective-permute-start.11
  490.5 7.7 %collective-permute-start.12 = (f32[48,128]{1,0:T(8,128)}, f32[48,128]{1,0:T(8,128)}, u32[]{:S(2)}, u32[]{:S(2)}) collective-permute-start(f32[48,128]{1,0:T(8,128)} %add.89), channel_id=1, source_target_pairs={{0,16},{1,17},{2,18},{3,19},{4,20},{5,21},{6,22},{7,23},{8,24},{9,... | collective-permute-start | bytes 73736 | tf_op jit(solution)/shard_map/ppermute | solution.py:317
  493.5 3.2 copy-start.2
  498.2 88.2 %copy-start.22 = (s32[256]{0:T(256)S(1)}, s32[256]{0:T(256)}, u32[]{:S(2)}) copy-start(s32[256]{0:T(256)} %copy-done.21) | copy-start | bytes 3076
  (17 other events, 23.9 us)
Sparse Core Ops, SparseCore 0:
  16.7 70.8 all-gather.1
  469.4 113.4 reduce-scatter.1

commit v2 on v1

--- a/solution.py
+++ b/solution.py
@@ -14,6 +14,7 @@
 EPS = 1e-06
 NN = (((1,), (0,)), ((), ()))
 NT = (((1,), (1,)), ((), ()))
+TN = (((0,), (0,)), ((), ()))
 LANES = 128
 WIDE = 256
 ABSENT = 16
@@ -276,6 +277,162 @@
         copy.wait()
 
 
+def weight_grad_kernel(d, ff, chunks, idx, place, hs, acts, ats, gbs, gjs, gqs, gks, gvs, obs, ngs, qkgs, ubs, out,
+                       h_v, big_v, side_v, at_v, gb_v, out_v, ins, outs):
+    slots, rows = h_v.shape[0], h_v.shape[1]
+    fc = ff // chunks
+    cin, cout = Copies(ins), Copies(outs)
+    hidden = cin.start(hs.at[pl.ds(0, slots)], h_v)
+
+    @pl.when(idx[0] == 0)
+    def _():
+        cin.used = 1
+        copies = [cin.start(gbs.at[pl.ds(0, slots)], gb_v)]
+        parts = [cin.start(acts.at[pl.ds(0, slots), c], big_v.at[c]) for c in range(chunks)]
+        copies.append(cin.start(ats.at[pl.ds(0, slots)], at_v))
+        values = cin.start(gvs.at[pl.ds(0, slots)], side_v.at[0])
+        pending = []
+        for copy in copies:
+            copy.wait()
+        gb = gb_v[...].reshape(slots * rows, d)
+        quarter = WIDE // 4
+        for c in range(chunks):
+            parts[c].wait()
+            got = lax.dot_general(big_v[c].reshape(slots * rows, fc), gb, TN, preferred_element_type=F32).astype(BF)
+            for b in range(fc // WIDE):
+                for j in range(4):
+                    at = quarter * (fc // WIDE * c + b)
+                    out_v[at : at + quarter, d * j : d * j + d] = got[WIDE * b + quarter * j : WIDE * b + quarter * (j + 1)]
+            span = pl.ds(quarter * (fc // WIDE) * c, quarter * (fc // WIDE))
+            pending.append(cout.start(out_v.at[span, pl.ds(0, 4 * d)], out.at[span, pl.ds(0, 4 * d)]))
+        total = mm(at_v[0], gb_v[0])
+        for s in range(1, slots):
+            total = total + mm(at_v[s], gb_v[s])
+        out_v[:, 4 * d : 5 * d] = total.astype(BF)
+        hidden.wait()
+        values.wait()
+        flat = h_v[...].reshape(slots * rows, d)
+        out_v[:, 5 * d : 6 * d] = lax.dot_general(
+            flat, side_v[0].reshape(slots * rows, d), TN, preferred_element_type=F32
+        ).astype(BF)
+        def over_slots(ref):
+            total = ref[0]
+            for s in range(1, slots):
+                total = total + ref[s]
+            return total
+
+        ub = over_slots(ubs)
+        up_rows = []
+        for j in range(4):
+            pieces = [ub[:, WIDE * b + quarter * j : WIDE * b + quarter * (j + 1)] for b in range(ff // WIDE)]
+            up_rows.append(jnp.concatenate(pieces, axis=1))
+        qk = over_slots(qkgs)
+        head_rows = []
+        for i in range(2):
+            lanes = qk[:, d * i : d * i + LANES]
+            for p in range(1, d // LANES):
+                lanes = lanes + qk[:, d * i + LANES * p : d * i + LANES * (p + 1)]
+            head_rows.append(lanes)
+        both = jnp.concatenate(head_rows + [jnp.zeros((6, LANES), F32)], axis=0)
+        placed = lax.dot_general(both, place[...], NN, precision=lax.Precision.HIGHEST, preferred_element_type=F32)
+        values8 = jnp.concatenate([over_slots(ngs), over_slots(obs)] + up_rows + [placed[0:1], placed[1:2]], axis=0)
+        top = values8.astype(BF).astype(F32)
+        table = jnp.concatenate([top, values8 - top, jnp.zeros((LANES - 16, d), F32)], axis=0)
+        out_v[:, 6 * d :] = table.T.astype(BF)
+        pending.append(cout.start(out_v.at[:, pl.ds(4 * d, 2 * d + LANES)], out.at[:, pl.ds(4 * d, 2 * d + LANES)]))
+        for copy in pending:
+            copy.wait()
+
+    @pl.when(idx[0] == 1)
+    def _():
+        cin.used, cout.used = 1, 0
+        parts = [cin.start(gjs.at[pl.ds(0, slots), c], big_v.at[c]) for c in range(chunks)]
+        sides = [cin.start(v.at[pl.ds(0, slots)], side_v.at[i]) for i, v in enumerate((gqs, gks))]
+        pending = []
+        hidden.wait()
+        turned = h_v[...].reshape(slots * rows, d).T
+        for c in range(chunks):
+            parts[c].wait()
+            span = pl.ds(fc * c, fc)
+            out_v[:, fc * c : fc * c + fc] = mm(turned, big_v[c].reshape(slots * rows, fc)).astype(BF)
+            pending.append(cout.start(out_v.at[:, span], out.at[:, span]))
+        for i in range(2):
+            sides[i].wait()
+            at = ff + d * i
+            out_v[:, at : at + d] = mm(turned, side_v[i].reshape(slots * rows, d)).astype(BF)
+        out_v[:, 6 * d :] = jnp.zeros((d, LANES), BF)
+        pending.append(cout.start(out_v.at[:, pl.ds(ff, 2 * d + LANES)], out.at[:, pl.ds(ff, 2 * d + LANES)]))
+        for copy in pending:
+            copy.wait()
+
+
+def pair_kernel(cut, idx, own, got, own4, got4, *refs):
+    firsts, seconds, (a_v, b_v, c_v, d_v, ins, outs) = refs[:4], refs[4:8], refs[8:]
+    y, z = idx[1], idx[2]
+    width = own.shape[2]
+    cin, cout = Copies(ins), Copies(outs)
+    loads = []
+    for s in range(4):
+        to_y, to_z = lax.rem(y + s, 4), lax.rem(z + s, 4)
+        loads.append((
+            cin.start(own.at[to_y, :, pl.ds(0, cut)], a_v.at[s]),
+            cin.start(got.at[to_y, :, pl.ds(0, cut)], b_v.at[s]),
+            cin.start(own4.at[:, to_z, :, pl.ds(cut, width - cut)], c_v.at[s]),
+            cin.start(got4.at[:, to_z, :, pl.ds(cut, width - cut)], d_v.at[s]),
+        ))
+    pending = []
+    for s in (1, 2, 3, 0):
+        for copy in loads[s]:
+            copy.wait()
+        a_v[s] = (a_v[s].astype(F32) + b_v[s].astype(F32)).astype(BF)
+        pending.append(cout.start(a_v.at[s], firsts[s]))
+        c_v[s] = added([c_v[s], d_v[s]])
+        pending.append(cout.start(c_v.at[s], seconds[s]))
+    for copy in pending:
+        copy.wait()
+
+
+def added(parts):
+    total = parts[0].astype(F32)
+    for part in parts[1:]:
+        total = total + part.astype(F32)
+    shape = total.shape
+    total = total.reshape(-1, shape[-1])
+    main, last = total[:, : shape[-1] - LANES], total[:, shape[-1] - LANES :]
+    last = last + pltpu.roll(last, LANES - 8, 1)
+    top = last.astype(BF).astype(F32)
+    lane = lax.broadcasted_iota(jnp.int32, last.shape, 1)
+    last = jnp.where(lane < 8, top, jnp.where(lane < 16, pltpu.roll(last - top, 8, 1), 0.0))
+    return jnp.concatenate([main, last], axis=1).astype(BF).reshape(shape)
+
+
+def mid_kernel(idx, *refs):
+    firsts, seconds, a_out, b_out, (a_v, b_v) = refs[:4], refs[4:8], refs[8:12], refs[12:16], refs[16:]
+    y, z = idx[1], idx[2]
+    total = firsts[0][...].astype(F32)
+    for part in firsts[1:]:
+        total = total + part[...].astype(F32)
+    a_v[...] = total.astype(BF).reshape(a_v.shape)
+    b_v[...] = added([part[...].reshape(-1, part.shape[-1]) for part in seconds]).reshape(b_v.shape)
+    for s in range(4):
+        a_out[s][...] = a_v[lax.rem(z + s, 4)]
+        b_out[s][...] = b_v[lax.rem(y + s, 4)]
+
+
+def last_kernel(idx, *refs):
+    firsts, seconds, mine, theirs, hold = refs[:4], refs[4:8], refs[8], refs[9], refs[10]
+    cut = firsts[0].shape[-1]
+    for group, at in ((firsts, 0), (seconds, cut)):
+        total = group[0][...].astype(F32)
+        for part in group[1:]:
+            total = total + part[...].astype(F32)
+        hold[:, at : at + total.shape[1]] = total
+    count = mine.shape[0]
+    core = idx[3]
+    mine[...] = hold[pl.ds(pl.multiple_of(core * count, 8), count), :]
+    theirs[...] = hold[pl.ds(pl.multiple_of((1 - core) * count, 8), count), :]
+
+
 ANY = pl.BlockSpec(memory_space=pl.ANY)
 
 
@@ -305,18 +462,31 @@
     return outs[0], outs[1:]
 
 
+def simple(kernel, idx, arrays, specs, out_shapes, out_specs, scratch, flops=1 << 24):
+    return pl.pallas_call(
+        kernel,
+        grid_spec=pltpu.PrefetchScalarGridSpec(
+            num_scalar_prefetch=1, grid=(1,), in_specs=specs, out_specs=out_specs, scratch_shapes=scratch
+        ),
+        out_shape=out_shapes,
+        compiler_params=pltpu.CompilerParams(dimension_semantics=("arbitrary",), vmem_limit_bytes=VMEM_LIMIT),
+        cost_estimate=pl.CostEstimate(flops=flops, bytes_accessed=16 << 20, transcendentals=0),
+    )(idx, *arrays)
+
+
+def along(x, step, size, by):
+    devices = lax.axis_size("dp")
+
+    def to(i):
+        digit = i // step % size
+        return i + ((digit + by) % size - digit) * step
+
+    return lax.ppermute(x, "dp", [(i, to(i)) for i in range(devices)])
+
+
 def shifted(x, by):
     devices = lax.axis_size("section")
     return lax.ppermute(x, "section", [(i, i + by) for i in range(devices) if 0 <= i + by < devices])
-
-
-def summed_everywhere(x):
-    devices = lax.axis_size("dp")
-    step = 1
-    while step < devices:
-        x = x + lax.ppermute(x, "dp", [(i, i ^ step) for i in range(devices)])
-        step *= 2
-    return x
 
 
 def body(tokens, cotangent, lengths, proj_in, proj_attn, proj_down, norm_gain, query_gain, key_gain, up_bias, out_bias):
@@ -344,7 +514,7 @@
 
     def shuffled(x, back=False):
         flat = x.reshape(-1, WIDE)
-        out = lax.dot_general(flat, shuffle, NT if back else NN, preferred_element_type=F32)
+        out = lax.dot_general(flat, shuffle.astype(x.dtype), NT if back else NN, precision=lax.Precision.HIGHEST, preferred_element_type=F32)
         return out.reshape(x.shape)
 
     small = jnp.concatenate(
@@ -452,40 +622,71 @@
 
     gbs, gjs, gqs, gks, gvs, grs, obs, ngs, qkgs, ubs = back
 
-    def over_rows(left, right):
-        return jnp.einsum("md,mj->dj", left[:slots].reshape(-1, left.shape[-1]), right[:slots].reshape(-1, right.shape[-1]),
-                          preferred_element_type=F32).astype(BF)
-
-    g_up = [jnp.einsum("smd,smj->dj", hs[:slots], gjs[:slots, c], preferred_element_type=F32).astype(BF) for c in range(chunks)]
-    g_heads = [over_rows(hs, v) for v in (gqs, gks, gvs)]
-    g_attn = jnp.einsum("sdm,smj->dj", ats[:slots], gbs[:slots], preferred_element_type=F32).astype(BF)
-    g_down = [jnp.einsum("smf,smj->fj", acts[:slots, c], gbs[:slots], preferred_element_type=F32).astype(BF) for c in range(chunks)]
-    g_down = jnp.concatenate(g_down).reshape(groups, fshare, WIDE // fshare, d).transpose(0, 2, 1, 3).reshape(d, fshare * d)
-    flat = jnp.concatenate([jnp.sum(v[:slots], axis=0)[0] for v in (ngs, obs, qkgs, ubs)]).reshape(-1, LANES)
-    flat = summed_everywhere(flat).reshape(-1)
-    g_ng, g_ob, g_q, g_k, g_ub = (flat[:d], flat[d : 2 * d], flat[2 * d : 3 * d], flat[3 * d : 4 * d], flat[4 * d :])
-    g_q, g_k = (jnp.sum(v.reshape(heads, head), axis=0) for v in (g_q, g_k))
-    g_ub = g_ub.reshape(-1, fshare, WIDE // fshare).transpose(0, 2, 1).reshape(-1)
-
-    def share(v):
-        size = v.shape[0] // ranks
-        return lax.dynamic_slice_in_dim(v, rank * size, size)[None]
-
-    total = lax.optimization_barrier(
-        lax.psum_scatter(jnp.concatenate(g_up + g_heads + [g_attn, g_down], axis=1), "dp", scatter_dimension=0, tiled=True)
+    side = math.isqrt(ranks // 2)
+    core, z, y = lax.rem(rank, 2), lax.rem(rank // 2, side), rank // (2 * side)
+    width = 6 * d + LANES
+    cut = 3 * d
+    share = 2 * dshare
+    position = jnp.arange(LANES, dtype=jnp.int32)[:, None] % head
+    place = (position // hshare * dshare + position % hshare == jnp.arange(d, dtype=jnp.int32)[None, :]).astype(F32)
+
+    def weight_grads(half):
+        return simple(
+            partial(weight_grad_kernel, d, ff, chunks),
+            jnp.stack([half, y, z, core]).astype(jnp.int32),
+            [place, hs, acts, ats, gbs, gjs, gqs, gks, gvs, obs, ngs, qkgs, ubs],
+            [whole((LANES, d))] + [ANY] * 8 + [whole(a.shape) for a in (obs, ngs, qkgs, ubs)],
+            jax.ShapeDtypeStruct((d, width), BF),
+            ANY,
+            [V((slots, rows, d), BF), V((chunks, slots, rows, fc), BF), V((2, slots, rows, d), BF), V((slots, d, rows), BF),
+             V((slots, rows, d), BF), V((d, width), BF), pltpu.SemaphoreType.DMA((16,)), pltpu.SemaphoreType.DMA((16,))],
+            2 * d * slots * rows * 6 * d,
+        )
+
+    here = jnp.stack([core, y, z, core]).astype(jnp.int32)
+    theirs = weight_grads(1 - core)
+    got = along(theirs, 1, 2, 1)
+    own = weight_grads(core)
+    by_y, by_z = (side, side * share, width), (side, side, share, width)
+    outs = simple(
+        partial(pair_kernel, cut), here,
+        [own.reshape(by_y), got.reshape(by_y), own.reshape(by_z), got.reshape(by_z)],
+        [ANY] * 4,
+        [jax.ShapeDtypeStruct((side * share, cut), BF)] * side + [jax.ShapeDtypeStruct((side, share, width - cut), BF)] * side,
+        [ANY] * 8,
+        [V((side, side * share, cut), BF)] * 2 + [V((side, side, share, width - cut), BF)] * 2
+        + [pltpu.SemaphoreType.DMA((16,)), pltpu.SemaphoreType.DMA((8,))],
     )
-    g_in = jnp.concatenate([total[:, ff:joined].astype(F32), shuffled(total[:, :ff], back=True)], axis=1)
+    firsts = [outs[0]] + [along(outs[s], 2 * side, side, s) for s in range(1, side)]
+    seconds = [outs[side]] + [along(outs[side + s], 2, side, s) for s in range(1, side)]
+    shapes = [(share, cut)] * side + [(share, width - cut)] * side
+    outs = simple(
+        mid_kernel, here, firsts + seconds, [whole(a.shape) for a in firsts + seconds],
+        [jax.ShapeDtypeStruct(s, BF) for s in shapes], [whole(s) for s in shapes],
+        [V((side, share, cut), BF), V((side, share, width - cut), BF)],
+    )
+    firsts = [outs[0]] + [along(outs[s], 2, side, s) for s in range(1, side)]
+    seconds = [outs[side]] + [along(outs[side + s], 2 * side, side, s) for s in range(1, side)]
+    mine, other = simple(
+        last_kernel, here, firsts + seconds, [whole(a.shape) for a in firsts + seconds],
+        [jax.ShapeDtypeStruct((dshare, width), F32)] * 2, [whole((dshare, width))] * 2,
+        [V((share, width), F32)],
+    )
+    other = along(other, 1, 2, 1)
+    half0, half1 = jnp.where(core == 0, mine, other), jnp.where(core == 0, other, mine)
+    g_in = jnp.concatenate([half1[:, ff : 6 * d], half0[:, 5 * d : 6 * d], shuffled(half1[:, :ff], back=True)], axis=1)
+    last = half0[:, 6 * d : 6 * d + 8] + half0[:, 6 * d + 8 : 6 * d + 16]
     return (
         ys[:slots].reshape(1, slots * rows, d),
         grs[:slots].reshape(1, slots * rows, d),
         g_in[None],
-        total[None, :, joined : joined + d].astype(F32),
-        total[:, joined + d : wide].astype(F32).reshape(1, dshare * fshare, d),
-        share(g_ng),
-        share(g_q),
-        share(g_k),
-        share(g_ub),
-        share(g_ob),
+        half0[None, :, 4 * d : 5 * d],
+        half0[:, : 4 * d].reshape(1, dshare * fshare, d),
+        last[None, :, 0],
+        last[None, :hshare, 6],
+        last[None, :hshare, 7],
+        last[:, 2:6].reshape(1, dshare * fshare),
+        last[None, :, 1],
     )
 
 

time: 606 us -> 561 us (0.926)
  Pallas kernels: 203 us -> 251 us
  waiting for transfers between devices: 235 us -> 193 us
  matrix products: 30.6 us -> 0.7 us
  local copies, waits for them, and re-layouts: 55.1 us -> 30.9 us
  starting transfers between devices: 36.7 us -> 46.2 us
    reduce_scatter x1 -> x0, waiting for transfers between devices: 80.2 us -> none  [body(): lax.psum_scatter(jnp.concatenate(g_up + g_heads + [g_attn, g_down], axis=...]
    pallas_call x0 -> x5, Pallas kernels: none -> 47.5 us  [simple(): pl.pallas_call(kernel, grid_spec=pltpu.PrefetchScalarGridSpec(num_scalar_...]
    ppermute x5 -> x14, waiting for transfers between devices: 5.95 us -> 45.1 us  [along(): return lax.ppermute(x, 'dp', [(i, to(i)) for i in range(devices)])]
    dot_general x13 -> x3, matrix products: 30.6 us -> 0.7 us  [shuffled(): lax.dot_general(flat, shuffle.astype(x.dtype), NT if back else NN, precis...]
    ppermute x5 -> x14, starting transfers between devices: 15 us -> 24.8 us  [along(): return lax.ppermute(x, 'dp', [(i, to(i)) for i in range(devices)])]
    convert_element_type x4 -> x0, local copies, waits for them, and re-layouts: 9.29 us -> none  [the longest x3 6.78 us: over_rows(): return jnp.einsum('md,mj->dj', left[:slots].reshape(-1, left.shape[-1]),...]
    unnamed x59 -> x54, local copies, waits for them, and re-layouts: 19.6 us -> 11.6 us
  transfers between devices with their start and end apart: 15 -> 23, of which waited for: 14 -> 16; matrix products, arithmetic and copies ran while one was open for 3% -> 3% of each run, Pallas kernels for 0% -> 2%
where the time goes in v2:
time: 561 us; the launch traced here: 552 us
  Pallas kernels  251 us (45%)
  waiting for transfers between devices  193 us (34%)
  starting transfers between devices  46.2 us (8%)
  local copies, waits for them, and re-layouts  30.9 us (6%)
  between operations  15.3 us (3%)
  other arithmetic  14.7 us (3%)
    pallas_call x10, Pallas kernels, call(): pl.pallas_call(kernel, grid_spec=pltpu.PrefetchScalarGridSpec(num_scalar_...  204 us
    ppermute x8, waiting for transfers between devices, shifted(): lax.ppermute(x, 'section', [(i, i + by) for i in range(devices) if 0 <= i...  81.2 us
    all_gather x1, waiting for transfers between devices, body(): g = lax.all_gather(local, 'dp', axis=0, tiled=True)  66.5 us
    pallas_call x5, Pallas kernels, simple(): pl.pallas_call(kernel, grid_spec=pltpu.PrefetchScalarGridSpec(num_scalar_...  47.5 us
    ppermute x14, waiting for transfers between devices, along(): return lax.ppermute(x, 'dp', [(i, to(i)) for i in range(devices)])  45.1 us
    ppermute x14, starting transfers between devices, along(): return lax.ppermute(x, 'dp', [(i, to(i)) for i in range(devices)])  24.8 us
    ppermute x8, starting transfers between devices, shifted(): lax.ppermute(x, 'section', [(i, i + by) for i in range(devices) if 0 <= i...  21.4 us
    unnamed x54, local copies, waits for them, and re-layouts  11.6 us
  transfers between devices with their start and end apart: 23, of which 16 were waited for; matrix products, arithmetic and copies ran while one was open for 3% of the time, Pallas kernels for 2%

profile of v2, /device:TPU:1, one launch (start us, length us, event | category | flops | bytes accessed | tf_op | source)
XLA Modules:
  0.0 551.9 jit_solution(16386534628514125954)
XLA Ops:
  21.0 66.5 %all-gather.2.cloned.1.call-done.g = bf16[768,9344]{1,0:T(8,128)(2,1)} async-done(((bf16[24,9344]{1,0:T(8,128)(2,1)}), bf16[768,9344]{1,0:T(8,128)(2,1)}) %all-gather.2.cloned.1.call-update) | async-done | bytes 14352400 | tf_op jit(solution)/shard_map/all_gather | solution.py:537
  94.0 18.2 %shard_map.199 = (bf16[384,768]{1,0:T(8,128)(2,1)}, bf16[3,384,768]{2,1,0:T(8,128)(2,1)}, bf16[3,384,768]{2,1,0:T(8,128)(2,1)}, bf16[3,384,768]{2,1,0:T(8,128)(2...) custom-call(s32[3]{0:T(128)} %add_add_fusion.4.idx, ...), custom_call_target="tpu_custom_call", output_to_operand_aliasing={{1}: (12, {}), {2}: (13, {}), {3}: (14, {}), {4}: (15, {}),... | custom-call | flops 5888802816 | bytes 31457280 | tf_op jit(solution)/shard_map/pallas_call | solution.py:448
  116.0 12.2 %collective-permute-done.recv = bf16[384,768]{1,0:T(8,128)(2,1)S(1)} collective-permute-done((bf16[384,768]{1,0:T(8,128)(2,1)}, bf16[384,768]{1,0:T(8,128)(2,1)S(1)}, u32[]{:S(2)}, u32[]{:S(2)}) %collective-permute-start) | collective-permute-done | bytes 589856 | tf_op jit(solution)/shard_map/ppermute | solution.py:489
  129.0 18.1 %shard_map.200 = (bf16[384,768]{1,0:T(8,128)(2,1)}, bf16[3,384,768]{2,1,0:T(8,128)(2,1)}, bf16[3,384,768]{2,1,0:T(8,128)(2,1)}, bf16[3,384,768]{2,1,0:T(8,128)(2...) custom-call(s32[3]{0:T(128)} %add_add_fusion.3.idx, ...), custom_call_target="tpu_custom_call", output_to_operand_aliasing={{1}: (12, {}), {2}: (13, {}), {3}: (14, {}), {4}: (15, {}),... | custom-call | flops 5888802816 | bytes 31457280 | tf_op jit(solution)/shard_map/pallas_call | solution.py:448
  152.1 10.8 %collective-permute-done.1.recv = bf16[384,768]{1,0:T(8,128)(2,1)S(1)} collective-permute-done((bf16[384,768]{1,0:T(8,128)(2,1)}, bf16[384,768]{1,0:T(8,128)(2,1)S(1)}, u32[]{:S(2)}, u32[]{:S(2)}) %collective-permute-start.1) | collective-permute-done | bytes 589856 | tf_op jit(solution)/shard_map/ppermute | solution.py:489
  163.8 18.1 %shard_map.201 = (bf16[384,768]{1,0:T(8,128)(2,1)}, bf16[3,384,768]{2,1,0:T(8,128)(2,1)}, bf16[3,384,768]{2,1,0:T(8,128)(2,1)}, bf16[3,384,768]{2,1,0:T(8,128)(2...) custom-call(s32[3]{0:T(128)} %add_add_fusion.2.idx, ...), custom_call_target="tpu_custom_call", output_to_operand_aliasing={{1}: (12, {}), {2}: (13, {}), {3}: (14, {}), {4}: (15, {}),... | custom-call | flops 5888802816 | bytes 31457280 | tf_op jit(solution)/shard_map/pallas_call | solution.py:448
  186.7 10.1 %collective-permute-done.2.recv = bf16[384,768]{1,0:T(8,128)(2,1)S(1)} collective-permute-done((bf16[384,768]{1,0:T(8,128)(2,1)}, bf16[384,768]{1,0:T(8,128)(2,1)S(1)}, u32[]{:S(2)}, u32[]{:S(2)}) %collective-permute-start.2) | collective-permute-done | bytes 589856 | tf_op jit(solution)/shard_map/ppermute | solution.py:489
  197.6 18.1 %shard_map.202 = (bf16[384,768]{1,0:T(8,128)(2,1)}, bf16[3,384,768]{2,1,0:T(8,128)(2,1)}, bf16[3,384,768]{2,1,0:T(8,128)(2,1)}, bf16[3,384,768]{2,1,0:T(8,128)(2...) custom-call(s32[3]{0:T(128)} %add_add_fusion.1.idx, ...), custom_call_target="tpu_custom_call", output_to_operand_aliasing={{1}: (12, {}), {2}: (13, {}), {3}: (14, {}), {4}: (15, {}),... | custom-call | flops 5888802816 | bytes 31457280 | tf_op jit(solution)/shard_map/pallas_call | solution.py:448
  221.4 8.5 %collective-permute-done.3.recv = bf16[384,768]{1,0:T(8,128)(2,1)S(1)} collective-permute-done((bf16[384,768]{1,0:T(8,128)(2,1)}, bf16[384,768]{1,0:T(8,128)(2,1)S(1)}, u32[]{:S(2)}, u32[]{:S(2)}) %collective-permute-start.3) | collective-permute-done | bytes 589856 | tf_op jit(solution)/shard_map/ppermute | solution.py:489
  230.7 18.1 %shard_map.203 = (bf16[384,768]{1,0:T(8,128)(2,1)}, bf16[3,384,768]{2,1,0:T(8,128)(2,1)}, bf16[3,384,768]{2,1,0:T(8,128)(2,1)}, bf16[3,384,768]{2,1,0:T(8,128)(2...) custom-call(s32[3]{0:T(128)} %add_add_fusion.idx, ...), custom_call_target="tpu_custom_call", output_to_operand_aliasing={{1}: (12, {}), {2}: (13, {}), {3}: (14, {}), {4}: (15, {}),... | custom-call | flops 5888802816 | bytes 31457280 | tf_op jit(solution)/shard_map/pallas_call | solution.py:448
  248.8 22.7 %shard_map.214 = (bf16[384,768]{1,0:T(8,128)(2,1)}, bf16[3,384,768]{2,1,0:T(8,128)(2,1)}, bf16[3,3,384,1024]{3,2,1,0:T(8,128)(2,1)}, bf16[3,384,768]{2,1,0:T(8,1...) custom-call(s32[3]{0:T(128)} %add_add_fusion.9.idx, ...), custom_call_target="tpu_custom_call", output_to_operand_aliasing={{1}: (19, {}), {2}: (20, {}), {3}: (21, {}), {4}: (22, {}),... | custom-call | flops 6341787648 | bytes 31457280 | tf_op jit(solution)/shard_map/pallas_call | solution.py:448
  273.6 11.9 %collective-permute-done.4.recv = bf16[384,768]{1,0:T(8,128)(2,1)S(1)} collective-permute-done((bf16[384,768]{1,0:T(8,128)(2,1)}, bf16[384,768]{1,0:T(8,128)(2,1)S(1)}, u32[]{:S(2)}, u32[]{:S(2)}) %collective-permute-start.4) | collective-permute-done | bytes 589856 | tf_op jit(solution)/shard_map/ppermute | solution.py:489
  286.4 22.7 %shard_map.215 = (bf16[384,768]{1,0:T(8,128)(2,1)}, bf16[3,384,768]{2,1,0:T(8,128)(2,1)}, bf16[3,3,384,1024]{3,2,1,0:T(8,128)(2,1)}, bf16[3,384,768]{2,1,0:T(8,1...) custom-call(s32[3]{0:T(128)} %add_add_fusion.8.idx, ...), custom_call_target="tpu_custom_call", output_to_operand_aliasing={{1}: (19, {}), {2}: (20, {}), {3}: (21, {}), {4}: (22, {}),... | custom-call | flops 6341787648 | bytes 31457280 | tf_op jit(solution)/shard_map/pallas_call | solution.py:448
  311.0 10.5 %collective-permute-done.5.recv = bf16[384,768]{1,0:T(8,128)(2,1)S(1)} collective-permute-done((bf16[384,768]{1,0:T(8,128)(2,1)}, bf16[384,768]{1,0:T(8,128)(2,1)S(1)}, u32[]{:S(2)}, u32[]{:S(2)}) %collective-permute-start.5) | collective-permute-done | bytes 589856 | tf_op jit(solution)/shard_map/ppermute | solution.py:489
  322.4 22.4 %shard_map.216 = (bf16[384,768]{1,0:T(8,128)(2,1)}, bf16[3,384,768]{2,1,0:T(8,128)(2,1)}, bf16[3,3,384,1024]{3,2,1,0:T(8,128)(2,1)}, bf16[3,384,768]{2,1,0:T(8,1...) custom-call(s32[3]{0:T(128)} %add_add_fusion.7.idx, ...), custom_call_target="tpu_custom_call", output_to_operand_aliasing={{1}: (19, {}), {2}: (20, {}), {3}: (21, {}), {4}: (22, {}),... | custom-call | flops 6341787648 | bytes 31457280 | tf_op jit(solution)/shard_map/pallas_call | solution.py:448
  346.8 9.6 %collective-permute-done.6.recv = bf16[384,768]{1,0:T(8,128)(2,1)S(1)} collective-permute-done((bf16[384,768]{1,0:T(8,128)(2,1)}, bf16[384,768]{1,0:T(8,128)(2,1)S(1)}, u32[]{:S(2)}, u32[]{:S(2)}) %collective-permute-start.6) | collective-permute-done | bytes 589856 | tf_op jit(solution)/shard_map/ppermute | solution.py:489
  357.3 22.7 %shard_map.217 = (bf16[384,768]{1,0:T(8,128)(2,1)}, bf16[3,384,768]{2,1,0:T(8,128)(2,1)}, bf16[3,3,384,1024]{3,2,1,0:T(8,128)(2,1)}, bf16[3,384,768]{2,1,0:T(8,1...) custom-call(s32[3]{0:T(128)} %add_add_fusion.6.idx, ...), custom_call_target="tpu_custom_call", output_to_operand_aliasing={{1}: (19, {}), {2}: (20, {}), {3}: (21, {}), {4}: (22, {}),... | custom-call | flops 6341787648 | bytes 31457280 | tf_op jit(solution)/shard_map/pallas_call | solution.py:448
  383.4 7.5 %collective-permute-done.7.recv = bf16[384,768]{1,0:T(8,128)(2,1)S(1)} collective-permute-done((bf16[384,768]{1,0:T(8,128)(2,1)}, bf16[384,768]{1,0:T(8,128)(2,1)S(1)}, u32[]{:S(2)}, u32[]{:S(2)}) %collective-permute-start.7) | collective-permute-done | bytes 589856 | tf_op jit(solution)/shard_map/ppermute | solution.py:489
  391.7 22.5 %shard_map.218 = (bf16[384,768]{1,0:T(8,128)(2,1)}, bf16[3,384,768]{2,1,0:T(8,128)(2,1)}, bf16[3,3,384,1024]{3,2,1,0:T(8,128)(2,1)}, bf16[3,384,768]{2,1,0:T(8,1...) custom-call(s32[3]{0:T(128)} %add_add_fusion.5.idx, ...), custom_call_target="tpu_custom_call", output_to_operand_aliasing={{1}: (19, {}), {2}: (20, {}), {3}: (21, {}), {4}: (22, {}),... | custom-call | flops 6341787648 | bytes 31457280 | tf_op jit(solution)/shard_map/pallas_call | solution.py:448
  414.2 14.5 %shard_map.220 = bf16[768,4736]{1,0:T(8,128)(2,1)} custom-call(s32[4]{0:T(128)} %add_add_fusion.11.idx, f32[128,768]{1,0:T(8,128)} %fusion.2.place, bf16[3,384,768]{2,1,0:T(8,128)(2,1)} %get-tuple-element.263.hs, bf16[3,3,384,1024]{3,2,1,0:T(8,128)(2,1)} %get-tuple-element.264.acts, bf16[3,768,384]{2,1,0:T(8,128)(2,1)} %get-tuple-element.217.refs_9_.ats, ...), custom_call_target="tpu_custom_call" | custom-call | flops 5435817984 | bytes 16777216 | tf_op jit(solution)/shard_map/pallas_call | solution.py:466
  434.7 12.4 %shard_map.219 = bf16[768,4736]{1,0:T(8,128)(2,1)} custom-call(s32[4]{0:T(128)} %add_add_fusion.10.idx, f32[128,768]{1,0:T(8,128)} %fusion.2.place, bf16[3,384,768]{2,1,0:T(8,128)(2,1)} %get-tuple-element.263.hs, bf16[3,3,384,1024]{3,2,1,0:T(8,128)(2,1)} %get-tuple-element.264.acts, bf16[3,768,384]{2,1,0:T(8,128)(2,1)} %get-tuple-element.217.refs_9_.ats, ...), custom_call_target="tpu_custom_call" | custom-call | flops 5435817984 | bytes 16777216 | tf_op jit(solution)/shard_map/pallas_call | solution.py:466
  447.1 10.1 %shard_map.221 = (bf16[192,2304]{1,0:T(8,128)(2,1)}, bf16[192,2304]{1,0:T(8,128)(2,1)}, bf16[192,2304]{1,0:T(8,128)(2,1)}, bf16[192,2304]{1,0:T(8,128)(2,1)}, bf...) custom-call(s32[4]{0:T(128)} %add_add_fusion.10.idx, ...), custom_call_target="tpu_custom_call" | custom-call | flops 16777216 | bytes 16777216 | tf_op jit(solution)/shard_map/pallas_call | solution.py:466
  464.1 13.7 %collective-permute-done.10.refs_2_ = bf16[192,2304]{1,0:T(8,128)(2,1)S(1)} collective-permute-done((bf16[192,2304]{1,0:T(8,128)(2,1)}, bf16[192,2304]{1,0:T(8,128)(2,1)S(1)}, u32[]{:S(2)}, u32[]{:S(2)}) %collective-permute-start.10) | collective-permute-done | bytes 884768 | tf_op jit(solution)/shard_map/ppermute | solution.py:484
  479.2 19.4 %collective-permute-done.11.refs_3_ = bf16[192,2304]{1,0:T(8,128)(2,1)S(1)} collective-permute-done((bf16[192,2304]{1,0:T(8,128)(2,1)}, bf16[192,2304]{1,0:T(8,128)(2,1)S(1)}, u32[]{:S(2)}, u32[]{:S(2)}) %collective-permute-start.11) | collective-permute-done | bytes 884768 | tf_op jit(solution)/shard_map/ppermute | solution.py:484
  (186 shorter events, 115.1 us)
Async XLA Ops:
  7.2 80.3 %all-gather.2.cloned.1.call-start = ((), (), s32[]{:S(2)}) async-start(), calls=%async_computation | async-start | bytes 14800896 | tf_op jit(solution)/shard_map/all_gather | solution.py:537
  7.2 85.0 %copy-start.23 = (s32[256]{0:T(256)}, s32[256]{0:T(256)S(1)}, u32[]{:S(2)}) copy-start(s32[256]{0:T(256)S(1)} %fusion.11) | copy-start | bytes 3076
  112.2 16.0 %collective-permute-start = (bf16[384,768]{1,0:T(8,128)(2,1)}, bf16[384,768]{1,0:T(8,128)(2,1)S(1)}, u32[]{:S(2)}, u32[]{:S(2)}) collective-permute-start(bf16[384,768]{1,0:T(8,128)(2,1)} %get-tuple-element.151), channel_id=1, source_target_pairs={{0,32},{32,64},{64,96},{1,33},{33,65},{65,97},{2,34},{34,66},{66,9... | collective-permute-start | bytes 1769480 | tf_op jit(solution)/shard_map/ppermute | solution.py:489
  147.1 15.9 %collective-permute-start.1 = (bf16[384,768]{1,0:T(8,128)(2,1)}, bf16[384,768]{1,0:T(8,128)(2,1)S(1)}, u32[]{:S(2)}, u32[]{:S(2)}) collective-permute-start(bf16[384,768]{1,0:T(8,128)(2,1)} %get-tuple-element.165), channel_id=1, source_target_pairs={{0,32},{32,64},{64,96},{1,33},{33,65},{65,97},{2,34},{34,66},{66,9... | collective-permute-start | bytes 1769480 | tf_op jit(solution)/shard_map/ppermute | solution.py:489
  181.9 14.9 %collective-permute-start.2 = (bf16[384,768]{1,0:T(8,128)(2,1)}, bf16[384,768]{1,0:T(8,128)(2,1)S(1)}, u32[]{:S(2)}, u32[]{:S(2)}) collective-permute-start(bf16[384,768]{1,0:T(8,128)(2,1)} %get-tuple-element.179), channel_id=1, source_target_pairs={{0,32},{32,64},{64,96},{1,33},{33,65},{65,97},{2,34},{34,66},{66,9... | collective-permute-start | bytes 1769480 | tf_op jit(solution)/shard_map/ppermute | solution.py:489
  215.8 14.0 %collective-permute-start.3 = (bf16[384,768]{1,0:T(8,128)(2,1)}, bf16[384,768]{1,0:T(8,128)(2,1)S(1)}, u32[]{:S(2)}, u32[]{:S(2)}) collective-permute-start(bf16[384,768]{1,0:T(8,128)(2,1)} %get-tuple-element.193), channel_id=1, source_target_pairs={{0,32},{32,64},{64,96},{1,33},{33,65},{65,97},{2,34},{34,66},{66,9... | collective-permute-start | bytes 1769480 | tf_op jit(solution)/shard_map/ppermute | solution.py:489
  271.6 14.0 %collective-permute-start.4 = (bf16[384,768]{1,0:T(8,128)(2,1)}, bf16[384,768]{1,0:T(8,128)(2,1)S(1)}, u32[]{:S(2)}, u32[]{:S(2)}) collective-permute-start(bf16[384,768]{1,0:T(8,128)(2,1)} %get-tuple-element.218), channel_id=1, source_target_pairs={{32,0},{64,32},{96,64},{33,1},{65,33},{97,65},{34,2},{66,34},{98,6... | collective-permute-start | bytes 1769480 | tf_op jit(solution)/shard_map/ppermute | solution.py:489
  309.1 12.4 %collective-permute-start.5 = (bf16[384,768]{1,0:T(8,128)(2,1)}, bf16[384,768]{1,0:T(8,128)(2,1)S(1)}, u32[]{:S(2)}, u32[]{:S(2)}) collective-permute-start(bf16[384,768]{1,0:T(8,128)(2,1)} %get-tuple-element.229), channel_id=1, source_target_pairs={{32,0},{64,32},{96,64},{33,1},{65,33},{97,65},{34,2},{66,34},{98,6... | collective-permute-start | bytes 1769480 | tf_op jit(solution)/shard_map/ppermute | solution.py:489
  344.9 11.5 %collective-permute-start.6 = (bf16[384,768]{1,0:T(8,128)(2,1)}, bf16[384,768]{1,0:T(8,128)(2,1)S(1)}, u32[]{:S(2)}, u32[]{:S(2)}) collective-permute-start(bf16[384,768]{1,0:T(8,128)(2,1)} %get-tuple-element.240), channel_id=1, source_target_pairs={{32,0},{64,32},{96,64},{33,1},{65,33},{97,65},{34,2},{66,34},{98,6... | collective-permute-start | bytes 1769480 | tf_op jit(solution)/shard_map/ppermute | solution.py:489
  380.0 10.8 %collective-permute-start.7 = (bf16[384,768]{1,0:T(8,128)(2,1)}, bf16[384,768]{1,0:T(8,128)(2,1)S(1)}, u32[]{:S(2)}, u32[]{:S(2)}) collective-permute-start(bf16[384,768]{1,0:T(8,128)(2,1)} %get-tuple-element.251), channel_id=1, source_target_pairs={{32,0},{64,32},{96,64},{33,1},{65,33},{97,65},{34,2},{66,34},{98,6... | collective-permute-start | bytes 1769480 | tf_op jit(solution)/shard_map/ppermute | solution.py:489
  428.7 18.4 %collective-permute-start.8 = (bf16[768,4736]{1,0:T(8,128)(2,1)}, bf16[768,4736]{1,0:T(8,128)(2,1)}, u32[]{:S(2)}, u32[]{:S(2)}) collective-permute-start(bf16[768,4736]{1,0:T(8,128)(2,1)} %shard_map.220), channel_id=1, source_target_pairs={{0,1},{1,0},{2,3},{3,2},{4,5},{5,4},{6,7},{7,6},{8,9},{9,8},{10,11... | collective-permute-start | bytes 21823496 | tf_op jit(solution)/shard_map/ppermute | solution.py:484
  457.3 20.6 %collective-permute-start.10 = (bf16[192,2304]{1,0:T(8,128)(2,1)}, bf16[192,2304]{1,0:T(8,128)(2,1)S(1)}, u32[]{:S(2)}, u32[]{:S(2)}) collective-permute-start(bf16[192,2304]{1,0:T(8,128)(2,1)} %get-tuple-element.276), channel_id=1, source_target_pairs={{0,16},{1,17},{2,18},{3,19},{4,20},{5,21},{6,22},{7,23},{8,24},{9,... | collective-permute-start | bytes 2654216 | tf_op jit(solution)/shard_map/ppermute | solution.py:484
  460.0 38.6 %collective-permute-start.12 = (bf16[4,48,2432]{2,1,0:T(8,128)(2,1)}, bf16[4,48,2432]{2,1,0:T(8,128)(2,1)S(1)}, u32[]{:S(2)}, u32[]{:S(2)}) collective-permute-start(bf16[4,48,2432]{2,1,0:T(8,128)(2,1)} %get-tuple-element.279), channel_id=1, source_target_pairs={{0,2},{1,3},{2,4},{3,5},{4,6},{5,7},{6,0},{7,1},{8,10},{9,11},{10,... | collective-permute-start | bytes 2801672 | tf_op jit(solution)/shard_map/ppermute | solution.py:484
  460.0 40.2 %collective-permute-start.13 = (bf16[4,48,2432]{2,1,0:T(8,128)(2,1)}, bf16[4,48,2432]{2,1,0:T(8,128)(2,1)S(1)}, u32[]{:S(2)}, u32[]{:S(2)}) collective-permute-start(bf16[4,48,2432]{2,1,0:T(8,128)(2,1)} %get-tuple-element.280), channel_id=1, source_target_pairs={{0,4},{1,5},{2,6},{3,7},{4,0},{5,1},{6,2},{7,3},{8,12},{9,13},{10,... | collective-permute-start | bytes 2801672 | tf_op jit(solution)/shard_map/ppermute | solution.py:484
  461.8 41.9 %collective-permute-start.14 = (bf16[4,48,2432]{2,1,0:T(8,128)(2,1)}, bf16[4,48,2432]{2,1,0:T(8,128)(2,1)S(1)}, u32[]{:S(2)}, u32[]{:S(2)}) collective-permute-start(bf16[4,48,2432]{2,1,0:T(8,128)(2,1)} %get-tuple-element.281), channel_id=1, source_target_pairs={{0,6},{1,7},{2,0},{3,1},{4,2},{5,3},{6,4},{7,5},{8,14},{9,15},{10,... | collective-permute-start | bytes 2801672 | tf_op jit(solution)/shard_map/ppermute | solution.py:484
  463.2 35.4 %collective-permute-start.11 = (bf16[192,2304]{1,0:T(8,128)(2,1)}, bf16[192,2304]{1,0:T(8,128)(2,1)S(1)}, u32[]{:S(2)}, u32[]{:S(2)}) collective-permute-start(bf16[192,2304]{1,0:T(8,128)(2,1)} %get-tuple-element.277), channel_id=1, source_target_pairs={{0,24},{1,25},{2,26},{3,27},{4,28},{5,29},{6,30},{7,31},{8,0},{9,1... | collective-permute-start | bytes 2654216 | tf_op jit(solution)/shard_map/ppermute | solution.py:484
  477.8 20.7 %collective-permute-start.9 = (bf16[192,2304]{1,0:T(8,128)(2,1)}, bf16[192,2304]{1,0:T(8,128)(2,1)S(1)}, u32[]{:S(2)}, u32[]{:S(2)}) collective-permute-start(bf16[192,2304]{1,0:T(8,128)(2,1)} %get-tuple-element.275), channel_id=1, source_target_pairs={{0,8},{1,9},{2,10},{3,11},{4,12},{5,13},{6,14},{7,15},{8,16},{9,17... | collective-permute-start | bytes 2654216 | tf_op jit(solution)/shard_map/ppermute | solution.py:484
  511.6 8.2 %collective-permute-start.15 = (bf16[48,2304]{1,0:T(8,128)(2,1)}, bf16[48,2304]{1,0:T(8,128)(2,1)S(1)}, u32[]{:S(2)}, u32[]{:S(2)}) collective-permute-start(bf16[48,2304]{1,0:T(8,128)(2,1)} %get-tuple-element.283), channel_id=1, source_target_pairs={{0,2},{1,3},{2,4},{3,5},{4,6},{5,7},{6,0},{7,1},{8,10},{9,11},{10,... | collective-permute-start | bytes 663560 | tf_op jit(solution)/shard_map/ppermute | solution.py:484
  513.0 14.5 %collective-permute-start.18 = (bf16[48,2432]{1,0:T(8,128)(2,1)}, bf16[48,2432]{1,0:T(8,128)(2,1)S(1)}, u32[]{:S(2)}, u32[]{:S(2)}) collective-permute-start(bf16[48,2432]{1,0:T(8,128)(2,1)} %get-tuple-element.287), channel_id=1, source_target_pairs={{0,8},{1,9},{2,10},{3,11},{4,12},{5,13},{6,14},{7,15},{8,16},{9,17... | collective-permute-start | bytes 700424 | tf_op jit(solution)/shard_map/ppermute | solution.py:484
  513.3 14.3 %collective-permute-start.19 = (bf16[48,2432]{1,0:T(8,128)(2,1)}, bf16[48,2432]{1,0:T(8,128)(2,1)S(1)}, u32[]{:S(2)}, u32[]{:S(2)}) collective-permute-start(bf16[48,2432]{1,0:T(8,128)(2,1)} %get-tuple-element.288), channel_id=1, source_target_pairs={{0,16},{1,17},{2,18},{3,19},{4,20},{5,21},{6,22},{7,23},{8,24},{9,... | collective-permute-start | bytes 700424 | tf_op jit(solution)/shard_map/ppermute | solution.py:484
  515.2 12.4 %collective-permute-start.20 = (bf16[48,2432]{1,0:T(8,128)(2,1)}, bf16[48,2432]{1,0:T(8,128)(2,1)}, u32[]{:S(2)}, u32[]{:S(2)}) collective-permute-start(bf16[48,2432]{1,0:T(8,128)(2,1)} %get-tuple-element.289), channel_id=1, source_target_pairs={{0,24},{1,25},{2,26},{3,27},{4,28},{5,29},{6,30},{7,31},{8,0},{9,1... | collective-permute-start | bytes 700424 | tf_op jit(solution)/shard_map/ppermute | solution.py:484
  516.0 10.1 %collective-permute-start.16 = (bf16[48,2304]{1,0:T(8,128)(2,1)}, bf16[48,2304]{1,0:T(8,128)(2,1)S(1)}, u32[]{:S(2)}, u32[]{:S(2)}) collective-permute-start(bf16[48,2304]{1,0:T(8,128)(2,1)} %get-tuple-element.284), channel_id=1, source_target_pairs={{0,4},{1,5},{2,6},{3,7},{4,0},{5,1},{6,2},{7,3},{8,12},{9,13},{10,... | collective-permute-start | bytes 663560 | tf_op jit(solution)/shard_map/ppermute | solution.py:484
  519.8 7.7 %collective-permute-start.17 = (bf16[48,2304]{1,0:T(8,128)(2,1)}, bf16[48,2304]{1,0:T(8,128)(2,1)S(1)}, u32[]{:S(2)}, u32[]{:S(2)}) collective-permute-start(bf16[48,2304]{1,0:T(8,128)(2,1)} %get-tuple-element.285), channel_id=1, source_target_pairs={{0,6},{1,7},{2,0},{3,1},{4,2},{5,3},{6,4},{7,5},{8,14},{9,15},{10,... | collective-permute-start | bytes 663560 | tf_op jit(solution)/shard_map/ppermute | solution.py:484
  531.9 6.6 %collective-permute-start.21 = (f32[24,4736]{1,0:T(8,128)}, f32[24,4736]{1,0:T(8,128)}, u32[]{:S(2)}, u32[]{:S(2)}) collective-permute-start(f32[24,4736]{1,0:T(8,128)} %get-tuple-element.290), channel_id=1, source_target_pairs={{0,1},{1,0},{2,3},{3,2},{4,5},{5,4},{6,7},{7,6},{8,9},{9,8},{10,11... | collective-permute-start | bytes 1363976 | tf_op jit(solution)/shard_map/ppermute | solution.py:484
  (25 other events, 110.6 us)
Sparse Core Ops, SparseCore 0:
  16.7 70.7 all-gather.1

commit v3 on v1

--- a/solution.py
+++ b/solution.py
@@ -14,6 +14,7 @@
 EPS = 1e-06
 NN = (((1,), (0,)), ((), ()))
 NT = (((1,), (1,)), ((), ()))
+TN = (((0,), (0,)), ((), ()))
 LANES = 128
 WIDE = 256
 ABSENT = 16
@@ -59,6 +60,13 @@
         self.used += 1
         copy.start()
         return copy
+
+
+def result_out(value, stack, entry, copies):
+    @pl.when(entry < stack.shape[0])
+    def _():
+        copy = copies.start(value, stack.at[entry])
+        copy.wait()
 
 
 def forward_kernel(d, ff, chunks, idx, tok, recv, g, g3, ids_col, ids_row, ngain, gains, ubias, obias, spread, *refs):
@@ -157,7 +165,7 @@
     y = keep * (keep * x_v[...].astype(F32) + acc_v[...] + mm(att_v[...], a_v[...]) + obias[...])
     y_v[...] = y
     ybf[...] = y.astype(BF)
-    pending.append(cout.start(y_v, y_out.at[st]))
+    result_out(y_v, y_out, st, cout)
     for copy in pending:
         copy.wait()
 
@@ -271,9 +279,186 @@
     out = keep * (keep * g_v[...].astype(F32) + gmask)
     out_v[...] = out
     gbf[...] = out.astype(BF)
-    pending += [cout.start(out_v, grs.at[st]), cout.start(ng_v, ngs.at[st])]
+    pending.append(cout.start(ng_v, ngs.at[st]))
+    result_out(out_v, grs, st, cout)
     for copy in pending:
         copy.wait()
+
+
+def split_small(values):
+    top = values.astype(BF).astype(F32)
+    lane = lax.broadcasted_iota(jnp.int32, values.shape, 1)
+    return jnp.where(lane < 8, top, jnp.where(lane < 16, pltpu.roll(values - top, 8, 1), 0.0)).astype(BF)
+
+
+def joined_small(parts):
+    return parts + pltpu.roll(parts, LANES - 8, 1)
+
+
+def small_table(d, ff, place, obs, ngs, qkgs, ubs):
+    def over_slots(ref):
+        total = ref[0]
+        for s in range(1, ref.shape[0] - 1):
+            total = total + ref[s]
+        return total
+
+    quarter = WIDE // 4
+    ub = over_slots(ubs)
+    up_rows = []
+    for j in range(4):
+        pieces = [ub[:, WIDE * b + quarter * j : WIDE * b + quarter * (j + 1)] for b in range(ff // WIDE)]
+        up_rows.append(jnp.concatenate(pieces, axis=1))
+    qk = over_slots(qkgs)
+    head_rows = []
+    for i in range(2):
+        lanes = qk[:, d * i : d * i + LANES]
+        for p in range(1, d // LANES):
+            lanes = lanes + qk[:, d * i + LANES * p : d * i + LANES * (p + 1)]
+        head_rows.append(lanes)
+    both = jnp.concatenate(head_rows + [jnp.zeros((6, LANES), F32)], axis=0)
+    placed = lax.dot_general(both, place[...], NN, precision=lax.Precision.HIGHEST, preferred_element_type=F32)
+    rows = [over_slots(ngs), over_slots(obs)] + up_rows + [placed[0:1], placed[1:2], jnp.zeros((LANES - 8, d), F32)]
+    return jnp.concatenate(rows, axis=0).T
+
+
+def weight_grad_kernel(d, ff, chunks, part, mine, idx, place, hs, acts, ats, gbs, gjs, gqk, gvs, obs, ngs, qkgs, ubs, *refs):
+    if mine:
+        got, refs = refs[0], refs[1:]
+    outs_hbm, (h_v, big_v, side_v, at_v, out_v, got_v, ins, outs) = refs[:-8], refs[-8:]
+    slots, rows = h_v.shape[0], h_v.shape[1]
+    fc = ff // chunks
+    blocks, quarter, half = fc // WIDE, WIDE // 4, ff // 2
+    y, z = idx[1], idx[2]
+    live = pl.ds(0, slots)
+    tokens = slots * rows
+    arrive = pltpu.make_async_copy(got, got_v, ins.at[15]) if mine else None
+    if mine:
+        arrive.start()
+
+    def put(rows_at, cols_at, value):
+        if mine:
+            value = value + got_v[rows_at, cols_at].astype(F32)
+        out_v[rows_at, cols_at] = value.astype(BF)
+
+    def send():
+        cout = Copies(outs)
+        if not mine:
+            return [cout.start(out_v, outs_hbm[0])]
+        share = d // 16
+        if part == 0:
+            return [cout.start(out_v.at[pl.ds(pl.multiple_of(lax.rem(y + s, 4) * 4 * share, 16), 4 * share)], outs_hbm[s])
+                    for s in (1, 2, 3, 0)]
+        return [
+            cout.start(out_v.at[pl.ds(pl.multiple_of((4 * i + lax.rem(z + s, 4)) * share, 16), share)], outs_hbm[s].at[i])
+            for s in (1, 2, 3, 0) for i in range(4)
+        ]
+
+    @pl.when(idx[0] == 0)
+    def _():
+        cin = Copies(ins)
+        grads = cin.start(gbs.at[live], h_v)
+        loads = [
+            [cin.start(acts.at[live, c, :, pl.ds(WIDE * b + LANES * part, LANES)],
+                       big_v.at[:, :, pl.ds(LANES * (blocks * c + b), LANES)]) for b in range(blocks)]
+            for c in range(chunks)
+        ]
+        last = [cin.start(ats.at[live], at_v)] if part == 0 else [
+            cin.start(hs.at[live], side_v.at[0]), cin.start(gvs.at[live], side_v.at[1])]
+        grads.wait()
+        gb = h_v[...].reshape(tokens, d)
+        if mine:
+            arrive.wait()
+        for c in range(chunks):
+            for copy in loads[c]:
+                copy.wait()
+            left = big_v[:, :, LANES * blocks * c : LANES * blocks * (c + 1)].reshape(tokens, LANES * blocks)
+            got_c = lax.dot_general(left, gb, TN, preferred_element_type=F32)
+            for b in range(blocks):
+                for j in range(2):
+                    at = quarter * (blocks * c + b)
+                    put(slice(at, at + quarter), slice(d * j, d * j + d),
+                        got_c[LANES * b + quarter * j : LANES * b + quarter * (j + 1)])
+        for copy in last:
+            copy.wait()
+        everything = slice(0, d)
+        if part == 0:
+            total = mm(at_v[0], h_v[0])
+            for s in range(1, slots):
+                total = total + mm(at_v[s], h_v[s])
+            put(everything, slice(2 * d, 3 * d), total)
+        else:
+            put(everything, slice(2 * d, 3 * d), lax.dot_general(
+                side_v[0].reshape(tokens, d), side_v[1].reshape(tokens, d), TN, preferred_element_type=F32))
+            table = small_table(d, ff, place, obs, ngs, qkgs, ubs)
+            if mine:
+                table = table + joined_small(got_v[:, 3 * d :].astype(F32))
+            out_v[:, 3 * d :] = split_small(table)
+        for copy in send():
+            copy.wait()
+
+    @pl.when(idx[0] == 1)
+    def _():
+        cin = Copies(ins)
+        hidden = cin.start(hs.at[live], h_v)
+        if part == 0:
+            loads = [cin.start(gjs.at[live, 0], big_v.at[:, :, pl.ds(0, fc)]),
+                     cin.start(gjs.at[live, 1, :, pl.ds(0, fc // 2)], big_v.at[:, :, pl.ds(fc, fc // 2)])]
+        else:
+            loads = [cin.start(gjs.at[live, 1, :, pl.ds(fc // 2, fc // 2)], big_v.at[:, :, pl.ds(0, fc // 2)]),
+                     cin.start(gjs.at[live, 2], big_v.at[:, :, pl.ds(fc // 2, fc)])]
+        loads.append(cin.start(gqk.at[live], side_v.at[0]))
+        hidden.wait()
+        turned = h_v[...].reshape(tokens, d).T
+        if mine:
+            arrive.wait()
+        for copy in loads:
+            copy.wait()
+        everything = slice(0, d)
+        for at in range(0, half, fc // 2):
+            put(everything, slice(at, at + fc // 2), mm(turned, big_v[:, :, at : at + fc // 2].reshape(tokens, fc // 2)))
+        put(everything, slice(half, half + d), mm(turned, side_v[0].reshape(tokens, d)))
+        if part == 1:
+            out_v[:, 3 * d :] = jnp.zeros((d, LANES), BF)
+        for copy in send():
+            copy.wait()
+
+
+def added(parts):
+    total = parts[0][...].astype(F32)
+    for part in parts[1:]:
+        total = total + part[...].astype(F32)
+    shape = total.shape
+    total = total.reshape(-1, shape[-1])
+    main, last = total[:, : shape[-1] - LANES], split_small(joined_small(total[:, shape[-1] - LANES :]))
+    return jnp.concatenate([main.astype(BF), last], axis=1).reshape(shape)
+
+
+def mid_kernel(part, idx, *refs):
+    came, outs, hold = refs[:4], refs[4:8], refs[8]
+    if part == 0:
+        total = came[0][...].astype(F32)
+        for piece in came[1:]:
+            total = total + piece[...].astype(F32)
+        hold[...] = total.astype(BF).reshape(hold.shape)
+    else:
+        hold[...] = added(came)
+    at = idx[2] if part == 0 else idx[1]
+    for s in range(4):
+        outs[s][...] = hold[lax.rem(at + s, 4)]
+
+
+def last_kernel(idx, *refs):
+    firsts, seconds, mine, theirs, hold = refs[:4], refs[4:8], refs[8], refs[9], refs[10]
+    cut = firsts[0].shape[-1]
+    for group, at in ((firsts, 0), (seconds, cut)):
+        total = group[0][...].astype(F32)
+        for part in group[1:]:
+            total = total + part[...].astype(F32)
+        hold[:, at : at + total.shape[1]] = total
+    count = mine.shape[0]
+    core = idx[3]
+    mine[...] = hold[pl.ds(pl.multiple_of(core * count, 8), count), :]
+    theirs[...] = hold[pl.ds(pl.multiple_of((1 - core) * count, 8), count), :]
 
 
 ANY = pl.BlockSpec(memory_space=pl.ANY)
@@ -305,18 +490,31 @@
     return outs[0], outs[1:]
 
 
+def simple(kernel, idx, arrays, specs, out_shapes, out_specs, scratch, flops=1 << 24):
+    return pl.pallas_call(
+        kernel,
+        grid_spec=pltpu.PrefetchScalarGridSpec(
+            num_scalar_prefetch=1, grid=(1,), in_specs=specs, out_specs=out_specs, scratch_shapes=scratch
+        ),
+        out_shape=out_shapes,
+        compiler_params=pltpu.CompilerParams(dimension_semantics=("arbitrary",), vmem_limit_bytes=VMEM_LIMIT),
+        cost_estimate=pl.CostEstimate(flops=flops, bytes_accessed=16 << 20, transcendentals=0),
+    )(idx, *arrays)
+
+
+def along(x, step, size, by):
+    devices = lax.axis_size("dp")
+
+    def to(i):
+        digit = i // step % size
+        return i + ((digit + by) % size - digit) * step
+
+    return lax.ppermute(x, "dp", [(i, to(i)) for i in range(devices)])
+
+
 def shifted(x, by):
     devices = lax.axis_size("section")
     return lax.ppermute(x, "section", [(i, i + by) for i in range(devices) if 0 <= i + by < devices])
-
-
-def summed_everywhere(x):
-    devices = lax.axis_size("dp")
-    step = 1
-    while step < devices:
-        x = x + lax.ppermute(x, "dp", [(i, i ^ step) for i in range(devices)])
-        step *= 2
-    return x
 
 
 def body(tokens, cotangent, lengths, proj_in, proj_attn, proj_down, norm_gain, query_gain, key_gain, up_bias, out_bias):
@@ -344,7 +542,7 @@
 
     def shuffled(x, back=False):
         flat = x.reshape(-1, WIDE)
-        out = lax.dot_general(flat, shuffle, NT if back else NN, preferred_element_type=F32)
+        out = lax.dot_general(flat, shuffle.astype(x.dtype), NT if back else NN, precision=lax.Precision.HIGHEST, preferred_element_type=F32)
         return out.reshape(x.shape)
 
     small = jnp.concatenate(
@@ -383,10 +581,10 @@
     image = jnp.where(position[None, :] < ends[:, 2:3], image, ABSENT + position[None, :])
     ids_col, ids_row = image[:, :, None], image[:, None, :]
 
-    def stash(*shape, dtype=BF):
+    def stash(*shape, dtype=BF, spare=1):
         return pl.pallas_call(
             lambda out: None,
-            out_shape=jax.ShapeDtypeStruct((slots + 1,) + shape, dtype),
+            out_shape=jax.ShapeDtypeStruct((slots + spare,) + shape, dtype),
             out_specs=pl.BlockSpec(memory_space=pl.ANY),
         )()
 
@@ -394,7 +592,7 @@
     groups = ff // WIDE
     kept = [stash(rows, d), stash(rows, d), stash(rows, d), stash(rows, d), stash(rows, d), stash(rows, 2 * d), stash(rows, 2 * d),
             stash(chunks, rows, fc), stash(chunks, rows, fc), stash(heads, rows, rows), stash(16, rows, dtype=F32),
-            stash(d, rows), stash(rows, d, dtype=F32)]
+            stash(d, rows), stash(rows, d, dtype=F32, spare=0)]
 
     def index_of(tick, distance, first):
         which = tick - distance
@@ -428,7 +626,7 @@
 
     xs, hs, qs, ks, vs, ns, nrs, acts, gps, es, rsums, ats, ys = kept
     back = [stash(rows, d), stash(chunks, rows, fc), stash(rows, d), stash(rows, d), stash(rows, d),
-            stash(rows, d, dtype=F32), stash(1, d, dtype=F32), stash(1, d, dtype=F32), stash(1, 2 * d, dtype=F32), stash(1, ff, dtype=F32)]
+            stash(rows, d, dtype=F32, spare=0), stash(1, d, dtype=F32), stash(1, d, dtype=F32), stash(1, 2 * d, dtype=F32), stash(1, ff, dtype=F32)]
     recv = nothing
     for t in range(ticks):
         gbf, back = call(
@@ -452,40 +650,70 @@
 
     gbs, gjs, gqs, gks, gvs, grs, obs, ngs, qkgs, ubs = back
 
-    def over_rows(left, right):
-        return jnp.einsum("md,mj->dj", left[:slots].reshape(-1, left.shape[-1]), right[:slots].reshape(-1, right.shape[-1]),
-                          preferred_element_type=F32).astype(BF)
-
-    g_up = [jnp.einsum("smd,smj->dj", hs[:slots], gjs[:slots, c], preferred_element_type=F32).astype(BF) for c in range(chunks)]
-    g_heads = [over_rows(hs, v) for v in (gqs, gks, gvs)]
-    g_attn = jnp.einsum("sdm,smj->dj", ats[:slots], gbs[:slots], preferred_element_type=F32).astype(BF)
-    g_down = [jnp.einsum("smf,smj->fj", acts[:slots, c], gbs[:slots], preferred_element_type=F32).astype(BF) for c in range(chunks)]
-    g_down = jnp.concatenate(g_down).reshape(groups, fshare, WIDE // fshare, d).transpose(0, 2, 1, 3).reshape(d, fshare * d)
-    flat = jnp.concatenate([jnp.sum(v[:slots], axis=0)[0] for v in (ngs, obs, qkgs, ubs)]).reshape(-1, LANES)
-    flat = summed_everywhere(flat).reshape(-1)
-    g_ng, g_ob, g_q, g_k, g_ub = (flat[:d], flat[d : 2 * d], flat[2 * d : 3 * d], flat[3 * d : 4 * d], flat[4 * d :])
-    g_q, g_k = (jnp.sum(v.reshape(heads, head), axis=0) for v in (g_q, g_k))
-    g_ub = g_ub.reshape(-1, fshare, WIDE // fshare).transpose(0, 2, 1).reshape(-1)
-
-    def share(v):
-        size = v.shape[0] // ranks
-        return lax.dynamic_slice_in_dim(v, rank * size, size)[None]
-
-    total = lax.optimization_barrier(
-        lax.psum_scatter(jnp.concatenate(g_up + g_heads + [g_attn, g_down], axis=1), "dp", scatter_dimension=0, tiled=True)
+    side = math.isqrt(ranks // 2)
+    core, z, y = lax.rem(rank, 2), lax.rem(rank // 2, side), rank // (2 * side)
+    width = 6 * d + LANES
+    widths = (3 * d, 3 * d + LANES)
+    share = 2 * dshare
+    position = jnp.arange(LANES, dtype=jnp.int32)[:, None] % head
+    place = (position // hshare * dshare + position % hshare == jnp.arange(d, dtype=jnp.int32)[None, :]).astype(F32)
+    here = jnp.stack([core, y, z, core]).astype(jnp.int32)
+    there = jnp.stack([1 - core, y, z, core]).astype(jnp.int32)
+
+    def weight_grads(idx, part, got=None):
+        w = widths[part]
+        mine = got is not None
+        if not mine:
+            shapes = [jax.ShapeDtypeStruct((d, w), BF)]
+        else:
+            shapes = [jax.ShapeDtypeStruct((side * share, w) if part == 0 else (side, share, w), BF)] * side
+        smalls = [obs, ngs, qkgs, ubs]
+        return simple(
+            partial(weight_grad_kernel, d, ff, chunks, part, mine), idx,
+            [place, hs, acts, ats, gbs, gjs, (gqs, gks)[part], gvs] + smalls + ([got] if mine else []),
+            [whole((LANES, d))] + [ANY] * 7 + [whole(a.shape) for a in smalls] + ([ANY] if mine else []),
+            shapes, [ANY] * len(shapes),
+            [V((slots, rows, d), BF), V((slots, rows, ff // 2), BF), V((2, slots, rows, d), BF), V((slots, d, rows), BF),
+             V((d, w), BF), V((d, w), BF),
+             pltpu.SemaphoreType.DMA((16,)), pltpu.SemaphoreType.DMA((16,))],
+            2 * d * slots * rows * 3 * d,
+        )
+
+    steps = ((2 * side, 2), (2, 2 * side))
+    got = [along(weight_grads(there, part)[0], 1, 2, 1) for part in range(2)]
+    arrived = []
+    for part in range(2):
+        outs = weight_grads(here, part, got[part])
+        first, second = steps[part]
+        came = [outs[0]] + [along(outs[s], first, side, s) for s in (1, 2, 3)]
+        outs = simple(
+            partial(mid_kernel, part), here, came, [whole(a.shape) for a in came],
+            [jax.ShapeDtypeStruct((share, widths[part]), BF)] * side, [whole((share, widths[part]))] * side,
+            [V((side, share, widths[part]), BF)],
+        )
+        arrived += [outs[0]] + [along(outs[s], second, side, s) for s in (1, 2, 3)]
+    mine, other = simple(
+        last_kernel, here, arrived, [whole(a.shape) for a in arrived],
+        [jax.ShapeDtypeStruct((dshare, width), F32)] * 2, [whole((dshare, width))] * 2,
+        [V((share, width), F32)],
     )
-    g_in = jnp.concatenate([total[:, ff:joined].astype(F32), shuffled(total[:, :ff], back=True)], axis=1)
+    other = along(other, 1, 2, 1)
+    half0, half1 = jnp.where(core == 0, mine, other), jnp.where(core == 0, other, mine)
+    ups = shuffled(jnp.concatenate([half1[:, : 2 * d], half1[:, 3 * d : 5 * d]], axis=1), back=True)
+    g_in = jnp.concatenate([half1[:, 2 * d : 3 * d], half1[:, 5 * d : 6 * d], half0[:, 5 * d : 6 * d], ups], axis=1)
+    g_down = jnp.concatenate([half0[:, : 2 * d], half0[:, 3 * d : 5 * d]], axis=1)
+    last = half0[:, 6 * d : 6 * d + 8] + half0[:, 6 * d + 8 : 6 * d + 16]
     return (
-        ys[:slots].reshape(1, slots * rows, d),
-        grs[:slots].reshape(1, slots * rows, d),
+        ys.reshape(1, slots * rows, d),
+        grs.reshape(1, slots * rows, d),
         g_in[None],
-        total[None, :, joined : joined + d].astype(F32),
-        total[:, joined + d : wide].astype(F32).reshape(1, dshare * fshare, d),
-        share(g_ng),
-        share(g_q),
-        share(g_k),
-        share(g_ub),
-        share(g_ob),
+        half0[None, :, 2 * d : 3 * d],
+        g_down.reshape(1, dshare * fshare, d),
+        last[None, :, 0],
+        last[None, :hshare, 6],
+        last[None, :hshare, 7],
+        last[:, 2:6].reshape(1, dshare * fshare),
+        last[None, :, 1],
     )
 
 

time: 606 us -> 561 us (0.926)
  Pallas kernels: 203 us -> 253 us
  waiting for transfers between devices: 235 us -> 193 us
  matrix products: 30.6 us -> 0.71 us
  local copies, waits for them, and re-layouts: 55.1 us -> 28.2 us
  starting transfers between devices: 36.7 us -> 46 us
    reduce_scatter x1 -> x0, waiting for transfers between devices: 80.2 us -> none  [body(): lax.psum_scatter(jnp.concatenate(g_up + g_heads + [g_attn, g_down], axis=...]
    pallas_call x0 -> x7, Pallas kernels: none -> 52.9 us  [simple(): pl.pallas_call(kernel, grid_spec=pltpu.PrefetchScalarGridSpec(num_scalar_...]
    ppermute x5 -> x15, waiting for transfers between devices: 5.95 us -> 45.5 us  [along(): return lax.ppermute(x, 'dp', [(i, to(i)) for i in range(devices)])]
    dot_general x13 -> x3, matrix products: 30.6 us -> 0.71 us  [shuffled(): lax.dot_general(flat, shuffle.astype(x.dtype), NT if back else NN, precis...]
    ppermute x5 -> x15, starting transfers between devices: 15 us -> 24.8 us  [along(): return lax.ppermute(x, 'dp', [(i, to(i)) for i in range(devices)])]
    convert_element_type x4 -> x0, local copies, waits for them, and re-layouts: 9.29 us -> none  [the longest x3 6.78 us: over_rows(): return jnp.einsum('md,mj->dj', left[:slots].reshape(-1, left.shape[-1]),...]
    unnamed x59 -> x50, local copies, waits for them, and re-layouts: 19.6 us -> 12 us
  transfers between devices with their start and end apart: 15 -> 24, of which waited for: 14 -> 17; matrix products, arithmetic and copies ran while one was open for 3% -> 2% of each run, Pallas kernels for 0% -> 7%
where the time goes in v3:
time: 561 us; the launch traced here: 551 us
  Pallas kernels  253 us (45%)
  waiting for transfers between devices  193 us (34%)
  starting transfers between devices  46 us (8%)
  local copies, waits for them, and re-layouts  28.2 us (5%)
  between operations  15.3 us (3%)
  other arithmetic  14.8 us (3%)
    pallas_call x10, Pallas kernels, call(): pl.pallas_call(kernel, grid_spec=pltpu.PrefetchScalarGridSpec(num_scalar_...  200 us
    ppermute x8, waiting for transfers between devices, shifted(): lax.ppermute(x, 'section', [(i, i + by) for i in range(devices) if 0 <= i...  81.3 us
    all_gather x1, waiting for transfers between devices, body(): g = lax.all_gather(local, 'dp', axis=0, tiled=True)  66.5 us
    pallas_call x7, Pallas kernels, simple(): pl.pallas_call(kernel, grid_spec=pltpu.PrefetchScalarGridSpec(num_scalar_...  52.9 us
    ppermute x15, waiting for transfers between devices, along(): return lax.ppermute(x, 'dp', [(i, to(i)) for i in range(devices)])  45.5 us
    ppermute x15, starting transfers between devices, along(): return lax.ppermute(x, 'dp', [(i, to(i)) for i in range(devices)])  24.8 us
    ppermute x8, starting transfers between devices, shifted(): lax.ppermute(x, 'section', [(i, i + by) for i in range(devices) if 0 <= i...  21.2 us
    unnamed x50, local copies, waits for them, and re-layouts  12 us
  transfers between devices with their start and end apart: 24, of which 17 were waited for; matrix products, arithmetic and copies ran while one was open for 2% of the time, Pallas kernels for 7%

profile of v3, /device:TPU:1, one launch (start us, length us, event | category | flops | bytes accessed | tf_op | source)
XLA Modules:
  0.0 550.9 jit_solution(6193188095556509400)
XLA Ops:
  21.0 66.5 %all-gather.2.cloned.1.call-done.g = bf16[768,9344]{1,0:T(8,128)(2,1)} async-done(((bf16[24,9344]{1,0:T(8,128)(2,1)}), bf16[768,9344]{1,0:T(8,128)(2,1)}) %all-gather.2.cloned.1.call-update) | async-done | bytes 14352400 | tf_op jit(solution)/shard_map/all_gather | solution.py:565
  94.0 18.3 %shard_map.199 = (bf16[384,768]{1,0:T(8,128)(2,1)}, bf16[3,384,768]{2,1,0:T(8,128)(2,1)}, bf16[3,384,768]{2,1,0:T(8,128)(2,1)}, bf16[3,384,768]{2,1,0:T(8,128)(2...) custom-call(s32[3]{0:T(128)} %add_add_fusion.4.idx, ...), custom_call_target="tpu_custom_call", output_to_operand_aliasing={{1}: (12, {}), {2}: (13, {}), {3}: (14, {}), {4}: (15, {}),... | custom-call | flops 5888802816 | bytes 31457280 | tf_op jit(solution)/shard_map/pallas_call | solution.py:476
  114.9 12.1 %collective-permute-done.recv = bf16[384,768]{1,0:T(8,128)(2,1)S(1)} collective-permute-done((bf16[384,768]{1,0:T(8,128)(2,1)}, bf16[384,768]{1,0:T(8,128)(2,1)S(1)}, u32[]{:S(2)}, u32[]{:S(2)}) %collective-permute-start) | collective-permute-done | bytes 589856 | tf_op jit(solution)/shard_map/ppermute | solution.py:517
  127.9 18.1 %shard_map.200 = (bf16[384,768]{1,0:T(8,128)(2,1)}, bf16[3,384,768]{2,1,0:T(8,128)(2,1)}, bf16[3,384,768]{2,1,0:T(8,128)(2,1)}, bf16[3,384,768]{2,1,0:T(8,128)(2...) custom-call(s32[3]{0:T(128)} %add_add_fusion.3.idx, ...), custom_call_target="tpu_custom_call", output_to_operand_aliasing={{1}: (12, {}), {2}: (13, {}), {3}: (14, {}), {4}: (15, {}),... | custom-call | flops 5888802816 | bytes 31457280 | tf_op jit(solution)/shard_map/pallas_call | solution.py:476
  151.1 10.8 %collective-permute-done.1.recv = bf16[384,768]{1,0:T(8,128)(2,1)S(1)} collective-permute-done((bf16[384,768]{1,0:T(8,128)(2,1)}, bf16[384,768]{1,0:T(8,128)(2,1)S(1)}, u32[]{:S(2)}, u32[]{:S(2)}) %collective-permute-start.1) | collective-permute-done | bytes 589856 | tf_op jit(solution)/shard_map/ppermute | solution.py:517
  162.7 17.3 %shard_map.201 = (bf16[384,768]{1,0:T(8,128)(2,1)}, bf16[3,384,768]{2,1,0:T(8,128)(2,1)}, bf16[3,384,768]{2,1,0:T(8,128)(2,1)}, bf16[3,384,768]{2,1,0:T(8,128)(2...) custom-call(s32[3]{0:T(128)} %add_add_fusion.2.idx, ...), custom_call_target="tpu_custom_call", output_to_operand_aliasing={{1}: (12, {}), {2}: (13, {}), {3}: (14, {}), {4}: (15, {}),... | custom-call | flops 5888802816 | bytes 31457280 | tf_op jit(solution)/shard_map/pallas_call | solution.py:476
  185.6 10.1 %collective-permute-done.2.recv = bf16[384,768]{1,0:T(8,128)(2,1)S(1)} collective-permute-done((bf16[384,768]{1,0:T(8,128)(2,1)}, bf16[384,768]{1,0:T(8,128)(2,1)S(1)}, u32[]{:S(2)}, u32[]{:S(2)}) %collective-permute-start.2) | collective-permute-done | bytes 589856 | tf_op jit(solution)/shard_map/ppermute | solution.py:517
  196.6 17.2 %shard_map.202 = (bf16[384,768]{1,0:T(8,128)(2,1)}, bf16[3,384,768]{2,1,0:T(8,128)(2,1)}, bf16[3,384,768]{2,1,0:T(8,128)(2,1)}, bf16[3,384,768]{2,1,0:T(8,128)(2...) custom-call(s32[3]{0:T(128)} %add_add_fusion.1.idx, ...), custom_call_target="tpu_custom_call", output_to_operand_aliasing={{1}: (12, {}), {2}: (13, {}), {3}: (14, {}), {4}: (15, {}),... | custom-call | flops 5888802816 | bytes 31457280 | tf_op jit(solution)/shard_map/pallas_call | solution.py:476
  219.3 8.4 %collective-permute-done.3.recv = bf16[384,768]{1,0:T(8,128)(2,1)S(1)} collective-permute-done((bf16[384,768]{1,0:T(8,128)(2,1)}, bf16[384,768]{1,0:T(8,128)(2,1)S(1)}, u32[]{:S(2)}, u32[]{:S(2)}) %collective-permute-start.3) | collective-permute-done | bytes 589856 | tf_op jit(solution)/shard_map/ppermute | solution.py:517
  228.6 17.2 %shard_map.203 = (bf16[384,768]{1,0:T(8,128)(2,1)}, bf16[3,384,768]{2,1,0:T(8,128)(2,1)}, bf16[3,384,768]{2,1,0:T(8,128)(2,1)}, bf16[3,384,768]{2,1,0:T(8,128)(2...) custom-call(s32[3]{0:T(128)} %add_add_fusion.idx, ...), custom_call_target="tpu_custom_call", output_to_operand_aliasing={{1}: (12, {}), {2}: (13, {}), {3}: (14, {}), {4}: (15, {}),... | custom-call | flops 5888802816 | bytes 31457280 | tf_op jit(solution)/shard_map/pallas_call | solution.py:476
  245.8 22.3 %shard_map.214 = (bf16[384,768]{1,0:T(8,128)(2,1)}, bf16[3,384,768]{2,1,0:T(8,128)(2,1)}, bf16[3,3,384,1024]{3,2,1,0:T(8,128)(2,1)}, bf16[3,384,768]{2,1,0:T(8,1...) custom-call(s32[3]{0:T(128)} %add_add_fusion.9.idx, ...), custom_call_target="tpu_custom_call", output_to_operand_aliasing={{1}: (19, {}), {2}: (20, {}), {3}: (21, {}), {4}: (22, {}),... | custom-call | flops 6341787648 | bytes 31457280 | tf_op jit(solution)/shard_map/pallas_call | solution.py:476
  270.2 12.0 %collective-permute-done.4.recv = bf16[384,768]{1,0:T(8,128)(2,1)S(1)} collective-permute-done((bf16[384,768]{1,0:T(8,128)(2,1)}, bf16[384,768]{1,0:T(8,128)(2,1)S(1)}, u32[]{:S(2)}, u32[]{:S(2)}) %collective-permute-start.4) | collective-permute-done | bytes 589856 | tf_op jit(solution)/shard_map/ppermute | solution.py:517
  283.0 22.2 %shard_map.215 = (bf16[384,768]{1,0:T(8,128)(2,1)}, bf16[3,384,768]{2,1,0:T(8,128)(2,1)}, bf16[3,3,384,1024]{3,2,1,0:T(8,128)(2,1)}, bf16[3,384,768]{2,1,0:T(8,1...) custom-call(s32[3]{0:T(128)} %add_add_fusion.8.idx, ...), custom_call_target="tpu_custom_call", output_to_operand_aliasing={{1}: (19, {}), {2}: (20, {}), {3}: (21, {}), {4}: (22, {}),... | custom-call | flops 6341787648 | bytes 31457280 | tf_op jit(solution)/shard_map/pallas_call | solution.py:476
  307.1 10.6 %collective-permute-done.5.recv = bf16[384,768]{1,0:T(8,128)(2,1)S(1)} collective-permute-done((bf16[384,768]{1,0:T(8,128)(2,1)}, bf16[384,768]{1,0:T(8,128)(2,1)S(1)}, u32[]{:S(2)}, u32[]{:S(2)}) %collective-permute-start.5) | collective-permute-done | bytes 589856 | tf_op jit(solution)/shard_map/ppermute | solution.py:517
  318.5 22.0 %shard_map.216 = (bf16[384,768]{1,0:T(8,128)(2,1)}, bf16[3,384,768]{2,1,0:T(8,128)(2,1)}, bf16[3,3,384,1024]{3,2,1,0:T(8,128)(2,1)}, bf16[3,384,768]{2,1,0:T(8,1...) custom-call(s32[3]{0:T(128)} %add_add_fusion.7.idx, ...), custom_call_target="tpu_custom_call", output_to_operand_aliasing={{1}: (19, {}), {2}: (20, {}), {3}: (21, {}), {4}: (22, {}),... | custom-call | flops 6341787648 | bytes 31457280 | tf_op jit(solution)/shard_map/pallas_call | solution.py:476
  342.4 9.9 %collective-permute-done.6.recv = bf16[384,768]{1,0:T(8,128)(2,1)S(1)} collective-permute-done((bf16[384,768]{1,0:T(8,128)(2,1)}, bf16[384,768]{1,0:T(8,128)(2,1)S(1)}, u32[]{:S(2)}, u32[]{:S(2)}) %collective-permute-start.6) | collective-permute-done | bytes 589856 | tf_op jit(solution)/shard_map/ppermute | solution.py:517
  353.1 22.7 %shard_map.217 = (bf16[384,768]{1,0:T(8,128)(2,1)}, bf16[3,384,768]{2,1,0:T(8,128)(2,1)}, bf16[3,3,384,1024]{3,2,1,0:T(8,128)(2,1)}, bf16[3,384,768]{2,1,0:T(8,1...) custom-call(s32[3]{0:T(128)} %add_add_fusion.6.idx, ...), custom_call_target="tpu_custom_call", output_to_operand_aliasing={{1}: (19, {}), {2}: (20, {}), {3}: (21, {}), {4}: (22, {}),... | custom-call | flops 6341787648 | bytes 31457280 | tf_op jit(solution)/shard_map/pallas_call | solution.py:476
  387.5 22.4 %shard_map.218 = (bf16[384,768]{1,0:T(8,128)(2,1)}, bf16[3,384,768]{2,1,0:T(8,128)(2,1)}, bf16[3,3,384,1024]{3,2,1,0:T(8,128)(2,1)}, bf16[3,384,768]{2,1,0:T(8,1...) custom-call(s32[3]{0:T(128)} %add_add_fusion.5.idx, ...), custom_call_target="tpu_custom_call", output_to_operand_aliasing={{1}: (19, {}), {2}: (20, {}), {3}: (21, {}), {4}: (22, {}),... | custom-call | flops 6341787648 | bytes 31457280 | tf_op jit(solution)/shard_map/pallas_call | solution.py:476
  409.9 10.0 %shard_map.219 = bf16[768,2304]{1,0:T(8,128)(2,1)} custom-call(s32[4]{0:T(128)} %add_add_fusion.11.idx, f32[128,768]{1,0:T(8,128)} %fusion.2.place, bf16[3,384,768]{2,1,0:T(8,128)(2,1)} %get-tuple-element.263.hs, bf16[3,3,384,1024]{3,2,1,0:T(8,128)(2,1)} %get-tuple-element.264.acts, bf16[3,768,384]{2,1,0:T(8,128)(2,1)} %get-tuple-element.217.refs_9_.ats, ...), custom_call_target="tpu_custom_call" | custom-call | flops 2717908992 | bytes 16777216 | tf_op jit(solution)/shard_map/pallas_call | solution.py:494
  426.5 9.9 %shard_map.222 = bf16[768,2432]{1,0:T(8,128)(2,1)} custom-call(s32[4]{0:T(128)} %add_add_fusion.11.idx, f32[128,768]{1,0:T(8,128)} %fusion.2.place, bf16[3,384,768]{2,1,0:T(8,128)(2,1)} %get-tuple-element.263.hs, bf16[3,3,384,1024]{3,2,1,0:T(8,128)(2,1)} %get-tuple-element.264.acts, bf16[3,768,384]{2,1,0:T(8,128)(2,1)} %get-tuple-element.217.refs_9_.ats, ...), custom_call_target="tpu_custom_call" | custom-call | flops 2717908992 | bytes 16777216 | tf_op jit(solution)/shard_map/pallas_call | solution.py:494
  437.0 10.1 %shard_map.220 = (bf16[192,2304]{1,0:T(8,128)(2,1)}, bf16[192,2304]{1,0:T(8,128)(2,1)}, bf16[192,2304]{1,0:T(8,128)(2,1)}, bf16[192,2304]{1,0:T(8,128)(2,1)}) custom-call(s32[4]{0:T(128)} %add_add_fusion.10.idx, f32[128,768]{1,0:T(8,128)} %fusion.2.place, bf16[3,384,768]{2,1,0:T(8,128)(2,1)} %get-tuple-element.263.hs, ...), custom_call_target="tpu_custom_call" | custom-call | flops 2717908992 | bytes 16777216 | tf_op jit(solution)/shard_map/pallas_call | solution.py:494
  453.3 10.3 %shard_map.223 = (bf16[4,48,2432]{2,1,0:T(8,128)(2,1)}, bf16[4,48,2432]{2,1,0:T(8,128)(2,1)}, bf16[4,48,2432]{2,1,0:T(8,128)(2,1)}, bf16[4,48,2432]{2,1,0:T(8,128)(2,1)}) custom-call(s32[4]{0:T(128)} %add_add_fusion.10.idx, f32[128,768]{1,0:T(8,128)} %fusion.2.place, bf16[3,384,768]{2,1,0:T(8,128)(2,1)} %get-tuple-element.263.hs, ...), custom_call_target="tpu_custom_call" | custom-call | flops 2717908992 | bytes 16777216 | tf_op jit(solution)/shard_map/pallas_call | solution.py:494
  471.0 17.5 %collective-permute-done.11.refs_3_ = bf16[192,2304]{1,0:T(8,128)(2,1)} collective-permute-done((bf16[192,2304]{1,0:T(8,128)(2,1)}, bf16[192,2304]{1,0:T(8,128)(2,1)}, u32[]{:S(2)}, u32[]{:S(2)}) %collective-permute-start.11) | collective-permute-done | bytes 884768 | tf_op jit(solution)/shard_map/ppermute | solution.py:512
  494.9 8.4 %collective-permute-done.17.refs_2_ = bf16[4,48,2432]{2,1,0:T(8,128)(2,1)S(1)} collective-permute-done((bf16[4,48,2432]{2,1,0:T(8,128)(2,1)}, bf16[4,48,2432]{2,1,0:T(8,128)(2,1)S(1)}, u32[]{:S(2)}, u32[]{:S(2)}) %collective-permute-start.17) | collective-permute-done | bytes 933920 | tf_op jit(solution)/shard_map/ppermute | solution.py:512
  (184 shorter events, 129.5 us)
Async XLA Ops:
  7.2 80.3 %all-gather.2.cloned.1.call-start = ((), (), s32[]{:S(2)}) async-start(), calls=%async_computation | async-start | bytes 14800896 | tf_op jit(solution)/shard_map/all_gather | solution.py:565
  112.2 14.8 %collective-permute-start = (bf16[384,768]{1,0:T(8,128)(2,1)}, bf16[384,768]{1,0:T(8,128)(2,1)S(1)}, u32[]{:S(2)}, u32[]{:S(2)}) collective-permute-start(bf16[384,768]{1,0:T(8,128)(2,1)} %get-tuple-element.151), channel_id=1, source_target_pairs={{0,32},{32,64},{64,96},{1,33},{33,65},{65,97},{2,34},{34,66},{66,9... | collective-permute-start | bytes 1769480 | tf_op jit(solution)/shard_map/ppermute | solution.py:517
  146.0 15.8 %collective-permute-start.1 = (bf16[384,768]{1,0:T(8,128)(2,1)}, bf16[384,768]{1,0:T(8,128)(2,1)S(1)}, u32[]{:S(2)}, u32[]{:S(2)}) collective-permute-start(bf16[384,768]{1,0:T(8,128)(2,1)} %get-tuple-element.165), channel_id=1, source_target_pairs={{0,32},{32,64},{64,96},{1,33},{33,65},{65,97},{2,34},{34,66},{66,9... | collective-permute-start | bytes 1769480 | tf_op jit(solution)/shard_map/ppermute | solution.py:517
  179.9 15.8 %collective-permute-start.2 = (bf16[384,768]{1,0:T(8,128)(2,1)}, bf16[384,768]{1,0:T(8,128)(2,1)S(1)}, u32[]{:S(2)}, u32[]{:S(2)}) collective-permute-start(bf16[384,768]{1,0:T(8,128)(2,1)} %get-tuple-element.179), channel_id=1, source_target_pairs={{0,32},{32,64},{64,96},{1,33},{33,65},{65,97},{2,34},{34,66},{66,9... | collective-permute-start | bytes 1769480 | tf_op jit(solution)/shard_map/ppermute | solution.py:517
  213.8 14.0 %collective-permute-start.3 = (bf16[384,768]{1,0:T(8,128)(2,1)}, bf16[384,768]{1,0:T(8,128)(2,1)S(1)}, u32[]{:S(2)}, u32[]{:S(2)}) collective-permute-start(bf16[384,768]{1,0:T(8,128)(2,1)} %get-tuple-element.193), channel_id=1, source_target_pairs={{0,32},{32,64},{64,96},{1,33},{33,65},{65,97},{2,34},{34,66},{66,9... | collective-permute-start | bytes 1769480 | tf_op jit(solution)/shard_map/ppermute | solution.py:517
  268.1 14.0 %collective-permute-start.4 = (bf16[384,768]{1,0:T(8,128)(2,1)}, bf16[384,768]{1,0:T(8,128)(2,1)S(1)}, u32[]{:S(2)}, u32[]{:S(2)}) collective-permute-start(bf16[384,768]{1,0:T(8,128)(2,1)} %get-tuple-element.218), channel_id=1, source_target_pairs={{32,0},{64,32},{96,64},{33,1},{65,33},{97,65},{34,2},{66,34},{98,6... | collective-permute-start | bytes 1769480 | tf_op jit(solution)/shard_map/ppermute | solution.py:517
  305.2 12.5 %collective-permute-start.5 = (bf16[384,768]{1,0:T(8,128)(2,1)}, bf16[384,768]{1,0:T(8,128)(2,1)S(1)}, u32[]{:S(2)}, u32[]{:S(2)}) collective-permute-start(bf16[384,768]{1,0:T(8,128)(2,1)} %get-tuple-element.229), channel_id=1, source_target_pairs={{32,0},{64,32},{96,64},{33,1},{65,33},{97,65},{34,2},{66,34},{98,6... | collective-permute-start | bytes 1769480 | tf_op jit(solution)/shard_map/ppermute | solution.py:517
  340.5 11.8 %collective-permute-start.6 = (bf16[384,768]{1,0:T(8,128)(2,1)}, bf16[384,768]{1,0:T(8,128)(2,1)S(1)}, u32[]{:S(2)}, u32[]{:S(2)}) collective-permute-start(bf16[384,768]{1,0:T(8,128)(2,1)} %get-tuple-element.240), channel_id=1, source_target_pairs={{32,0},{64,32},{96,64},{33,1},{65,33},{97,65},{34,2},{66,34},{98,6... | collective-permute-start | bytes 1769480 | tf_op jit(solution)/shard_map/ppermute | solution.py:517
  375.8 10.8 %collective-permute-start.7 = (bf16[384,768]{1,0:T(8,128)(2,1)}, bf16[384,768]{1,0:T(8,128)(2,1)S(1)}, u32[]{:S(2)}, u32[]{:S(2)}) collective-permute-start(bf16[384,768]{1,0:T(8,128)(2,1)} %get-tuple-element.251), channel_id=1, source_target_pairs={{32,0},{64,32},{96,64},{33,1},{65,33},{97,65},{34,2},{66,34},{98,6... | collective-permute-start | bytes 1769480 | tf_op jit(solution)/shard_map/ppermute | solution.py:517
  419.9 17.1 %collective-permute-start.8 = (bf16[768,2304]{1,0:T(8,128)(2,1)}, bf16[768,2304]{1,0:T(8,128)(2,1)}, u32[]{:S(2)}, u32[]{:S(2)}) collective-permute-start(bf16[768,2304]{1,0:T(8,128)(2,1)} %shard_map.219), channel_id=1, source_target_pairs={{0,1},{1,0},{2,3},{3,2},{4,5},{5,4},{6,7},{7,6},{8,9},{9,8},{10,11... | collective-permute-start | bytes 10616840 | tf_op jit(solution)/shard_map/ppermute | solution.py:512
  436.4 15.1 %collective-permute-start.15 = (bf16[768,2432]{1,0:T(8,128)(2,1)}, bf16[768,2432]{1,0:T(8,128)(2,1)S(1)}, u32[]{:S(2)}, u32[]{:S(2)}) collective-permute-start(bf16[768,2432]{1,0:T(8,128)(2,1)} %shard_map.222), channel_id=1, source_target_pairs={{0,1},{1,0},{2,3},{3,2},{4,5},{5,4},{6,7},{7,6},{8,9},{9,8},{10,11... | collective-permute-start | bytes 11206664 | tf_op jit(solution)/shard_map/ppermute | solution.py:512
  447.1 21.7 %collective-permute-start.10 = (bf16[192,2304]{1,0:T(8,128)(2,1)}, bf16[192,2304]{1,0:T(8,128)(2,1)}, u32[]{:S(2)}, u32[]{:S(2)}) collective-permute-start(bf16[192,2304]{1,0:T(8,128)(2,1)} %get-tuple-element.275), channel_id=1, source_target_pairs={{0,16},{1,17},{2,18},{3,19},{4,20},{5,21},{6,22},{7,23},{8,24},{9,... | collective-permute-start | bytes 2654216 | tf_op jit(solution)/shard_map/ppermute | solution.py:512
  450.0 38.5 %collective-permute-start.11 = (bf16[192,2304]{1,0:T(8,128)(2,1)}, bf16[192,2304]{1,0:T(8,128)(2,1)}, u32[]{:S(2)}, u32[]{:S(2)}) collective-permute-start(bf16[192,2304]{1,0:T(8,128)(2,1)} %get-tuple-element.276), channel_id=1, source_target_pairs={{0,24},{1,25},{2,26},{3,27},{4,28},{5,29},{6,30},{7,31},{8,0},{9,1... | collective-permute-start | bytes 2654216 | tf_op jit(solution)/shard_map/ppermute | solution.py:512
  450.9 38.7 %collective-permute-start.9 = (bf16[192,2304]{1,0:T(8,128)(2,1)}, bf16[192,2304]{1,0:T(8,128)(2,1)}, u32[]{:S(2)}, u32[]{:S(2)}) collective-permute-start(bf16[192,2304]{1,0:T(8,128)(2,1)} %get-tuple-element.274), channel_id=1, source_target_pairs={{0,8},{1,9},{2,10},{3,11},{4,12},{5,13},{6,14},{7,15},{8,16},{9,17... | collective-permute-start | bytes 2654216 | tf_op jit(solution)/shard_map/ppermute | solution.py:512
  463.5 31.4 %collective-permute-start.16 = (bf16[4,48,2432]{2,1,0:T(8,128)(2,1)}, bf16[4,48,2432]{2,1,0:T(8,128)(2,1)S(1)}, u32[]{:S(2)}, u32[]{:S(2)}) collective-permute-start(bf16[4,48,2432]{2,1,0:T(8,128)(2,1)} %get-tuple-element.283), channel_id=1, source_target_pairs={{0,2},{1,3},{2,4},{3,5},{4,6},{5,7},{6,0},{7,1},{8,10},{9,11},{10,... | collective-permute-start | bytes 2801672 | tf_op jit(solution)/shard_map/ppermute | solution.py:512
  463.6 39.7 %collective-permute-start.17 = (bf16[4,48,2432]{2,1,0:T(8,128)(2,1)}, bf16[4,48,2432]{2,1,0:T(8,128)(2,1)S(1)}, u32[]{:S(2)}, u32[]{:S(2)}) collective-permute-start(bf16[4,48,2432]{2,1,0:T(8,128)(2,1)} %get-tuple-element.284), channel_id=1, source_target_pairs={{0,4},{1,5},{2,6},{3,7},{4,0},{5,1},{6,2},{7,3},{8,12},{9,13},{10,... | collective-permute-start | bytes 2801672 | tf_op jit(solution)/shard_map/ppermute | solution.py:512
  468.8 38.5 %collective-permute-start.18 = (bf16[4,48,2432]{2,1,0:T(8,128)(2,1)}, bf16[4,48,2432]{2,1,0:T(8,128)(2,1)S(1)}, u32[]{:S(2)}, u32[]{:S(2)}) collective-permute-start(bf16[4,48,2432]{2,1,0:T(8,128)(2,1)} %get-tuple-element.285), channel_id=1, source_target_pairs={{0,6},{1,7},{2,0},{3,1},{4,2},{5,3},{6,4},{7,5},{8,14},{9,15},{10,... | collective-permute-start | bytes 2801672 | tf_op jit(solution)/shard_map/ppermute | solution.py:512
  494.0 23.6 %collective-permute-start.12 = (bf16[48,2304]{1,0:T(8,128)(2,1)}, bf16[48,2304]{1,0:T(8,128)(2,1)S(1)}, u32[]{:S(2)}, u32[]{:S(2)}) collective-permute-start(bf16[48,2304]{1,0:T(8,128)(2,1)} %get-tuple-element.278), channel_id=1, source_target_pairs={{0,2},{1,3},{2,4},{3,5},{4,6},{5,7},{6,0},{7,1},{8,10},{9,11},{10,... | collective-permute-start | bytes 663560 | tf_op jit(solution)/shard_map/ppermute | solution.py:512
  513.0 16.8 %collective-permute-start.19 = (bf16[48,2432]{1,0:T(8,128)(2,1)}, bf16[48,2432]{1,0:T(8,128)(2,1)S(1)}, u32[]{:S(2)}, u32[]{:S(2)}) collective-permute-start(bf16[48,2432]{1,0:T(8,128)(2,1)} %get-tuple-element.287), channel_id=1, source_target_pairs={{0,8},{1,9},{2,10},{3,11},{4,12},{5,13},{6,14},{7,15},{8,16},{9,17... | collective-permute-start | bytes 700424 | tf_op jit(solution)/shard_map/ppermute | solution.py:512
  513.2 16.6 %collective-permute-start.20 = (bf16[48,2432]{1,0:T(8,128)(2,1)}, bf16[48,2432]{1,0:T(8,128)(2,1)S(1)}, u32[]{:S(2)}, u32[]{:S(2)}) collective-permute-start(bf16[48,2432]{1,0:T(8,128)(2,1)} %get-tuple-element.288), channel_id=1, source_target_pairs={{0,16},{1,17},{2,18},{3,19},{4,20},{5,21},{6,22},{7,23},{8,24},{9,... | collective-permute-start | bytes 700424 | tf_op jit(solution)/shard_map/ppermute | solution.py:512
  516.3 13.5 %collective-permute-start.21 = (bf16[48,2432]{1,0:T(8,128)(2,1)}, bf16[48,2432]{1,0:T(8,128)(2,1)S(1)}, u32[]{:S(2)}, u32[]{:S(2)}) collective-permute-start(bf16[48,2432]{1,0:T(8,128)(2,1)} %get-tuple-element.289), channel_id=1, source_target_pairs={{0,24},{1,25},{2,26},{3,27},{4,28},{5,29},{6,30},{7,31},{8,0},{9,1... | collective-permute-start | bytes 700424 | tf_op jit(solution)/shard_map/ppermute | solution.py:512
  516.3 6.3 %collective-permute-start.13 = (bf16[48,2304]{1,0:T(8,128)(2,1)S(1)}, bf16[48,2304]{1,0:T(8,128)(2,1)S(1)}, u32[]{:S(2)}, u32[]{:S(2)}) collective-permute-start(bf16[48,2304]{1,0:T(8,128)(2,1)S(1)} %copy-done.23), channel_id=1, source_target_pairs={{0,4},{1,5},{2,6},{3,7},{4,0},{5,1},{6,2},{7,3},{8,12},{9,13},{10,... | collective-permute-start | bytes 663560 | tf_op jit(solution)/shard_map/ppermute | solution.py:512
  517.6 12.1 %collective-permute-start.14 = (bf16[48,2304]{1,0:T(8,128)(2,1)S(1)}, bf16[48,2304]{1,0:T(8,128)(2,1)S(1)}, u32[]{:S(2)}, u32[]{:S(2)}) collective-permute-start(bf16[48,2304]{1,0:T(8,128)(2,1)S(1)} %copy-done.22), channel_id=1, source_target_pairs={{0,6},{1,7},{2,0},{3,1},{4,2},{5,3},{6,4},{7,5},{8,14},{9,15},{10,... | collective-permute-start | bytes 663560 | tf_op jit(solution)/shard_map/ppermute | solution.py:512
  534.2 3.2 collective-permute-start.22
  (24 other events, 163.3 us)
Sparse Core Ops, SparseCore 0:
  16.7 70.7 all-gather.1

commit v4 on v1

v4 whole, which is shorter than its diff:
```python
from functools import partial
import math

import jax
import jax.numpy as jnp
from jax import lax
from jax.experimental import pallas as pl
from jax.experimental.pallas import tpu as pltpu
from jax.sharding import PartitionSpec as P

BF = jnp.bfloat16
F32 = jnp.float32
VMEM_LIMIT = 60 * 1024 * 1024
EPS = 1e-06
NN = (((1,), (0,)), ((), ()))
NT = (((1,), (1,)), ((), ()))
TN = (((0,), (0,)), ((), ()))
LANES = 128
WIDE = 256
ABSENT = 16


def mm(a, b, dims=NN):
    return lax.dot_general(a, b, dims, preferred_element_type=F32)


def head_mean(x, spread, exact):
    parts = []
    for at in range(0, x.shape[1], WIDE):
        piece = x[:, at : at + WIDE]
        top = piece.astype(BF)
        total = mm(top, spread)
        if exact:
            total = total + mm((piece - top.astype(F32)).astype(BF), spread)
        parts.append(total)
    return jnp.concatenate(parts, axis=1)


def row_norm(x):
    centered = x - jnp.mean(x, axis=-1, keepdims=True)
    rstd = lax.rsqrt(jnp.mean(centered * centered, axis=-1, keepdims=True) + EPS)
    return centered * rstd, rstd


def norm_back(grad, normal, rstd, spread):
    return rstd * (grad - head_mean(grad, spread, False) - normal * head_mean(grad * normal, spread, False))


def lane_half(x, second):
    lane = lax.broadcasted_iota(jnp.int32, x.shape, 1)
    return jnp.where((lane >= LANES // 2) if second else (lane < LANES // 2), x, jnp.zeros_like(x))


class Copies:
    def __init__(self, sems):
        self.sems, self.used = sems, 0

    def start(self, src, dst):
        copy = pltpu.make_async_copy(src, dst, self.sems.at[self.used])
        self.used += 1
        copy.start()
        return copy

    def either(self, flag, src, yes, no):
        sem = self.sems.at[self.used]
        self.used += 1

        @pl.when(flag == 1)
        def _():
            pltpu.make_async_copy(src, yes, sem).start()

        @pl.when(flag != 1)
        def _():
            pltpu.make_async_copy(src, no, sem).start()

        return pltpu.make_async_copy(src, yes, sem)


def forward_kernel(d, ff, chunks, base, first, idx, x_in, g, g3, ids_col, ids_row, ngain, gains, ubias, obias, spread, *refs):
    @pl.when(idx[0] == 1)
    def _():
        forward_work(d, ff, chunks, base, first, idx, x_in, g, g3, ids_col, ids_row, ngain, gains, ubias, obias, spread, *refs)


def forward_work(d, ff, chunks, base, first, idx, x_in, g, g3, ids_col, ids_row, ngain, gains, ubias, obias, spread, *refs):
    refs = refs[13:]
    ybf, xs, qs, ks, vs, ns, nrs, gps, es, small, kept, sent, y_out, y_send = refs[:14]
    (x_v, h_v, w_v, u_v, d_v, a_v, q_v, k_v, v_v, n_v, r_v, act_v, gp_v, e_v, rs_v, att_v, acc_v, y_v, ins, outs) = refs[14:]
    rows = x_v.shape[0]
    fc = ff // chunks
    core, slot, home = idx[1], idx[2], idx[3]
    cin, cout = Copies(ins), Copies(outs)
    x_copy = cin.start(x_in.at[slot] if first else x_in, x_v)
    wq = [cin.start(g.at[:, pl.ds(base + ff + d * i, d)], w_v.at[:, pl.ds(d * i, d)]) for i in range(3)]
    groups = fc // WIDE
    wff = []
    for c in range(chunks):
        wff.append([cin.start(g.at[:, pl.ds(base + fc * c, fc)], u_v.at[c])] + [
            cin.start(g3.at[pl.ds(groups * c, groups), :, pl.ds(base + ff + 4 * d + d * j, d)], d_v.at[pl.ds(groups * c, groups), j])
            for j in range(4)
        ])
    wa = cin.start(g.at[:, pl.ds(base + ff + 3 * d, d)], a_v)

    pending = []

    def side(i):
        return pl.ds(ff + d * i, d)

    x_copy.wait()
    keep = jnp.where(ids_col[0] < ABSENT, 1.0, 0.0)
    masked = keep * x_v[...].astype(F32)
    h_v[...] = (row_norm(masked)[0] * ngain[...]).astype(BF)
    pending += [cout.start(x_v, xs), cout.start(h_v, kept.at[:, side(2)]), cout.start(h_v, sent.at[:, side(2)])]
    bias_mask = jnp.where(ids_col[0] == ids_row[0], 0.0, -1e9)
    for i in range(3):
        wq[i].wait()
        raw = mm(h_v[...], w_v[:, d * i : d * i + d])
        if i == 2:
            v_v[...] = raw.astype(BF)
            pending.append(cout.start(v_v, vs))
        else:
            centered = raw - head_mean(raw, spread[...], True)
            rstd = lax.rsqrt(head_mean(centered * centered, spread[...], True) + EPS)
            normal = centered * rstd
            scaled = (normal * gains[i]).astype(BF)
            n_v[:, d * i : d * i + d] = normal.astype(BF)
            r_v[:, d * i : d * i + d] = rstd.astype(BF)
            if i == 0:
                q_v[...] = scaled * jnp.asarray(0.125, BF)
                pending.append(cout.start(q_v, qs))
            else:
                k_v[...] = scaled
                pending.append(cout.start(k_v, ks))
    pending += [cout.start(n_v, ns), cout.start(r_v, nrs)]
    ones = jnp.ones((16, rows), BF)
    pairs = d // LANES // chunks
    for c in range(chunks):
        for copy in wff[c]:
            copy.wait()
        pre = mm(h_v[...], u_v[c]) + ubias[:, fc * c : fc * c + fc]
        cdf = 0.5 * (1.0 + lax.erf(pre * (1.0 / math.sqrt(2.0))))
        density = jnp.exp(-0.5 * pre * pre) * (1.0 / math.sqrt(2.0 * math.pi))
        act = (pre * cdf).astype(BF)
        act_v[c] = act
        gp_v[c] = (cdf + pre * density).astype(BF)
        total = mm(act, d_v[groups * c : groups * c + groups].reshape(fc, d))
        if c == 0:
            acc_v[...] = total
        else:
            acc_v[...] += total
        for p in range(pairs * c, pairs * c + pairs):
            cols = slice(LANES * p, LANES * p + LANES)
            vals_t = v_v[:, cols].T
            pair = q_v[:, cols]
            both = []
            for half in range(2):
                h = 2 * p + half
                e = jnp.exp(mm(k_v[:, cols], lane_half(pair, half), NT) + bias_mask).astype(BF)
                e_v[h] = e
                got = mm(jnp.concatenate([vals_t[64 * half : 64 * half + 64], ones], axis=0), e)
                inv = 1.0 / got[64:65]
                rs_v[h : h + 1, :] = inv
                both.append((got[:64] * inv).astype(BF))
            att_v[:, cols] = jnp.concatenate(both, axis=0).T
        span = pl.ds(fc * c, fc)
        pending += [cout.either(core, act_v.at[c], sent.at[:, span], kept.at[:, span]), cout.start(gp_v.at[c], gps.at[c]),
                    cout.start(e_v.at[pl.ds(2 * pairs * c, 2 * pairs)], es.at[pl.ds(2 * pairs * c, 2 * pairs)])]
    pending += [cout.start(rs_v, small), cout.either(core, att_v, sent.at[:, side(3)], kept.at[:, side(3)])]
    wa.wait()
    y = keep * (keep * x_v[...].astype(F32) + acc_v[...] + mm(att_v[...], a_v[...]) + obias[...])
    y_v[...] = y
    ybf[...] = y.astype(BF)
    pending.append(cout.either(home, y_v, y_out.at[slot], y_send))
    for copy in pending:
        copy.wait()


def backward_kernel(d, ff, chunks, base, first, idx, g_in, g, g3, ids_col, ngain, gains, spread, *refs):
    @pl.when(idx[0] == 1)
    def _():
        backward_work(d, ff, chunks, base, first, idx, g_in, g, g3, ids_col, ngain, gains, spread, *refs)


def backward_work(d, ff, chunks, base, first, idx, g_in, g, g3, ids_col, ngain, gains, spread, *refs):
    xs, qs, ks, vs, ns, nrs, gps, es, small = refs[:9]
    refs = refs[9 + 5 :]
    gbf, kept, sent, table, gr_out, gr_send = refs[:6]
    (g_v, gb_v, w_v, u_v, d_v, a_v, x_v, q_v, k_v, v_v, n_v, r_v, gp_v, e_v, rs_v, gat_v, gqt_v, gk_v,
     gq_b, gk_b, gv_b, gj_v, acc_v, out_v, sm_v, ins, outs) = refs[6:]
    rows = x_v.shape[0]
    fc = ff // chunks
    groups = fc // WIDE
    core, slot, home = idx[1], idx[2], idx[3]
    cin, cout = Copies(ins), Copies(outs)
    g_copy = cin.start(g_in.at[slot] if first else g_in, g_v)
    wa = cin.start(g.at[:, pl.ds(base + ff + 3 * d, d)], a_v)
    heads = [cin.start(s, v) for s, v in ((small, rs_v), (ks, k_v), (vs, v_v), (qs, q_v))]
    pairs = d // LANES // chunks
    wff = []
    for c in range(chunks):
        wff.append(
            [cin.start(g3.at[pl.ds(groups * c, groups), :, pl.ds(base + ff + 4 * d + d * j, d)], d_v.at[pl.ds(groups * c, groups), j])
             for j in range(4)]
            + [cin.start(gps.at[c], gp_v.at[c]), cin.start(g.at[:, pl.ds(base + fc * c, fc)], u_v.at[c]),
               cin.start(es.at[pl.ds(2 * pairs * c, 2 * pairs)], e_v.at[pl.ds(2 * pairs * c, 2 * pairs)])]
        )
    norms = [cin.start(ns, n_v), cin.start(nrs, r_v)]
    wq = [cin.start(g.at[:, pl.ds(base + ff + d * i, d)], w_v.at[:, pl.ds(d * i, d)]) for i in range(3)]
    rows_in = cin.start(xs, x_v)

    pending = []

    def side(i):
        return pl.ds(ff + d * i, d)

    def summed(at, value):
        sm_v[:, at : at + value.shape[1]] = jnp.sum(value, axis=0, keepdims=True)

    g_copy.wait()
    keep = jnp.where(ids_col[0] < ABSENT, 1.0, 0.0)
    gres = keep * g_v[...].astype(F32)
    summed(d, gres)
    gb_v[...] = gres.astype(BF)
    pending.append(cout.either(core, gb_v, sent.at[:, side(0)], kept.at[:, side(0)]))
    wa.wait()
    gat_v[...] = mm(a_v[...], gb_v[...], NT).astype(BF)
    for copy in heads:
        copy.wait()
    zeros = jnp.zeros((LANES // 2, rows), BF)
    for c in range(chunks):
        for copy in wff[c]:
            copy.wait()
        gup = mm(gb_v[...], d_v[groups * c : groups * c + groups].reshape(fc, d), NT) * gp_v[c].astype(F32)
        summed(4 * d + fc * c, gup)
        gup = gup.astype(BF)
        gj_v[c] = gup
        span = pl.ds(fc * c, fc)
        pending.append(cout.either(core, gj_v.at[c], kept.at[:, span], sent.at[:, span]))
        total = mm(gup, u_v[c], NT)
        if c == 0:
            acc_v[...] = total
        else:
            acc_v[...] += total
        for p in range(pairs * c, pairs * c + pairs):
            cols = slice(LANES * p, LANES * p + LANES)
            keys, vals, pair = k_v[:, cols], v_v[:, cols], q_v[:, cols]
            keys_t = keys.T
            gk, gv = None, None
            for half in range(2):
                h = 2 * p + half
                at_rows = slice(64 * h, 64 * h + 64)
                inv = rs_v[h : h + 1, :]
                ga = (gat_v[at_rows, :].astype(F32) * inv).astype(BF)
                ga = jnp.concatenate([zeros, ga] if half else [ga, zeros], axis=0)
                e = e_v[h]
                ef = e.astype(F32)
                gp = ef * mm(vals, ga)
                dot = jnp.sum(gp, axis=0, keepdims=True) * inv
                gs = (gp - ef * dot).astype(BF)
                gk_h = mm(gs, lane_half(pair, half))
                gv_h = mm(e, ga, NT)
                gk = gk_h if gk is None else gk + gk_h
                gv = gv_h if gv is None else gv + gv_h
                gqt_v[at_rows, :] = mm(keys_t[64 * half : 64 * half + 64], gs) * 0.125
            gk_v[:, cols] = gk
            gv_b[:, cols] = gv.astype(BF)
    pending.append(cout.either(core, gv_b, sent.at[:, side(1)], kept.at[:, side(1)]))
    for copy in norms:
        copy.wait()
    for i, (grad, out) in enumerate(((gqt_v[...].T, gq_b), (gk_v[...], gk_b))):
        normal = n_v[:, d * i : d * i + d].astype(F32)
        summed(2 * d + d * i, grad * normal)
        out[...] = norm_back(grad * gains[i], normal, r_v[:, d * i : d * i + d].astype(F32), spread[...]).astype(BF)
        pending.append(cout.either(core, out, kept.at[:, side(i)], sent.at[:, side(i)]))
    for copy in wq:
        copy.wait()
    ghid = acc_v[...]
    for i, part in enumerate((gq_b, gk_b, gv_b)):
        ghid = ghid + mm(part[...], w_v[:, d * i : d * i + d], NT)
    rows_in.wait()
    xhat, rstd = row_norm(keep * x_v[...].astype(F32))
    summed(0, ghid * xhat)
    pending.append(cout.start(sm_v, table))
    gx = ghid * ngain[...]
    gmask = rstd * (gx - jnp.mean(gx, axis=-1, keepdims=True) - xhat * jnp.mean(gx * xhat, axis=-1, keepdims=True))
    out = keep * (keep * g_v[...].astype(F32) + gmask)
    out_v[...] = out
    gbf[...] = out.astype(BF)
    pending.append(cout.either(home, out_v, gr_out.at[slot], gr_send))
    for copy in pending:
        copy.wait()


def split_small(values):
    top = values.astype(BF).astype(F32)
    lane = lax.broadcasted_iota(jnp.int32, values.shape, 1)
    return jnp.where(lane < 8, top, jnp.where(lane < 16, pltpu.roll(values - top, 8, 1), 0.0)).astype(BF)


def joined_small(parts):
    return parts + pltpu.roll(parts, LANES - 8, 1)


def small_table(d, ff, place, mine, theirs):
    total = mine[...] + theirs[...]
    quarter = WIDE // 4
    ub = total[:, 4 * d :]
    up_rows = []
    for j in range(4):
        pieces = [ub[:, WIDE * b + quarter * j : WIDE * b + quarter * (j + 1)] for b in range(ff // WIDE)]
        up_rows.append(jnp.concatenate(pieces, axis=1))
    head_rows = []
    for i in range(2, 4):
        lanes = total[:, d * i : d * i + LANES]
        for p in range(1, d // LANES):
            lanes = lanes + total[:, d * i + LANES * p : d * i + LANES * (p + 1)]
        head_rows.append(lanes)
    both = jnp.concatenate(head_rows + [jnp.zeros((6, LANES), F32)], axis=0)
    placed = lax.dot_general(both, place[...], NN, precision=lax.Precision.HIGHEST, preferred_element_type=F32)
    rows = [total[:, :d], total[:, d : 2 * d]] + up_rows + [placed[0:1], placed[1:2], jnp.zeros((LANES - 8, d), F32)]
    return jnp.concatenate(rows, axis=0).T


def weight_grad_kernel(d, ff, part, idx, place, mine, theirs, kept, got, *refs):
    outs_hbm, (big_v, a_v, b_v, out_v, ins, outs) = refs[:-6], refs[-6:]
    rows = kept.shape[0]
    tokens = 2 * rows
    quarter, half, blocks = WIDE // 4, ff // 2, ff // WIDE
    y, z, core = idx[0], idx[1], idx[2]

    def load(cin, at, width, to, to_at):
        return [cin.start(src.at[:, pl.ds(at, width)], to.at[i, :, pl.ds(to_at, width)]) for i, src in enumerate((kept, got))]

    def put(rows_at, cols_at, value):
        out_v[rows_at, cols_at] = value.astype(BF)

    def send():
        cout = Copies(outs)
        share = d // 16
        if part == 0:
            return [cout.start(out_v.at[pl.ds(pl.multiple_of(lax.rem(y + s, 4) * 4 * share, 16), 4 * share)], outs_hbm[s])
                    for s in (1, 2, 3, 0)]
        return [
            cout.start(out_v.at[pl.ds(pl.multiple_of((4 * i + lax.rem(z + s, 4)) * share, 16), share)], outs_hbm[s].at[i])
            for s in (1, 2, 3, 0) for i in range(4)
        ]

    everything = slice(0, d)

    @pl.when(core == 0)
    def _():
        cin = Copies(ins)
        grads = load(cin, ff, d, a_v, 0)
        third = blocks // 3
        loads = [[c for b in range(third * k, third * k + third) for c in load(cin, WIDE * b + LANES * part, LANES, big_v, LANES * b)]
                 for k in range(3)]
        if part == 0:
            last = load(cin, ff + 3 * d, d, b_v, 0)
        else:
            last = load(cin, ff + 2 * d, d, b_v, 0) + load(cin, ff + d, d, big_v, LANES * blocks)
        for copy in grads:
            copy.wait()
        gb = a_v[...].reshape(tokens, d)
        for k in range(3):
            for copy in loads[k]:
                copy.wait()
            left = big_v[:, :, LANES * third * k : LANES * third * (k + 1)].reshape(tokens, LANES * third)
            found = lax.dot_general(left, gb, TN, preferred_element_type=F32)
            for b in range(third):
                for j in range(2):
                    at = quarter * (third * k + b)
                    put(slice(at, at + quarter), slice(d * j, d * j + d),
                        found[LANES * b + quarter * j : LANES * b + quarter * (j + 1)])
        for copy in last:
            copy.wait()
        if part == 0:
            put(everything, slice(2 * d, 3 * d), lax.dot_general(b_v[...].reshape(tokens, d), gb, TN, preferred_element_type=F32))
        else:
            values = big_v[:, :, LANES * blocks :].reshape(tokens, d)
            put(everything, slice(2 * d, 3 * d), lax.dot_general(
                b_v[...].reshape(tokens, d), values, TN, preferred_element_type=F32))
            out_v[:, 3 * d :] = split_small(small_table(d, ff, place, mine, theirs))
        for copy in send():
            copy.wait()

    @pl.when(core == 1)
    def _():
        cin = Copies(ins)
        hidden = load(cin, ff + 2 * d, d, a_v, 0)
        step = half // 3
        loads = [load(cin, half * part + step * k, step, big_v, step * k) for k in range(3)]
        loads.append(load(cin, ff + d * part, d, b_v, 0))
        for copy in hidden:
            copy.wait()
        turned = a_v[...].reshape(tokens, d).T
        for k in range(3):
            for copy in loads[k]:
                copy.wait()
            put(everything, slice(step * k, step * k + step), mm(turned, big_v[:, :, step * k : step * k + step].reshape(tokens, step)))
        for copy in loads[3]:
            copy.wait()
        put(everything, slice(half, half + d), mm(turned, b_v[...].reshape(tokens, d)))
        if part == 1:
            out_v[:, 3 * d :] = jnp.zeros((d, LANES), BF)
        for copy in send():
            copy.wait()


def added(parts):
    total = parts[0][...].astype(F32)
    for part in parts[1:]:
        total = total + part[...].astype(F32)
    shape = total.shape
    total = total.reshape(-1, shape[-1])
    main, last = total[:, : shape[-1] - LANES], split_small(joined_small(total[:, shape[-1] - LANES :]))
    return jnp.concatenate([main.astype(BF), last], axis=1).reshape(shape)


def mid_kernel(part, idx, *refs):
    came, outs, hold = refs[:4], refs[4:8], refs[8]
    if part == 0:
        total = came[0][...].astype(F32)
        for piece in came[1:]:
            total = total + piece[...].astype(F32)
        hold[...] = total.astype(BF).reshape(hold.shape)
    else:
        hold[...] = added(came)
    at = idx[1] if part == 0 else idx[0]
    for s in range(4):
        outs[s][...] = hold[lax.rem(at + s, 4)]


def last_kernel(idx, *refs):
    firsts, seconds, mine, theirs, hold = refs[:4], refs[4:8], refs[8], refs[9], refs[10]
    cut = firsts[0].shape[-1]
    total = firsts[0][...].astype(F32)
    for piece in firsts[1:]:
        total = total + piece[...].astype(F32)
    hold[:, :cut] = total
    hold[:, cut:] = added(seconds).astype(F32)
    count = mine.shape[0]
    core = idx[2]
    mine[...] = hold[pl.ds(pl.multiple_of(core * count, 8), count), :]
    theirs[...] = hold[pl.ds(pl.multiple_of((1 - core) * count, 8), count), :]


def place_kernel(idx, y_in, y_got, g_in, g_got, y_out, g_out, sems):
    copies = Copies(sems)
    for copy in [copies.start(y_got, y_out.at[1 - idx[3]]), copies.start(g_got, g_out.at[1 - idx[3]])]:
        copy.wait()


ANY = pl.BlockSpec(memory_space=pl.ANY)


def whole(shape):
    return pl.BlockSpec(shape, lambda i, idx: (0,) * len(shape))


def pick(shape):
    return pl.BlockSpec((1,) + shape, lambda i, idx: (idx[2],) + (0,) * len(shape))


def call(kernel, idx, ins, fresh, stashes, scratch, flops):
    outs = pl.pallas_call(
        kernel,
        grid_spec=pltpu.PrefetchScalarGridSpec(
            num_scalar_prefetch=1,
            grid=(1,),
            in_specs=[s for _, s in ins] + [ANY] * len(stashes),
            out_specs=[whole(fresh[0])] + [ANY] * len(stashes),
            scratch_shapes=scratch,
        ),
        out_shape=[jax.ShapeDtypeStruct(*fresh)] + [jax.ShapeDtypeStruct(a.shape, a.dtype) for a in stashes],
        input_output_aliases={1 + len(ins) + i: 1 + i for i in range(len(stashes))},
        compiler_params=pltpu.CompilerParams(dimension_semantics=("arbitrary",), vmem_limit_bytes=VMEM_LIMIT),
        cost_estimate=pl.CostEstimate(flops=flops, bytes_accessed=1 << 10, transcendentals=0),
    )(idx, *[a for a, _ in ins], *stashes)
    return outs[0], list(outs[1:])


def simple(kernel, idx, arrays, specs, out_shapes, out_specs, scratch, flops=1 << 10):
    return pl.pallas_call(
        kernel,
        grid_spec=pltpu.PrefetchScalarGridSpec(
            num_scalar_prefetch=1, grid=(1,), in_specs=specs, out_specs=out_specs, scratch_shapes=scratch
        ),
        out_shape=out_shapes,
        compiler_params=pltpu.CompilerParams(dimension_semantics=("arbitrary",), vmem_limit_bytes=VMEM_LIMIT),
        cost_estimate=pl.CostEstimate(flops=flops, bytes_accessed=1 << 10, transcendentals=0),
    )(idx, *arrays)


def along(x, step, size, by):
    devices = lax.axis_size("dp")

    def to(i):
        digit = i // step % size
        return i + ((digit + by) % size - digit) * step

    return lax.ppermute(x, "dp", [(i, to(i)) for i in range(devices)])


def paired(x):
    return lax.ppermute(x, "section", [(0, 1), (1, 0), (2, 3), (3, 2)])


def body(tokens, cotangent, lengths, proj_in, proj_attn, proj_down, norm_gain, query_gain, key_gain, up_bias, out_bias):
    ranks = lax.axis_size("dp")
    section = lax.axis_index("section")
    rank = lax.axis_index("dp")
    slots = lengths.shape[0]
    rows = tokens.shape[0] // slots
    d = tokens.shape[1]
    joined = proj_in.shape[2]
    ff = proj_down.shape[1] * ranks
    head = query_gain.shape[1] * ranks
    heads = d // head
    dshare = proj_in.shape[1]
    fshare = proj_down.shape[1] // dshare
    hshare = query_gain.shape[1]
    chunks = 3
    wide = joined + d + ff
    stride = wide + LANES
    side = math.isqrt(ranks // 2)
    core, z, y = lax.rem(rank, 2), lax.rem(rank // 2, side), rank // (2 * side)
    stage, odd = section // 2, lax.rem(section, 2)
    slot = lax.rem(stage + odd, 2)

    place = jnp.arange(WIDE, dtype=jnp.int32)
    source = (place % (WIDE // fshare)) * fshare + place // (WIDE // fshare)
    shuffle = (place[:, None] == source[None, :]).astype(BF)

    def shuffled(x, back=False):
        flat = x.reshape(-1, WIDE)
        out = lax.dot_general(
            flat, shuffle.astype(x.dtype), NT if back else NN, precision=lax.Precision.HIGHEST, preferred_element_type=F32
        )
        return out.reshape(x.shape)

    small = jnp.concatenate(
        [
            norm_gain[0][:, None],
            out_bias[0][:, None],
            up_bias[0].reshape(dshare, fshare),
            jnp.pad(query_gain[0], (0, dshare - hshare))[:, None],
            jnp.pad(key_gain[0], (0, dshare - hshare))[:, None],
            jnp.zeros((dshare, LANES - 4 - fshare), BF),
        ],
        axis=1,
    )
    heads_part = joined - ff
    local = jnp.concatenate(
        [shuffled(proj_in[0][:, heads_part:]).astype(BF), proj_in[0][:, :heads_part], proj_attn[0],
         proj_down[0].reshape(dshare, fshare * d), small],
        axis=1,
    )
    other = paired(local)
    both = jnp.where(odd == 0, jnp.concatenate([local, other], axis=1), jnp.concatenate([other, local], axis=1))
    g = lax.all_gather(both, "dp", axis=0, tiled=True)
    g3 = g.reshape(ff // WIDE, WIDE // fshare, g.shape[1])
    smalls = []
    for layer in range(2):
        at = stride * layer + wide
        tail = g[:, at : at + LANES].astype(F32)
        qk_gain = tail[:, 2 + fshare : 4 + fshare].reshape(ranks, dshare, 2)[:, :hshare].reshape(head, 2).T
        smalls.append((
            tail[:, 0].reshape(1, d),
            jnp.tile(qk_gain, (1, heads)).reshape(2, 1, d),
            shuffled(tail[:, 2 : 2 + fshare].reshape(1, ff).astype(BF)),
            tail[:, 1].reshape(1, d),
        ))
    column = jnp.arange(WIDE, dtype=jnp.int32) // head
    spread = jnp.where(column[:, None] == column[None, :], 1.0 / head, 0.0).astype(BF)

    toks = tokens.reshape(slots, rows, d)
    seeds = cotangent.reshape(slots, rows, d)
    ends = jnp.cumsum(lengths, axis=-1)
    position = jnp.arange(rows, dtype=jnp.int32)
    image = jnp.sum((position[None, :, None] >= ends[:, None, :]).astype(jnp.int32), axis=-1)
    image = jnp.where(position[None, :] < ends[:, 2:3], image, ABSENT + position[None, :])
    ids_col, ids_row = image[:, :, None], image[:, None, :]

    def stash(*shape, dtype=BF):
        return pl.pallas_call(
            lambda out: None, out_shape=jax.ShapeDtypeStruct(shape, dtype), out_specs=pl.BlockSpec(memory_space=pl.ANY)
        )()

    fc = ff // chunks
    groups = ff // WIDE

    def index_of(layer, active_stage):
        return jnp.stack([stage == active_stage, core, slot, odd == layer]).astype(jnp.int32)

    V = pltpu.VMEM
    weights_v = [V((d, heads_part), BF), V((chunks, d, fc), BF), V((groups, fshare, WIDE // fshare, d), BF), V((d, d), BF)]
    sems = [pltpu.SemaphoreType.DMA((48,)), pltpu.SemaphoreType.DMA((48,))]
    stacked = ff + 4 * d
    operands = [[stash(rows, stacked), stash(rows, stacked)] for _ in range(2)]
    kept = [[stash(rows, d) for _ in range(4)] + [stash(rows, 2 * d), stash(rows, 2 * d), stash(chunks, rows, fc),
             stash(heads, rows, rows), stash(16, rows, dtype=F32)] for _ in range(2)]
    results = [stash(slots, rows, d, dtype=F32), stash(rows, d, dtype=F32)]
    here_x = toks
    for t in range(4):
        layer = t % 2
        ngain, gains, ubias, obias = smalls[layer]
        ybf, done = call(
            partial(forward_kernel, d, ff, chunks, stride * layer, t == 0),
            index_of(layer, t // 2),
            [(here_x, ANY), (g, ANY), (g3, ANY), (ids_col, pick((rows, 1))), (ids_row, pick((1, rows))),
             (ngain, whole((1, d))), (gains, whole((2, 1, d))), (ubias, whole((1, ff))), (obias, whole((1, d))),
             (spread, whole((WIDE, WIDE)))],
            ((rows, d), BF),
            kept[layer][:9] + operands[layer] + results,
            [V((rows, d), BF), V((rows, d), BF)] + weights_v
            + [V((rows, d), BF)] * 3 + [V((rows, 2 * d), BF)] * 2 + [V((chunks, rows, fc), BF)] * 2
            + [V((heads, rows, rows), BF), V((16, rows), F32), V((rows, d), BF), V((rows, d), F32), V((rows, d), F32)]
            + sems,
            1 << 10,
        )
        kept[layer], operands[layer], results = done[:9], done[9:11], done[11:]
        here_x = lax.ppermute(ybf, "section", [(0, 3), (1, 2)]) if t == 1 else ybf
    y_out, y_send = results
    y_got = paired(y_send)

    results = [stash(slots, rows, d, dtype=F32), stash(rows, d, dtype=F32)]
    tables = [stash(1, stacked, dtype=F32) for _ in range(2)]
    steps = ((2 * side, 2), (2, 2 * side))
    widths = (3 * d, 3 * d + LANES)
    width = widths[0] + widths[1]
    share = 2 * dshare
    position = jnp.arange(LANES, dtype=jnp.int32)[:, None] % head
    place = (position // hshare * dshare + position % hshare == jnp.arange(d, dtype=jnp.int32)[None, :]).astype(F32)
    here = jnp.stack([y, z, core, slot]).astype(jnp.int32)

    def grads_by_place(layer, ahead=None):
        mine, sent = operands[layer]
        if ahead is not None:
            sent, ahead = lax.optimization_barrier((sent, ahead))
        got, table_got = along(sent, 1, 2, 1), along(tables[layer], 1, 2, 1)
        made = []
        for part in range(2):
            w = widths[part]
            shape = (side * share, w) if part == 0 else (side, share, w)
            made.append(simple(
                partial(weight_grad_kernel, d, ff, part), here,
                [place, tables[layer], table_got, mine, got],
                [whole((LANES, d)), whole(table_got.shape), whole(table_got.shape), ANY, ANY],
                [jax.ShapeDtypeStruct(shape, BF)] * side, [ANY] * side,
                [V((2, rows, ff // 2 + d), BF), V((2, rows, d), BF), V((2, rows, d), BF), V((d, w), BF),
                 pltpu.SemaphoreType.DMA((32,)), pltpu.SemaphoreType.DMA((16,))],
                1 << 10,
            ))
        return made, ahead

    def first_leg(made):
        return [[outs[0]] + [along(outs[s], steps[part][0], side, s) for s in (1, 2, 3)] for part, outs in enumerate(made)]

    def second_leg(legs):
        arrived = []
        for part, came in enumerate(legs):
            w = widths[part]
            outs = simple(
                partial(mid_kernel, part), here, came, [whole(a.shape) for a in came],
                [jax.ShapeDtypeStruct((share, w), BF)] * side, [whole((share, w))] * side, [V((side, share, w), BF)],
            )
            arrived += [outs[0]] + [along(outs[s], steps[part][1], side, s) for s in (1, 2, 3)]
        return simple(
            last_kernel, here, arrived, [whole(a.shape) for a in arrived],
            [jax.ShapeDtypeStruct((dshare, width), F32)] * 2, [whole((dshare, width))] * 2, [V((share, width), F32)],
        )

    sums = [None, None]
    here_g = seeds
    for t in range(4):
        layer = 1 - t % 2
        ngain, gains, ubias, obias = smalls[layer]
        gbf, done = call(
            partial(backward_kernel, d, ff, chunks, stride * layer, t == 0),
            index_of(layer, 1 - t // 2),
            [(here_g, ANY), (g, ANY), (g3, ANY), (ids_col, pick((rows, 1))), (ngain, whole((1, d))), (gains, whole((2, 1, d))),
             (spread, whole((WIDE, WIDE)))] + [(a, ANY) for a in kept[layer]],
            ((rows, d), BF),
            operands[layer] + [tables[layer]] + results,
            [V((rows, d), BF), V((rows, d), BF)] + weights_v
            + [V((rows, d), BF)] * 4 + [V((rows, 2 * d), BF)] * 2
            + [V((chunks, rows, fc), BF), V((heads, rows, rows), BF), V((16, rows), F32)]
            + [V((d, rows), BF), V((d, rows), F32), V((rows, d), F32)]
            + [V((rows, d), BF)] * 3 + [V((chunks, rows, fc), BF), V((rows, d), F32), V((rows, d), F32), V((1, stacked), F32)]
            + sems,
            1 << 10,
        )
        operands[layer], tables[layer], results = done[:2], done[2], done[3:]
        here_g = lax.ppermute(gbf, "section", [(3, 0), (2, 1)]) if t == 1 else gbf
        if t == 1:
            here_g, y_got = lax.optimization_barrier((here_g, y_got))
        if t == 2:
            made, _ = grads_by_place(layer)
            here_g, made = lax.optimization_barrier((here_g, made))
            legs = first_leg(made)
        if t == 3:
            made, early = grads_by_place(layer, [legs[p][s] for p in (0, 1) for s in (1, 3)])
            (legs[0][1], legs[0][3], legs[1][1], legs[1][3]) = early
            sums[1 - layer] = second_leg(legs)
            gr_got = paired(results[1])
            legs, gr_got = lax.optimization_barrier((first_leg(made), gr_got))
            sums[layer] = second_leg(legs)
    gr_out = results[0]
    y_out, gr_out = pl.pallas_call(
        place_kernel,
        grid_spec=pltpu.PrefetchScalarGridSpec(
            num_scalar_prefetch=1, grid=(1,), in_specs=[ANY] * 4, out_specs=[ANY] * 2,
            scratch_shapes=[pltpu.SemaphoreType.DMA((2,))],
        ),
        out_shape=[jax.ShapeDtypeStruct(y_out.shape, F32)] * 2,
        input_output_aliases={1: 0, 3: 1},
    )(here, y_out, y_got, gr_out, gr_got)

    home = [jnp.where(odd == 1, b, a) for a, b in zip(*sums)]
    away = [jnp.where(odd == 1, a, b).astype(BF) for a, b in zip(*sums)]
    sections = lax.axis_size("section")
    cross = [(s * ranks + i, (s ^ 1) * ranks + (i ^ 1)) for s in range(sections) for i in range(ranks)]
    mine = home[0] + paired(away[0]).astype(F32)
    other = along(home[1].astype(BF), 1, 2, 1).astype(F32) + lax.ppermute(away[1], ("section", "dp"), cross).astype(F32)
    half0, half1 = jnp.where(core == 0, mine, other), jnp.where(core == 0, other, mine)
    ups = shuffled(jnp.concatenate([half1[:, : 2 * d], half1[:, 3 * d : 5 * d]], axis=1), back=True)
    g_in = jnp.concatenate([half1[:, 2 * d : 3 * d], half1[:, 5 * d : 6 * d], half0[:, 5 * d : 6 * d], ups], axis=1)
    g_down = jnp.concatenate([half0[:, : 2 * d], half0[:, 3 * d : 5 * d]], axis=1)
    last = half0[:, 6 * d : 6 * d + 8] + half0[:, 6 * d + 8 : 6 * d + 16]
    return (
        y_out.reshape(1, slots * rows, d),
        gr_out.reshape(1, slots * rows, d),
        g_in[None],
        half0[None, :, 2 * d : 3 * d],
        g_down.reshape(1, dshare * fshare, d),
        last[None, :, 0],
        last[None, :hshare, 6],
        last[None, :hshare, 7],
        last[:, 2:6].reshape(1, dshare * fshare),
        last[None, :, 1],
    )


def solution(mesh):
    in_specs = (P("dp", None),) * 3 + (P("section", "dp", None),) * 3 + (P("section", "dp"),) * 5
    out_specs = (P("section", "dp", None),) * 5 + (P("section", "dp"),) * 5
    return jax.shard_map(body, mesh=mesh, in_specs=in_specs, out_specs=out_specs, check_vma=False)
```

time: 606 us -> 591 us (0.975)
  Pallas kernels: 203 us -> 256 us
  local copies, waits for them, and re-layouts: 55.1 us -> 24.7 us
  matrix products: 30.6 us -> 0.87 us
  starting transfers between devices: 36.7 us -> 46.1 us
  other arithmetic: 19.4 us -> 12.2 us
    pallas_call x23 -> x39, Pallas kernels: 0.04 us -> 137 us  [the longest x1 73.4 us: body(): pl.pallas_call(place_kernel, grid_spec=pltpu.PrefetchScalarGridSpec(num_s...]
    pallas_call x10 -> x8, Pallas kernels: 203 us -> 119 us  [call(): pl.pallas_call(kernel, grid_spec=pltpu.PrefetchScalarGridSpec(num_scalar_...]
    reduce_scatter x1 -> x0, waiting for transfers between devices: 80.2 us -> none  [body(): lax.psum_scatter(jnp.concatenate(g_up + g_heads + [g_attn, g_down], axis=...]
    ppermute x13 -> x36, waiting for transfers between devices: 88.3 us -> 131 us  [the longest x1 59.7 us: body(): here_g = lax.ppermute(gbf, 'section', [(3, 0), (2, 1)]) if t == 1 else gbf]
    all_gather x1, waiting for transfers between devices: 66.5 us -> 100 us  [body(): g = lax.all_gather(both, 'dp', axis=0, tiled=True)]
    dot_general x13 -> x4, matrix products: 30.6 us -> 0.87 us  [shuffled(): lax.dot_general(flat, shuffle.astype(x.dtype), NT if back else NN, precis...]
    unnamed x59, local copies, waits for them, and re-layouts: 19.6 us -> 5.98 us
    ppermute x13 -> x36, starting transfers between devices: 36.6 us -> 46.1 us  [the longest x29 32.2 us: along(): return lax.ppermute(x, 'dp', [(i, to(i)) for i in range(devices)])]
  transfers between devices with their start and end apart: 15 -> 37, of which waited for: 14 -> 15; matrix products, arithmetic and copies ran while one was open for 3% -> 1% of each run, Pallas kernels for 0% -> 28%
where the time goes in v4:
time: 591 us; the launch traced here: 587 us
  Pallas kernels  256 us (43%)
  waiting for transfers between devices  231 us (39%)
  starting transfers between devices  46.1 us (8%)
  local copies, waits for them, and re-layouts  24.7 us (4%)
  between operations  15.2 us (3%)
  other arithmetic  12.2 us (2%)
    pallas_call x8, Pallas kernels, call(): pl.pallas_call(kernel, grid_spec=pltpu.PrefetchScalarGridSpec(num_scalar_...  119 us
    all_gather x1, waiting for transfers between devices, body(): g = lax.all_gather(both, 'dp', axis=0, tiled=True)  100 us
    pallas_call x1, Pallas kernels, body(): pl.pallas_call(place_kernel, grid_spec=pltpu.PrefetchScalarGridSpec(num_s...  73.4 us
    pallas_call x10, Pallas kernels, simple(): pl.pallas_call(kernel, grid_spec=pltpu.PrefetchScalarGridSpec(num_scalar_...  64 us
    ppermute x1, waiting for transfers between devices, body(): here_g = lax.ppermute(gbf, 'section', [(3, 0), (2, 1)]) if t == 1 else gbf  59.7 us
    ppermute x29, waiting for transfers between devices, along(): return lax.ppermute(x, 'dp', [(i, to(i)) for i in range(devices)])  49.8 us
    ppermute x29, starting transfers between devices, along(): return lax.ppermute(x, 'dp', [(i, to(i)) for i in range(devices)])  32.2 us
    ppermute x1, waiting for transfers between devices, body(): here_x = lax.ppermute(ybf, 'section', [(0, 3), (1, 2)]) if t == 1 else ybf  11.9 us
  transfers between devices with their start and end apart: 37, of which 15 were waited for; matrix products, arithmetic and copies ran while one was open for 1% of the time, Pallas kernels for 28%

profile of v4, /device:TPU:1, one launch (start us, length us, event | category | flops | bytes accessed | tf_op | source)
XLA Modules:
  0.0 586.6 jit_solution(11215408926477115843)
XLA Ops:
  18.7 9.5 %collective-permute-done = bf16[24,9344]{1,0:T(8,128)(2,1)S(1)} collective-permute-done((bf16[24,9344]{1,0:T(8,128)(2,1)S(1)}, bf16[24,9344]{1,0:T(8,128)(2,1)S(1)}, u32[]{:S(2)}, u32[]{:S(2)}) %collective-permute-start) | collective-permute-done | bytes 448544 | tf_op jit(solution)/shard_map/ppermute | solution.py:505
  35.1 100.4 %all-gather.2.cloned.1.call-done.g = bf16[768,18688]{1,0:T(8,128)(2,1)} async-done(((bf16[24,18688]{1,0:T(8,128)(2,1)}), bf16[768,18688]{1,0:T(8,128)(2,1)}) %all-gather.2.cloned.1.call-update) | async-done | bytes 28704784 | tf_op jit(solution)/shard_map/all_gather | solution.py:560
  144.8 18.2 %shard_map.199 = (bf16[384,768]{1,0:T(8,128)(2,1)}, bf16[384,768]{1,0:T(8,128)(2,1)}, bf16[384,768]{1,0:T(8,128)(2,1)}, bf16[384,768]{1,0:T(8,128)(2,1)}, bf16[3...) custom-call(s32[4]{0:T(128)} %get-tuple-element.300.idx, ...), custom_call_target="tpu_custom_call", output_to_operand_aliasing={{1}: (11, {}), {2}: (12, {}), {3}: (13, {}), {4}: (14, {}),... | custom-call | flops 1024 | bytes 1024 | tf_op jit(solution)/shard_map/pallas_call | solution.py:465
  163.0 18.3 %shard_map.211 = (bf16[384,768]{1,0:T(8,128)(2,1)}, bf16[384,768]{1,0:T(8,128)(2,1)}, bf16[384,768]{1,0:T(8,128)(2,1)}, bf16[384,768]{1,0:T(8,128)(2,1)}, bf16[3...) custom-call(s32[4]{0:T(128)} %pad_add_fusion.1.idx, ...), custom_call_target="tpu_custom_call", output_to_operand_aliasing={{1}: (11, {}), {2}: (12, {}), {3}: (13, {}), {4}: (14, {}),... | custom-call | flops 1024 | bytes 1024 | tf_op jit(solution)/shard_map/pallas_call | solution.py:465
  183.8 11.9 %collective-permute-done.1.x_in = bf16[384,768]{1,0:T(8,128)(2,1)S(1)} collective-permute-done((bf16[384,768]{1,0:T(8,128)(2,1)}, bf16[384,768]{1,0:T(8,128)(2,1)S(1)}, u32[]{:S(2)}, u32[]{:S(2)}) %collective-permute-start.1) | collective-permute-done | bytes 589856 | tf_op jit(solution)/shard_map/ppermute | solution.py:622
  200.4 7.7 %shard_map.213 = (bf16[384,768]{1,0:T(8,128)(2,1)}, bf16[384,768]{1,0:T(8,128)(2,1)}, bf16[384,768]{1,0:T(8,128)(2,1)}, bf16[384,768]{1,0:T(8,128)(2,1)}, bf16[3...) custom-call(s32[4]{0:T(128)} %pad_add_fusion.2.idx, ...), custom_call_target="tpu_custom_call", output_to_operand_aliasing={{1}: (11, {}), {2}: (12, {}), {3}: (13, {}), {4}: (14, {}),... | custom-call | flops 1024 | bytes 1024 | tf_op jit(solution)/shard_map/pallas_call | solution.py:465
  209.3 16.8 %shard_map.217 = (bf16[384,768]{1,0:T(8,128)(2,1)}, bf16[384,6144]{1,0:T(8,128)(2,1)}, bf16[384,6144]{1,0:T(8,128)(2,1)}, f32[1,6144]{1,0:T(1,128)}, f32[2,384,768]{2,1,0:T(8,128)}, /*index=5*/f32[384,768]{1,0:T(8,128)}) custom-call(s32[4]{0:T(128)} %pad_add_fusion.2.idx, ...), custom_call_target="tpu_custom_call", output_to_operand_aliasing={{1}: (17, {}), {2}: (18, {}), {3}: (19, {}), {4}: (20, {}),... | custom-call | flops 1024 | bytes 1024 | tf_op jit(solution)/shard_map/pallas_call | solution.py:465
  226.1 9.4 %shard_map.219 = (bf16[384,768]{1,0:T(8,128)(2,1)}, bf16[384,6144]{1,0:T(8,128)(2,1)}, bf16[384,6144]{1,0:T(8,128)(2,1)}, f32[1,6144]{1,0:T(1,128)}, f32[2,384,768]{2,1,0:T(8,128)}, /*index=5*/f32[384,768]{1,0:T(8,128)}) custom-call(s32[4]{0:T(128)} %get-tuple-element.302.idx, ...), custom_call_target="tpu_custom_call", output_to_operand_aliasing={{1}: (17, {}), {2}: (18, {}), {3}: (19, {}), {4}: (20, {}),... | custom-call | flops 1024 | bytes 1024 | tf_op jit(solution)/shard_map/pallas_call | solution.py:465
  236.8 59.7 %collective-permute-done.2.g_in = bf16[384,768]{1,0:T(8,128)(2,1)S(1)} collective-permute-done((bf16[384,768]{1,0:T(8,128)(2,1)}, bf16[384,768]{1,0:T(8,128)(2,1)S(1)}, u32[]{:S(2)}, u32[]{:S(2)}) %collective-permute-start.2) | collective-permute-done | bytes 589856 | tf_op jit(solution)/shard_map/ppermute | solution.py:694
  297.4 22.2 %shard_map.220 = (bf16[384,768]{1,0:T(8,128)(2,1)}, bf16[384,6144]{1,0:T(8,128)(2,1)}, bf16[384,6144]{1,0:T(8,128)(2,1)}, f32[1,6144]{1,0:T(1,128)}, f32[2,384,768]{2,1,0:T(8,128)}, /*index=5*/f32[384,768]{1,0:T(8,128)}) custom-call(s32[4]{0:T(128)} %pad_add_fusion.1.idx, ...), custom_call_target="tpu_custom_call", output_to_operand_aliasing={{1}: (17, {}), {2}: (18, {}), {3}: (19, {}), {4}: (20, {}),... | custom-call | flops 1024 | bytes 1024 | tf_op jit(solution)/shard_map/pallas_call | solution.py:465
  322.9 6.3 %collective-permute-done.4.theirs = f32[1,6144]{1,0:T(1,128)S(1)} collective-permute-done((f32[1,6144]{1,0:T(1,128)}, f32[1,6144]{1,0:T(1,128)S(1)}, u32[]{:S(2)}, u32[]{:S(2)}) %collective-permute-start.4) | collective-permute-done | bytes 24608 | tf_op jit(solution)/shard_map/ppermute | solution.py:501
  329.7 9.5 %shard_map.221 = (bf16[192,2304]{1,0:T(8,128)(2,1)}, bf16[192,2304]{1,0:T(8,128)(2,1)}, bf16[192,2304]{1,0:T(8,128)(2,1)}, bf16[192,2304]{1,0:T(8,128)(2,1)}) custom-call(s32[4]{0:T(128)} %pad_add_fusion.idx, f32[128,768]{1,0:T(8,128)} %fusion.4.place, f32[1,6144]{1,0:T(1,128)} %get-tuple-element.218.mine, f32[1,6144]{1,0:T(1,128)} %copy-done.23, ...), custom_call_target="tpu_custom_call" | custom-call | flops 1024 | bytes 1024 | tf_op jit(solution)/shard_map/pallas_call | solution.py:483
  339.2 9.9 %shard_map.222 = (bf16[4,48,2432]{2,1,0:T(8,128)(2,1)}, bf16[4,48,2432]{2,1,0:T(8,128)(2,1)}, bf16[4,48,2432]{2,1,0:T(8,128)(2,1)}, bf16[4,48,2432]{2,1,0:T(8,128)(2,1)}) custom-call(s32[4]{0:T(128)} %pad_add_fusion.idx, f32[128,768]{1,0:T(8,128)} %fusion.4.place, f32[1,6144]{1,0:T(1,128)} %get-tuple-element.218.mine, f32[1,6144]{1,0:T(1,128)} %copy-done.23, ...), custom_call_target="tpu_custom_call" | custom-call | flops 1024 | bytes 1024 | tf_op jit(solution)/shard_map/pallas_call | solution.py:483
  354.6 22.4 %shard_map.223 = (bf16[384,768]{1,0:T(8,128)(2,1)}, bf16[384,6144]{1,0:T(8,128)(2,1)}, bf16[384,6144]{1,0:T(8,128)(2,1)}, f32[1,6144]{1,0:T(1,128)}, f32[2,384,768]{2,1,0:T(8,128)}, /*index=5*/f32[384,768]{1,0:T(8,128)}) custom-call(s32[4]{0:T(128)} %get-tuple-element.300.idx, ...), custom_call_target="tpu_custom_call", output_to_operand_aliasing={{1}: (17, {}), {2}: (18, {}), {3}: (19, {}), {4}: (20, {}),... | custom-call | flops 1024 | bytes 1024 | tf_op jit(solution)/shard_map/pallas_call | solution.py:465
  382.5 4.7 collective-permute-done.6.theirs
  387.7 9.5 %shard_map.224 = (bf16[192,2304]{1,0:T(8,128)(2,1)}, bf16[192,2304]{1,0:T(8,128)(2,1)}, bf16[192,2304]{1,0:T(8,128)(2,1)}, bf16[192,2304]{1,0:T(8,128)(2,1)}) custom-call(s32[4]{0:T(128)} %pad_add_fusion.idx, f32[128,768]{1,0:T(8,128)} %fusion.4.place, f32[1,6144]{1,0:T(1,128)} %get-tuple-element.236.mine, f32[1,6144]{1,0:T(1,128)} %copy-done.22, ...), custom_call_target="tpu_custom_call" | custom-call | flops 1024 | bytes 1024 | tf_op jit(solution)/shard_map/pallas_call | solution.py:483
  407.5 9.8 %shard_map.225 = (bf16[4,48,2432]{2,1,0:T(8,128)(2,1)}, bf16[4,48,2432]{2,1,0:T(8,128)(2,1)}, bf16[4,48,2432]{2,1,0:T(8,128)(2,1)}, bf16[4,48,2432]{2,1,0:T(8,128)(2,1)}) custom-call(s32[4]{0:T(128)} %pad_add_fusion.idx, f32[128,768]{1,0:T(8,128)} %fusion.4.place, f32[1,6144]{1,0:T(1,128)} %get-tuple-element.236.mine, f32[1,6144]{1,0:T(1,128)} %copy-done.22, ...), custom_call_target="tpu_custom_call" | custom-call | flops 1024 | bytes 1024 | tf_op jit(solution)/shard_map/pallas_call | solution.py:483
  422.3 17.1 %collective-permute-done.13.refs_2_ = bf16[192,2304]{1,0:T(8,128)(2,1)} collective-permute-done((bf16[192,2304]{1,0:T(8,128)(2,1)}, bf16[192,2304]{1,0:T(8,128)(2,1)}, u32[]{:S(2)}, u32[]{:S(2)}) %collective-permute-start.13) | collective-permute-done | bytes 884768 | tf_op jit(solution)/shard_map/ppermute | solution.py:501
  440.3 4.6 shard_map.228
  449.5 8.2 %collective-permute-done.16.refs_2_ = bf16[4,48,2432]{2,1,0:T(8,128)(2,1)S(1)} collective-permute-done((bf16[4,48,2432]{2,1,0:T(8,128)(2,1)}, bf16[4,48,2432]{2,1,0:T(8,128)(2,1)S(1)}, u32[]{:S(2)}, u32[]{:S(2)}) %collective-permute-start.16) | collective-permute-done | bytes 933920 | tf_op jit(solution)/shard_map/ppermute | solution.py:501
  457.7 5.8 collective-permute-done.17.refs_3_
  470.4 4.6 shard_map.231
  493.2 6.2 %collective-permute-start.34 = (bf16[24,4736]{1,0:T(8,128)(2,1)S(1)}, bf16[24,4736]{1,0:T(8,128)(2,1)S(1)}, u32[]{:S(2)}, u32[]{:S(2)}) collective-permute-start(bf16[24,4736]{1,0:T(8,128)(2,1)S(1)} %get-tuple-element.311), channel_id=1, source_target_pairs={{0,33},{1,32},{2,35},{3,34},{4,37},{5,36},{6,39},{7,38},{8,41},{9,... | collective-permute-start | bytes 681992 | tf_op jit(solution)/shard_map/ppermute | solution.py:724
  500.8 73.4 %shard_map.226 = (f32[2,384,768]{2,1,0:T(8,128)}, f32[2,384,768]{2,1,0:T(8,128)}) custom-call(s32[4]{0:T(128)} %pad_add_fusion.idx, f32[2,384,768]{2,1,0:T(8,128)} %get-tuple-element.182.y_in, f32[384,768]{1,0:T(8,128)} %copy-done.2, f32[2,384,768]{2,1,0:T(8,128)} %get-tuple-element.235.g_in, ...), custom_call_target="tpu_custom_call", output_to_operand_aliasing={{0}: (1, {}), {1}: (3, {})} | custom-call | tf_op jit(solution)/shard_map/pallas_call | solution.py:709
  (234 shorter events, 105.5 us)
Async XLA Ops:
  7.2 128.3 %all-gather.2.cloned.1.call-start = ((), (), s32[]{:S(2)}) async-start(), calls=%async_computation | async-start | bytes 29601792 | tf_op jit(solution)/shard_map/all_gather | solution.py:560
  208.1 88.5 %collective-permute-start.3 = (f32[384,768]{1,0:T(8,128)}, f32[384,768]{1,0:T(8,128)S(1)}, u32[]{:S(2)}, u32[]{:S(2)}) collective-permute-start(f32[384,768]{1,0:T(8,128)} %get-tuple-element.209), channel_id=1, source_target_pairs={{0,32},{32,0},{64,96},{96,64},{1,33},{33,1},{65,97},{97,65},{2,34}... | collective-permute-start | bytes 3538952 | tf_op jit(solution)/shard_map/ppermute | solution.py:505
  235.5 61.0 %collective-permute-start.2 = (bf16[384,768]{1,0:T(8,128)(2,1)}, bf16[384,768]{1,0:T(8,128)(2,1)S(1)}, u32[]{:S(2)}, u32[]{:S(2)}) collective-permute-start(bf16[384,768]{1,0:T(8,128)(2,1)} %get-tuple-element.208), channel_id=1, source_target_pairs={{96,0},{64,32},{97,1},{65,33},{98,2},{66,34},{99,3},{67,35},{100,4... | collective-permute-start | bytes 1769480 | tf_op jit(solution)/shard_map/ppermute | solution.py:694
  349.1 27.9 %collective-permute-start.9 = (bf16[4,48,2432]{2,1,0:T(8,128)(2,1)}, bf16[4,48,2432]{2,1,0:T(8,128)(2,1)S(1)}, u32[]{:S(2)}, u32[]{:S(2)}) collective-permute-start(bf16[4,48,2432]{2,1,0:T(8,128)(2,1)} %get-tuple-element.241), channel_id=1, source_target_pairs={{0,2},{1,3},{2,4},{3,5},{4,6},{5,7},{6,0},{7,1},{8,10},{9,11},{10,... | collective-permute-start | bytes 2801672 | tf_op jit(solution)/shard_map/ppermute | solution.py:501
  349.7 27.4 %collective-permute-start.10 = (bf16[4,48,2432]{2,1,0:T(8,128)(2,1)}, bf16[4,48,2432]{2,1,0:T(8,128)(2,1)S(1)}, u32[]{:S(2)}, u32[]{:S(2)}) collective-permute-start(bf16[4,48,2432]{2,1,0:T(8,128)(2,1)} %get-tuple-element.242), channel_id=1, source_target_pairs={{0,6},{1,7},{2,0},{3,1},{4,2},{5,3},{6,4},{7,5},{8,14},{9,15},{10,... | collective-permute-start | bytes 2801672 | tf_op jit(solution)/shard_map/ppermute | solution.py:501
  351.9 25.1 %collective-permute-start.7 = (bf16[192,2304]{1,0:T(8,128)(2,1)}, bf16[192,2304]{1,0:T(8,128)(2,1)S(1)}, u32[]{:S(2)}, u32[]{:S(2)}) collective-permute-start(bf16[192,2304]{1,0:T(8,128)(2,1)} %get-tuple-element.239), channel_id=1, source_target_pairs={{0,8},{1,9},{2,10},{3,11},{4,12},{5,13},{6,14},{7,15},{8,16},{9,17... | collective-permute-start | bytes 2654216 | tf_op jit(solution)/shard_map/ppermute | solution.py:501
  353.1 23.9 %collective-permute-start.8 = (bf16[192,2304]{1,0:T(8,128)(2,1)}, bf16[192,2304]{1,0:T(8,128)(2,1)}, u32[]{:S(2)}, u32[]{:S(2)}) collective-permute-start(bf16[192,2304]{1,0:T(8,128)(2,1)} %get-tuple-element.240), channel_id=1, source_target_pairs={{0,24},{1,25},{2,26},{3,27},{4,28},{5,29},{6,30},{7,31},{8,0},{9,1... | collective-permute-start | bytes 2654216 | tf_op jit(solution)/shard_map/ppermute | solution.py:501
  379.3 41.8 %collective-permute-start.18 = (f32[384,768]{1,0:T(8,128)}, f32[384,768]{1,0:T(8,128)S(1)}, u32[]{:S(2)}, u32[]{:S(2)}) collective-permute-start(f32[384,768]{1,0:T(8,128)} %get-tuple-element.252), channel_id=1, source_target_pairs={{0,32},{32,0},{64,96},{96,64},{1,33},{33,1},{65,97},{97,65},{2,34}... | collective-permute-start | bytes 3538952 | tf_op jit(solution)/shard_map/ppermute | solution.py:505
  379.6 21.9 %collective-permute-start.19 = (bf16[192,2304]{1,0:T(8,128)(2,1)}, bf16[192,2304]{1,0:T(8,128)(2,1)}, u32[]{:S(2)}, u32[]{:S(2)}) collective-permute-start(bf16[192,2304]{1,0:T(8,128)(2,1)} %get-tuple-element.258), channel_id=1, source_target_pairs={{0,16},{1,17},{2,18},{3,19},{4,20},{5,21},{6,22},{7,23},{8,24},{9,... | collective-permute-start | bytes 2654216 | tf_op jit(solution)/shard_map/ppermute | solution.py:501
  381.1 36.1 %collective-permute-start.23 = (bf16[4,48,2432]{2,1,0:T(8,128)(2,1)S(1)}, bf16[4,48,2432]{2,1,0:T(8,128)(2,1)}, u32[]{:S(2)}, u32[]{:S(2)}) collective-permute-start(bf16[4,48,2432]{2,1,0:T(8,128)(2,1)S(1)} %copy-done.27), channel_id=1, source_target_pairs={{0,4},{1,5},{2,6},{3,7},{4,0},{5,1},{6,2},{7,3},{8,12},{9,13},{10,... | collective-permute-start | bytes 2801672 | tf_op jit(solution)/shard_map/ppermute | solution.py:501
  397.2 25.1 %collective-permute-start.12 = (bf16[192,2304]{1,0:T(8,128)(2,1)}, bf16[192,2304]{1,0:T(8,128)(2,1)}, u32[]{:S(2)}, u32[]{:S(2)}) collective-permute-start(bf16[192,2304]{1,0:T(8,128)(2,1)} %get-tuple-element.245), channel_id=1, source_target_pairs={{0,8},{1,9},{2,10},{3,11},{4,12},{5,13},{6,14},{7,15},{8,16},{9,17... | collective-permute-start | bytes 2654216 | tf_op jit(solution)/shard_map/ppermute | solution.py:501
  406.0 33.5 %collective-permute-start.13 = (bf16[192,2304]{1,0:T(8,128)(2,1)}, bf16[192,2304]{1,0:T(8,128)(2,1)}, u32[]{:S(2)}, u32[]{:S(2)}) collective-permute-start(bf16[192,2304]{1,0:T(8,128)(2,1)} %get-tuple-element.246), channel_id=1, source_target_pairs={{0,16},{1,17},{2,18},{3,19},{4,20},{5,21},{6,22},{7,23},{8,24},{9,... | collective-permute-start | bytes 2654216 | tf_op jit(solution)/shard_map/ppermute | solution.py:501
  417.2 30.1 %collective-permute-start.15 = (bf16[4,48,2432]{2,1,0:T(8,128)(2,1)}, bf16[4,48,2432]{2,1,0:T(8,128)(2,1)S(1)}, u32[]{:S(2)}, u32[]{:S(2)}) collective-permute-start(bf16[4,48,2432]{2,1,0:T(8,128)(2,1)} %get-tuple-element.249), channel_id=1, source_target_pairs={{0,2},{1,3},{2,4},{3,5},{4,6},{5,7},{6,0},{7,1},{8,10},{9,11},{10,... | collective-permute-start | bytes 2801672 | tf_op jit(solution)/shard_map/ppermute | solution.py:501
  417.3 40.4 %collective-permute-start.16 = (bf16[4,48,2432]{2,1,0:T(8,128)(2,1)}, bf16[4,48,2432]{2,1,0:T(8,128)(2,1)S(1)}, u32[]{:S(2)}, u32[]{:S(2)}) collective-permute-start(bf16[4,48,2432]{2,1,0:T(8,128)(2,1)} %get-tuple-element.250), channel_id=1, source_target_pairs={{0,4},{1,5},{2,6},{3,7},{4,0},{5,1},{6,2},{7,3},{8,12},{9,13},{10,... | collective-permute-start | bytes 2801672 | tf_op jit(solution)/shard_map/ppermute | solution.py:501
  421.2 42.3 %collective-permute-start.17 = (bf16[4,48,2432]{2,1,0:T(8,128)(2,1)}, bf16[4,48,2432]{2,1,0:T(8,128)(2,1)}, u32[]{:S(2)}, u32[]{:S(2)}) collective-permute-start(bf16[4,48,2432]{2,1,0:T(8,128)(2,1)} %get-tuple-element.251), channel_id=1, source_target_pairs={{0,6},{1,7},{2,0},{3,1},{4,2},{5,3},{6,4},{7,5},{8,14},{9,15},{10,... | collective-permute-start | bytes 2801672 | tf_op jit(solution)/shard_map/ppermute | solution.py:501
  422.3 22.6 %collective-permute-start.14 = (bf16[192,2304]{1,0:T(8,128)(2,1)}, bf16[192,2304]{1,0:T(8,128)(2,1)}, u32[]{:S(2)}, u32[]{:S(2)}) collective-permute-start(bf16[192,2304]{1,0:T(8,128)(2,1)} %get-tuple-element.247), channel_id=1, source_target_pairs={{0,24},{1,25},{2,26},{3,27},{4,28},{5,29},{6,30},{7,31},{8,0},{9,1... | collective-permute-start | bytes 2654216 | tf_op jit(solution)/shard_map/ppermute | solution.py:501
  439.5 29.2 %collective-permute-start.21 = (bf16[48,2304]{1,0:T(8,128)(2,1)}, bf16[48,2304]{1,0:T(8,128)(2,1)}, u32[]{:S(2)}, u32[]{:S(2)}) collective-permute-start(bf16[48,2304]{1,0:T(8,128)(2,1)} %get-tuple-element.262), channel_id=1, source_target_pairs={{0,4},{1,5},{2,6},{3,7},{4,0},{5,1},{6,2},{7,3},{8,12},{9,13},{10,... | collective-permute-start | bytes 663560 | tf_op jit(solution)/shard_map/ppermute | solution.py:501
  444.9 30.7 %collective-permute-start.24 = (bf16[48,2432]{1,0:T(8,128)(2,1)}, bf16[48,2432]{1,0:T(8,128)(2,1)S(1)}, u32[]{:S(2)}, u32[]{:S(2)}) collective-permute-start(bf16[48,2432]{1,0:T(8,128)(2,1)} %get-tuple-element.269), channel_id=1, source_target_pairs={{0,8},{1,9},{2,10},{3,11},{4,12},{5,13},{6,14},{7,15},{8,16},{9,17... | collective-permute-start | bytes 700424 | tf_op jit(solution)/shard_map/ppermute | solution.py:501
  447.4 30.7 %collective-permute-start.25 = (bf16[48,2432]{1,0:T(8,128)(2,1)}, bf16[48,2432]{1,0:T(8,128)(2,1)S(1)}, u32[]{:S(2)}, u32[]{:S(2)}) collective-permute-start(bf16[48,2432]{1,0:T(8,128)(2,1)} %get-tuple-element.270), channel_id=1, source_target_pairs={{0,16},{1,17},{2,18},{3,19},{4,20},{5,21},{6,22},{7,23},{8,24},{9,... | collective-permute-start | bytes 700424 | tf_op jit(solution)/shard_map/ppermute | solution.py:501
  457.7 17.3 %collective-permute-start.22 = (bf16[48,2304]{1,0:T(8,128)(2,1)}, bf16[48,2304]{1,0:T(8,128)(2,1)}, u32[]{:S(2)}, u32[]{:S(2)}) collective-permute-start(bf16[48,2304]{1,0:T(8,128)(2,1)} %get-tuple-element.263), channel_id=1, source_target_pairs={{0,6},{1,7},{2,0},{3,1},{4,2},{5,3},{6,4},{7,5},{8,14},{9,15},{10,... | collective-permute-start | bytes 663560 | tf_op jit(solution)/shard_map/ppermute | solution.py:501
  463.5 15.1 %collective-permute-start.26 = (bf16[48,2432]{1,0:T(8,128)(2,1)}, bf16[48,2432]{1,0:T(8,128)(2,1)S(1)}, u32[]{:S(2)}, u32[]{:S(2)}) collective-permute-start(bf16[48,2432]{1,0:T(8,128)(2,1)} %get-tuple-element.271), channel_id=1, source_target_pairs={{0,24},{1,25},{2,26},{3,27},{4,28},{5,29},{6,30},{7,31},{8,0},{9,1... | collective-permute-start | bytes 700424 | tf_op jit(solution)/shard_map/ppermute | solution.py:501
  493.2 81.0 %collective-permute-start.34 = (bf16[24,4736]{1,0:T(8,128)(2,1)S(1)}, bf16[24,4736]{1,0:T(8,128)(2,1)S(1)}, u32[]{:S(2)}, u32[]{:S(2)}) collective-permute-start(bf16[24,4736]{1,0:T(8,128)(2,1)S(1)} %get-tuple-element.311), channel_id=1, source_target_pairs={{0,33},{1,32},{2,35},{3,34},{4,37},{5,36},{6,39},{7,38},{8,41},{9,... | collective-permute-start | bytes 681992 | tf_op jit(solution)/shard_map/ppermute | solution.py:724
  499.4 74.8 %collective-permute-start.33 = (bf16[24,4736]{1,0:T(8,128)(2,1)S(1)}, bf16[24,4736]{1,0:T(8,128)(2,1)S(1)}, u32[]{:S(2)}, u32[]{:S(2)}) collective-permute-start(bf16[24,4736]{1,0:T(8,128)(2,1)S(1)} %get-tuple-element.310), channel_id=1, source_target_pairs={{0,1},{1,0},{2,3},{3,2},{4,5},{5,4},{6,7},{7,6},{8,9},{9,8},{10,11... | collective-permute-start | bytes 681992 | tf_op jit(solution)/shard_map/ppermute | solution.py:501
  499.5 74.8 %collective-permute-start.35 = (bf16[24,4736]{1,0:T(8,128)(2,1)S(1)}, bf16[24,4736]{1,0:T(8,128)(2,1)S(1)}, u32[]{:S(2)}, u32[]{:S(2)}) collective-permute-start(bf16[24,4736]{1,0:T(8,128)(2,1)S(1)} %select_convert_fusion), channel_id=1, source_target_pairs={{0,32},{32,0},{64,96},{96,64},{1,33},{33,1},{65,97},{97,65},{2,34}... | collective-permute-start | bytes 681992 | tf_op jit(solution)/shard_map/ppermute | solution.py:505
  (41 other events, 631.2 us)
Sparse Core Ops, SparseCore 0:
  30.0 105.4 all-gather.1

commit v5 on v4

--- a/solution.py
+++ b/solution.py
@@ -321,89 +321,85 @@
     return jnp.concatenate(rows, axis=0).T
 
 
-def weight_grad_kernel(d, ff, part, idx, place, mine, theirs, kept, got, *refs):
-    outs_hbm, (big_v, a_v, b_v, out_v, ins, outs) = refs[:-6], refs[-6:]
+def weight_grad_kernel(d, ff, idx, place, mine, theirs, kept, got, *refs):
+    firsts, seconds, (big_v, a_v, b_v, c_v, p_v, q_v, ins, outs) = refs[:4], refs[4:8], refs[8:]
     rows = kept.shape[0]
     tokens = 2 * rows
-    quarter, half, blocks = WIDE // 4, ff // 2, ff // WIDE
+    quarter, half, third = WIDE // 4, ff // 2, ff // 3
+    blocks = third // WIDE
+    share = d // 16
     y, z, core = idx[0], idx[1], idx[2]
 
     def load(cin, at, width, to, to_at):
         return [cin.start(src.at[:, pl.ds(at, width)], to.at[i, :, pl.ds(to_at, width)]) for i, src in enumerate((kept, got))]
 
-    def put(rows_at, cols_at, value):
-        out_v[rows_at, cols_at] = value.astype(BF)
-
-    def send():
-        cout = Copies(outs)
-        share = d // 16
-        if part == 0:
-            return [cout.start(out_v.at[pl.ds(pl.multiple_of(lax.rem(y + s, 4) * 4 * share, 16), 4 * share)], outs_hbm[s])
-                    for s in (1, 2, 3, 0)]
+    def wait(copies):
+        for copy in copies:
+            copy.wait()
+
+    def both(ref, at=0, width=d):
+        return ref[:, :, at : at + width].reshape(tokens, width)
+
+    def send_first(cout):
+        return [cout.start(p_v.at[pl.ds(pl.multiple_of(lax.rem(y + s, 4) * 4 * share, 16), 4 * share)], firsts[s])
+                for s in (2, 1, 3, 0)]
+
+    def send_second(cout):
         return [
-            cout.start(out_v.at[pl.ds(pl.multiple_of((4 * i + lax.rem(z + s, 4)) * share, 16), share)], outs_hbm[s].at[i])
-            for s in (1, 2, 3, 0) for i in range(4)
+            cout.start(q_v.at[pl.ds(pl.multiple_of((4 * i + lax.rem(z + s, 4)) * share, 16), share)], seconds[s].at[i])
+            for s in (2, 1, 3, 0) for i in range(4)
         ]
-
-    everything = slice(0, d)
 
     @pl.when(core == 0)
     def _():
-        cin = Copies(ins)
+        cin, cout = Copies(ins), Copies(outs)
         grads = load(cin, ff, d, a_v, 0)
-        third = blocks // 3
-        loads = [[c for b in range(third * k, third * k + third) for c in load(cin, WIDE * b + LANES * part, LANES, big_v, LANES * b)]
-                 for k in range(3)]
-        if part == 0:
-            last = load(cin, ff + 3 * d, d, b_v, 0)
-        else:
-            last = load(cin, ff + 2 * d, d, b_v, 0) + load(cin, ff + d, d, big_v, LANES * blocks)
-        for copy in grads:
-            copy.wait()
-        gb = a_v[...].reshape(tokens, d)
+        loads = [load(cin, third * k, third, big_v, third * k) for k in range(3)]
+        attended = load(cin, ff + 3 * d, d, b_v, 0)
+        hidden, values = load(cin, ff + 2 * d, d, c_v, 0), load(cin, ff + d, d, c_v, d)
+        wait(grads)
+        gb = both(a_v)
         for k in range(3):
-            for copy in loads[k]:
-                copy.wait()
-            left = big_v[:, :, LANES * third * k : LANES * third * (k + 1)].reshape(tokens, LANES * third)
-            found = lax.dot_general(left, gb, TN, preferred_element_type=F32)
-            for b in range(third):
-                for j in range(2):
-                    at = quarter * (third * k + b)
-                    put(slice(at, at + quarter), slice(d * j, d * j + d),
-                        found[LANES * b + quarter * j : LANES * b + quarter * (j + 1)])
-        for copy in last:
-            copy.wait()
-        if part == 0:
-            put(everything, slice(2 * d, 3 * d), lax.dot_general(b_v[...].reshape(tokens, d), gb, TN, preferred_element_type=F32))
-        else:
-            values = big_v[:, :, LANES * blocks :].reshape(tokens, d)
-            put(everything, slice(2 * d, 3 * d), lax.dot_general(
-                b_v[...].reshape(tokens, d), values, TN, preferred_element_type=F32))
-            out_v[:, 3 * d :] = split_small(small_table(d, ff, place, mine, theirs))
-        for copy in send():
-            copy.wait()
+            wait(loads[k])
+            found = lax.dot_general(both(big_v, third * k, third), gb, TN, preferred_element_type=F32).astype(BF)
+            for b in range(blocks):
+                at = quarter * (blocks * k + b)
+                for j in range(4):
+                    to = p_v if j < 2 else q_v
+                    to[at : at + quarter, d * (j % 2) : d * (j % 2) + d] = found[WIDE * b + quarter * j : WIDE * b + quarter * (j + 1)]
+        wait(attended)
+        p_v[:, 2 * d :] = lax.dot_general(both(b_v), gb, TN, preferred_element_type=F32).astype(BF)
+        pending = send_first(cout)
+        wait(hidden + values)
+        q_v[:, 2 * d : 3 * d] = lax.dot_general(both(c_v), both(c_v, d), TN, preferred_element_type=F32).astype(BF)
+        q_v[:, 3 * d :] = split_small(small_table(d, ff, place, mine, theirs))
+        wait(pending + send_second(cout))
 
     @pl.when(core == 1)
     def _():
-        cin = Copies(ins)
+        cin, cout = Copies(ins), Copies(outs)
         hidden = load(cin, ff + 2 * d, d, a_v, 0)
-        step = half // 3
-        loads = [load(cin, half * part + step * k, step, big_v, step * k) for k in range(3)]
-        loads.append(load(cin, ff + d * part, d, b_v, 0))
-        for copy in hidden:
-            copy.wait()
-        turned = a_v[...].reshape(tokens, d).T
-        for k in range(3):
-            for copy in loads[k]:
-                copy.wait()
-            put(everything, slice(step * k, step * k + step), mm(turned, big_v[:, :, step * k : step * k + step].reshape(tokens, step)))
-        for copy in loads[3]:
-            copy.wait()
-        put(everything, slice(half, half + d), mm(turned, b_v[...].reshape(tokens, d)))
-        if part == 1:
-            out_v[:, 3 * d :] = jnp.zeros((d, LANES), BF)
-        for copy in send():
-            copy.wait()
+        loads = [load(cin, third * k, third, big_v, third * k) for k in range(2)]
+        queries = load(cin, ff, d, b_v, 0)
+        loads.append(load(cin, 2 * third, third, big_v, 2 * third))
+        keys = load(cin, ff + d, d, c_v, 0)
+        wait(hidden)
+        turned = both(a_v).T
+        wait(loads[0])
+        p_v[:, :third] = mm(turned, both(big_v, 0, third)).astype(BF)
+        wait(loads[1])
+        found = mm(turned, both(big_v, third, third)).astype(BF)
+        p_v[:, third:half] = found[:, : half - third]
+        q_v[:, : 2 * third - half] = found[:, half - third :]
+        wait(queries)
+        p_v[:, half:] = mm(turned, both(b_v)).astype(BF)
+        pending = send_first(cout)
+        wait(loads[2])
+        q_v[:, 2 * third - half : half] = mm(turned, both(big_v, 2 * third, third)).astype(BF)
+        wait(keys)
+        q_v[:, half : half + d] = mm(turned, both(c_v)).astype(BF)
+        q_v[:, half + d :] = jnp.zeros((d, LANES), BF)
+        wait(pending + send_second(cout))
 
 
 def added(parts):
@@ -448,6 +444,88 @@
     copies = Copies(sems)
     for copy in [copies.start(y_got, y_out.at[1 - idx[3]]), copies.start(g_got, g_out.at[1 - idx[3]])]:
         copy.wait()
+
+
+def picked(rows, columns, wanted):
+    row = lax.broadcasted_iota(jnp.int32, (rows, columns), 0)
+    column = lax.broadcasted_iota(jnp.int32, (rows, columns), 1)
+    return row, column, jnp.where(column == wanted(row), 1.0, 0.0)
+
+
+def prepare_kernel(d, ff, p_in, p_attn, p_down, n_gain, o_bias, u_bias, q_gain, k_gain, shuffle, out):
+    share = p_in.shape[0]
+    heads_part = p_in.shape[1] - ff
+    for at in range(0, ff, WIDE):
+        out[:, at : at + WIDE] = mm(p_in[:, heads_part + at : heads_part + at + WIDE], shuffle[...]).astype(BF)
+    out[:, ff : ff + heads_part] = p_in[:, :heads_part]
+    at = ff + heads_part
+    out[:, at : at + d] = p_attn[...]
+    down = p_down[...]
+    for j in range(4):
+        take = picked(share, down.shape[0], lambda row: 4 * row + j)[2].astype(BF)
+        out[:, at + d * (j + 1) : at + d * (j + 2)] = mm(take, down).astype(BF)
+
+    def column_of(ref, wanted, where):
+        values = ref[...].astype(F32)
+        take = picked(share, values.shape[1], wanted)[2]
+        lane = lax.broadcasted_iota(jnp.int32, (share, LANES), 1)
+        return jnp.where(lane == where, jnp.sum(take * values, axis=1, keepdims=True), 0.0)
+
+    table = column_of(n_gain, lambda row: row, 0) + column_of(o_bias, lambda row: row, 1)
+    for j in range(4):
+        table = table + column_of(u_bias, lambda row: 4 * row + j, 2 + j)
+    table = table + column_of(q_gain, lambda row: row, 6) + column_of(k_gain, lambda row: row, 7)
+    out[:, at + 5 * d :] = table.astype(BF)
+
+
+def smalls_kernel(d, ff, base, stride, g, place, ngain, gains, ubias, obias, t_v, sems):
+    copies = Copies(sems)
+    loads = [copies.start(g.at[:, pl.ds(base + stride * layer, LANES)], t_v.at[layer]) for layer in range(2)]
+    quarter = WIDE // 4
+    for layer in range(2):
+        loads[layer].wait()
+        table = t_v[layer].astype(F32).T
+        ngain[layer] = table[0:1]
+        obias[layer] = table[1:2]
+        pieces = [table[2 + j : 3 + j, quarter * b : quarter * (b + 1)] for b in range(ff // WIDE) for j in range(4)]
+        ubias[layer] = jnp.concatenate(pieces, axis=1)
+        both = mm(table[0:8].astype(BF), place[...])
+        gains[layer, 0] = both[6:7]
+        gains[layer, 1] = both[7:8]
+
+
+def finish_kernel(d, ff, idx, own, a_in, b_in, c_in, shuffle, g_in, g_attn, g_down, g_ng, g_q, g_k, g_ub, g_ob):
+    core = idx[2]
+    share = own.shape[0]
+    mine = own[...] + a_in[...].astype(F32)
+    theirs = b_in[...].astype(F32) + c_in[...].astype(F32)
+    half0 = jnp.where(core == 0, mine, theirs)
+    half1 = jnp.where(core == 0, theirs, mine)
+    g_in[:, :d] = half1[:, 2 * d : 3 * d]
+    g_in[:, d : 2 * d] = half1[:, 5 * d : 6 * d]
+    g_in[:, 2 * d : 3 * d] = half0[:, 5 * d : 6 * d]
+    for at in range(0, ff, WIDE):
+        start = at if at < 2 * d else at + d
+        g_in[:, 3 * d + at : 3 * d + at + WIDE] = lax.dot_general(
+            half1[:, start : start + WIDE], shuffle[...], NT, precision=lax.Precision.HIGHEST, preferred_element_type=F32)
+    g_attn[...] = half0[:, 2 * d : 3 * d]
+    stacked = jnp.concatenate([half0[:, at : at + d] for at in (0, d, 3 * d, 4 * d)], axis=0)
+    row, column, _ = picked(4 * share, 4 * share, lambda row: row)
+    turn = jnp.where(column == lax.rem(row, 4) * share + row // 4, 1.0, 0.0)
+    g_down[...] = lax.dot_general(turn, stacked, NN, precision=lax.Precision.HIGHEST, preferred_element_type=F32)
+    small = joined_small(half0[:, 6 * d :])
+    turned = jnp.concatenate([small, jnp.zeros((LANES - share, LANES), F32)], axis=0).T
+    g_ng[...] = turned[0:1, :share]
+    g_ob[...] = turned[1:2, :share]
+    g_q[...] = turned[6:7, : g_q.shape[1]]
+    g_k[...] = turned[7:8, : g_k.shape[1]]
+    total = jnp.zeros((8, 4 * share), F32)
+    for j in range(4):
+        row, column, _ = picked(LANES, 4 * share, lambda row: row)
+        spread_out = jnp.where(column == 4 * row + j, 1.0, 0.0)
+        total = total + jnp.where(lax.broadcasted_iota(jnp.int32, (8, 4 * share), 0) == 2 + j, 1.0, 0.0) * lax.dot_general(
+            turned[0:8], spread_out, NN, precision=lax.Precision.HIGHEST, preferred_element_type=F32)
+    g_ub[...] = jnp.sum(total, axis=0, keepdims=True)
 
 
 ANY = pl.BlockSpec(memory_space=pl.ANY)
@@ -477,6 +555,14 @@
         cost_estimate=pl.CostEstimate(flops=flops, bytes_accessed=1 << 10, transcendentals=0),
     )(idx, *[a for a, _ in ins], *stashes)
     return outs[0], list(outs[1:])
+
+
+def plain(kernel, arrays, specs, out_shapes, out_specs, scratch):
+    return pl.pallas_call(
+        kernel, grid=(1,), in_specs=specs, out_specs=out_specs, scratch_shapes=scratch, out_shape=out_shapes,
+        compiler_params=pltpu.CompilerParams(dimension_semantics=("arbitrary",), vmem_limit_bytes=VMEM_LIMIT),
+        cost_estimate=pl.CostEstimate(flops=1 << 10, bytes_accessed=1 << 10, transcendentals=0),
+    )(*arrays)
 
 
 def simple(kernel, idx, arrays, specs, out_shapes, out_specs, scratch, flops=1 << 10):
@@ -531,45 +617,28 @@
     source = (place % (WIDE // fshare)) * fshare + place // (WIDE // fshare)
     shuffle = (place[:, None] == source[None, :]).astype(BF)
 
-    def shuffled(x, back=False):
-        flat = x.reshape(-1, WIDE)
-        out = lax.dot_general(
-            flat, shuffle.astype(x.dtype), NT if back else NN, precision=lax.Precision.HIGHEST, preferred_element_type=F32
-        )
-        return out.reshape(x.shape)
-
-    small = jnp.concatenate(
-        [
-            norm_gain[0][:, None],
-            out_bias[0][:, None],
-            up_bias[0].reshape(dshare, fshare),
-            jnp.pad(query_gain[0], (0, dshare - hshare))[:, None],
-            jnp.pad(key_gain[0], (0, dshare - hshare))[:, None],
-            jnp.zeros((dshare, LANES - 4 - fshare), BF),
-        ],
-        axis=1,
-    )
+    def full(a):
+        return pl.BlockSpec(a.shape, lambda i: (0,) * a.ndim)
+
+    shares = [proj_in[0], proj_attn[0], proj_down[0], norm_gain, out_bias, up_bias, query_gain, key_gain, shuffle]
     heads_part = joined - ff
-    local = jnp.concatenate(
-        [shuffled(proj_in[0][:, heads_part:]).astype(BF), proj_in[0][:, :heads_part], proj_attn[0],
-         proj_down[0].reshape(dshare, fshare * d), small],
-        axis=1,
-    )
+    local = jax.ShapeDtypeStruct((dshare, stride), BF)
+    local = plain(partial(prepare_kernel, d, ff), shares, [full(a) for a in shares], local, full(local), [])
     other = paired(local)
     both = jnp.where(odd == 0, jnp.concatenate([local, other], axis=1), jnp.concatenate([other, local], axis=1))
     g = lax.all_gather(both, "dp", axis=0, tiled=True)
     g3 = g.reshape(ff // WIDE, WIDE // fshare, g.shape[1])
-    smalls = []
-    for layer in range(2):
-        at = stride * layer + wide
-        tail = g[:, at : at + LANES].astype(F32)
-        qk_gain = tail[:, 2 + fshare : 4 + fshare].reshape(ranks, dshare, 2)[:, :hshare].reshape(head, 2).T
-        smalls.append((
-            tail[:, 0].reshape(1, d),
-            jnp.tile(qk_gain, (1, heads)).reshape(2, 1, d),
-            shuffled(tail[:, 2 : 2 + fshare].reshape(1, ff).astype(BF)),
-            tail[:, 1].reshape(1, d),
-        ))
+    element = jnp.arange(d, dtype=jnp.int32) % head
+    spread_gain = (jnp.arange(d, dtype=jnp.int32)[:, None] == (element // hshare * dshare + element % hshare)[None, :]).astype(BF)
+    tables = [jax.ShapeDtypeStruct(s, F32) for s in ((2, 1, d), (2, 2, 1, d), (2, 1, ff), (2, 1, d))]
+    ngain, gains, ubias, obias = plain(
+        partial(smalls_kernel, d, ff, wide, stride), [g, spread_gain], [ANY, full(spread_gain)], tables,
+        [full(a) for a in tables], [pltpu.VMEM((2, d, LANES), BF), pltpu.SemaphoreType.DMA((2,))],
+    )
+
+    def of_layer(a, layer):
+        return (a, pl.BlockSpec((None,) + a.shape[1:], lambda i, idx: (layer,) + (0,) * (a.ndim - 1)))
+
     column = jnp.arange(WIDE, dtype=jnp.int32) // head
     spread = jnp.where(column[:, None] == column[None, :], 1.0 / head, 0.0).astype(BF)
 
@@ -603,12 +672,11 @@
     here_x = toks
     for t in range(4):
         layer = t % 2
-        ngain, gains, ubias, obias = smalls[layer]
         ybf, done = call(
             partial(forward_kernel, d, ff, chunks, stride * layer, t == 0),
             index_of(layer, t // 2),
             [(here_x, ANY), (g, ANY), (g3, ANY), (ids_col, pick((rows, 1))), (ids_row, pick((1, rows))),
-             (ngain, whole((1, d))), (gains, whole((2, 1, d))), (ubias, whole((1, ff))), (obias, whole((1, d))),
+             of_layer(ngain, layer), of_layer(gains, layer), of_layer(ubias, layer), of_layer(obias, layer),
              (spread, whole((WIDE, WIDE)))],
             ((rows, d), BF),
             kept[layer][:9] + operands[layer] + results,
@@ -638,19 +706,16 @@
         if ahead is not None:
             sent, ahead = lax.optimization_barrier((sent, ahead))
         got, table_got = along(sent, 1, 2, 1), along(tables[layer], 1, 2, 1)
-        made = []
-        for part in range(2):
-            w = widths[part]
-            shape = (side * share, w) if part == 0 else (side, share, w)
-            made.append(simple(
-                partial(weight_grad_kernel, d, ff, part), here,
-                [place, tables[layer], table_got, mine, got],
-                [whole((LANES, d)), whole(table_got.shape), whole(table_got.shape), ANY, ANY],
-                [jax.ShapeDtypeStruct(shape, BF)] * side, [ANY] * side,
-                [V((2, rows, ff // 2 + d), BF), V((2, rows, d), BF), V((2, rows, d), BF), V((d, w), BF),
-                 pltpu.SemaphoreType.DMA((32,)), pltpu.SemaphoreType.DMA((16,))],
-                1 << 10,
-            ))
+        shapes = [(side * share, widths[0])] * side + [(side, share, widths[1])] * side
+        outs = simple(
+            partial(weight_grad_kernel, d, ff), here,
+            [place, tables[layer], table_got, mine, got],
+            [whole((LANES, d)), whole(table_got.shape), whole(table_got.shape), ANY, ANY],
+            [jax.ShapeDtypeStruct(s, BF) for s in shapes], [ANY] * (2 * side),
+            [V((2, rows, ff), BF), V((2, rows, d), BF), V((2, rows, d), BF), V((2, rows, 2 * d), BF),
+             V((d, widths[0]), BF), V((d, widths[1]), BF), pltpu.SemaphoreType.DMA((32,)), pltpu.SemaphoreType.DMA((32,))],
+        )
+        made = [outs[:side], outs[side:]]
         return made, ahead
 
     def first_leg(made):
@@ -674,11 +739,10 @@
     here_g = seeds
     for t in range(4):
         layer = 1 - t % 2
-        ngain, gains, ubias, obias = smalls[layer]
         gbf, done = call(
             partial(backward_kernel, d, ff, chunks, stride * layer, t == 0),
             index_of(layer, 1 - t // 2),
-            [(here_g, ANY), (g, ANY), (g3, ANY), (ids_col, pick((rows, 1))), (ngain, whole((1, d))), (gains, whole((2, 1, d))),
+            [(here_g, ANY), (g, ANY), (g3, ANY), (ids_col, pick((rows, 1))), of_layer(ngain, layer), of_layer(gains, layer),
              (spread, whole((WIDE, WIDE)))] + [(a, ANY) for a in kept[layer]],
             ((rows, d), BF),
             operands[layer] + [tables[layer]] + results,
@@ -709,7 +773,7 @@
     y_out, gr_out = pl.pallas_call(
         place_kernel,
         grid_spec=pltpu.PrefetchScalarGridSpec(
-            num_scalar_prefetch=1, grid=(1,), in_specs=[ANY] * 4, out_specs=[ANY] * 2,
+            num_scalar_prefetch=1, grid=(1,), in_specs=[ANY, whole((rows, d)), ANY, whole((rows, d))], out_specs=[ANY] * 2,
             scratch_shapes=[pltpu.SemaphoreType.DMA((2,))],
         ),
         out_shape=[jax.ShapeDtypeStruct(y_out.shape, F32)] * 2,
@@ -720,25 +784,16 @@
     away = [jnp.where(odd == 1, a, b).astype(BF) for a, b in zip(*sums)]
     sections = lax.axis_size("section")
     cross = [(s * ranks + i, (s ^ 1) * ranks + (i ^ 1)) for s in range(sections) for i in range(ranks)]
-    mine = home[0] + paired(away[0]).astype(F32)
-    other = along(home[1].astype(BF), 1, 2, 1).astype(F32) + lax.ppermute(away[1], ("section", "dp"), cross).astype(F32)
-    half0, half1 = jnp.where(core == 0, mine, other), jnp.where(core == 0, other, mine)
-    ups = shuffled(jnp.concatenate([half1[:, : 2 * d], half1[:, 3 * d : 5 * d]], axis=1), back=True)
-    g_in = jnp.concatenate([half1[:, 2 * d : 3 * d], half1[:, 5 * d : 6 * d], half0[:, 5 * d : 6 * d], ups], axis=1)
-    g_down = jnp.concatenate([half0[:, : 2 * d], half0[:, 3 * d : 5 * d]], axis=1)
-    last = half0[:, 6 * d : 6 * d + 8] + half0[:, 6 * d + 8 : 6 * d + 16]
-    return (
-        y_out.reshape(1, slots * rows, d),
-        gr_out.reshape(1, slots * rows, d),
-        g_in[None],
-        half0[None, :, 2 * d : 3 * d],
-        g_down.reshape(1, dshare * fshare, d),
-        last[None, :, 0],
-        last[None, :hshare, 6],
-        last[None, :hshare, 7],
-        last[:, 2:6].reshape(1, dshare * fshare),
-        last[None, :, 1],
+    arrays = [home[0], paired(away[0]), along(home[1].astype(BF), 1, 2, 1), lax.ppermute(away[1], ("section", "dp"), cross),
+              shuffle.astype(F32)]
+    shapes = [(dshare, joined), (dshare, d), (dshare * fshare, d), (1, dshare), (1, hshare), (1, hshare), (1, dshare * fshare),
+              (1, dshare)]
+    g_in, g_attn, g_down, g_ng, g_q, g_k, g_ub, g_ob = simple(
+        partial(finish_kernel, d, ff), here, arrays, [whole(a.shape) for a in arrays],
+        [jax.ShapeDtypeStruct(s, F32) for s in shapes], [whole(s) for s in shapes], [],
     )
+    return (y_out.reshape(1, slots * rows, d), gr_out.reshape(1, slots * rows, d), g_in[None], g_attn[None], g_down[None],
+            g_ng, g_q, g_k, g_ub, g_ob)
 
 
 def solution(mesh):

time: 591 us -> 505 us (0.85)
  Pallas kernels: 256 us -> 186 us
  local copies, waits for them, and re-layouts: 24.7 us -> 6.14 us
  waiting for transfers between devices: 231 us -> 238 us
    pallas_call x1, Pallas kernels: 73.4 us -> 3.84 us  [body(): pl.pallas_call(place_kernel, grid_spec=pltpu.PrefetchScalarGridSpec(num_s...]
    pallas_call x10 -> x9, Pallas kernels: 64 us -> 56.8 us  [simple(): pl.pallas_call(kernel, grid_spec=pltpu.PrefetchScalarGridSpec(num_scalar_...]
    another operation x12 -> x0, local copies, waits for them, and re-layouts: 6.34 us -> none  [the longest x4 1.37 us: body(): jnp.tile(qk_gain, (1, heads)).reshape(2, 1, d)]
    ppermute x1, waiting for transfers between devices: 0.01 us -> 6.31 us  [body(): lax.ppermute(away[1], ('section', 'dp'), cross)]
    ppermute x1, starting transfers between devices: 6.2 us -> 0.13 us  [body(): lax.ppermute(away[1], ('section', 'dp'), cross)]
    pallas_call x0 -> x2, Pallas kernels: none -> 5.99 us  [plain(): pl.pallas_call(kernel, grid=(1,), in_specs=specs, out_specs=out_specs, sc...]
  transfers between devices with their start and end apart: 37 -> 37, of which waited for: 15 -> 16; matrix products, arithmetic and copies ran while one was open for 1% -> 2% of each run, Pallas kernels for 28% -> 17%
where the time goes in v5:
time: 505 us; the launch traced here: 502 us
  waiting for transfers between devices  238 us (47%)
  Pallas kernels  186 us (37%)
  starting transfers between devices  44.1 us (9%)
  between operations  14.9 us (3%)
  other arithmetic  12.9 us (3%)
  local copies, waits for them, and re-layouts  6.14 us (1%)
    pallas_call x8, Pallas kernels, call(): pl.pallas_call(kernel, grid_spec=pltpu.PrefetchScalarGridSpec(num_scalar_...  119 us
    all_gather x1, waiting for transfers between devices, body(): g = lax.all_gather(both, 'dp', axis=0, tiled=True)  99 us
    ppermute x1, waiting for transfers between devices, body(): here_g = lax.ppermute(gbf, 'section', [(3, 0), (2, 1)]) if t == 1 else gbf  59.7 us
    pallas_call x9, Pallas kernels, simple(): pl.pallas_call(kernel, grid_spec=pltpu.PrefetchScalarGridSpec(num_scalar_...  56.8 us
    ppermute x29, waiting for transfers between devices, along(): return lax.ppermute(x, 'dp', [(i, to(i)) for i in range(devices)])  51 us
    ppermute x29, starting transfers between devices, along(): return lax.ppermute(x, 'dp', [(i, to(i)) for i in range(devices)])  35.9 us
    ppermute x1, waiting for transfers between devices, body(): here_x = lax.ppermute(ybf, 'section', [(0, 3), (1, 2)]) if t == 1 else ybf  11.9 us
  transfers between devices with their start and end apart: 37, of which 16 were waited for; matrix products, arithmetic and copies ran while one was open for 2% of the time, Pallas kernels for 17%

profile of v5, /device:TPU:1, one launch (start us, length us, event | category | flops | bytes accessed | tf_op | source)
XLA Modules:
  0.0 501.6 jit_solution(15598703425502989783)
XLA Ops:
  12.5 9.7 %collective-permute-done = bf16[24,9344]{1,0:T(8,128)(2,1)S(1)} collective-permute-done((bf16[24,9344]{1,0:T(8,128)(2,1)}, bf16[24,9344]{1,0:T(8,128)(2,1)S(1)}, u32[]{:S(2)}, u32[]{:S(2)}) %collective-permute-start) | collective-permute-done | bytes 448544 | tf_op jit(solution)/shard_map/ppermute | solution.py:591
  31.1 99.0 %all-gather.2.cloned.1.call-done.g = bf16[768,18688]{1,0:T(8,128)(2,1)} async-done(((bf16[24,18688]{1,0:T(8,128)(2,1)}), bf16[768,18688]{1,0:T(8,128)(2,1)}) %all-gather.2.cloned.1.call-update) | async-done | bytes 28704784 | tf_op jit(solution)/shard_map/all_gather | solution.py:629
  133.7 18.4 %shard_map.201 = (bf16[384,768]{1,0:T(8,128)(2,1)}, bf16[384,768]{1,0:T(8,128)(2,1)}, bf16[384,768]{1,0:T(8,128)(2,1)}, bf16[384,768]{1,0:T(8,128)(2,1)}, bf16[3...) custom-call(s32[4]{0:T(128)} %get-tuple-element.316.idx, ...), custom_call_target="tpu_custom_call", output_to_operand_aliasing={{1}: (11, {}), {2}: (12, {}), {3}: (13, {}), {4}: (14, {}),... | custom-call | flops 1024 | bytes 1024 | tf_op jit(solution)/shard_map/pallas_call | solution.py:543
  152.0 18.6 %shard_map.213 = (bf16[384,768]{1,0:T(8,128)(2,1)}, bf16[384,768]{1,0:T(8,128)(2,1)}, bf16[384,768]{1,0:T(8,128)(2,1)}, bf16[384,768]{1,0:T(8,128)(2,1)}, bf16[3...) custom-call(s32[4]{0:T(128)} %pad_add_fusion.1.idx, ...), custom_call_target="tpu_custom_call", output_to_operand_aliasing={{1}: (11, {}), {2}: (12, {}), {3}: (13, {}), {4}: (14, {}),... | custom-call | flops 1024 | bytes 1024 | tf_op jit(solution)/shard_map/pallas_call | solution.py:543
  173.2 11.9 %collective-permute-done.1.x_in = bf16[384,768]{1,0:T(8,128)(2,1)S(1)} collective-permute-done((bf16[384,768]{1,0:T(8,128)(2,1)}, bf16[384,768]{1,0:T(8,128)(2,1)S(1)}, u32[]{:S(2)}, u32[]{:S(2)}) %collective-permute-start.1) | collective-permute-done | bytes 589856 | tf_op jit(solution)/shard_map/ppermute | solution.py:690
  189.4 7.8 %shard_map.215 = (bf16[384,768]{1,0:T(8,128)(2,1)}, bf16[384,768]{1,0:T(8,128)(2,1)}, bf16[384,768]{1,0:T(8,128)(2,1)}, bf16[384,768]{1,0:T(8,128)(2,1)}, bf16[3...) custom-call(s32[4]{0:T(128)} %pad_add_fusion.2.idx, ...), custom_call_target="tpu_custom_call", output_to_operand_aliasing={{1}: (11, {}), {2}: (12, {}), {3}: (13, {}), {4}: (14, {}),... | custom-call | flops 1024 | bytes 1024 | tf_op jit(solution)/shard_map/pallas_call | solution.py:543
  198.4 16.8 %shard_map.219 = (bf16[384,768]{1,0:T(8,128)(2,1)}, bf16[384,6144]{1,0:T(8,128)(2,1)}, bf16[384,6144]{1,0:T(8,128)(2,1)}, f32[1,6144]{1,0:T(1,128)}, f32[2,384,768]{2,1,0:T(8,128)}, /*index=5*/f32[384,768]{1,0:T(8,128)}) custom-call(s32[4]{0:T(128)} %pad_add_fusion.2.idx, ...), custom_call_target="tpu_custom_call", output_to_operand_aliasing={{1}: (17, {}), {2}: (18, {}), {3}: (19, {}), {4}: (20, {}),... | custom-call | flops 1024 | bytes 1024 | tf_op jit(solution)/shard_map/pallas_call | solution.py:543
  215.3 9.4 %shard_map.221 = (bf16[384,768]{1,0:T(8,128)(2,1)}, bf16[384,6144]{1,0:T(8,128)(2,1)}, bf16[384,6144]{1,0:T(8,128)(2,1)}, f32[1,6144]{1,0:T(1,128)}, f32[2,384,768]{2,1,0:T(8,128)}, /*index=5*/f32[384,768]{1,0:T(8,128)}) custom-call(s32[4]{0:T(128)} %get-tuple-element.318.idx, ...), custom_call_target="tpu_custom_call", output_to_operand_aliasing={{1}: (17, {}), {2}: (18, {}), {3}: (19, {}), {4}: (20, {}),... | custom-call | flops 1024 | bytes 1024 | tf_op jit(solution)/shard_map/pallas_call | solution.py:543
  226.0 59.7 %collective-permute-done.2.g_in = bf16[384,768]{1,0:T(8,128)(2,1)S(1)} collective-permute-done((bf16[384,768]{1,0:T(8,128)(2,1)}, bf16[384,768]{1,0:T(8,128)(2,1)S(1)}, u32[]{:S(2)}, u32[]{:S(2)}) %collective-permute-start.2) | collective-permute-done | bytes 589856 | tf_op jit(solution)/shard_map/ppermute | solution.py:758
  286.5 22.2 %shard_map.222 = (bf16[384,768]{1,0:T(8,128)(2,1)}, bf16[384,6144]{1,0:T(8,128)(2,1)}, bf16[384,6144]{1,0:T(8,128)(2,1)}, f32[1,6144]{1,0:T(1,128)}, f32[2,384,768]{2,1,0:T(8,128)}, /*index=5*/f32[384,768]{1,0:T(8,128)}) custom-call(s32[4]{0:T(128)} %pad_add_fusion.1.idx, ...), custom_call_target="tpu_custom_call", output_to_operand_aliasing={{1}: (17, {}), {2}: (18, {}), {3}: (19, {}), {4}: (20, {}),... | custom-call | flops 1024 | bytes 1024 | tf_op jit(solution)/shard_map/pallas_call | solution.py:543
  312.0 6.2 %collective-permute-done.4.theirs = f32[1,6144]{1,0:T(1,128)S(1)} collective-permute-done((f32[1,6144]{1,0:T(1,128)}, f32[1,6144]{1,0:T(1,128)S(1)}, u32[]{:S(2)}, u32[]{:S(2)}) %collective-permute-start.4) | collective-permute-done | bytes 24608 | tf_op jit(solution)/shard_map/ppermute | solution.py:587
  318.8 12.7 %shard_map.223 = (bf16[192,2304]{1,0:T(8,128)(2,1)}, bf16[192,2304]{1,0:T(8,128)(2,1)}, bf16[192,2304]{1,0:T(8,128)(2,1)}, bf16[192,2304]{1,0:T(8,128)(2,1)}, bf...) custom-call(s32[4]{0:T(128)} %pad_add_fusion.idx, ...), custom_call_target="tpu_custom_call" | custom-call | flops 1024 | bytes 1024 | tf_op jit(solution)/shard_map/pallas_call | solution.py:569
  337.0 22.6 %shard_map.224 = (bf16[384,768]{1,0:T(8,128)(2,1)}, bf16[384,6144]{1,0:T(8,128)(2,1)}, bf16[384,6144]{1,0:T(8,128)(2,1)}, f32[1,6144]{1,0:T(1,128)}, f32[2,384,768]{2,1,0:T(8,128)}, /*index=5*/f32[384,768]{1,0:T(8,128)}) custom-call(s32[4]{0:T(128)} %get-tuple-element.316.idx, ...), custom_call_target="tpu_custom_call", output_to_operand_aliasing={{1}: (17, {}), {2}: (18, {}), {3}: (19, {}), {4}: (20, {}),... | custom-call | flops 1024 | bytes 1024 | tf_op jit(solution)/shard_map/pallas_call | solution.py:543
  365.8 4.7 collective-permute-done.6.theirs
  371.1 12.9 %shard_map.225 = (bf16[192,2304]{1,0:T(8,128)(2,1)}, bf16[192,2304]{1,0:T(8,128)(2,1)}, bf16[192,2304]{1,0:T(8,128)(2,1)}, bf16[192,2304]{1,0:T(8,128)(2,1)}, bf...) custom-call(s32[4]{0:T(128)} %pad_add_fusion.idx, ...), custom_call_target="tpu_custom_call" | custom-call | flops 1024 | bytes 1024 | tf_op jit(solution)/shard_map/pallas_call | solution.py:569
  385.0 4.4 shard_map.227
  391.0 5.0 collective-permute-done.20.refs_1_
  397.4 7.8 %collective-permute-done.12.refs_1_ = bf16[192,2304]{1,0:T(8,128)(2,1)} collective-permute-done((bf16[192,2304]{1,0:T(8,128)(2,1)}, bf16[192,2304]{1,0:T(8,128)(2,1)}, u32[]{:S(2)}, u32[]{:S(2)}) %collective-permute-start.12) | collective-permute-done | bytes 884768 | tf_op jit(solution)/shard_map/ppermute | solution.py:587
  405.3 18.4 %collective-permute-done.13.refs_2_ = bf16[192,2304]{1,0:T(8,128)(2,1)} collective-permute-done((bf16[192,2304]{1,0:T(8,128)(2,1)}, bf16[192,2304]{1,0:T(8,128)(2,1)}, u32[]{:S(2)}, u32[]{:S(2)}) %collective-permute-start.13) | collective-permute-done | bytes 884768 | tf_op jit(solution)/shard_map/ppermute | solution.py:587
  423.7 4.6 shard_map.228
  448.2 4.7 shard_map.231
  473.2 7.4 %collective-permute-start.34 = (bf16[24,4736]{1,0:T(8,128)(2,1)S(1)}, bf16[24,4736]{1,0:T(8,128)(2,1)S(1)}, u32[]{:S(2)}, u32[]{:S(2)}) collective-permute-start(bf16[24,4736]{1,0:T(8,128)(2,1)S(1)} %get-tuple-element.321), channel_id=1, source_target_pairs={{0,1},{1,0},{2,3},{3,2},{4,5},{5,4},{6,7},{7,6},{8,9},{9,8},{10,11... | collective-permute-start | bytes 681992 | tf_op jit(solution)/shard_map/ppermute | solution.py:587
  481.7 6.3 %collective-permute-done.35.c_in = bf16[24,4736]{1,0:T(8,128)(2,1)S(1)} collective-permute-done((bf16[24,4736]{1,0:T(8,128)(2,1)S(1)}, bf16[24,4736]{1,0:T(8,128)(2,1)S(1)}, u32[]{:S(2)}, u32[]{:S(2)}) %collective-permute-start.35) | collective-permute-done | bytes 227360 | tf_op jit(solution)/shard_map/ppermute | solution.py:787
  488.7 5.9 %shard_map.233 = (f32[24,5376]{1,0:T(8,128)}, f32[24,768]{1,0:T(8,128)}, f32[96,768]{1,0:T(8,128)}, f32[1,24]{1,0:T(1,128)}, f32[1,2]{1,0:T(1,128)}, /*index=5*/...) custom-call(s32[4]{0:T(128)} %pad_add_fusion.idx, f32[24,4736]{1,0:T(8,128)} %broadcast_select_fusion.own, ...), custom_call_target="tpu_custom_call" | custom-call | flops 1024 | bytes 1024 | tf_op jit(solution)/shard_map/pallas_call | solution.py:569
  (186 shorter events, 89.6 us)
Async XLA Ops:
  7.2 122.9 %all-gather.2.cloned.1.call-start = ((), (), s32[]{:S(2)}) async-start(), calls=%async_computation | async-start | bytes 29601792 | tf_op jit(solution)/shard_map/all_gather | solution.py:629
  170.6 14.4 %collective-permute-start.1 = (bf16[384,768]{1,0:T(8,128)(2,1)}, bf16[384,768]{1,0:T(8,128)(2,1)S(1)}, u32[]{:S(2)}, u32[]{:S(2)}) collective-permute-start(bf16[384,768]{1,0:T(8,128)(2,1)} %get-tuple-element.170), channel_id=1, source_target_pairs={{0,96},{32,64},{1,97},{33,65},{2,98},{34,66},{3,99},{35,67},{4,100... | collective-permute-start | bytes 1769480 | tf_op jit(solution)/shard_map/ppermute | solution.py:690
  197.2 88.5 %collective-permute-start.3 = (f32[384,768]{1,0:T(8,128)}, f32[384,768]{1,0:T(8,128)S(1)}, u32[]{:S(2)}, u32[]{:S(2)}) collective-permute-start(f32[384,768]{1,0:T(8,128)} %get-tuple-element.225), channel_id=1, source_target_pairs={{0,32},{32,0},{64,96},{96,64},{1,33},{33,1},{65,97},{97,65},{2,34}... | collective-permute-start | bytes 3538952 | tf_op jit(solution)/shard_map/ppermute | solution.py:591
  224.7 61.0 %collective-permute-start.2 = (bf16[384,768]{1,0:T(8,128)(2,1)}, bf16[384,768]{1,0:T(8,128)(2,1)S(1)}, u32[]{:S(2)}, u32[]{:S(2)}) collective-permute-start(bf16[384,768]{1,0:T(8,128)(2,1)} %get-tuple-element.224), channel_id=1, source_target_pairs={{96,0},{64,32},{97,1},{65,33},{98,2},{66,34},{99,3},{67,35},{100,4... | collective-permute-start | bytes 1769480 | tf_op jit(solution)/shard_map/ppermute | solution.py:758
  331.5 28.1 %collective-permute-start.9 = (bf16[4,48,2432]{2,1,0:T(8,128)(2,1)}, bf16[4,48,2432]{2,1,0:T(8,128)(2,1)S(1)}, u32[]{:S(2)}, u32[]{:S(2)}) collective-permute-start(bf16[4,48,2432]{2,1,0:T(8,128)(2,1)} %get-tuple-element.257), channel_id=1, source_target_pairs={{0,2},{1,3},{2,4},{3,5},{4,6},{5,7},{6,0},{7,1},{8,10},{9,11},{10,... | collective-permute-start | bytes 2801672 | tf_op jit(solution)/shard_map/ppermute | solution.py:587
  332.1 27.6 %collective-permute-start.10 = (bf16[4,48,2432]{2,1,0:T(8,128)(2,1)}, bf16[4,48,2432]{2,1,0:T(8,128)(2,1)S(1)}, u32[]{:S(2)}, u32[]{:S(2)}) collective-permute-start(bf16[4,48,2432]{2,1,0:T(8,128)(2,1)} %get-tuple-element.258), channel_id=1, source_target_pairs={{0,6},{1,7},{2,0},{3,1},{4,2},{5,3},{6,4},{7,5},{8,14},{9,15},{10,... | collective-permute-start | bytes 2801672 | tf_op jit(solution)/shard_map/ppermute | solution.py:587
  334.3 25.3 %collective-permute-start.7 = (bf16[192,2304]{1,0:T(8,128)(2,1)}, bf16[192,2304]{1,0:T(8,128)(2,1)S(1)}, u32[]{:S(2)}, u32[]{:S(2)}) collective-permute-start(bf16[192,2304]{1,0:T(8,128)(2,1)} %get-tuple-element.255), channel_id=1, source_target_pairs={{0,8},{1,9},{2,10},{3,11},{4,12},{5,13},{6,14},{7,15},{8,16},{9,17... | collective-permute-start | bytes 2654216 | tf_op jit(solution)/shard_map/ppermute | solution.py:587
  335.5 24.2 %collective-permute-start.8 = (bf16[192,2304]{1,0:T(8,128)(2,1)}, bf16[192,2304]{1,0:T(8,128)(2,1)S(1)}, u32[]{:S(2)}, u32[]{:S(2)}) collective-permute-start(bf16[192,2304]{1,0:T(8,128)(2,1)} %get-tuple-element.256), channel_id=1, source_target_pairs={{0,24},{1,25},{2,26},{3,27},{4,28},{5,29},{6,30},{7,31},{8,0},{9,1... | collective-permute-start | bytes 2654216 | tf_op jit(solution)/shard_map/ppermute | solution.py:587
  362.8 33.2 %collective-permute-start.18 = (f32[384,768]{1,0:T(8,128)}, f32[384,768]{1,0:T(8,128)S(1)}, u32[]{:S(2)}, u32[]{:S(2)}) collective-permute-start(f32[384,768]{1,0:T(8,128)} %get-tuple-element.268), channel_id=1, source_target_pairs={{0,32},{32,0},{64,96},{96,64},{1,33},{33,1},{65,97},{97,65},{2,34}... | collective-permute-start | bytes 3538952 | tf_op jit(solution)/shard_map/ppermute | solution.py:591
  363.0 21.9 %collective-permute-start.19 = (bf16[192,2304]{1,0:T(8,128)(2,1)}, bf16[192,2304]{1,0:T(8,128)(2,1)}, u32[]{:S(2)}, u32[]{:S(2)}) collective-permute-start(bf16[192,2304]{1,0:T(8,128)(2,1)} %get-tuple-element.274), channel_id=1, source_target_pairs={{0,16},{1,17},{2,18},{3,19},{4,20},{5,21},{6,22},{7,23},{8,24},{9,... | collective-permute-start | bytes 2654216 | tf_op jit(solution)/shard_map/ppermute | solution.py:587
  364.5 26.5 %collective-permute-start.23 = (bf16[4,48,2432]{2,1,0:T(8,128)(2,1)}, bf16[4,48,2432]{2,1,0:T(8,128)(2,1)S(1)}, u32[]{:S(2)}, u32[]{:S(2)}) collective-permute-start(bf16[4,48,2432]{2,1,0:T(8,128)(2,1)} %get-tuple-element.282), channel_id=1, source_target_pairs={{0,4},{1,5},{2,6},{3,7},{4,0},{5,1},{6,2},{7,3},{8,12},{9,13},{10,... | collective-permute-start | bytes 2801672 | tf_op jit(solution)/shard_map/ppermute | solution.py:587
  384.1 21.2 %collective-permute-start.12 = (bf16[192,2304]{1,0:T(8,128)(2,1)}, bf16[192,2304]{1,0:T(8,128)(2,1)}, u32[]{:S(2)}, u32[]{:S(2)}) collective-permute-start(bf16[192,2304]{1,0:T(8,128)(2,1)} %get-tuple-element.261), channel_id=1, source_target_pairs={{0,8},{1,9},{2,10},{3,11},{4,12},{5,13},{6,14},{7,15},{8,16},{9,17... | collective-permute-start | bytes 2654216 | tf_op jit(solution)/shard_map/ppermute | solution.py:587
  389.4 34.3 %collective-permute-start.13 = (bf16[192,2304]{1,0:T(8,128)(2,1)}, bf16[192,2304]{1,0:T(8,128)(2,1)}, u32[]{:S(2)}, u32[]{:S(2)}) collective-permute-start(bf16[192,2304]{1,0:T(8,128)(2,1)} %get-tuple-element.262), channel_id=1, source_target_pairs={{0,16},{1,17},{2,18},{3,19},{4,20},{5,21},{6,22},{7,23},{8,24},{9,... | collective-permute-start | bytes 2654216 | tf_op jit(solution)/shard_map/ppermute | solution.py:587
  391.0 40.2 %collective-permute-start.15 = (bf16[4,48,2432]{2,1,0:T(8,128)(2,1)}, bf16[4,48,2432]{2,1,0:T(8,128)(2,1)S(1)}, u32[]{:S(2)}, u32[]{:S(2)}) collective-permute-start(bf16[4,48,2432]{2,1,0:T(8,128)(2,1)} %get-tuple-element.265), channel_id=1, source_target_pairs={{0,2},{1,3},{2,4},{3,5},{4,6},{5,7},{6,0},{7,1},{8,10},{9,11},{10,... | collective-permute-start | bytes 2801672 | tf_op jit(solution)/shard_map/ppermute | solution.py:587
  396.0 39.4 %collective-permute-start.16 = (bf16[4,48,2432]{2,1,0:T(8,128)(2,1)}, bf16[4,48,2432]{2,1,0:T(8,128)(2,1)S(1)}, u32[]{:S(2)}, u32[]{:S(2)}) collective-permute-start(bf16[4,48,2432]{2,1,0:T(8,128)(2,1)} %get-tuple-element.266), channel_id=1, source_target_pairs={{0,4},{1,5},{2,6},{3,7},{4,0},{5,1},{6,2},{7,3},{8,12},{9,13},{10,... | collective-permute-start | bytes 2801672 | tf_op jit(solution)/shard_map/ppermute | solution.py:587
  396.7 42.1 %collective-permute-start.17 = (bf16[4,48,2432]{2,1,0:T(8,128)(2,1)}, bf16[4,48,2432]{2,1,0:T(8,128)(2,1)}, u32[]{:S(2)}, u32[]{:S(2)}) collective-permute-start(bf16[4,48,2432]{2,1,0:T(8,128)(2,1)} %get-tuple-element.267), channel_id=1, source_target_pairs={{0,6},{1,7},{2,0},{3,1},{4,2},{5,3},{6,4},{7,5},{8,14},{9,15},{10,... | collective-permute-start | bytes 2801672 | tf_op jit(solution)/shard_map/ppermute | solution.py:587
  405.3 23.0 %collective-permute-start.14 = (bf16[192,2304]{1,0:T(8,128)(2,1)}, bf16[192,2304]{1,0:T(8,128)(2,1)}, u32[]{:S(2)}, u32[]{:S(2)}) collective-permute-start(bf16[192,2304]{1,0:T(8,128)(2,1)} %get-tuple-element.263), channel_id=1, source_target_pairs={{0,24},{1,25},{2,26},{3,27},{4,28},{5,29},{6,30},{7,31},{8,0},{9,1... | collective-permute-start | bytes 2654216 | tf_op jit(solution)/shard_map/ppermute | solution.py:587
  423.7 21.6 %collective-permute-start.21 = (bf16[48,2304]{1,0:T(8,128)(2,1)}, bf16[48,2304]{1,0:T(8,128)(2,1)}, u32[]{:S(2)}, u32[]{:S(2)}) collective-permute-start(bf16[48,2304]{1,0:T(8,128)(2,1)} %get-tuple-element.278), channel_id=1, source_target_pairs={{0,4},{1,5},{2,6},{3,7},{4,0},{5,1},{6,2},{7,3},{8,12},{9,13},{10,... | collective-permute-start | bytes 663560 | tf_op jit(solution)/shard_map/ppermute | solution.py:587
  428.3 24.7 %collective-permute-start.24 = (bf16[48,2432]{1,0:T(8,128)(2,1)}, bf16[48,2432]{1,0:T(8,128)(2,1)S(1)}, u32[]{:S(2)}, u32[]{:S(2)}) collective-permute-start(bf16[48,2432]{1,0:T(8,128)(2,1)} %get-tuple-element.285), channel_id=1, source_target_pairs={{0,8},{1,9},{2,10},{3,11},{4,12},{5,13},{6,14},{7,15},{8,16},{9,17... | collective-permute-start | bytes 700424 | tf_op jit(solution)/shard_map/ppermute | solution.py:587
  431.2 22.9 %collective-permute-start.25 = (bf16[48,2432]{1,0:T(8,128)(2,1)}, bf16[48,2432]{1,0:T(8,128)(2,1)S(1)}, u32[]{:S(2)}, u32[]{:S(2)}) collective-permute-start(bf16[48,2432]{1,0:T(8,128)(2,1)} %get-tuple-element.286), channel_id=1, source_target_pairs={{0,16},{1,17},{2,18},{3,19},{4,20},{5,21},{6,22},{7,23},{8,24},{9,... | collective-permute-start | bytes 700424 | tf_op jit(solution)/shard_map/ppermute | solution.py:587
  435.4 17.4 %collective-permute-start.22 = (bf16[48,2304]{1,0:T(8,128)(2,1)}, bf16[48,2304]{1,0:T(8,128)(2,1)S(1)}, u32[]{:S(2)}, u32[]{:S(2)}) collective-permute-start(bf16[48,2304]{1,0:T(8,128)(2,1)} %get-tuple-element.279), channel_id=1, source_target_pairs={{0,6},{1,7},{2,0},{3,1},{4,2},{5,3},{6,4},{7,5},{8,14},{9,15},{10,... | collective-permute-start | bytes 663560 | tf_op jit(solution)/shard_map/ppermute | solution.py:587
  438.8 16.9 %collective-permute-start.26 = (bf16[48,2432]{1,0:T(8,128)(2,1)}, bf16[48,2432]{1,0:T(8,128)(2,1)S(1)}, u32[]{:S(2)}, u32[]{:S(2)}) collective-permute-start(bf16[48,2432]{1,0:T(8,128)(2,1)} %get-tuple-element.287), channel_id=1, source_target_pairs={{0,24},{1,25},{2,26},{3,27},{4,28},{5,29},{6,30},{7,31},{8,0},{9,1... | collective-permute-start | bytes 700424 | tf_op jit(solution)/shard_map/ppermute | solution.py:587
  452.9 12.8 %collective-permute-start.30 = (bf16[48,2432]{1,0:T(8,128)(2,1)}, bf16[48,2432]{1,0:T(8,128)(2,1)S(1)}, u32[]{:S(2)}, u32[]{:S(2)}) collective-permute-start(bf16[48,2432]{1,0:T(8,128)(2,1)} %get-tuple-element.302), channel_id=1, source_target_pairs={{0,8},{1,9},{2,10},{3,11},{4,12},{5,13},{6,14},{7,15},{8,16},{9,17... | collective-permute-start | bytes 700424 | tf_op jit(solution)/shard_map/ppermute | solution.py:587
  453.0 12.7 %collective-permute-start.31 = (bf16[48,2432]{1,0:T(8,128)(2,1)}, bf16[48,2432]{1,0:T(8,128)(2,1)S(1)}, u32[]{:S(2)}, u32[]{:S(2)}) collective-permute-start(bf16[48,2432]{1,0:T(8,128)(2,1)} %get-tuple-element.303), channel_id=1, source_target_pairs={{0,16},{1,17},{2,18},{3,19},{4,20},{5,21},{6,22},{7,23},{8,24},{9,... | collective-permute-start | bytes 700424 | tf_op jit(solution)/shard_map/ppermute | solution.py:587
  (44 other events, 382.3 us)
Sparse Core Ops, SparseCore 0:
  24.6 105.4 all-gather.1

commit v6 on v5

--- a/solution.py
+++ b/solution.py
@@ -322,12 +322,13 @@
 
 
 def weight_grad_kernel(d, ff, idx, place, mine, theirs, kept, got, *refs):
-    firsts, seconds, (big_v, a_v, b_v, c_v, p_v, q_v, ins, outs) = refs[:4], refs[4:8], refs[8:]
+    results, (big_v, a_v, b_v, c_v, out_v, ins, outs) = refs[:4], refs[4:]
     rows = kept.shape[0]
     tokens = 2 * rows
     quarter, half, third = WIDE // 4, ff // 2, ff // 3
     blocks = third // WIDE
     share = d // 16
+    cut = 3 * d
     y, z, core = idx[0], idx[1], idx[2]
 
     def load(cin, at, width, to, to_at):
@@ -340,15 +341,23 @@
     def both(ref, at=0, width=d):
         return ref[:, :, at : at + width].reshape(tokens, width)
 
-    def send_first(cout):
-        return [cout.start(p_v.at[pl.ds(pl.multiple_of(lax.rem(y + s, 4) * 4 * share, 16), 4 * share)], firsts[s])
+    def put(rows_at, cols_at, value):
+        out_v[rows_at, cols_at] = value.astype(BF)
+
+    def send_by_y(cout, at, width):
+        cols = pl.ds(at, width)
+        return [cout.start(out_v.at[pl.ds(pl.multiple_of(lax.rem(y + s, 4) * 4 * share, 16), 4 * share), cols], results[s].at[:, cols])
                 for s in (2, 1, 3, 0)]
 
-    def send_second(cout):
+    def send_by_z(cout, at, width):
+        cols = pl.ds(at, width)
         return [
-            cout.start(q_v.at[pl.ds(pl.multiple_of((4 * i + lax.rem(z + s, 4)) * share, 16), share)], seconds[s].at[i])
+            cout.start(out_v.at[pl.ds(pl.multiple_of((4 * i + lax.rem(z + s, 4)) * share, 16), share), cols],
+                       results[s].at[pl.ds(share * i, share), cols])
             for s in (2, 1, 3, 0) for i in range(4)
         ]
+
+    everything = slice(0, d)
 
     @pl.when(core == 0)
     def _():
@@ -365,15 +374,14 @@
             for b in range(blocks):
                 at = quarter * (blocks * k + b)
                 for j in range(4):
-                    to = p_v if j < 2 else q_v
-                    to[at : at + quarter, d * (j % 2) : d * (j % 2) + d] = found[WIDE * b + quarter * j : WIDE * b + quarter * (j + 1)]
+                    put(slice(at, at + quarter), slice(d * j, d * j + d), found[WIDE * b + quarter * j : WIDE * b + quarter * (j + 1)])
+        pending = send_by_y(cout, 0, 4 * d)
         wait(attended)
-        p_v[:, 2 * d :] = lax.dot_general(both(b_v), gb, TN, preferred_element_type=F32).astype(BF)
-        pending = send_first(cout)
+        put(everything, slice(4 * d, 5 * d), lax.dot_general(both(b_v), gb, TN, preferred_element_type=F32))
         wait(hidden + values)
-        q_v[:, 2 * d : 3 * d] = lax.dot_general(both(c_v), both(c_v, d), TN, preferred_element_type=F32).astype(BF)
-        q_v[:, 3 * d :] = split_small(small_table(d, ff, place, mine, theirs))
-        wait(pending + send_second(cout))
+        put(everything, slice(5 * d, 6 * d), lax.dot_general(both(c_v), both(c_v, d), TN, preferred_element_type=F32))
+        put(everything, slice(6 * d, 6 * d + LANES), split_small(small_table(d, ff, place, mine, theirs)))
+        wait(pending + send_by_y(cout, 4 * d, 2 * d + LANES))
 
     @pl.when(core == 1)
     def _():
@@ -385,21 +393,19 @@
         keys = load(cin, ff + d, d, c_v, 0)
         wait(hidden)
         turned = both(a_v).T
-        wait(loads[0])
-        p_v[:, :third] = mm(turned, both(big_v, 0, third)).astype(BF)
-        wait(loads[1])
-        found = mm(turned, both(big_v, third, third)).astype(BF)
-        p_v[:, third:half] = found[:, : half - third]
-        q_v[:, : 2 * third - half] = found[:, half - third :]
+        pending = []
+        for k in range(2):
+            wait(loads[k])
+            put(everything, slice(third * k, third * k + third), mm(turned, both(big_v, third * k, third)))
+        pending = send_by_z(cout, 0, 2 * third)
         wait(queries)
-        p_v[:, half:] = mm(turned, both(b_v)).astype(BF)
-        pending = send_first(cout)
+        put(everything, slice(ff, ff + d), mm(turned, both(b_v)))
         wait(loads[2])
-        q_v[:, 2 * third - half : half] = mm(turned, both(big_v, 2 * third, third)).astype(BF)
+        put(everything, slice(2 * third, ff), mm(turned, both(big_v, 2 * third, third)))
         wait(keys)
-        q_v[:, half : half + d] = mm(turned, both(c_v)).astype(BF)
-        q_v[:, half + d :] = jnp.zeros((d, LANES), BF)
-        wait(pending + send_second(cout))
+        put(everything, slice(ff + d, ff + 2 * d), mm(turned, both(c_v)))
+        out_v[:, 6 * d :] = jnp.zeros((d, LANES), BF)
+        wait(pending + send_by_z(cout, 2 * third, 6 * d + LANES - 2 * third))
 
 
 def added(parts):
@@ -412,32 +418,28 @@
     return jnp.concatenate([main.astype(BF), last], axis=1).reshape(shape)
 
 
-def mid_kernel(part, idx, *refs):
+def mid_kernel(idx, *refs):
     came, outs, hold = refs[:4], refs[4:8], refs[8]
-    if part == 0:
-        total = came[0][...].astype(F32)
-        for piece in came[1:]:
-            total = total + piece[...].astype(F32)
-        hold[...] = total.astype(BF).reshape(hold.shape)
-    else:
-        hold[...] = added(came)
-    at = idx[1] if part == 0 else idx[0]
+    hold[...] = added(came).reshape(hold.shape)
+    at = jnp.where(idx[2] == 0, idx[1], idx[0])
     for s in range(4):
         outs[s][...] = hold[lax.rem(at + s, 4)]
 
 
 def last_kernel(idx, *refs):
-    firsts, seconds, mine, theirs, hold = refs[:4], refs[4:8], refs[8], refs[9], refs[10]
-    cut = firsts[0].shape[-1]
-    total = firsts[0][...].astype(F32)
-    for piece in firsts[1:]:
-        total = total + piece[...].astype(F32)
-    hold[:, :cut] = total
-    hold[:, cut:] = added(seconds).astype(F32)
-    count = mine.shape[0]
-    core = idx[2]
-    mine[...] = hold[pl.ds(pl.multiple_of(core * count, 8), count), :]
-    theirs[...] = hold[pl.ds(pl.multiple_of((1 - core) * count, 8), count), :]
+    layers, (home_mine, home_other, away_mine, away_other), holds = (refs[:4], refs[4:8]), refs[8:12], refs[12:]
+    core, odd = idx[2], idx[4]
+    for came, hold in zip(layers, holds):
+        hold[...] = added(came).astype(F32)
+    count = home_mine.shape[0]
+
+    def rows_of(hold, which):
+        return hold[pl.ds(pl.multiple_of(which * count, 8), count), :]
+
+    for which, home, away in ((core, home_mine, away_mine), (1 - core, home_other, away_other)):
+        lower, upper = rows_of(holds[0], which), rows_of(holds[1], which)
+        home[...] = jnp.where(odd == 1, upper, lower).astype(home.dtype)
+        away[...] = jnp.where(odd == 1, lower, upper).astype(away.dtype)
 
 
 def place_kernel(idx, y_in, y_got, g_in, g_got, y_out, g_out, sems):
@@ -501,15 +503,13 @@
     theirs = b_in[...].astype(F32) + c_in[...].astype(F32)
     half0 = jnp.where(core == 0, mine, theirs)
     half1 = jnp.where(core == 0, theirs, mine)
-    g_in[:, :d] = half1[:, 2 * d : 3 * d]
-    g_in[:, d : 2 * d] = half1[:, 5 * d : 6 * d]
+    g_in[:, : 2 * d] = half1[:, ff : ff + 2 * d]
     g_in[:, 2 * d : 3 * d] = half0[:, 5 * d : 6 * d]
     for at in range(0, ff, WIDE):
-        start = at if at < 2 * d else at + d
         g_in[:, 3 * d + at : 3 * d + at + WIDE] = lax.dot_general(
-            half1[:, start : start + WIDE], shuffle[...], NT, precision=lax.Precision.HIGHEST, preferred_element_type=F32)
-    g_attn[...] = half0[:, 2 * d : 3 * d]
-    stacked = jnp.concatenate([half0[:, at : at + d] for at in (0, d, 3 * d, 4 * d)], axis=0)
+            half1[:, at : at + WIDE], shuffle[...], NT, precision=lax.Precision.HIGHEST, preferred_element_type=F32)
+    g_attn[...] = half0[:, 4 * d : 5 * d]
+    stacked = jnp.concatenate([half0[:, at : at + d] for at in range(0, 4 * d, d)], axis=0)
     row, column, _ = picked(4 * share, 4 * share, lambda row: row)
     turn = jnp.where(column == lax.rem(row, 4) * share + row // 4, 1.0, 0.0)
     g_down[...] = lax.dot_general(turn, stacked, NN, precision=lax.Precision.HIGHEST, preferred_element_type=F32)
@@ -693,50 +693,42 @@
 
     results = [stash(slots, rows, d, dtype=F32), stash(rows, d, dtype=F32)]
     tables = [stash(1, stacked, dtype=F32) for _ in range(2)]
-    steps = ((2 * side, 2), (2, 2 * side))
-    widths = (3 * d, 3 * d + LANES)
-    width = widths[0] + widths[1]
+    width = 6 * d + LANES
     share = 2 * dshare
     position = jnp.arange(LANES, dtype=jnp.int32)[:, None] % head
     place = (position // hshare * dshare + position % hshare == jnp.arange(d, dtype=jnp.int32)[None, :]).astype(F32)
-    here = jnp.stack([y, z, core, slot]).astype(jnp.int32)
-
-    def grads_by_place(layer, ahead=None):
-        mine, sent = operands[layer]
-        if ahead is not None:
-            sent, ahead = lax.optimization_barrier((sent, ahead))
-        got, table_got = along(sent, 1, 2, 1), along(tables[layer], 1, 2, 1)
-        shapes = [(side * share, widths[0])] * side + [(side, share, widths[1])] * side
-        outs = simple(
+    here = jnp.stack([y, z, core, slot, odd]).astype(jnp.int32)
+
+    def moved(x, leg, by):
+        def to(i):
+            step = 2 * side if i % 2 == leg else 2
+            digit = i // step % side
+            return i + ((digit + by) % side - digit) * step
+
+        return lax.ppermute(x, "dp", [(i, to(i)) for i in range(ranks)])
+
+    def grads_by_place(layer, got, table_got):
+        return simple(
             partial(weight_grad_kernel, d, ff), here,
-            [place, tables[layer], table_got, mine, got],
+            [place, tables[layer], table_got, operands[layer][0], got],
             [whole((LANES, d)), whole(table_got.shape), whole(table_got.shape), ANY, ANY],
-            [jax.ShapeDtypeStruct(s, BF) for s in shapes], [ANY] * (2 * side),
-            [V((2, rows, ff), BF), V((2, rows, d), BF), V((2, rows, d), BF), V((2, rows, 2 * d), BF),
-             V((d, widths[0]), BF), V((d, widths[1]), BF), pltpu.SemaphoreType.DMA((32,)), pltpu.SemaphoreType.DMA((32,))],
+            [jax.ShapeDtypeStruct((side * share, width), BF)] * side, [ANY] * side,
+            [V((2, rows, ff), BF), V((2, rows, d), BF), V((2, rows, d), BF), V((2, rows, 2 * d), BF), V((d, width), BF),
+             pltpu.SemaphoreType.DMA((32,)), pltpu.SemaphoreType.DMA((32,))],
         )
-        made = [outs[:side], outs[side:]]
-        return made, ahead
-
-    def first_leg(made):
-        return [[outs[0]] + [along(outs[s], steps[part][0], side, s) for s in (1, 2, 3)] for part, outs in enumerate(made)]
-
-    def second_leg(legs):
-        arrived = []
-        for part, came in enumerate(legs):
-            w = widths[part]
-            outs = simple(
-                partial(mid_kernel, part), here, came, [whole(a.shape) for a in came],
-                [jax.ShapeDtypeStruct((share, w), BF)] * side, [whole((share, w))] * side, [V((side, share, w), BF)],
-            )
-            arrived += [outs[0]] + [along(outs[s], steps[part][1], side, s) for s in (1, 2, 3)]
+
+    def leg(outs, which):
+        far, near, back = (moved(outs[s], which, s) for s in (2, 1, 3))
+        return [outs[0], near, far, back]
+
+    def by_second_axis(came):
         return simple(
-            last_kernel, here, arrived, [whole(a.shape) for a in arrived],
-            [jax.ShapeDtypeStruct((dshare, width), F32)] * 2, [whole((dshare, width))] * 2, [V((share, width), F32)],
+            mid_kernel, here, came, [whole(a.shape) for a in came],
+            [jax.ShapeDtypeStruct((share, width), BF)] * side, [whole((share, width))] * side, [V((side, share, width), BF)],
         )
 
-    sums = [None, None]
     here_g = seeds
+    swaps = []
     for t in range(4):
         layer = 1 - t % 2
         gbf, done = call(
@@ -758,17 +750,14 @@
         here_g = lax.ppermute(gbf, "section", [(3, 0), (2, 1)]) if t == 1 else gbf
         if t == 1:
             here_g, y_got = lax.optimization_barrier((here_g, y_got))
-        if t == 2:
-            made, _ = grads_by_place(layer)
-            here_g, made = lax.optimization_barrier((here_g, made))
-            legs = first_leg(made)
         if t == 3:
-            made, early = grads_by_place(layer, [legs[p][s] for p in (0, 1) for s in (1, 3)])
-            (legs[0][1], legs[0][3], legs[1][1], legs[1][3]) = early
-            sums[1 - layer] = second_leg(legs)
-            gr_got = paired(results[1])
-            legs, gr_got = lax.optimization_barrier((first_leg(made), gr_got))
-            sums[layer] = second_leg(legs)
+            operands[layer][1], swaps[0] = lax.optimization_barrier((operands[layer][1], swaps[0]))
+        if t >= 2:
+            swaps.append((along(operands[layer][1], 1, 2, 1), along(tables[layer], 1, 2, 1)))
+    gr_got = paired(results[1])
+    legs = [leg(grads_by_place(1, *swaps[0]), 0), leg(grads_by_place(0, *swaps[1]), 0)]
+    legs[1], gr_got = lax.optimization_barrier((legs[1], gr_got))
+    arrived = [leg(by_second_axis(came), 1) for came in legs]
     gr_out = results[0]
     y_out, gr_out = pl.pallas_call(
         place_kernel,
@@ -780,11 +769,15 @@
         input_output_aliases={1: 0, 3: 1},
     )(here, y_out, y_got, gr_out, gr_got)
 
-    home = [jnp.where(odd == 1, b, a) for a, b in zip(*sums)]
-    away = [jnp.where(odd == 1, a, b).astype(BF) for a, b in zip(*sums)]
+    both = arrived[1] + arrived[0]
+    home_mine, home_other, away_mine, away_other = simple(
+        last_kernel, here, both, [whole(a.shape) for a in both],
+        [jax.ShapeDtypeStruct((dshare, width), t) for t in (F32, BF, BF, BF)], [whole((dshare, width))] * 4,
+        [V((share, width), F32)] * 2,
+    )
     sections = lax.axis_size("section")
     cross = [(s * ranks + i, (s ^ 1) * ranks + (i ^ 1)) for s in range(sections) for i in range(ranks)]
-    arrays = [home[0], paired(away[0]), along(home[1].astype(BF), 1, 2, 1), lax.ppermute(away[1], ("section", "dp"), cross),
+    arrays = [home_mine, paired(away_mine), along(home_other, 1, 2, 1), lax.ppermute(away_other, ("section", "dp"), cross),
               shuffle.astype(F32)]
     shapes = [(dshare, joined), (dshare, d), (dshare * fshare, d), (1, dshare), (1, hshare), (1, hshare), (1, dshare * fshare),
               (1, dshare)]

time: 505 us -> 499 us (0.988)
  starting transfers between devices: 44.1 us -> 52.7 us
  Pallas kernels: 186 us -> 180 us
    ppermute x29 -> x5, waiting for transfers between devices: 51 us -> 0.86 us  [along(): return lax.ppermute(x, 'dp', [(i, to(i)) for i in range(devices)])]
    ppermute x1 -> x13, starting transfers between devices: 0.13 us -> 38.3 us  [the longest x12 37.2 us: moved(): return lax.ppermute(x, 'dp', [(i, to(i)) for i in range(ranks)])]
    ppermute x1 -> x13, waiting for transfers between devices: 6.31 us -> 35.5 us  [the longest x12 30.5 us: moved(): return lax.ppermute(x, 'dp', [(i, to(i)) for i in range(ranks)])]
    ppermute x29 -> x5, starting transfers between devices: 35.9 us -> 7.98 us  [along(): return lax.ppermute(x, 'dp', [(i, to(i)) for i in range(devices)])]
    ppermute x4, waiting for transfers between devices: 9.73 us -> 26.3 us  [paired(): return lax.ppermute(x, 'section', [(0, 1), (1, 0), (2, 3), (3, 2)])]
    pallas_call x9 -> x6, Pallas kernels: 56.8 us -> 50.8 us  [simple(): pl.pallas_call(kernel, grid_spec=pltpu.PrefetchScalarGridSpec(num_scalar_...]
  transfers between devices with their start and end apart: 37 -> 25, of which waited for: 16 -> 11; matrix products, arithmetic and copies ran while one was open for 2% -> 2% of each run, Pallas kernels for 17% -> 19%
where the time goes in v6:
time: 499 us; the launch traced here: 496 us
  waiting for transfers between devices  233 us (47%)
  Pallas kernels  180 us (36%)
  starting transfers between devices  52.7 us (11%)
  between operations  14.8 us (3%)
  other arithmetic  10.4 us (2%)
  local copies, waits for them, and re-layouts  5.47 us (1%)
    pallas_call x8, Pallas kernels, call(): pl.pallas_call(kernel, grid_spec=pltpu.PrefetchScalarGridSpec(num_scalar_...  119 us
    all_gather x1, waiting for transfers between devices, body(): g = lax.all_gather(both, 'dp', axis=0, tiled=True)  99 us
    ppermute x1, waiting for transfers between devices, body(): here_g = lax.ppermute(gbf, 'section', [(3, 0), (2, 1)]) if t == 1 else gbf  59.7 us
    pallas_call x6, Pallas kernels, simple(): pl.pallas_call(kernel, grid_spec=pltpu.PrefetchScalarGridSpec(num_scalar_...  50.8 us
    ppermute x12, starting transfers between devices, moved(): return lax.ppermute(x, 'dp', [(i, to(i)) for i in range(ranks)])  37.2 us
    ppermute x12, waiting for transfers between devices, moved(): return lax.ppermute(x, 'dp', [(i, to(i)) for i in range(ranks)])  30.5 us
    ppermute x4, waiting for transfers between devices, paired(): return lax.ppermute(x, 'section', [(0, 1), (1, 0), (2, 3), (3, 2)])  26.3 us
    ppermute x1, waiting for transfers between devices, body(): here_x = lax.ppermute(ybf, 'section', [(0, 3), (1, 2)]) if t == 1 else ybf  11.8 us
  transfers between devices with their start and end apart: 25, of which 11 were waited for; matrix products, arithmetic and copies ran while one was open for 2% of the time, Pallas kernels for 19%

profile of v6, /device:TPU:1, one launch (start us, length us, event | category | flops | bytes accessed | tf_op | source)
XLA Modules:
  0.0 496.0 jit_solution(3217050207736526235)
XLA Ops:
  12.5 9.7 %collective-permute-done = bf16[24,9344]{1,0:T(8,128)(2,1)S(1)} collective-permute-done((bf16[24,9344]{1,0:T(8,128)(2,1)}, bf16[24,9344]{1,0:T(8,128)(2,1)S(1)}, u32[]{:S(2)}, u32[]{:S(2)}) %collective-permute-start) | collective-permute-done | bytes 448544 | tf_op jit(solution)/shard_map/ppermute | solution.py:591
  31.2 99.0 %all-gather.2.cloned.1.call-done.g = bf16[768,18688]{1,0:T(8,128)(2,1)} async-done(((bf16[24,18688]{1,0:T(8,128)(2,1)}), bf16[768,18688]{1,0:T(8,128)(2,1)}) %all-gather.2.cloned.1.call-update) | async-done | bytes 28704784 | tf_op jit(solution)/shard_map/all_gather | solution.py:629
  133.7 18.2 %shard_map.201 = (bf16[384,768]{1,0:T(8,128)(2,1)}, bf16[384,768]{1,0:T(8,128)(2,1)}, bf16[384,768]{1,0:T(8,128)(2,1)}, bf16[384,768]{1,0:T(8,128)(2,1)}, bf16[3...) custom-call(s32[4]{0:T(128)} %get-tuple-element.254.idx, ...), custom_call_target="tpu_custom_call", output_to_operand_aliasing={{1}: (11, {}), {2}: (12, {}), {3}: (13, {}), {4}: (14, {}),... | custom-call | flops 1024 | bytes 1024 | tf_op jit(solution)/shard_map/pallas_call | solution.py:543
  152.0 18.3 %shard_map.213 = (bf16[384,768]{1,0:T(8,128)(2,1)}, bf16[384,768]{1,0:T(8,128)(2,1)}, bf16[384,768]{1,0:T(8,128)(2,1)}, bf16[384,768]{1,0:T(8,128)(2,1)}, bf16[3...) custom-call(s32[4]{0:T(128)} %pad_add_fusion.idx, ...), custom_call_target="tpu_custom_call", output_to_operand_aliasing={{1}: (11, {}), {2}: (12, {}), {3}: (13, {}), {4}: (14, {}),... | custom-call | flops 1024 | bytes 1024 | tf_op jit(solution)/shard_map/pallas_call | solution.py:543
  172.9 11.8 %collective-permute-done.1.x_in = bf16[384,768]{1,0:T(8,128)(2,1)S(1)} collective-permute-done((bf16[384,768]{1,0:T(8,128)(2,1)}, bf16[384,768]{1,0:T(8,128)(2,1)S(1)}, u32[]{:S(2)}, u32[]{:S(2)}) %collective-permute-start.1) | collective-permute-done | bytes 589856 | tf_op jit(solution)/shard_map/ppermute | solution.py:690
  185.5 3.8 shard_map.214
  189.3 7.7 %shard_map.215 = (bf16[384,768]{1,0:T(8,128)(2,1)}, bf16[384,768]{1,0:T(8,128)(2,1)}, bf16[384,768]{1,0:T(8,128)(2,1)}, bf16[384,768]{1,0:T(8,128)(2,1)}, bf16[3...) custom-call(s32[4]{0:T(128)} %pad_add_fusion.1.idx, ...), custom_call_target="tpu_custom_call", output_to_operand_aliasing={{1}: (11, {}), {2}: (12, {}), {3}: (13, {}), {4}: (14, {}),... | custom-call | flops 1024 | bytes 1024 | tf_op jit(solution)/shard_map/pallas_call | solution.py:543
  198.3 16.8 %shard_map.219 = (bf16[384,768]{1,0:T(8,128)(2,1)}, bf16[384,6144]{1,0:T(8,128)(2,1)}, bf16[384,6144]{1,0:T(8,128)(2,1)}, f32[1,6144]{1,0:T(1,128)}, f32[2,384,768]{2,1,0:T(8,128)}, /*index=5*/f32[384,768]{1,0:T(8,128)}) custom-call(s32[4]{0:T(128)} %pad_add_fusion.1.idx, ...), custom_call_target="tpu_custom_call", output_to_operand_aliasing={{1}: (17, {}), {2}: (18, {}), {3}: (19, {}), {4}: (20, {}),... | custom-call | flops 1024 | bytes 1024 | tf_op jit(solution)/shard_map/pallas_call | solution.py:543
  215.1 9.4 %shard_map.221 = (bf16[384,768]{1,0:T(8,128)(2,1)}, bf16[384,6144]{1,0:T(8,128)(2,1)}, bf16[384,6144]{1,0:T(8,128)(2,1)}, f32[1,6144]{1,0:T(1,128)}, f32[2,384,768]{2,1,0:T(8,128)}, /*index=5*/f32[384,768]{1,0:T(8,128)}) custom-call(s32[4]{0:T(128)} %get-tuple-element.256.idx, ...), custom_call_target="tpu_custom_call", output_to_operand_aliasing={{1}: (17, {}), {2}: (18, {}), {3}: (19, {}), {4}: (20, {}),... | custom-call | flops 1024 | bytes 1024 | tf_op jit(solution)/shard_map/pallas_call | solution.py:543
  225.8 59.7 %collective-permute-done.2.g_in = bf16[384,768]{1,0:T(8,128)(2,1)S(1)} collective-permute-done((bf16[384,768]{1,0:T(8,128)(2,1)}, bf16[384,768]{1,0:T(8,128)(2,1)S(1)}, u32[]{:S(2)}, u32[]{:S(2)}) %collective-permute-start.2) | collective-permute-done | bytes 589856 | tf_op jit(solution)/shard_map/ppermute | solution.py:750
  286.3 22.2 %shard_map.222 = (bf16[384,768]{1,0:T(8,128)(2,1)}, bf16[384,6144]{1,0:T(8,128)(2,1)}, bf16[384,6144]{1,0:T(8,128)(2,1)}, f32[1,6144]{1,0:T(1,128)}, f32[2,384,768]{2,1,0:T(8,128)}, /*index=5*/f32[384,768]{1,0:T(8,128)}) custom-call(s32[4]{0:T(128)} %pad_add_fusion.idx, ...), custom_call_target="tpu_custom_call", output_to_operand_aliasing={{1}: (17, {}), {2}: (18, {}), {3}: (19, {}), {4}: (20, {}),... | custom-call | flops 1024 | bytes 1024 | tf_op jit(solution)/shard_map/pallas_call | solution.py:543
  310.4 22.5 %shard_map.223 = (bf16[384,768]{1,0:T(8,128)(2,1)}, bf16[384,6144]{1,0:T(8,128)(2,1)}, bf16[384,6144]{1,0:T(8,128)(2,1)}, f32[1,6144]{1,0:T(1,128)}, f32[2,384,768]{2,1,0:T(8,128)}, /*index=5*/f32[384,768]{1,0:T(8,128)}) custom-call(s32[4]{0:T(128)} %get-tuple-element.254.idx, ...), custom_call_target="tpu_custom_call", output_to_operand_aliasing={{1}: (17, {}), {2}: (18, {}), {3}: (19, {}), {4}: (20, {}),... | custom-call | flops 1024 | bytes 1024 | tf_op jit(solution)/shard_map/pallas_call | solution.py:543
  334.8 13.0 %shard_map.227 = (bf16[192,4736]{1,0:T(8,128)(2,1)}, bf16[192,4736]{1,0:T(8,128)(2,1)}, bf16[192,4736]{1,0:T(8,128)(2,1)}, bf16[192,4736]{1,0:T(8,128)(2,1)}) custom-call(s32[5]{0:T(128)} %stack.45.idx, f32[128,768]{1,0:T(8,128)} %fusion.2.place, f32[1,6144]{1,0:T(1,128)} %get-tuple-element.213.mine, f32[1,6144]{1,0:T(1,128)} %copy-done.15, ...), custom_call_target="tpu_custom_call" | custom-call | flops 1024 | bytes 1024 | tf_op jit(solution)/shard_map/pallas_call | solution.py:569
  356.2 13.3 %shard_map.224 = (bf16[192,4736]{1,0:T(8,128)(2,1)}, bf16[192,4736]{1,0:T(8,128)(2,1)}, bf16[192,4736]{1,0:T(8,128)(2,1)}, bf16[192,4736]{1,0:T(8,128)(2,1)}) custom-call(s32[5]{0:T(128)} %stack.45.idx, f32[128,768]{1,0:T(8,128)} %fusion.2.place, f32[1,6144]{1,0:T(1,128)} %get-tuple-element.209.mine, f32[1,6144]{1,0:T(1,128)} %copy-done.16, ...), custom_call_target="tpu_custom_call" | custom-call | flops 1024 | bytes 1024 | tf_op jit(solution)/shard_map/pallas_call | solution.py:569
  372.6 19.1 %collective-permute-done.16.refs_2_ = bf16[192,4736]{1,0:T(8,128)(2,1)} collective-permute-done((bf16[192,4736]{1,0:T(8,128)(2,1)}, bf16[192,4736]{1,0:T(8,128)(2,1)}, u32[]{:S(2)}, u32[]{:S(2)}) %collective-permute-start.16) | collective-permute-done | bytes 1818656 | tf_op jit(solution)/shard_map/ppermute | solution.py:708
  392.0 7.0 %shard_map.228 = (bf16[48,4736]{1,0:T(8,128)(2,1)}, bf16[48,4736]{1,0:T(8,128)(2,1)}, bf16[48,4736]{1,0:T(8,128)(2,1)}, bf16[48,4736]{1,0:T(8,128)(2,1)}) custom-call(s32[5]{0:T(128)} %stack.45.idx, bf16[192,4736]{1,0:T(8,128)(2,1)} %get-tuple-element.234.refs_0_, bf16[192,4736]{1,0:T(8,128)(2,1)} %collective-permute-done.15.refs_1_, ...), custom_call_target="tpu_custom_call" | custom-call | flops 1024 | bytes 1024 | tf_op jit(solution)/shard_map/pallas_call | solution.py:569
  400.1 16.6 %collective-permute-done.11.g_got = f32[384,768]{1,0:T(8,128)} collective-permute-done((f32[384,768]{1,0:T(8,128)S(1)}, f32[384,768]{1,0:T(8,128)}, u32[]{:S(2)}, u32[]{:S(2)}) %collective-permute-start.11) | collective-permute-done | bytes 1179680 | tf_op jit(solution)/shard_map/ppermute | solution.py:591
  416.7 4.0 collective-permute-start.19
  420.7 21.6 %collective-permute-start.20 = (bf16[48,4736]{1,0:T(8,128)(2,1)}, bf16[48,4736]{1,0:T(8,128)(2,1)S(1)}, u32[]{:S(2)}, u32[]{:S(2)}) collective-permute-start(bf16[48,4736]{1,0:T(8,128)(2,1)} %get-tuple-element.241), channel_id=1, source_target_pairs={{0,6},{1,25},{2,0},{3,27},{4,2},{5,29},{6,4},{7,31},{8,14},{9,1},{... | collective-permute-start | bytes 1363976 | tf_op jit(solution)/shard_map/ppermute | solution.py:708
  442.3 7.0 %shard_map.226 = (bf16[48,4736]{1,0:T(8,128)(2,1)}, bf16[48,4736]{1,0:T(8,128)(2,1)}, bf16[48,4736]{1,0:T(8,128)(2,1)}, bf16[48,4736]{1,0:T(8,128)(2,1)}) custom-call(s32[5]{0:T(128)} %stack.45.idx, bf16[192,4736]{1,0:T(8,128)(2,1)} %get-tuple-element.223.refs_0_, bf16[192,4736]{1,0:T(8,128)(2,1)} %copy-done.1, ...), custom_call_target="tpu_custom_call" | custom-call | flops 1024 | bytes 1024 | tf_op jit(solution)/shard_map/pallas_call | solution.py:569
  452.9 10.2 %collective-permute-done.12.refs_1_ = bf16[48,4736]{1,0:T(8,128)(2,1)S(1)} collective-permute-done((bf16[48,4736]{1,0:T(8,128)(2,1)}, bf16[48,4736]{1,0:T(8,128)(2,1)S(1)}, u32[]{:S(2)}, u32[]{:S(2)}) %collective-permute-start.12) | collective-permute-done | bytes 454688 | tf_op jit(solution)/shard_map/ppermute | solution.py:708
  464.6 4.6 shard_map.229
  477.4 5.0 %collective-permute-done.23.c_in = bf16[24,4736]{1,0:T(8,128)(2,1)S(1)} collective-permute-done((bf16[24,4736]{1,0:T(8,128)(2,1)}, bf16[24,4736]{1,0:T(8,128)(2,1)S(1)}, u32[]{:S(2)}, u32[]{:S(2)}) %collective-permute-start.23) | collective-permute-done | bytes 227360 | tf_op jit(solution)/shard_map/ppermute | solution.py:780
  483.0 5.9 %shard_map.230 = (f32[24,5376]{1,0:T(8,128)}, f32[24,768]{1,0:T(8,128)}, f32[96,768]{1,0:T(8,128)}, f32[1,24]{1,0:T(1,128)}, f32[1,2]{1,0:T(1,128)}, /*index=5*/...) custom-call(s32[5]{0:T(128)} %stack.45.idx, f32[24,4736]{1,0:T(8,128)} %get-tuple-element.242.own, ...), custom_call_target="tpu_custom_call" | custom-call | flops 1024 | bytes 1024 | tf_op jit(solution)/shard_map/pallas_call | solution.py:569
  (130 shorter events, 54.8 us)
Async XLA Ops:
  7.2 123.0 %all-gather.2.cloned.1.call-start = ((), (), s32[]{:S(2)}) async-start(), calls=%async_computation | async-start | bytes 29601792 | tf_op jit(solution)/shard_map/all_gather | solution.py:629
  10.5 11.8 %collective-permute-start = (bf16[24,9344]{1,0:T(8,128)(2,1)}, bf16[24,9344]{1,0:T(8,128)(2,1)S(1)}, u32[]{:S(2)}, u32[]{:S(2)}) collective-permute-start(bf16[24,9344]{1,0:T(8,128)(2,1)} %shard_map.186), channel_id=1, source_target_pairs={{0,32},{32,0},{64,96},{96,64},{1,33},{33,1},{65,97},{97,65},{2,34}... | collective-permute-start | bytes 1345544 | tf_op jit(solution)/shard_map/ppermute | solution.py:591
  170.3 14.4 %collective-permute-start.1 = (bf16[384,768]{1,0:T(8,128)(2,1)}, bf16[384,768]{1,0:T(8,128)(2,1)S(1)}, u32[]{:S(2)}, u32[]{:S(2)}) collective-permute-start(bf16[384,768]{1,0:T(8,128)(2,1)} %get-tuple-element.139), channel_id=1, source_target_pairs={{0,96},{32,64},{1,97},{33,65},{2,98},{34,66},{3,99},{35,67},{4,100... | collective-permute-start | bytes 1769480 | tf_op jit(solution)/shard_map/ppermute | solution.py:690
  197.0 88.4 %collective-permute-start.3 = (f32[384,768]{1,0:T(8,128)}, f32[384,768]{1,0:T(8,128)S(1)}, u32[]{:S(2)}, u32[]{:S(2)}) collective-permute-start(f32[384,768]{1,0:T(8,128)} %get-tuple-element.194), channel_id=1, source_target_pairs={{0,32},{32,0},{64,96},{96,64},{1,33},{33,1},{65,97},{97,65},{2,34}... | collective-permute-start | bytes 3538952 | tf_op jit(solution)/shard_map/ppermute | solution.py:591
  224.5 61.0 %collective-permute-start.2 = (bf16[384,768]{1,0:T(8,128)(2,1)}, bf16[384,768]{1,0:T(8,128)(2,1)S(1)}, u32[]{:S(2)}, u32[]{:S(2)}) collective-permute-start(bf16[384,768]{1,0:T(8,128)(2,1)} %get-tuple-element.193), channel_id=1, source_target_pairs={{96,0},{64,32},{97,1},{65,33},{98,2},{66,34},{99,3},{67,35},{100,4... | collective-permute-start | bytes 1769480 | tf_op jit(solution)/shard_map/ppermute | solution.py:750
  308.6 24.3 %collective-permute-start.5 = (bf16[384,6144]{1,0:T(8,128)(2,1)}, bf16[384,6144]{1,0:T(8,128)(2,1)}, u32[]{:S(2)}, u32[]{:S(2)}) collective-permute-start(bf16[384,6144]{1,0:T(8,128)(2,1)} %get-tuple-element.212), channel_id=1, source_target_pairs={{0,1},{1,0},{2,3},{3,2},{4,5},{5,4},{6,7},{7,6},{8,9},{9,8},{10,11... | collective-permute-start | bytes 14155784 | tf_op jit(solution)/shard_map/ppermute | solution.py:587
  310.3 22.6 %collective-permute-start.6 = (f32[1,6144]{1,0:T(1,128)}, f32[1,6144]{1,0:T(1,128)S(1)}, u32[]{:S(2)}, u32[]{:S(2)}) collective-permute-start(f32[1,6144]{1,0:T(1,128)} %get-tuple-element.213.mine), channel_id=1, source_target_pairs={{0,1},{1,0},{2,3},{3,2},{4,5},{5,4},{6,7},{7,6},{8,9},{9,8},{10,11... | collective-permute-start | bytes 73736 | tf_op jit(solution)/shard_map/ppermute | solution.py:587
  332.9 22.8 %collective-permute-start.7 = (bf16[384,6144]{1,0:T(8,128)(2,1)}, bf16[384,6144]{1,0:T(8,128)(2,1)}, u32[]{:S(2)}, u32[]{:S(2)}) collective-permute-start(bf16[384,6144]{1,0:T(8,128)(2,1)} %get-tuple-element.214), channel_id=1, source_target_pairs={{0,1},{1,0},{2,3},{3,2},{4,5},{5,4},{6,7},{7,6},{8,9},{9,8},{10,11... | collective-permute-start | bytes 14155784 | tf_op jit(solution)/shard_map/ppermute | solution.py:587
  347.9 24.0 %collective-permute-start.15 = (bf16[192,4736]{1,0:T(8,128)(2,1)}, bf16[192,4736]{1,0:T(8,128)(2,1)}, u32[]{:S(2)}, u32[]{:S(2)}) collective-permute-start(bf16[192,4736]{1,0:T(8,128)(2,1)} %get-tuple-element.235), channel_id=1, source_target_pairs={{0,8},{1,3},{2,10},{3,5},{4,12},{5,7},{6,14},{7,1},{8,16},{9,11},{... | collective-permute-start | bytes 5455880 | tf_op jit(solution)/shard_map/ppermute | solution.py:708
  348.6 43.1 %collective-permute-start.16 = (bf16[192,4736]{1,0:T(8,128)(2,1)}, bf16[192,4736]{1,0:T(8,128)(2,1)}, u32[]{:S(2)}, u32[]{:S(2)}) collective-permute-start(bf16[192,4736]{1,0:T(8,128)(2,1)} %get-tuple-element.236), channel_id=1, source_target_pairs={{0,16},{1,5},{2,18},{3,7},{4,20},{5,1},{6,22},{7,3},{8,24},{9,13},... | collective-permute-start | bytes 5455880 | tf_op jit(solution)/shard_map/ppermute | solution.py:708
  351.1 40.9 %collective-permute-start.17 = (bf16[192,4736]{1,0:T(8,128)(2,1)}, bf16[192,4736]{1,0:T(8,128)(2,1)}, u32[]{:S(2)}, u32[]{:S(2)}) collective-permute-start(bf16[192,4736]{1,0:T(8,128)(2,1)} %get-tuple-element.237), channel_id=1, source_target_pairs={{0,24},{1,7},{2,26},{3,1},{4,28},{5,3},{6,30},{7,5},{8,0},{9,15},{... | collective-permute-start | bytes 5455880 | tf_op jit(solution)/shard_map/ppermute | solution.py:708
  369.6 51.1 %collective-permute-start.8 = (bf16[192,4736]{1,0:T(8,128)(2,1)}, bf16[192,4736]{1,0:T(8,128)(2,1)S(1)}, u32[]{:S(2)}, u32[]{:S(2)}) collective-permute-start(bf16[192,4736]{1,0:T(8,128)(2,1)} %get-tuple-element.216), channel_id=1, source_target_pairs={{0,8},{1,3},{2,10},{3,5},{4,12},{5,7},{6,14},{7,1},{8,16},{9,11},{... | collective-permute-start | bytes 5455880 | tf_op jit(solution)/shard_map/ppermute | solution.py:708
  369.6 72.6 %collective-permute-start.9 = (bf16[192,4736]{1,0:T(8,128)(2,1)}, bf16[192,4736]{1,0:T(8,128)(2,1)}, u32[]{:S(2)}, u32[]{:S(2)}) collective-permute-start(bf16[192,4736]{1,0:T(8,128)(2,1)} %get-tuple-element.217), channel_id=1, source_target_pairs={{0,16},{1,5},{2,18},{3,7},{4,20},{5,1},{6,22},{7,3},{8,24},{9,13},... | collective-permute-start | bytes 5455880 | tf_op jit(solution)/shard_map/ppermute | solution.py:708
  371.8 70.4 %collective-permute-start.10 = (bf16[192,4736]{1,0:T(8,128)(2,1)}, bf16[192,4736]{1,0:T(8,128)(2,1)}, u32[]{:S(2)}, u32[]{:S(2)}) collective-permute-start(bf16[192,4736]{1,0:T(8,128)(2,1)} %get-tuple-element.218), channel_id=1, source_target_pairs={{0,24},{1,7},{2,26},{3,1},{4,28},{5,3},{6,30},{7,5},{8,0},{9,15},{... | collective-permute-start | bytes 5455880 | tf_op jit(solution)/shard_map/ppermute | solution.py:708
  391.7 25.0 %collective-permute-start.11 = (f32[384,768]{1,0:T(8,128)S(1)}, f32[384,768]{1,0:T(8,128)}, u32[]{:S(2)}, u32[]{:S(2)}) collective-permute-start(f32[384,768]{1,0:T(8,128)S(1)} %copy-done), channel_id=1, source_target_pairs={{0,32},{32,0},{64,96},{96,64},{1,33},{33,1},{65,97},{97,65},{2,34}... | collective-permute-start | bytes 3538952 | tf_op jit(solution)/shard_map/ppermute | solution.py:591
  399.0 52.7 %collective-permute-start.18 = (bf16[48,4736]{1,0:T(8,128)(2,1)}, bf16[48,4736]{1,0:T(8,128)(2,1)S(1)}, u32[]{:S(2)}, u32[]{:S(2)}) collective-permute-start(bf16[48,4736]{1,0:T(8,128)(2,1)} %get-tuple-element.239), channel_id=1, source_target_pairs={{0,2},{1,9},{2,4},{3,11},{4,6},{5,13},{6,0},{7,15},{8,10},{9,17},{... | collective-permute-start | bytes 1363976 | tf_op jit(solution)/shard_map/ppermute | solution.py:708
  416.7 36.2 %collective-permute-start.19 = (bf16[48,4736]{1,0:T(8,128)(2,1)}, bf16[48,4736]{1,0:T(8,128)(2,1)S(1)}, u32[]{:S(2)}, u32[]{:S(2)}) collective-permute-start(bf16[48,4736]{1,0:T(8,128)(2,1)} %get-tuple-element.240), channel_id=1, source_target_pairs={{0,4},{1,17},{2,6},{3,19},{4,0},{5,21},{6,2},{7,23},{8,12},{9,25},... | collective-permute-start | bytes 1363976 | tf_op jit(solution)/shard_map/ppermute | solution.py:708
  420.7 32.2 %collective-permute-start.20 = (bf16[48,4736]{1,0:T(8,128)(2,1)}, bf16[48,4736]{1,0:T(8,128)(2,1)S(1)}, u32[]{:S(2)}, u32[]{:S(2)}) collective-permute-start(bf16[48,4736]{1,0:T(8,128)(2,1)} %get-tuple-element.241), channel_id=1, source_target_pairs={{0,6},{1,25},{2,0},{3,27},{4,2},{5,29},{6,4},{7,31},{8,14},{9,1},{... | collective-permute-start | bytes 1363976 | tf_op jit(solution)/shard_map/ppermute | solution.py:708
  449.3 13.9 %collective-permute-start.12 = (bf16[48,4736]{1,0:T(8,128)(2,1)}, bf16[48,4736]{1,0:T(8,128)(2,1)S(1)}, u32[]{:S(2)}, u32[]{:S(2)}) collective-permute-start(bf16[48,4736]{1,0:T(8,128)(2,1)} %get-tuple-element.228), channel_id=1, source_target_pairs={{0,2},{1,9},{2,4},{3,11},{4,6},{5,13},{6,0},{7,15},{8,10},{9,17},{... | collective-permute-start | bytes 1363976 | tf_op jit(solution)/shard_map/ppermute | solution.py:708
  449.3 13.9 %collective-permute-start.13 = (bf16[48,4736]{1,0:T(8,128)(2,1)}, bf16[48,4736]{1,0:T(8,128)(2,1)S(1)}, u32[]{:S(2)}, u32[]{:S(2)}) collective-permute-start(bf16[48,4736]{1,0:T(8,128)(2,1)} %get-tuple-element.229), channel_id=1, source_target_pairs={{0,4},{1,17},{2,6},{3,19},{4,0},{5,21},{6,2},{7,23},{8,12},{9,25},... | collective-permute-start | bytes 1363976 | tf_op jit(solution)/shard_map/ppermute | solution.py:708
  451.7 12.1 %collective-permute-start.14 = (bf16[48,4736]{1,0:T(8,128)(2,1)}, bf16[48,4736]{1,0:T(8,128)(2,1)S(1)}, u32[]{:S(2)}, u32[]{:S(2)}) collective-permute-start(bf16[48,4736]{1,0:T(8,128)(2,1)} %get-tuple-element.230), channel_id=1, source_target_pairs={{0,6},{1,25},{2,0},{3,27},{4,2},{5,29},{6,4},{7,31},{8,14},{9,1},{... | collective-permute-start | bytes 1363976 | tf_op jit(solution)/shard_map/ppermute | solution.py:708
  469.1 8.2 %collective-permute-start.21 = (bf16[24,4736]{1,0:T(8,128)(2,1)}, bf16[24,4736]{1,0:T(8,128)(2,1)S(1)}, u32[]{:S(2)}, u32[]{:S(2)}) collective-permute-start(bf16[24,4736]{1,0:T(8,128)(2,1)} %get-tuple-element.243), channel_id=1, source_target_pairs={{0,32},{32,0},{64,96},{96,64},{1,33},{33,1},{65,97},{97,65},{2,34}... | collective-permute-start | bytes 681992 | tf_op jit(solution)/shard_map/ppermute | solution.py:591
  469.4 8.0 %collective-permute-start.22 = (bf16[24,4736]{1,0:T(8,128)(2,1)}, bf16[24,4736]{1,0:T(8,128)(2,1)S(1)}, u32[]{:S(2)}, u32[]{:S(2)}) collective-permute-start(bf16[24,4736]{1,0:T(8,128)(2,1)} %get-tuple-element.244), channel_id=1, source_target_pairs={{0,1},{1,0},{2,3},{3,2},{4,5},{5,4},{6,7},{7,6},{8,9},{9,8},{10,11... | collective-permute-start | bytes 681992 | tf_op jit(solution)/shard_map/ppermute | solution.py:587
  472.5 9.8 %collective-permute-start.23 = (bf16[24,4736]{1,0:T(8,128)(2,1)}, bf16[24,4736]{1,0:T(8,128)(2,1)S(1)}, u32[]{:S(2)}, u32[]{:S(2)}) collective-permute-start(bf16[24,4736]{1,0:T(8,128)(2,1)} %get-tuple-element.245), channel_id=1, source_target_pairs={{0,33},{1,32},{2,35},{3,34},{4,37},{5,36},{6,39},{7,38},{8,41},{9,... | collective-permute-start | bytes 681992 | tf_op jit(solution)/shard_map/ppermute | solution.py:780
  (19 other events, 152.9 us)
Sparse Core Ops, SparseCore 0:
  24.6 105.4 all-gather.1

commit v7 on v6

--- a/solution.py
+++ b/solution.py
@@ -76,6 +76,23 @@
         return pltpu.make_async_copy(src, yes, sem)
 
 
+def result_out(home, value, result, rounded, send, copies):
+    sem = copies.sems.at[copies.used]
+    copies.used += 1
+
+    @pl.when(home == 1)
+    def _():
+        copy = pltpu.make_async_copy(value, result, sem)
+        copy.start()
+        copy.wait()
+
+    @pl.when(home != 1)
+    def _():
+        copy = pltpu.make_async_copy(rounded, send, sem)
+        copy.start()
+        copy.wait()
+
+
 def forward_kernel(d, ff, chunks, base, first, idx, x_in, g, g3, ids_col, ids_row, ngain, gains, ubias, obias, spread, *refs):
     @pl.when(idx[0] == 1)
     def _():
@@ -85,7 +102,7 @@
 def forward_work(d, ff, chunks, base, first, idx, x_in, g, g3, ids_col, ids_row, ngain, gains, ubias, obias, spread, *refs):
     refs = refs[13:]
     ybf, xs, qs, ks, vs, ns, nrs, gps, es, small, kept, sent, y_out, y_send = refs[:14]
-    (x_v, h_v, w_v, u_v, d_v, a_v, q_v, k_v, v_v, n_v, r_v, act_v, gp_v, e_v, rs_v, att_v, acc_v, y_v, ins, outs) = refs[14:]
+    (x_v, h_v, w_v, u_v, d_v, a_v, q_v, k_v, v_v, n_v, r_v, act_v, gp_v, e_v, rs_v, att_v, acc_v, y_v, yb_v, ins, outs) = refs[14:]
     rows = x_v.shape[0]
     fc = ff // chunks
     core, slot, home = idx[1], idx[2], idx[3]
@@ -170,7 +187,8 @@
     y = keep * (keep * x_v[...].astype(F32) + acc_v[...] + mm(att_v[...], a_v[...]) + obias[...])
     y_v[...] = y
     ybf[...] = y.astype(BF)
-    pending.append(cout.either(home, y_v, y_out.at[slot], y_send))
+    yb_v[...] = y.astype(BF)
+    result_out(home, y_v, y_out.at[slot], yb_v, y_send, cout)
     for copy in pending:
         copy.wait()
 
@@ -186,7 +204,7 @@
     refs = refs[9 + 5 :]
     gbf, kept, sent, table, gr_out, gr_send = refs[:6]
     (g_v, gb_v, w_v, u_v, d_v, a_v, x_v, q_v, k_v, v_v, n_v, r_v, gp_v, e_v, rs_v, gat_v, gqt_v, gk_v,
-     gq_b, gk_b, gv_b, gj_v, acc_v, out_v, sm_v, ins, outs) = refs[6:]
+     gq_b, gk_b, gv_b, gj_v, acc_v, out_v, ob_v, sm_v, ins, outs) = refs[6:]
     rows = x_v.shape[0]
     fc = ff // chunks
     groups = fc // WIDE
@@ -286,7 +304,8 @@
     out = keep * (keep * g_v[...].astype(F32) + gmask)
     out_v[...] = out
     gbf[...] = out.astype(BF)
-    pending.append(cout.either(home, out_v, gr_out.at[slot], gr_send))
+    ob_v[...] = out.astype(BF)
+    result_out(home, out_v, gr_out.at[slot], ob_v, gr_send, cout)
     for copy in pending:
         copy.wait()
 
@@ -442,9 +461,13 @@
         away[...] = jnp.where(odd == 1, lower, upper).astype(away.dtype)
 
 
-def place_kernel(idx, y_in, y_got, g_in, g_got, y_out, g_out, sems):
+def place_kernel(idx, y_in, y_got, g_in, g_got, y_out, g_out, y_v, g_v, sems):
     copies = Copies(sems)
-    for copy in [copies.start(y_got, y_out.at[1 - idx[3]]), copies.start(g_got, g_out.at[1 - idx[3]])]:
+    pending = []
+    for got, wide_v, out in ((y_got, y_v, y_out), (g_got, g_v, g_out)):
+        wide_v[...] = got[...].astype(F32)
+        pending.append(copies.start(wide_v, out.at[1 - idx[3]]))
+    for copy in pending:
         copy.wait()
 
 
@@ -668,7 +691,7 @@
     operands = [[stash(rows, stacked), stash(rows, stacked)] for _ in range(2)]
     kept = [[stash(rows, d) for _ in range(4)] + [stash(rows, 2 * d), stash(rows, 2 * d), stash(chunks, rows, fc),
              stash(heads, rows, rows), stash(16, rows, dtype=F32)] for _ in range(2)]
-    results = [stash(slots, rows, d, dtype=F32), stash(rows, d, dtype=F32)]
+    results = [stash(slots, rows, d, dtype=F32), stash(rows, d)]
     here_x = toks
     for t in range(4):
         layer = t % 2
@@ -682,7 +705,7 @@
             kept[layer][:9] + operands[layer] + results,
             [V((rows, d), BF), V((rows, d), BF)] + weights_v
             + [V((rows, d), BF)] * 3 + [V((rows, 2 * d), BF)] * 2 + [V((chunks, rows, fc), BF)] * 2
-            + [V((heads, rows, rows), BF), V((16, rows), F32), V((rows, d), BF), V((rows, d), F32), V((rows, d), F32)]
+            + [V((heads, rows, rows), BF), V((16, rows), F32), V((rows, d), BF), V((rows, d), F32), V((rows, d), F32), V((rows, d), BF)]
             + sems,
             1 << 10,
         )
@@ -691,7 +714,7 @@
     y_out, y_send = results
     y_got = paired(y_send)
 
-    results = [stash(slots, rows, d, dtype=F32), stash(rows, d, dtype=F32)]
+    results = [stash(slots, rows, d, dtype=F32), stash(rows, d)]
     tables = [stash(1, stacked, dtype=F32) for _ in range(2)]
     width = 6 * d + LANES
     share = 2 * dshare
@@ -742,7 +765,7 @@
             + [V((rows, d), BF)] * 4 + [V((rows, 2 * d), BF)] * 2
             + [V((chunks, rows, fc), BF), V((heads, rows, rows), BF), V((16, rows), F32)]
             + [V((d, rows), BF), V((d, rows), F32), V((rows, d), F32)]
-            + [V((rows, d), BF)] * 3 + [V((chunks, rows, fc), BF), V((rows, d), F32), V((rows, d), F32), V((1, stacked), F32)]
+            + [V((rows, d), BF)] * 3 + [V((chunks, rows, fc), BF), V((rows, d), F32), V((rows, d), F32), V((rows, d), BF), V((1, stacked), F32)]
             + sems,
             1 << 10,
         )
@@ -755,15 +778,15 @@
         if t >= 2:
             swaps.append((along(operands[layer][1], 1, 2, 1), along(tables[layer], 1, 2, 1)))
     gr_got = paired(results[1])
-    legs = [leg(grads_by_place(1, *swaps[0]), 0), leg(grads_by_place(0, *swaps[1]), 0)]
-    legs[1], gr_got = lax.optimization_barrier((legs[1], gr_got))
+    upper, gr_got = lax.optimization_barrier((grads_by_place(1, *swaps[0]), gr_got))
+    legs = [leg(upper, 0), leg(grads_by_place(0, *swaps[1]), 0)]
     arrived = [leg(by_second_axis(came), 1) for came in legs]
     gr_out = results[0]
     y_out, gr_out = pl.pallas_call(
         place_kernel,
         grid_spec=pltpu.PrefetchScalarGridSpec(
             num_scalar_prefetch=1, grid=(1,), in_specs=[ANY, whole((rows, d)), ANY, whole((rows, d))], out_specs=[ANY] * 2,
-            scratch_shapes=[pltpu.SemaphoreType.DMA((2,))],
+            scratch_shapes=[V((rows, d), F32), V((rows, d), F32), pltpu.SemaphoreType.DMA((2,))],
         ),
         out_shape=[jax.ShapeDtypeStruct(y_out.shape, F32)] * 2,
         input_output_aliases={1: 0, 3: 1},

time: 499 us -> 498 us (level)
    ppermute x4, waiting for transfers between devices: 26.3 us -> 10.2 us  [paired(): return lax.ppermute(x, 'section', [(0, 1), (1, 0), (2, 3), (3, 2)])]
    ppermute x12, waiting for transfers between devices: 30.5 us -> 43.1 us  [moved(): return lax.ppermute(x, 'dp', [(i, to(i)) for i in range(ranks)])]
  transfers between devices with their start and end apart: 25 -> 25, of which waited for: 11 -> 13; matrix products, arithmetic and copies ran while one was open for 2% -> 2% of each run, Pallas kernels for 19% -> 13%
where the time goes in v7:
time: 498 us; the launch traced here: 495 us
  waiting for transfers between devices  229 us (46%)
  Pallas kernels  179 us (36%)
  starting transfers between devices  56.4 us (11%)
  between operations  14.7 us (3%)
  other arithmetic  10.4 us (2%)
  local copies, waits for them, and re-layouts  5.67 us (1%)
    pallas_call x8, Pallas kernels, call(): pl.pallas_call(kernel, grid_spec=pltpu.PrefetchScalarGridSpec(num_scalar_...  119 us
    all_gather x1, waiting for transfers between devices, body(): g = lax.all_gather(both, 'dp', axis=0, tiled=True)  99 us
    ppermute x1, waiting for transfers between devices, body(): here_g = lax.ppermute(gbf, 'section', [(3, 0), (2, 1)]) if t == 1 else gbf  58.6 us
    pallas_call x6, Pallas kernels, simple(): pl.pallas_call(kernel, grid_spec=pltpu.PrefetchScalarGridSpec(num_scalar_...  50.7 us
    ppermute x12, waiting for transfers between devices, moved(): return lax.ppermute(x, 'dp', [(i, to(i)) for i in range(ranks)])  43.1 us
    ppermute x12, starting transfers between devices, moved(): return lax.ppermute(x, 'dp', [(i, to(i)) for i in range(ranks)])  41.5 us
    ppermute x1, waiting for transfers between devices, body(): here_x = lax.ppermute(ybf, 'section', [(0, 3), (1, 2)]) if t == 1 else ybf  11.8 us
    ppermute x4, waiting for transfers between devices, paired(): return lax.ppermute(x, 'section', [(0, 1), (1, 0), (2, 3), (3, 2)])  10.2 us
  transfers between devices with their start and end apart: 25, of which 13 were waited for; matrix products, arithmetic and copies ran while one was open for 2% of the time, Pallas kernels for 13%

profile of v7, /device:TPU:1, one launch (start us, length us, event | category | flops | bytes accessed | tf_op | source)
XLA Modules:
  0.0 495.3 jit_solution(3847603055947140048)
XLA Ops:
  12.5 9.7 %collective-permute-done = bf16[24,9344]{1,0:T(8,128)(2,1)S(1)} collective-permute-done((bf16[24,9344]{1,0:T(8,128)(2,1)}, bf16[24,9344]{1,0:T(8,128)(2,1)S(1)}, u32[]{:S(2)}, u32[]{:S(2)}) %collective-permute-start) | collective-permute-done | bytes 448544 | tf_op jit(solution)/shard_map/ppermute | solution.py:614
  31.2 99.0 %all-gather.2.cloned.1.call-done.g = bf16[768,18688]{1,0:T(8,128)(2,1)} async-done(((bf16[24,18688]{1,0:T(8,128)(2,1)}), bf16[768,18688]{1,0:T(8,128)(2,1)}) %all-gather.2.cloned.1.call-update) | async-done | bytes 28704784 | tf_op jit(solution)/shard_map/all_gather | solution.py:652
  130.1 3.6 shard_map.187
  133.7 18.4 %shard_map.201 = (bf16[384,768]{1,0:T(8,128)(2,1)}, bf16[384,768]{1,0:T(8,128)(2,1)}, bf16[384,768]{1,0:T(8,128)(2,1)}, bf16[384,768]{1,0:T(8,128)(2,1)}, bf16[3...) custom-call(s32[4]{0:T(128)} %get-tuple-element.254.idx, ...), custom_call_target="tpu_custom_call", output_to_operand_aliasing={{1}: (11, {}), {2}: (12, {}), {3}: (13, {}), {4}: (14, {}),... | custom-call | flops 1024 | bytes 1024 | tf_op jit(solution)/shard_map/pallas_call | solution.py:566
  152.1 18.2 %shard_map.213 = (bf16[384,768]{1,0:T(8,128)(2,1)}, bf16[384,768]{1,0:T(8,128)(2,1)}, bf16[384,768]{1,0:T(8,128)(2,1)}, bf16[384,768]{1,0:T(8,128)(2,1)}, bf16[3...) custom-call(s32[4]{0:T(128)} %pad_add_fusion.idx, ...), custom_call_target="tpu_custom_call", output_to_operand_aliasing={{1}: (11, {}), {2}: (12, {}), {3}: (13, {}), {4}: (14, {}),... | custom-call | flops 1024 | bytes 1024 | tf_op jit(solution)/shard_map/pallas_call | solution.py:566
  172.9 11.8 %collective-permute-done.1.x_in = bf16[384,768]{1,0:T(8,128)(2,1)S(1)} collective-permute-done((bf16[384,768]{1,0:T(8,128)(2,1)}, bf16[384,768]{1,0:T(8,128)(2,1)S(1)}, u32[]{:S(2)}, u32[]{:S(2)}) %collective-permute-start.1) | collective-permute-done | bytes 589856 | tf_op jit(solution)/shard_map/ppermute | solution.py:713
  185.5 4.0 shard_map.214
  189.5 15.5 %shard_map.215 = (bf16[384,768]{1,0:T(8,128)(2,1)}, bf16[384,768]{1,0:T(8,128)(2,1)}, bf16[384,768]{1,0:T(8,128)(2,1)}, bf16[384,768]{1,0:T(8,128)(2,1)}, bf16[3...) custom-call(s32[4]{0:T(128)} %pad_add_fusion.1.idx, ...), custom_call_target="tpu_custom_call", output_to_operand_aliasing={{1}: (11, {}), {2}: (12, {}), {3}: (13, {}), {4}: (14, {}),... | custom-call | flops 1024 | bytes 1024 | tf_op jit(solution)/shard_map/pallas_call | solution.py:566
  205.0 9.3 %shard_map.219 = (bf16[384,768]{1,0:T(8,128)(2,1)}, bf16[384,6144]{1,0:T(8,128)(2,1)}, bf16[384,6144]{1,0:T(8,128)(2,1)}, f32[1,6144]{1,0:T(1,128)}, f32[2,384,768]{2,1,0:T(8,128)}, /*index=5*/bf16[384,768]{1,0:T(8,128)(2,1)}) custom-call(s32[4]{0:T(128)} %pad_add_fusion.1.idx, ...), custom_call_target="tpu_custom_call", output_to_operand_aliasing={{1}: (17, {}), {2}: (18, {}), {3}: (19, {}), {4}: (20, {}),... | custom-call | flops 1024 | bytes 1024 | tf_op jit(solution)/shard_map/pallas_call | solution.py:566
  214.4 9.3 %shard_map.221 = (bf16[384,768]{1,0:T(8,128)(2,1)}, bf16[384,6144]{1,0:T(8,128)(2,1)}, bf16[384,6144]{1,0:T(8,128)(2,1)}, f32[1,6144]{1,0:T(1,128)}, f32[2,384,768]{2,1,0:T(8,128)}, /*index=5*/bf16[384,768]{1,0:T(8,128)(2,1)}) custom-call(s32[4]{0:T(128)} %get-tuple-element.256.idx, ...), custom_call_target="tpu_custom_call", output_to_operand_aliasing={{1}: (17, {}), {2}: (18, {}), {3}: (19, {}), {4}: (20, {}),... | custom-call | flops 1024 | bytes 1024 | tf_op jit(solution)/shard_map/pallas_call | solution.py:566
  226.2 58.6 %collective-permute-done.2.g_in = bf16[384,768]{1,0:T(8,128)(2,1)S(1)} collective-permute-done((bf16[384,768]{1,0:T(8,128)(2,1)}, bf16[384,768]{1,0:T(8,128)(2,1)S(1)}, u32[]{:S(2)}, u32[]{:S(2)}) %collective-permute-start.2) | collective-permute-done | bytes 589856 | tf_op jit(solution)/shard_map/ppermute | solution.py:773
  285.8 22.3 %shard_map.222 = (bf16[384,768]{1,0:T(8,128)(2,1)}, bf16[384,6144]{1,0:T(8,128)(2,1)}, bf16[384,6144]{1,0:T(8,128)(2,1)}, f32[1,6144]{1,0:T(1,128)}, f32[2,384,768]{2,1,0:T(8,128)}, /*index=5*/bf16[384,768]{1,0:T(8,128)(2,1)}) custom-call(s32[4]{0:T(128)} %pad_add_fusion.idx, ...), custom_call_target="tpu_custom_call", output_to_operand_aliasing={{1}: (17, {}), {2}: (18, {}), {3}: (19, {}), {4}: (20, {}),... | custom-call | flops 1024 | bytes 1024 | tf_op jit(solution)/shard_map/pallas_call | solution.py:566
  309.6 22.2 %shard_map.223 = (bf16[384,768]{1,0:T(8,128)(2,1)}, bf16[384,6144]{1,0:T(8,128)(2,1)}, bf16[384,6144]{1,0:T(8,128)(2,1)}, f32[1,6144]{1,0:T(1,128)}, f32[2,384,768]{2,1,0:T(8,128)}, /*index=5*/bf16[384,768]{1,0:T(8,128)(2,1)}) custom-call(s32[4]{0:T(128)} %get-tuple-element.254.idx, ...), custom_call_target="tpu_custom_call", output_to_operand_aliasing={{1}: (17, {}), {2}: (18, {}), {3}: (19, {}), {4}: (20, {}),... | custom-call | flops 1024 | bytes 1024 | tf_op jit(solution)/shard_map/pallas_call | solution.py:566
  333.8 13.1 %shard_map.224 = (bf16[192,4736]{1,0:T(8,128)(2,1)}, bf16[192,4736]{1,0:T(8,128)(2,1)}, bf16[192,4736]{1,0:T(8,128)(2,1)}, bf16[192,4736]{1,0:T(8,128)(2,1)}) custom-call(s32[5]{0:T(128)} %stack.45.idx, f32[128,768]{1,0:T(8,128)} %fusion.2.place, f32[1,6144]{1,0:T(1,128)} %get-tuple-element.209.mine, f32[1,6144]{1,0:T(1,128)} %copy-done.17, ...), custom_call_target="tpu_custom_call" | custom-call | flops 1024 | bytes 1024 | tf_op jit(solution)/shard_map/pallas_call | solution.py:592
  355.6 13.2 %shard_map.226 = (bf16[192,4736]{1,0:T(8,128)(2,1)}, bf16[192,4736]{1,0:T(8,128)(2,1)}, bf16[192,4736]{1,0:T(8,128)(2,1)}, bf16[192,4736]{1,0:T(8,128)(2,1)}) custom-call(s32[5]{0:T(128)} %stack.45.idx, f32[128,768]{1,0:T(8,128)} %fusion.2.place, f32[1,6144]{1,0:T(1,128)} %get-tuple-element.223.mine, f32[1,6144]{1,0:T(1,128)} %copy-done.18, ...), custom_call_target="tpu_custom_call" | custom-call | flops 1024 | bytes 1024 | tf_op jit(solution)/shard_map/pallas_call | solution.py:592
  371.9 19.3 %collective-permute-done.16.refs_2_ = bf16[192,4736]{1,0:T(8,128)(2,1)} collective-permute-done((bf16[192,4736]{1,0:T(8,128)(2,1)}, bf16[192,4736]{1,0:T(8,128)(2,1)}, u32[]{:S(2)}, u32[]{:S(2)}) %collective-permute-start.16) | collective-permute-done | bytes 1818656 | tf_op jit(solution)/shard_map/ppermute | solution.py:731
  391.5 7.0 %shard_map.228 = (bf16[48,4736]{1,0:T(8,128)(2,1)}, bf16[48,4736]{1,0:T(8,128)(2,1)}, bf16[48,4736]{1,0:T(8,128)(2,1)}, bf16[48,4736]{1,0:T(8,128)(2,1)}) custom-call(s32[5]{0:T(128)} %stack.45.idx, bf16[192,4736]{1,0:T(8,128)(2,1)} %get-tuple-element.234.refs_0_, bf16[192,4736]{1,0:T(8,128)(2,1)} %copy-done.2, ...), custom_call_target="tpu_custom_call" | custom-call | flops 1024 | bytes 1024 | tf_op jit(solution)/shard_map/pallas_call | solution.py:592
  402.7 12.8 %collective-permute-done.9.refs_1_ = bf16[192,4736]{1,0:T(8,128)(2,1)S(1)} collective-permute-done((bf16[192,4736]{1,0:T(8,128)(2,1)}, bf16[192,4736]{1,0:T(8,128)(2,1)S(1)}, u32[]{:S(2)}, u32[]{:S(2)}) %collective-permute-start.9) | collective-permute-done | bytes 1818656 | tf_op jit(solution)/shard_map/ppermute | solution.py:731
  415.5 26.1 %collective-permute-start.20 = (bf16[48,4736]{1,0:T(8,128)(2,1)}, bf16[48,4736]{1,0:T(8,128)(2,1)S(1)}, u32[]{:S(2)}, u32[]{:S(2)}) collective-permute-start(bf16[48,4736]{1,0:T(8,128)(2,1)} %get-tuple-element.241), channel_id=1, source_target_pairs={{0,6},{1,25},{2,0},{3,27},{4,2},{5,29},{6,4},{7,31},{8,14},{9,1},{... | collective-permute-start | bytes 1363976 | tf_op jit(solution)/shard_map/ppermute | solution.py:731
  441.6 7.0 %shard_map.227 = (bf16[48,4736]{1,0:T(8,128)(2,1)}, bf16[48,4736]{1,0:T(8,128)(2,1)}, bf16[48,4736]{1,0:T(8,128)(2,1)}, bf16[48,4736]{1,0:T(8,128)(2,1)}) custom-call(s32[5]{0:T(128)} %stack.45.idx, bf16[192,4736]{1,0:T(8,128)(2,1)} %get-tuple-element.226.refs_0_, bf16[192,4736]{1,0:T(8,128)(2,1)} %copy-done.1, ...), custom_call_target="tpu_custom_call" | custom-call | flops 1024 | bytes 1024 | tf_op jit(solution)/shard_map/pallas_call | solution.py:592
  452.9 9.6 %collective-permute-done.12.refs_1_ = bf16[48,4736]{1,0:T(8,128)(2,1)S(1)} collective-permute-done((bf16[48,4736]{1,0:T(8,128)(2,1)}, bf16[48,4736]{1,0:T(8,128)(2,1)S(1)}, u32[]{:S(2)}, u32[]{:S(2)}) %collective-permute-start.12) | collective-permute-done | bytes 454688 | tf_op jit(solution)/shard_map/ppermute | solution.py:731
  463.9 4.6 shard_map.229
  476.5 5.2 %collective-permute-done.23.c_in = bf16[24,4736]{1,0:T(8,128)(2,1)S(1)} collective-permute-done((bf16[24,4736]{1,0:T(8,128)(2,1)}, bf16[24,4736]{1,0:T(8,128)(2,1)S(1)}, u32[]{:S(2)}, u32[]{:S(2)}) %collective-permute-start.23) | collective-permute-done | bytes 227360 | tf_op jit(solution)/shard_map/ppermute | solution.py:803
  482.4 5.9 %shard_map.230 = (f32[24,5376]{1,0:T(8,128)}, f32[24,768]{1,0:T(8,128)}, f32[96,768]{1,0:T(8,128)}, f32[1,24]{1,0:T(1,128)}, f32[1,2]{1,0:T(1,128)}, /*index=5*/...) custom-call(s32[5]{0:T(128)} %stack.45.idx, f32[24,4736]{1,0:T(8,128)} %get-tuple-element.242.own, ...), custom_call_target="tpu_custom_call" | custom-call | flops 1024 | bytes 1024 | tf_op jit(solution)/shard_map/pallas_call | solution.py:592
  (134 shorter events, 55.0 us)
Async XLA Ops:
  7.2 123.0 %all-gather.2.cloned.1.call-start = ((), (), s32[]{:S(2)}) async-start(), calls=%async_computation | async-start | bytes 29601792 | tf_op jit(solution)/shard_map/all_gather | solution.py:652
  10.5 11.8 %collective-permute-start = (bf16[24,9344]{1,0:T(8,128)(2,1)}, bf16[24,9344]{1,0:T(8,128)(2,1)S(1)}, u32[]{:S(2)}, u32[]{:S(2)}) collective-permute-start(bf16[24,9344]{1,0:T(8,128)(2,1)} %shard_map.186), channel_id=1, source_target_pairs={{0,32},{32,0},{64,96},{96,64},{1,33},{33,1},{65,97},{97,65},{2,34}... | collective-permute-start | bytes 1345544 | tf_op jit(solution)/shard_map/ppermute | solution.py:614
  170.3 14.4 %collective-permute-start.1 = (bf16[384,768]{1,0:T(8,128)(2,1)}, bf16[384,768]{1,0:T(8,128)(2,1)S(1)}, u32[]{:S(2)}, u32[]{:S(2)}) collective-permute-start(bf16[384,768]{1,0:T(8,128)(2,1)} %get-tuple-element.139), channel_id=1, source_target_pairs={{0,96},{32,64},{1,97},{33,65},{2,98},{34,66},{3,99},{35,67},{4,100... | collective-permute-start | bytes 1769480 | tf_op jit(solution)/shard_map/ppermute | solution.py:713
  223.7 61.1 %collective-permute-start.2 = (bf16[384,768]{1,0:T(8,128)(2,1)}, bf16[384,768]{1,0:T(8,128)(2,1)S(1)}, u32[]{:S(2)}, u32[]{:S(2)}) collective-permute-start(bf16[384,768]{1,0:T(8,128)(2,1)} %get-tuple-element.193), channel_id=1, source_target_pairs={{96,0},{64,32},{97,1},{65,33},{98,2},{66,34},{99,3},{67,35},{100,4... | collective-permute-start | bytes 1769480 | tf_op jit(solution)/shard_map/ppermute | solution.py:773
  225.0 59.8 %collective-permute-start.3 = (bf16[384,768]{1,0:T(8,128)(2,1)S(1)}, bf16[384,768]{1,0:T(8,128)(2,1)S(1)}, u32[]{:S(2)}, u32[]{:S(2)}) collective-permute-start(bf16[384,768]{1,0:T(8,128)(2,1)S(1)} %copy-done), channel_id=1, source_target_pairs={{0,32},{32,0},{64,96},{96,64},{1,33},{33,1},{65,97},{97,65},{2,34}... | collective-permute-start | bytes 1769480 | tf_op jit(solution)/shard_map/ppermute | solution.py:614
  308.1 23.7 %collective-permute-start.4 = (bf16[384,6144]{1,0:T(8,128)(2,1)}, bf16[384,6144]{1,0:T(8,128)(2,1)}, u32[]{:S(2)}, u32[]{:S(2)}) collective-permute-start(bf16[384,6144]{1,0:T(8,128)(2,1)} %get-tuple-element.211), channel_id=1, source_target_pairs={{0,1},{1,0},{2,3},{3,2},{4,5},{5,4},{6,7},{7,6},{8,9},{9,8},{10,11... | collective-permute-start | bytes 14155784 | tf_op jit(solution)/shard_map/ppermute | solution.py:610
  309.5 22.3 %collective-permute-start.5 = (f32[1,6144]{1,0:T(1,128)}, f32[1,6144]{1,0:T(1,128)S(1)}, u32[]{:S(2)}, u32[]{:S(2)}) collective-permute-start(f32[1,6144]{1,0:T(1,128)} %get-tuple-element.209.mine), channel_id=1, source_target_pairs={{0,1},{1,0},{2,3},{3,2},{4,5},{5,4},{6,7},{7,6},{8,9},{9,8},{10,11... | collective-permute-start | bytes 73736 | tf_op jit(solution)/shard_map/ppermute | solution.py:610
  331.8 23.1 %collective-permute-start.8 = (bf16[384,6144]{1,0:T(8,128)(2,1)}, bf16[384,6144]{1,0:T(8,128)(2,1)}, u32[]{:S(2)}, u32[]{:S(2)}) collective-permute-start(bf16[384,6144]{1,0:T(8,128)(2,1)} %get-tuple-element.225), channel_id=1, source_target_pairs={{0,1},{1,0},{2,3},{3,2},{4,5},{5,4},{6,7},{7,6},{8,9},{9,8},{10,11... | collective-permute-start | bytes 14155784 | tf_op jit(solution)/shard_map/ppermute | solution.py:610
  332.3 15.1 %collective-permute-start.6 = (bf16[384,768]{1,0:T(8,128)(2,1)}, bf16[384,768]{1,0:T(8,128)(2,1)S(1)}, u32[]{:S(2)}, u32[]{:S(2)}) collective-permute-start(bf16[384,768]{1,0:T(8,128)(2,1)} %get-tuple-element.219), channel_id=1, source_target_pairs={{0,32},{32,0},{64,96},{96,64},{1,33},{33,1},{65,97},{97,65},{2,34}... | collective-permute-start | bytes 1769480 | tf_op jit(solution)/shard_map/ppermute | solution.py:614
  347.4 23.8 %collective-permute-start.15 = (bf16[192,4736]{1,0:T(8,128)(2,1)}, bf16[192,4736]{1,0:T(8,128)(2,1)S(1)}, u32[]{:S(2)}, u32[]{:S(2)}) collective-permute-start(bf16[192,4736]{1,0:T(8,128)(2,1)} %get-tuple-element.235), channel_id=1, source_target_pairs={{0,8},{1,3},{2,10},{3,5},{4,12},{5,7},{6,14},{7,1},{8,16},{9,11},{... | collective-permute-start | bytes 5455880 | tf_op jit(solution)/shard_map/ppermute | solution.py:731
  348.1 43.2 %collective-permute-start.16 = (bf16[192,4736]{1,0:T(8,128)(2,1)}, bf16[192,4736]{1,0:T(8,128)(2,1)}, u32[]{:S(2)}, u32[]{:S(2)}) collective-permute-start(bf16[192,4736]{1,0:T(8,128)(2,1)} %get-tuple-element.236), channel_id=1, source_target_pairs={{0,16},{1,5},{2,18},{3,7},{4,20},{5,1},{6,22},{7,3},{8,24},{9,13},... | collective-permute-start | bytes 5455880 | tf_op jit(solution)/shard_map/ppermute | solution.py:731
  350.7 40.8 %collective-permute-start.17 = (bf16[192,4736]{1,0:T(8,128)(2,1)}, bf16[192,4736]{1,0:T(8,128)(2,1)}, u32[]{:S(2)}, u32[]{:S(2)}) collective-permute-start(bf16[192,4736]{1,0:T(8,128)(2,1)} %get-tuple-element.237), channel_id=1, source_target_pairs={{0,24},{1,7},{2,26},{3,1},{4,28},{5,3},{6,30},{7,5},{8,0},{9,15},{... | collective-permute-start | bytes 5455880 | tf_op jit(solution)/shard_map/ppermute | solution.py:731
  368.8 46.7 %collective-permute-start.9 = (bf16[192,4736]{1,0:T(8,128)(2,1)}, bf16[192,4736]{1,0:T(8,128)(2,1)S(1)}, u32[]{:S(2)}, u32[]{:S(2)}) collective-permute-start(bf16[192,4736]{1,0:T(8,128)(2,1)} %get-tuple-element.227), channel_id=1, source_target_pairs={{0,8},{1,3},{2,10},{3,5},{4,12},{5,7},{6,14},{7,1},{8,16},{9,11},{... | collective-permute-start | bytes 5455880 | tf_op jit(solution)/shard_map/ppermute | solution.py:731
  368.9 72.7 %collective-permute-start.10 = (bf16[192,4736]{1,0:T(8,128)(2,1)}, bf16[192,4736]{1,0:T(8,128)(2,1)}, u32[]{:S(2)}, u32[]{:S(2)}) collective-permute-start(bf16[192,4736]{1,0:T(8,128)(2,1)} %get-tuple-element.228), channel_id=1, source_target_pairs={{0,16},{1,5},{2,18},{3,7},{4,20},{5,1},{6,22},{7,3},{8,24},{9,13},... | collective-permute-start | bytes 5455880 | tf_op jit(solution)/shard_map/ppermute | solution.py:731
  371.2 70.3 %collective-permute-start.11 = (bf16[192,4736]{1,0:T(8,128)(2,1)}, bf16[192,4736]{1,0:T(8,128)(2,1)}, u32[]{:S(2)}, u32[]{:S(2)}) collective-permute-start(bf16[192,4736]{1,0:T(8,128)(2,1)} %get-tuple-element.229), channel_id=1, source_target_pairs={{0,24},{1,7},{2,26},{3,1},{4,28},{5,3},{6,30},{7,5},{8,0},{9,15},{... | collective-permute-start | bytes 5455880 | tf_op jit(solution)/shard_map/ppermute | solution.py:731
  398.5 52.6 %collective-permute-start.18 = (bf16[48,4736]{1,0:T(8,128)(2,1)}, bf16[48,4736]{1,0:T(8,128)(2,1)S(1)}, u32[]{:S(2)}, u32[]{:S(2)}) collective-permute-start(bf16[48,4736]{1,0:T(8,128)(2,1)} %get-tuple-element.239), channel_id=1, source_target_pairs={{0,2},{1,9},{2,4},{3,11},{4,6},{5,13},{6,0},{7,15},{8,10},{9,17},{... | collective-permute-start | bytes 1363976 | tf_op jit(solution)/shard_map/ppermute | solution.py:731
  399.8 53.0 %collective-permute-start.19 = (bf16[48,4736]{1,0:T(8,128)(2,1)}, bf16[48,4736]{1,0:T(8,128)(2,1)S(1)}, u32[]{:S(2)}, u32[]{:S(2)}) collective-permute-start(bf16[48,4736]{1,0:T(8,128)(2,1)} %get-tuple-element.240), channel_id=1, source_target_pairs={{0,4},{1,17},{2,6},{3,19},{4,0},{5,21},{6,2},{7,23},{8,12},{9,25},... | collective-permute-start | bytes 1363976 | tf_op jit(solution)/shard_map/ppermute | solution.py:731
  415.5 37.4 %collective-permute-start.20 = (bf16[48,4736]{1,0:T(8,128)(2,1)}, bf16[48,4736]{1,0:T(8,128)(2,1)S(1)}, u32[]{:S(2)}, u32[]{:S(2)}) collective-permute-start(bf16[48,4736]{1,0:T(8,128)(2,1)} %get-tuple-element.241), channel_id=1, source_target_pairs={{0,6},{1,25},{2,0},{3,27},{4,2},{5,29},{6,4},{7,31},{8,14},{9,1},{... | collective-permute-start | bytes 1363976 | tf_op jit(solution)/shard_map/ppermute | solution.py:731
  448.6 13.9 %collective-permute-start.12 = (bf16[48,4736]{1,0:T(8,128)(2,1)}, bf16[48,4736]{1,0:T(8,128)(2,1)S(1)}, u32[]{:S(2)}, u32[]{:S(2)}) collective-permute-start(bf16[48,4736]{1,0:T(8,128)(2,1)} %get-tuple-element.231), channel_id=1, source_target_pairs={{0,2},{1,9},{2,4},{3,11},{4,6},{5,13},{6,0},{7,15},{8,10},{9,17},{... | collective-permute-start | bytes 1363976 | tf_op jit(solution)/shard_map/ppermute | solution.py:731
  448.6 13.9 %collective-permute-start.13 = (bf16[48,4736]{1,0:T(8,128)(2,1)}, bf16[48,4736]{1,0:T(8,128)(2,1)S(1)}, u32[]{:S(2)}, u32[]{:S(2)}) collective-permute-start(bf16[48,4736]{1,0:T(8,128)(2,1)} %get-tuple-element.232), channel_id=1, source_target_pairs={{0,4},{1,17},{2,6},{3,19},{4,0},{5,21},{6,2},{7,23},{8,12},{9,25},... | collective-permute-start | bytes 1363976 | tf_op jit(solution)/shard_map/ppermute | solution.py:731
  451.0 12.0 %collective-permute-start.14 = (bf16[48,4736]{1,0:T(8,128)(2,1)}, bf16[48,4736]{1,0:T(8,128)(2,1)S(1)}, u32[]{:S(2)}, u32[]{:S(2)}) collective-permute-start(bf16[48,4736]{1,0:T(8,128)(2,1)} %get-tuple-element.233), channel_id=1, source_target_pairs={{0,6},{1,25},{2,0},{3,27},{4,2},{5,29},{6,4},{7,31},{8,14},{9,1},{... | collective-permute-start | bytes 1363976 | tf_op jit(solution)/shard_map/ppermute | solution.py:731
  468.5 8.0 %collective-permute-start.21 = (bf16[24,4736]{1,0:T(8,128)(2,1)}, bf16[24,4736]{1,0:T(8,128)(2,1)S(1)}, u32[]{:S(2)}, u32[]{:S(2)}) collective-permute-start(bf16[24,4736]{1,0:T(8,128)(2,1)} %get-tuple-element.243), channel_id=1, source_target_pairs={{0,32},{32,0},{64,96},{96,64},{1,33},{33,1},{65,97},{97,65},{2,34}... | collective-permute-start | bytes 681992 | tf_op jit(solution)/shard_map/ppermute | solution.py:614
  469.7 6.8 %collective-permute-start.22 = (bf16[24,4736]{1,0:T(8,128)(2,1)}, bf16[24,4736]{1,0:T(8,128)(2,1)S(1)}, u32[]{:S(2)}, u32[]{:S(2)}) collective-permute-start(bf16[24,4736]{1,0:T(8,128)(2,1)} %get-tuple-element.244), channel_id=1, source_target_pairs={{0,1},{1,0},{2,3},{3,2},{4,5},{5,4},{6,7},{7,6},{8,9},{9,8},{10,11... | collective-permute-start | bytes 681992 | tf_op jit(solution)/shard_map/ppermute | solution.py:610
  473.1 8.7 %collective-permute-start.23 = (bf16[24,4736]{1,0:T(8,128)(2,1)}, bf16[24,4736]{1,0:T(8,128)(2,1)S(1)}, u32[]{:S(2)}, u32[]{:S(2)}) collective-permute-start(bf16[24,4736]{1,0:T(8,128)(2,1)} %get-tuple-element.245), channel_id=1, source_target_pairs={{0,33},{1,32},{2,35},{3,34},{4,37},{5,36},{6,39},{7,38},{8,41},{9,... | collective-permute-start | bytes 681992 | tf_op jit(solution)/shard_map/ppermute | solution.py:803
  (21 other events, 151.5 us)
Sparse Core Ops, SparseCore 0:
  24.6 105.4 all-gather.1

commit v8 on v7

--- a/solution.py
+++ b/solution.py
@@ -341,7 +341,7 @@
 
 
 def weight_grad_kernel(d, ff, idx, place, mine, theirs, kept, got, *refs):
-    results, (big_v, a_v, b_v, c_v, out_v, ins, outs) = refs[:4], refs[4:]
+    results, (big_v, a_v, b_v, c_v, out_v, ins, outs) = refs[:5], refs[5:]
     rows = kept.shape[0]
     tokens = 2 * rows
     quarter, half, third = WIDE // 4, ff // 2, ff // 3
@@ -365,15 +365,24 @@
 
     def send_by_y(cout, at, width):
         cols = pl.ds(at, width)
-        return [cout.start(out_v.at[pl.ds(pl.multiple_of(lax.rem(y + s, 4) * 4 * share, 16), 4 * share), cols], results[s].at[:, cols])
-                for s in (2, 1, 3, 0)]
+
+        def rows_of(s, first, count):
+            return out_v.at[pl.ds(pl.multiple_of(lax.rem(y + s, 4) * 4 * share + first, 16), count), cols]
+
+        return [cout.start(rows_of(2, 0, 2 * share), results[3].at[:, cols]),
+                cout.start(rows_of(2, 2 * share, 2 * share), results[4].at[:, cols])] + [
+            cout.start(rows_of(s, 0, 4 * share), results[r].at[:, cols]) for r, s in ((1, 1), (2, 3), (0, 0))]
 
     def send_by_z(cout, at, width):
         cols = pl.ds(at, width)
+
+        def rows_of(i, s):
+            return out_v.at[pl.ds(pl.multiple_of((4 * i + lax.rem(z + s, 4)) * share, 16), share), cols]
+
         return [
-            cout.start(out_v.at[pl.ds(pl.multiple_of((4 * i + lax.rem(z + s, 4)) * share, 16), share), cols],
-                       results[s].at[pl.ds(share * i, share), cols])
-            for s in (2, 1, 3, 0) for i in range(4)
+            cout.start(rows_of(i, s), results[r].at[pl.ds(share * (i - base), share), cols])
+            for r, s, base, count in ((3, 2, 0, 2), (4, 2, 2, 2), (1, 1, 0, 4), (2, 3, 0, 4), (0, 0, 0, 4))
+            for i in range(base, base + count)
         ]
 
     everything = slice(0, d)
@@ -437,8 +446,22 @@
     return jnp.concatenate([main.astype(BF), last], axis=1).reshape(shape)
 
 
+def relay_kernel(idx, up_in, down_in, up_got, down_got, up, down, up_v, down_v, ins, outs):
+    half = up_got.shape[0]
+    cin, cout = Copies(ins), Copies(outs)
+    pending = []
+    loads = [(cin.start(block.at[pl.ds(at, half)], hold), got, hold, out.at[pl.ds(at, half)])
+             for block, at, got, hold, out in ((up_in, 0, up_got, up_v, up), (down_in, half, down_got, down_v, down))]
+    for copy, got, hold, out in loads:
+        copy.wait()
+        hold[...] = added([hold, got])
+        pending.append(cout.start(hold, out))
+    for copy in pending:
+        copy.wait()
+
+
 def mid_kernel(idx, *refs):
-    came, outs, hold = refs[:4], refs[4:8], refs[8]
+    came, outs, hold = refs[:3], refs[3:7], refs[7]
     hold[...] = added(came).reshape(hold.shape)
     at = jnp.where(idx[2] == 0, idx[1], idx[0])
     for s in range(4):
@@ -735,13 +758,33 @@
             partial(weight_grad_kernel, d, ff), here,
             [place, tables[layer], table_got, operands[layer][0], got],
             [whole((LANES, d)), whole(table_got.shape), whole(table_got.shape), ANY, ANY],
-            [jax.ShapeDtypeStruct((side * share, width), BF)] * side, [ANY] * side,
+            [jax.ShapeDtypeStruct((side * share, width), BF)] * 3 + [jax.ShapeDtypeStruct((side // 2 * share, width), BF)] * 2,
+            [ANY] * 5,
             [V((2, rows, ff), BF), V((2, rows, d), BF), V((2, rows, d), BF), V((2, rows, 2 * d), BF), V((d, width), BF),
              pltpu.SemaphoreType.DMA((32,)), pltpu.SemaphoreType.DMA((32,))],
         )
 
-    def leg(outs, which):
-        far, near, back = (moved(outs[s], which, s) for s in (2, 1, 3))
+    def halves(made):
+        return moved(made[3], 0, 1), moved(made[4], 0, -1)
+
+    def first_leg(made, came):
+        own, up, down = made[:3]
+        part = (side // 2 * share, width)
+        up, down = pl.pallas_call(
+            relay_kernel,
+            grid_spec=pltpu.PrefetchScalarGridSpec(
+                num_scalar_prefetch=1, grid=(1,), in_specs=[ANY, ANY, whole(part), whole(part)], out_specs=[ANY] * 2,
+                scratch_shapes=[V(part, BF), V(part, BF), pltpu.SemaphoreType.DMA((2,)), pltpu.SemaphoreType.DMA((2,))],
+            ),
+            out_shape=[jax.ShapeDtypeStruct(up.shape, BF)] * 2,
+            input_output_aliases={1: 0, 2: 1},
+            compiler_params=pltpu.CompilerParams(dimension_semantics=("arbitrary",), vmem_limit_bytes=VMEM_LIMIT),
+            cost_estimate=pl.CostEstimate(flops=1 << 10, bytes_accessed=1 << 10, transcendentals=0),
+        )(here, up, down, *came)
+        return [own, moved(up, 0, 1), moved(down, 0, -1)]
+
+    def second_leg(outs):
+        far, near, back = (moved(outs[s], 1, s) for s in (2, 1, 3))
         return [outs[0], near, far, back]
 
     def by_second_axis(came):
@@ -779,8 +822,11 @@
             swaps.append((along(operands[layer][1], 1, 2, 1), along(tables[layer], 1, 2, 1)))
     gr_got = paired(results[1])
     upper, gr_got = lax.optimization_barrier((grads_by_place(1, *swaps[0]), gr_got))
-    legs = [leg(upper, 0), leg(grads_by_place(0, *swaps[1]), 0)]
-    arrived = [leg(by_second_axis(came), 1) for came in legs]
+    upper_came = halves(upper)
+    lower = grads_by_place(0, *swaps[1])
+    lower_came = halves(lower)
+    legs = [first_leg(upper, upper_came), first_leg(lower, lower_came)]
+    arrived = [second_leg(by_second_axis(came)) for came in legs]
     gr_out = results[0]
     y_out, gr_out = pl.pallas_call(
         place_kernel,

time: 498 us -> 489 us (0.982)
  starting transfers between devices: 56.4 us -> 36 us
  Pallas kernels: 179 us -> 188 us
  local copies, waits for them, and re-layouts: 5.67 us -> 11 us
    ppermute x12 -> x14, starting transfers between devices: 41.5 us -> 19.8 us  [moved(): return lax.ppermute(x, 'dp', [(i, to(i)) for i in range(ranks)])]
    pallas_call x0 -> x2, Pallas kernels: none -> 10.5 us  [first_leg(): pl.pallas_call(relay_kernel, grid_spec=pltpu.PrefetchScalarGridSpec(num_s...]
    unnamed x40 -> x44, local copies, waits for them, and re-layouts: 4.59 us -> 9.95 us
    ppermute x12 -> x14, waiting for transfers between devices: 43.1 us -> 40.2 us  [moved(): return lax.ppermute(x, 'dp', [(i, to(i)) for i in range(ranks)])]
  transfers between devices with their start and end apart: 25 -> 27, of which waited for: 13 -> 13; matrix products, arithmetic and copies ran while one was open for 2% -> 2% of each run, Pallas kernels for 13% -> 15%
where the time goes in v8:
time: 489 us; the launch traced here: 486 us
  waiting for transfers between devices  226 us (46%)
  Pallas kernels  188 us (38%)
  starting transfers between devices  36 us (7%)
  between operations  14.8 us (3%)
  local copies, waits for them, and re-layouts  11 us (2%)
  other arithmetic  10.4 us (2%)
    pallas_call x8, Pallas kernels, call(): pl.pallas_call(kernel, grid_spec=pltpu.PrefetchScalarGridSpec(num_scalar_...  119 us
    all_gather x1, waiting for transfers between devices, body(): g = lax.all_gather(both, 'dp', axis=0, tiled=True)  99 us
    ppermute x1, waiting for transfers between devices, body(): here_g = lax.ppermute(gbf, 'section', [(3, 0), (2, 1)]) if t == 1 else gbf  58.5 us
    pallas_call x6, Pallas kernels, simple(): pl.pallas_call(kernel, grid_spec=pltpu.PrefetchScalarGridSpec(num_scalar_...  48.8 us
    ppermute x14, waiting for transfers between devices, moved(): return lax.ppermute(x, 'dp', [(i, to(i)) for i in range(ranks)])  40.2 us
    ppermute x14, starting transfers between devices, moved(): return lax.ppermute(x, 'dp', [(i, to(i)) for i in range(ranks)])  19.8 us
    ppermute x1, waiting for transfers between devices, body(): here_x = lax.ppermute(ybf, 'section', [(0, 3), (1, 2)]) if t == 1 else ybf  11.8 us
    pallas_call x2, Pallas kernels, first_leg(): pl.pallas_call(relay_kernel, grid_spec=pltpu.PrefetchScalarGridSpec(num_s...  10.5 us
  transfers between devices with their start and end apart: 27, of which 13 were waited for; matrix products, arithmetic and copies ran while one was open for 2% of the time, Pallas kernels for 15%

profile of v8, /device:TPU:1, one launch (start us, length us, event | category | flops | bytes accessed | tf_op | source)
XLA Modules:
  0.0 485.8 jit_solution(4495452874364216308)
XLA Ops:
  12.5 9.7 %collective-permute-done = bf16[24,9344]{1,0:T(8,128)(2,1)S(1)} collective-permute-done((bf16[24,9344]{1,0:T(8,128)(2,1)}, bf16[24,9344]{1,0:T(8,128)(2,1)S(1)}, u32[]{:S(2)}, u32[]{:S(2)}) %collective-permute-start) | collective-permute-done | bytes 448544 | tf_op jit(solution)/shard_map/ppermute | solution.py:637
  31.2 99.0 %all-gather.2.cloned.1.call-done.g = bf16[768,18688]{1,0:T(8,128)(2,1)} async-done(((bf16[24,18688]{1,0:T(8,128)(2,1)}), bf16[768,18688]{1,0:T(8,128)(2,1)}) %all-gather.2.cloned.1.call-update) | async-done | bytes 28704784 | tf_op jit(solution)/shard_map/all_gather | solution.py:675
  133.7 18.6 %shard_map.201 = (bf16[384,768]{1,0:T(8,128)(2,1)}, bf16[384,768]{1,0:T(8,128)(2,1)}, bf16[384,768]{1,0:T(8,128)(2,1)}, bf16[384,768]{1,0:T(8,128)(2,1)}, bf16[3...) custom-call(s32[4]{0:T(128)} %get-tuple-element.268.idx, ...), custom_call_target="tpu_custom_call", output_to_operand_aliasing={{1}: (11, {}), {2}: (12, {}), {3}: (13, {}), {4}: (14, {}),... | custom-call | flops 1024 | bytes 1024 | tf_op jit(solution)/shard_map/pallas_call | solution.py:589
  152.3 18.1 %shard_map.213 = (bf16[384,768]{1,0:T(8,128)(2,1)}, bf16[384,768]{1,0:T(8,128)(2,1)}, bf16[384,768]{1,0:T(8,128)(2,1)}, bf16[384,768]{1,0:T(8,128)(2,1)}, bf16[3...) custom-call(s32[4]{0:T(128)} %pad_add_fusion.idx, ...), custom_call_target="tpu_custom_call", output_to_operand_aliasing={{1}: (11, {}), {2}: (12, {}), {3}: (13, {}), {4}: (14, {}),... | custom-call | flops 1024 | bytes 1024 | tf_op jit(solution)/shard_map/pallas_call | solution.py:589
  173.0 11.8 %collective-permute-done.1.x_in = bf16[384,768]{1,0:T(8,128)(2,1)S(1)} collective-permute-done((bf16[384,768]{1,0:T(8,128)(2,1)}, bf16[384,768]{1,0:T(8,128)(2,1)S(1)}, u32[]{:S(2)}, u32[]{:S(2)}) %collective-permute-start.1) | collective-permute-done | bytes 589856 | tf_op jit(solution)/shard_map/ppermute | solution.py:736
  189.4 15.5 %shard_map.215 = (bf16[384,768]{1,0:T(8,128)(2,1)}, bf16[384,768]{1,0:T(8,128)(2,1)}, bf16[384,768]{1,0:T(8,128)(2,1)}, bf16[384,768]{1,0:T(8,128)(2,1)}, bf16[3...) custom-call(s32[4]{0:T(128)} %pad_add_fusion.1.idx, ...), custom_call_target="tpu_custom_call", output_to_operand_aliasing={{1}: (11, {}), {2}: (12, {}), {3}: (13, {}), {4}: (14, {}),... | custom-call | flops 1024 | bytes 1024 | tf_op jit(solution)/shard_map/pallas_call | solution.py:589
  205.0 9.3 %shard_map.219 = (bf16[384,768]{1,0:T(8,128)(2,1)}, bf16[384,6144]{1,0:T(8,128)(2,1)}, bf16[384,6144]{1,0:T(8,128)(2,1)}, f32[1,6144]{1,0:T(1,128)}, f32[2,384,768]{2,1,0:T(8,128)}, /*index=5*/bf16[384,768]{1,0:T(8,128)(2,1)}) custom-call(s32[4]{0:T(128)} %pad_add_fusion.1.idx, ...), custom_call_target="tpu_custom_call", output_to_operand_aliasing={{1}: (17, {}), {2}: (18, {}), {3}: (19, {}), {4}: (20, {}),... | custom-call | flops 1024 | bytes 1024 | tf_op jit(solution)/shard_map/pallas_call | solution.py:589
  214.3 9.3 %shard_map.221 = (bf16[384,768]{1,0:T(8,128)(2,1)}, bf16[384,6144]{1,0:T(8,128)(2,1)}, bf16[384,6144]{1,0:T(8,128)(2,1)}, f32[1,6144]{1,0:T(1,128)}, f32[2,384,768]{2,1,0:T(8,128)}, /*index=5*/bf16[384,768]{1,0:T(8,128)(2,1)}) custom-call(s32[4]{0:T(128)} %get-tuple-element.270.idx, ...), custom_call_target="tpu_custom_call", output_to_operand_aliasing={{1}: (17, {}), {2}: (18, {}), {3}: (19, {}), {4}: (20, {}),... | custom-call | flops 1024 | bytes 1024 | tf_op jit(solution)/shard_map/pallas_call | solution.py:589
  226.2 58.5 %collective-permute-done.2.g_in = bf16[384,768]{1,0:T(8,128)(2,1)S(1)} collective-permute-done((bf16[384,768]{1,0:T(8,128)(2,1)}, bf16[384,768]{1,0:T(8,128)(2,1)S(1)}, u32[]{:S(2)}, u32[]{:S(2)}) %collective-permute-start.2) | collective-permute-done | bytes 589856 | tf_op jit(solution)/shard_map/ppermute | solution.py:816
  285.7 22.3 %shard_map.222 = (bf16[384,768]{1,0:T(8,128)(2,1)}, bf16[384,6144]{1,0:T(8,128)(2,1)}, bf16[384,6144]{1,0:T(8,128)(2,1)}, f32[1,6144]{1,0:T(1,128)}, f32[2,384,768]{2,1,0:T(8,128)}, /*index=5*/bf16[384,768]{1,0:T(8,128)(2,1)}) custom-call(s32[4]{0:T(128)} %pad_add_fusion.idx, ...), custom_call_target="tpu_custom_call", output_to_operand_aliasing={{1}: (17, {}), {2}: (18, {}), {3}: (19, {}), {4}: (20, {}),... | custom-call | flops 1024 | bytes 1024 | tf_op jit(solution)/shard_map/pallas_call | solution.py:589
  309.5 22.2 %shard_map.223 = (bf16[384,768]{1,0:T(8,128)(2,1)}, bf16[384,6144]{1,0:T(8,128)(2,1)}, bf16[384,6144]{1,0:T(8,128)(2,1)}, f32[1,6144]{1,0:T(1,128)}, f32[2,384,768]{2,1,0:T(8,128)}, /*index=5*/bf16[384,768]{1,0:T(8,128)(2,1)}) custom-call(s32[4]{0:T(128)} %get-tuple-element.268.idx, ...), custom_call_target="tpu_custom_call", output_to_operand_aliasing={{1}: (17, {}), {2}: (18, {}), {3}: (19, {}), {4}: (20, {}),... | custom-call | flops 1024 | bytes 1024 | tf_op jit(solution)/shard_map/pallas_call | solution.py:589
  333.8 13.2 %shard_map.224 = (bf16[192,4736]{1,0:T(8,128)(2,1)}, bf16[192,4736]{1,0:T(8,128)(2,1)}, bf16[192,4736]{1,0:T(8,128)(2,1)}, bf16[96,4736]{1,0:T(8,128)(2,1)}, bf16[96,4736]{1,0:T(8,128)(2,1)}) custom-call(s32[5]{0:T(128)} %stack.45.idx, f32[128,768]{1,0:T(8,128)} %fusion.2.place, f32[1,6144]{1,0:T(1,128)} %get-tuple-element.216.mine, f32[1,6144]{1,0:T(1,128)} %copy-done.19, ...), custom_call_target="tpu_custom_call" | custom-call | flops 1024 | bytes 1024 | tf_op jit(solution)/shard_map/pallas_call | solution.py:615
  354.2 13.0 %shard_map.226 = (bf16[192,4736]{1,0:T(8,128)(2,1)}, bf16[192,4736]{1,0:T(8,128)(2,1)}, bf16[192,4736]{1,0:T(8,128)(2,1)}, bf16[96,4736]{1,0:T(8,128)(2,1)}, bf16[96,4736]{1,0:T(8,128)(2,1)}) custom-call(s32[5]{0:T(128)} %stack.45.idx, f32[128,768]{1,0:T(8,128)} %fusion.2.place, f32[1,6144]{1,0:T(1,128)} %get-tuple-element.231.mine, f32[1,6144]{1,0:T(1,128)} %copy-done.20, ...), custom_call_target="tpu_custom_call" | custom-call | flops 1024 | bytes 1024 | tf_op jit(solution)/shard_map/pallas_call | solution.py:615
  372.0 5.3 %shard_map.229 = (bf16[192,4736]{1,0:T(8,128)(2,1)}, bf16[192,4736]{1,0:T(8,128)(2,1)}) custom-call(s32[5]{0:T(128)} %stack.45.idx, bf16[192,4736]{1,0:T(8,128)(2,1)} %get-tuple-element.246.up_in, bf16[192,4736]{1,0:T(8,128)(2,1)} %get-tuple-element.247.down_in, bf16[96,4736]{1,0:T(8,128)(2,1)} %copy-done.3, ...), custom_call_target="tpu_custom_call", output_to_operand_aliasing={{0}: (1, {}), {1}: (2, {})} | custom-call | flops 1024 | bytes 1024 | tf_op jit(solution)/shard_map/pallas_call | solution.py:773
  382.5 5.2 %shard_map.227 = (bf16[192,4736]{1,0:T(8,128)(2,1)}, bf16[192,4736]{1,0:T(8,128)(2,1)}) custom-call(s32[5]{0:T(128)} %stack.45.idx, bf16[192,4736]{1,0:T(8,128)(2,1)} %get-tuple-element.235.up_in, bf16[192,4736]{1,0:T(8,128)(2,1)} %get-tuple-element.236.down_in, bf16[96,4736]{1,0:T(8,128)(2,1)} %copy-done.5, ...), custom_call_target="tpu_custom_call", output_to_operand_aliasing={{0}: (1, {}), {1}: (2, {})} | custom-call | flops 1024 | bytes 1024 | tf_op jit(solution)/shard_map/pallas_call | solution.py:773
  390.5 10.6 %collective-permute-done.18.refs_1_ = bf16[192,4736]{1,0:T(8,128)(2,1)} collective-permute-done((bf16[192,4736]{1,0:T(8,128)(2,1)}, bf16[192,4736]{1,0:T(8,128)(2,1)}, u32[]{:S(2)}, u32[]{:S(2)}) %collective-permute-start.18) | collective-permute-done | bytes 1818656 | tf_op jit(solution)/shard_map/ppermute | solution.py:754
  401.1 6.1 %shard_map.230 = (bf16[48,4736]{1,0:T(8,128)(2,1)}, bf16[48,4736]{1,0:T(8,128)(2,1)}, bf16[48,4736]{1,0:T(8,128)(2,1)}, bf16[48,4736]{1,0:T(8,128)(2,1)}) custom-call(s32[5]{0:T(128)} %stack.45.idx, bf16[192,4736]{1,0:T(8,128)(2,1)} %get-tuple-element.245.refs_0_, bf16[192,4736]{1,0:T(8,128)(2,1)} %collective-permute-done.18.refs_1_, ...), custom_call_target="tpu_custom_call" | custom-call | flops 1024 | bytes 1024 | tf_op jit(solution)/shard_map/pallas_call | solution.py:615
  410.6 15.5 %collective-permute-done.11.refs_1_ = bf16[192,4736]{1,0:T(8,128)(2,1)S(1)} collective-permute-done((bf16[192,4736]{1,0:T(8,128)(2,1)}, bf16[192,4736]{1,0:T(8,128)(2,1)S(1)}, u32[]{:S(2)}, u32[]{:S(2)}) %collective-permute-start.11) | collective-permute-done | bytes 1818656 | tf_op jit(solution)/shard_map/ppermute | solution.py:754
  430.5 6.0 %shard_map.228 = (bf16[48,4736]{1,0:T(8,128)(2,1)}, bf16[48,4736]{1,0:T(8,128)(2,1)}, bf16[48,4736]{1,0:T(8,128)(2,1)}, bf16[48,4736]{1,0:T(8,128)(2,1)}) custom-call(s32[5]{0:T(128)} %stack.45.idx, bf16[192,4736]{1,0:T(8,128)(2,1)} %get-tuple-element.234.refs_0_, bf16[192,4736]{1,0:T(8,128)(2,1)} %copy-done.1, bf16[192,4736]{1,0:T(8,128)(2,1)} %copy-done.2), custom_call_target="tpu_custom_call" | custom-call | flops 1024 | bytes 1024 | tf_op jit(solution)/shard_map/pallas_call | solution.py:615
  445.5 5.7 %collective-permute-done.14.refs_2_ = bf16[48,4736]{1,0:T(8,128)(2,1)S(1)} collective-permute-done((bf16[48,4736]{1,0:T(8,128)(2,1)}, bf16[48,4736]{1,0:T(8,128)(2,1)S(1)}, u32[]{:S(2)}, u32[]{:S(2)}) %collective-permute-start.14) | collective-permute-done | bytes 454688 | tf_op jit(solution)/shard_map/ppermute | solution.py:754
  452.1 4.6 shard_map.231
  457.9 5.6 %collective-permute-start.24 = (bf16[24,4736]{1,0:T(8,128)(2,1)}, bf16[24,4736]{1,0:T(8,128)(2,1)S(1)}, u32[]{:S(2)}, u32[]{:S(2)}) collective-permute-start(bf16[24,4736]{1,0:T(8,128)(2,1)} %get-tuple-element.258), channel_id=1, source_target_pairs={{0,1},{1,0},{2,3},{3,2},{4,5},{5,4},{6,7},{7,6},{8,9},{9,8},{10,11... | collective-permute-start | bytes 681992 | tf_op jit(solution)/shard_map/ppermute | solution.py:633
  467.0 5.2 %collective-permute-done.25.c_in = bf16[24,4736]{1,0:T(8,128)(2,1)S(1)} collective-permute-done((bf16[24,4736]{1,0:T(8,128)(2,1)}, bf16[24,4736]{1,0:T(8,128)(2,1)S(1)}, u32[]{:S(2)}, u32[]{:S(2)}) %collective-permute-start.25) | collective-permute-done | bytes 227360 | tf_op jit(solution)/shard_map/ppermute | solution.py:849
  472.9 5.9 %shard_map.232 = (f32[24,5376]{1,0:T(8,128)}, f32[24,768]{1,0:T(8,128)}, f32[96,768]{1,0:T(8,128)}, f32[1,24]{1,0:T(1,128)}, f32[1,2]{1,0:T(1,128)}, /*index=5*/...) custom-call(s32[5]{0:T(128)} %stack.45.idx, f32[24,4736]{1,0:T(8,128)} %get-tuple-element.256.own, ...), custom_call_target="tpu_custom_call" | custom-call | flops 1024 | bytes 1024 | tf_op jit(solution)/shard_map/pallas_call | solution.py:615
  (144 shorter events, 74.7 us)
Async XLA Ops:
  7.2 123.0 %all-gather.2.cloned.1.call-start = ((), (), s32[]{:S(2)}) async-start(), calls=%async_computation | async-start | bytes 29601792 | tf_op jit(solution)/shard_map/all_gather | solution.py:675
  10.4 11.8 %collective-permute-start = (bf16[24,9344]{1,0:T(8,128)(2,1)}, bf16[24,9344]{1,0:T(8,128)(2,1)S(1)}, u32[]{:S(2)}, u32[]{:S(2)}) collective-permute-start(bf16[24,9344]{1,0:T(8,128)(2,1)} %shard_map.186), channel_id=1, source_target_pairs={{0,32},{32,0},{64,96},{96,64},{1,33},{33,1},{65,97},{97,65},{2,34}... | collective-permute-start | bytes 1345544 | tf_op jit(solution)/shard_map/ppermute | solution.py:637
  170.4 14.4 %collective-permute-start.1 = (bf16[384,768]{1,0:T(8,128)(2,1)}, bf16[384,768]{1,0:T(8,128)(2,1)S(1)}, u32[]{:S(2)}, u32[]{:S(2)}) collective-permute-start(bf16[384,768]{1,0:T(8,128)(2,1)} %get-tuple-element.146), channel_id=1, source_target_pairs={{0,96},{32,64},{1,97},{33,65},{2,98},{34,66},{3,99},{35,67},{4,100... | collective-permute-start | bytes 1769480 | tf_op jit(solution)/shard_map/ppermute | solution.py:736
  223.6 61.1 %collective-permute-start.2 = (bf16[384,768]{1,0:T(8,128)(2,1)}, bf16[384,768]{1,0:T(8,128)(2,1)S(1)}, u32[]{:S(2)}, u32[]{:S(2)}) collective-permute-start(bf16[384,768]{1,0:T(8,128)(2,1)} %get-tuple-element.200), channel_id=1, source_target_pairs={{96,0},{64,32},{97,1},{65,33},{98,2},{66,34},{99,3},{67,35},{100,4... | collective-permute-start | bytes 1769480 | tf_op jit(solution)/shard_map/ppermute | solution.py:816
  224.9 59.8 %collective-permute-start.3 = (bf16[384,768]{1,0:T(8,128)(2,1)S(1)}, bf16[384,768]{1,0:T(8,128)(2,1)S(1)}, u32[]{:S(2)}, u32[]{:S(2)}) collective-permute-start(bf16[384,768]{1,0:T(8,128)(2,1)S(1)} %copy-done), channel_id=1, source_target_pairs={{0,32},{32,0},{64,96},{96,64},{1,33},{33,1},{65,97},{97,65},{2,34}... | collective-permute-start | bytes 1769480 | tf_op jit(solution)/shard_map/ppermute | solution.py:637
  308.0 23.8 %collective-permute-start.4 = (bf16[384,6144]{1,0:T(8,128)(2,1)}, bf16[384,6144]{1,0:T(8,128)(2,1)}, u32[]{:S(2)}, u32[]{:S(2)}) collective-permute-start(bf16[384,6144]{1,0:T(8,128)(2,1)} %get-tuple-element.218), channel_id=1, source_target_pairs={{0,1},{1,0},{2,3},{3,2},{4,5},{5,4},{6,7},{7,6},{8,9},{9,8},{10,11... | collective-permute-start | bytes 14155784 | tf_op jit(solution)/shard_map/ppermute | solution.py:633
  309.4 22.3 %collective-permute-start.5 = (f32[1,6144]{1,0:T(1,128)}, f32[1,6144]{1,0:T(1,128)S(1)}, u32[]{:S(2)}, u32[]{:S(2)}) collective-permute-start(f32[1,6144]{1,0:T(1,128)} %get-tuple-element.216.mine), channel_id=1, source_target_pairs={{0,1},{1,0},{2,3},{3,2},{4,5},{5,4},{6,7},{7,6},{8,9},{9,8},{10,11... | collective-permute-start | bytes 73736 | tf_op jit(solution)/shard_map/ppermute | solution.py:633
  331.8 21.8 %collective-permute-start.8 = (bf16[384,6144]{1,0:T(8,128)(2,1)}, bf16[384,6144]{1,0:T(8,128)(2,1)}, u32[]{:S(2)}, u32[]{:S(2)}) collective-permute-start(bf16[384,6144]{1,0:T(8,128)(2,1)} %get-tuple-element.233), channel_id=1, source_target_pairs={{0,1},{1,0},{2,3},{3,2},{4,5},{5,4},{6,7},{7,6},{8,9},{9,8},{10,11... | collective-permute-start | bytes 14155784 | tf_op jit(solution)/shard_map/ppermute | solution.py:633
  332.3 15.1 %collective-permute-start.6 = (bf16[384,768]{1,0:T(8,128)(2,1)}, bf16[384,768]{1,0:T(8,128)(2,1)S(1)}, u32[]{:S(2)}, u32[]{:S(2)}) collective-permute-start(bf16[384,768]{1,0:T(8,128)(2,1)} %get-tuple-element.227), channel_id=1, source_target_pairs={{0,32},{32,0},{64,96},{96,64},{1,33},{33,1},{65,97},{97,65},{2,34}... | collective-permute-start | bytes 1769480 | tf_op jit(solution)/shard_map/ppermute | solution.py:637
  348.2 21.8 %collective-permute-start.16 = (bf16[96,4736]{1,0:T(8,128)(2,1)}, bf16[96,4736]{1,0:T(8,128)(2,1)S(1)}, u32[]{:S(2)}, u32[]{:S(2)}) collective-permute-start(bf16[96,4736]{1,0:T(8,128)(2,1)} %get-tuple-element.248), channel_id=1, source_target_pairs={{0,8},{1,3},{2,10},{3,5},{4,12},{5,7},{6,14},{7,1},{8,16},{9,11},{... | collective-permute-start | bytes 2727944 | tf_op jit(solution)/shard_map/ppermute | solution.py:754
  349.1 21.0 %collective-permute-start.17 = (bf16[96,4736]{1,0:T(8,128)(2,1)}, bf16[96,4736]{1,0:T(8,128)(2,1)S(1)}, u32[]{:S(2)}, u32[]{:S(2)}) collective-permute-start(bf16[96,4736]{1,0:T(8,128)(2,1)} %get-tuple-element.249), channel_id=1, source_target_pairs={{0,24},{1,7},{2,26},{3,1},{4,28},{5,3},{6,30},{7,5},{8,0},{9,15},{... | collective-permute-start | bytes 2727944 | tf_op jit(solution)/shard_map/ppermute | solution.py:754
  367.1 14.1 %collective-permute-start.9 = (bf16[96,4736]{1,0:T(8,128)(2,1)}, bf16[96,4736]{1,0:T(8,128)(2,1)S(1)}, u32[]{:S(2)}, u32[]{:S(2)}) collective-permute-start(bf16[96,4736]{1,0:T(8,128)(2,1)} %get-tuple-element.237), channel_id=1, source_target_pairs={{0,8},{1,3},{2,10},{3,5},{4,12},{5,7},{6,14},{7,1},{8,16},{9,11},{... | collective-permute-start | bytes 2727944 | tf_op jit(solution)/shard_map/ppermute | solution.py:754
  367.8 13.4 %collective-permute-start.10 = (bf16[96,4736]{1,0:T(8,128)(2,1)}, bf16[96,4736]{1,0:T(8,128)(2,1)S(1)}, u32[]{:S(2)}, u32[]{:S(2)}) collective-permute-start(bf16[96,4736]{1,0:T(8,128)(2,1)} %get-tuple-element.238), channel_id=1, source_target_pairs={{0,24},{1,7},{2,26},{3,1},{4,28},{5,3},{6,30},{7,5},{8,0},{9,15},{... | collective-permute-start | bytes 2727944 | tf_op jit(solution)/shard_map/ppermute | solution.py:754
  377.3 23.8 %collective-permute-start.18 = (bf16[192,4736]{1,0:T(8,128)(2,1)}, bf16[192,4736]{1,0:T(8,128)(2,1)}, u32[]{:S(2)}, u32[]{:S(2)}) collective-permute-start(bf16[192,4736]{1,0:T(8,128)(2,1)} %get-tuple-element.250), channel_id=1, source_target_pairs={{0,8},{1,3},{2,10},{3,5},{4,12},{5,7},{6,14},{7,1},{8,16},{9,11},{... | collective-permute-start | bytes 5455880 | tf_op jit(solution)/shard_map/ppermute | solution.py:754
  377.4 23.7 %collective-permute-start.19 = (bf16[192,4736]{1,0:T(8,128)(2,1)}, bf16[192,4736]{1,0:T(8,128)(2,1)}, u32[]{:S(2)}, u32[]{:S(2)}) collective-permute-start(bf16[192,4736]{1,0:T(8,128)(2,1)} %get-tuple-element.251), channel_id=1, source_target_pairs={{0,24},{1,7},{2,26},{3,1},{4,28},{5,3},{6,30},{7,5},{8,0},{9,15},{... | collective-permute-start | bytes 5455880 | tf_op jit(solution)/shard_map/ppermute | solution.py:754
  387.7 38.3 %collective-permute-start.11 = (bf16[192,4736]{1,0:T(8,128)(2,1)}, bf16[192,4736]{1,0:T(8,128)(2,1)S(1)}, u32[]{:S(2)}, u32[]{:S(2)}) collective-permute-start(bf16[192,4736]{1,0:T(8,128)(2,1)} %get-tuple-element.239), channel_id=1, source_target_pairs={{0,8},{1,3},{2,10},{3,5},{4,12},{5,7},{6,14},{7,1},{8,16},{9,11},{... | collective-permute-start | bytes 5455880 | tf_op jit(solution)/shard_map/ppermute | solution.py:754
  388.1 41.2 %collective-permute-start.12 = (bf16[192,4736]{1,0:T(8,128)(2,1)}, bf16[192,4736]{1,0:T(8,128)(2,1)S(1)}, u32[]{:S(2)}, u32[]{:S(2)}) collective-permute-start(bf16[192,4736]{1,0:T(8,128)(2,1)} %get-tuple-element.240), channel_id=1, source_target_pairs={{0,24},{1,7},{2,26},{3,1},{4,28},{5,3},{6,30},{7,5},{8,0},{9,15},{... | collective-permute-start | bytes 5455880 | tf_op jit(solution)/shard_map/ppermute | solution.py:754
  407.2 32.8 %collective-permute-start.20 = (bf16[48,4736]{1,0:T(8,128)(2,1)}, bf16[48,4736]{1,0:T(8,128)(2,1)S(1)}, u32[]{:S(2)}, u32[]{:S(2)}) collective-permute-start(bf16[48,4736]{1,0:T(8,128)(2,1)} %get-tuple-element.253), channel_id=1, source_target_pairs={{0,2},{1,9},{2,4},{3,11},{4,6},{5,13},{6,0},{7,15},{8,10},{9,17},{... | collective-permute-start | bytes 1363976 | tf_op jit(solution)/shard_map/ppermute | solution.py:754
  407.2 34.3 %collective-permute-start.21 = (bf16[48,4736]{1,0:T(8,128)(2,1)}, bf16[48,4736]{1,0:T(8,128)(2,1)}, u32[]{:S(2)}, u32[]{:S(2)}) collective-permute-start(bf16[48,4736]{1,0:T(8,128)(2,1)} %get-tuple-element.254), channel_id=1, source_target_pairs={{0,4},{1,17},{2,6},{3,19},{4,0},{5,21},{6,2},{7,23},{8,12},{9,25},... | collective-permute-start | bytes 1363976 | tf_op jit(solution)/shard_map/ppermute | solution.py:754
  409.7 31.7 %collective-permute-start.22 = (bf16[48,4736]{1,0:T(8,128)(2,1)}, bf16[48,4736]{1,0:T(8,128)(2,1)}, u32[]{:S(2)}, u32[]{:S(2)}) collective-permute-start(bf16[48,4736]{1,0:T(8,128)(2,1)} %get-tuple-element.255), channel_id=1, source_target_pairs={{0,6},{1,25},{2,0},{3,27},{4,2},{5,29},{6,4},{7,31},{8,14},{9,1},{... | collective-permute-start | bytes 1363976 | tf_op jit(solution)/shard_map/ppermute | solution.py:754
  437.9 13.3 %collective-permute-start.14 = (bf16[48,4736]{1,0:T(8,128)(2,1)}, bf16[48,4736]{1,0:T(8,128)(2,1)S(1)}, u32[]{:S(2)}, u32[]{:S(2)}) collective-permute-start(bf16[48,4736]{1,0:T(8,128)(2,1)} %get-tuple-element.243), channel_id=1, source_target_pairs={{0,4},{1,17},{2,6},{3,19},{4,0},{5,21},{6,2},{7,23},{8,12},{9,25},... | collective-permute-start | bytes 1363976 | tf_op jit(solution)/shard_map/ppermute | solution.py:754
  440.0 11.2 %collective-permute-start.15 = (bf16[48,4736]{1,0:T(8,128)(2,1)}, bf16[48,4736]{1,0:T(8,128)(2,1)S(1)}, u32[]{:S(2)}, u32[]{:S(2)}) collective-permute-start(bf16[48,4736]{1,0:T(8,128)(2,1)} %get-tuple-element.244), channel_id=1, source_target_pairs={{0,6},{1,25},{2,0},{3,27},{4,2},{5,29},{6,4},{7,31},{8,14},{9,1},{... | collective-permute-start | bytes 1363976 | tf_op jit(solution)/shard_map/ppermute | solution.py:754
  456.7 10.2 %collective-permute-start.23 = (bf16[24,4736]{1,0:T(8,128)(2,1)}, bf16[24,4736]{1,0:T(8,128)(2,1)S(1)}, u32[]{:S(2)}, u32[]{:S(2)}) collective-permute-start(bf16[24,4736]{1,0:T(8,128)(2,1)} %get-tuple-element.257), channel_id=1, source_target_pairs={{0,32},{32,0},{64,96},{96,64},{1,33},{33,1},{65,97},{97,65},{2,34}... | collective-permute-start | bytes 681992 | tf_op jit(solution)/shard_map/ppermute | solution.py:637
  457.9 9.1 %collective-permute-start.24 = (bf16[24,4736]{1,0:T(8,128)(2,1)}, bf16[24,4736]{1,0:T(8,128)(2,1)S(1)}, u32[]{:S(2)}, u32[]{:S(2)}) collective-permute-start(bf16[24,4736]{1,0:T(8,128)(2,1)} %get-tuple-element.258), channel_id=1, source_target_pairs={{0,1},{1,0},{2,3},{3,2},{4,5},{5,4},{6,7},{7,6},{8,9},{9,8},{10,11... | collective-permute-start | bytes 681992 | tf_op jit(solution)/shard_map/ppermute | solution.py:633
  (25 other events, 93.3 us)
Sparse Core Ops, SparseCore 0:
  24.7 105.4 all-gather.1

commit v9 on v8

--- a/solution.py
+++ b/solution.py
@@ -93,21 +93,33 @@
         copy.wait()
 
 
-def forward_kernel(d, ff, chunks, base, first, idx, x_in, g, g3, ids_col, ids_row, ngain, gains, ubias, obias, spread, *refs):
+def forward_kernel(d, ff, chunks, layer, base, first, idx, *refs):
     @pl.when(idx[0] == 1)
     def _():
-        forward_work(d, ff, chunks, base, first, idx, x_in, g, g3, ids_col, ids_row, ngain, gains, ubias, obias, spread, *refs)
-
-
-def forward_work(d, ff, chunks, base, first, idx, x_in, g, g3, ids_col, ids_row, ngain, gains, ubias, obias, spread, *refs):
+        forward_work(d, ff, chunks, layer, base, first, idx, *refs)
+
+
+def head_spread(head):
+    row = lax.broadcasted_iota(jnp.int32, (WIDE, WIDE), 0) // head
+    column = lax.broadcasted_iota(jnp.int32, (WIDE, WIDE), 1) // head
+    return jnp.where(row == column, 1.0 / head, 0.0).astype(BF)
+
+
+def as_column(row):
+    return jnp.broadcast_to(row, (LANES, row.shape[1])).T[:, :1]
+
+
+def forward_work(d, ff, chunks, layer, base, first, idx, x_in, g, g3, ids, smalls, *refs):
     refs = refs[13:]
     ybf, xs, qs, ks, vs, ns, nrs, gps, es, small, kept, sent, y_out, y_send = refs[:14]
-    (x_v, h_v, w_v, u_v, d_v, a_v, q_v, k_v, v_v, n_v, r_v, act_v, gp_v, e_v, rs_v, att_v, acc_v, y_v, yb_v, ins, outs) = refs[14:]
+    (x_v, h_v, w_v, u_v, d_v, a_v, q_v, k_v, v_v, n_v, r_v, act_v, gp_v, e_v, rs_v, att_v, acc_v, y_v, yb_v, id_v, sm_v, ins, outs) = refs[14:]
     rows = x_v.shape[0]
+    body_rows = pl.ds(0, rows)
     fc = ff // chunks
     core, slot, home = idx[1], idx[2], idx[3]
     cin, cout = Copies(ins), Copies(outs)
     x_copy = cin.start(x_in.at[slot] if first else x_in, x_v)
+    small_copies = [cin.start(ids.at[slot], id_v), cin.start(smalls.at[layer], sm_v)]
     wq = [cin.start(g.at[:, pl.ds(base + ff + d * i, d)], w_v.at[:, pl.ds(d * i, d)]) for i in range(3)]
     groups = fc // WIDE
     wff = []
@@ -123,12 +135,17 @@
     def side(i):
         return pl.ds(ff + d * i, d)
 
+    spread = head_spread(64)
+    for copy in small_copies:
+        copy.wait()
+    ids_row = id_v[0:1]
+    ids_col = as_column(ids_row)
+    keep = jnp.where(ids_col < ABSENT, 1.0, 0.0)
     x_copy.wait()
-    keep = jnp.where(ids_col[0] < ABSENT, 1.0, 0.0)
     masked = keep * x_v[...].astype(F32)
-    h_v[...] = (row_norm(masked)[0] * ngain[...]).astype(BF)
-    pending += [cout.start(x_v, xs), cout.start(h_v, kept.at[:, side(2)]), cout.start(h_v, sent.at[:, side(2)])]
-    bias_mask = jnp.where(ids_col[0] == ids_row[0], 0.0, -1e9)
+    h_v[...] = (row_norm(masked)[0] * sm_v[0:1, :d]).astype(BF)
+    pending += [cout.start(x_v, xs), cout.start(h_v, kept.at[body_rows, side(2)]), cout.start(h_v, sent.at[body_rows, side(2)])]
+    bias_mask = jnp.where(ids_col == ids_row, 0.0, -1e9)
     for i in range(3):
         wq[i].wait()
         raw = mm(h_v[...], w_v[:, d * i : d * i + d])
@@ -136,10 +153,10 @@
             v_v[...] = raw.astype(BF)
             pending.append(cout.start(v_v, vs))
         else:
-            centered = raw - head_mean(raw, spread[...], True)
-            rstd = lax.rsqrt(head_mean(centered * centered, spread[...], True) + EPS)
+            centered = raw - head_mean(raw, spread, True)
+            rstd = lax.rsqrt(head_mean(centered * centered, spread, True) + EPS)
             normal = centered * rstd
-            scaled = (normal * gains[i]).astype(BF)
+            scaled = (normal * sm_v[0:1, d * (2 + i) : d * (3 + i)]).astype(BF)
             n_v[:, d * i : d * i + d] = normal.astype(BF)
             r_v[:, d * i : d * i + d] = rstd.astype(BF)
             if i == 0:
@@ -154,7 +171,7 @@
     for c in range(chunks):
         for copy in wff[c]:
             copy.wait()
-        pre = mm(h_v[...], u_v[c]) + ubias[:, fc * c : fc * c + fc]
+        pre = mm(h_v[...], u_v[c]) + sm_v[1:2, fc * c : fc * c + fc]
         cdf = 0.5 * (1.0 + lax.erf(pre * (1.0 / math.sqrt(2.0))))
         density = jnp.exp(-0.5 * pre * pre) * (1.0 / math.sqrt(2.0 * math.pi))
         act = (pre * cdf).astype(BF)
@@ -180,37 +197,39 @@
                 both.append((got[:64] * inv).astype(BF))
             att_v[:, cols] = jnp.concatenate(both, axis=0).T
         span = pl.ds(fc * c, fc)
-        pending += [cout.either(core, act_v.at[c], sent.at[:, span], kept.at[:, span]), cout.start(gp_v.at[c], gps.at[c]),
+        pending += [cout.either(core, act_v.at[c], sent.at[body_rows, span], kept.at[body_rows, span]), cout.start(gp_v.at[c], gps.at[c]),
                     cout.start(e_v.at[pl.ds(2 * pairs * c, 2 * pairs)], es.at[pl.ds(2 * pairs * c, 2 * pairs)])]
-    pending += [cout.start(rs_v, small), cout.either(core, att_v, sent.at[:, side(3)], kept.at[:, side(3)])]
+    pending += [cout.start(rs_v, small), cout.either(core, att_v, sent.at[body_rows, side(3)], kept.at[body_rows, side(3)])]
     wa.wait()
-    y = keep * (keep * x_v[...].astype(F32) + acc_v[...] + mm(att_v[...], a_v[...]) + obias[...])
+    y = keep * (keep * x_v[...].astype(F32) + acc_v[...] + mm(att_v[...], a_v[...]) + sm_v[0:1, d : 2 * d])
     y_v[...] = y
-    ybf[...] = y.astype(BF)
     yb_v[...] = y.astype(BF)
+    pending.append(cout.start(yb_v, ybf))
     result_out(home, y_v, y_out.at[slot], yb_v, y_send, cout)
     for copy in pending:
         copy.wait()
 
 
-def backward_kernel(d, ff, chunks, base, first, idx, g_in, g, g3, ids_col, ngain, gains, spread, *refs):
+def backward_kernel(d, ff, chunks, layer, base, first, idx, *refs):
     @pl.when(idx[0] == 1)
     def _():
-        backward_work(d, ff, chunks, base, first, idx, g_in, g, g3, ids_col, ngain, gains, spread, *refs)
-
-
-def backward_work(d, ff, chunks, base, first, idx, g_in, g, g3, ids_col, ngain, gains, spread, *refs):
+        backward_work(d, ff, chunks, layer, base, first, idx, *refs)
+
+
+def backward_work(d, ff, chunks, layer, base, first, idx, g_in, g, g3, ids, smalls, *refs):
     xs, qs, ks, vs, ns, nrs, gps, es, small = refs[:9]
-    refs = refs[9 + 5 :]
-    gbf, kept, sent, table, gr_out, gr_send = refs[:6]
+    refs = refs[9 + 4 :]
+    gbf, kept, sent, gr_out, gr_send = refs[:5]
     (g_v, gb_v, w_v, u_v, d_v, a_v, x_v, q_v, k_v, v_v, n_v, r_v, gp_v, e_v, rs_v, gat_v, gqt_v, gk_v,
-     gq_b, gk_b, gv_b, gj_v, acc_v, out_v, ob_v, sm_v, ins, outs) = refs[6:]
+     gq_b, gk_b, gv_b, gj_v, acc_v, out_v, ob_v, sm_v, sp_v, id_v, gain_v, ins, outs) = refs[5:]
     rows = x_v.shape[0]
+    body_rows = pl.ds(0, rows)
     fc = ff // chunks
     groups = fc // WIDE
     core, slot, home = idx[1], idx[2], idx[3]
     cin, cout = Copies(ins), Copies(outs)
     g_copy = cin.start(g_in.at[slot] if first else g_in, g_v)
+    small_copies = [cin.start(ids.at[slot], id_v), cin.start(smalls.at[layer], gain_v)]
     wa = cin.start(g.at[:, pl.ds(base + ff + 3 * d, d)], a_v)
     heads = [cin.start(s, v) for s, v in ((small, rs_v), (ks, k_v), (vs, v_v), (qs, q_v))]
     pairs = d // LANES // chunks
@@ -234,12 +253,15 @@
     def summed(at, value):
         sm_v[:, at : at + value.shape[1]] = jnp.sum(value, axis=0, keepdims=True)
 
+    spread = head_spread(64)
+    for copy in small_copies:
+        copy.wait()
+    keep = jnp.where(as_column(id_v[0:1]) < ABSENT, 1.0, 0.0)
     g_copy.wait()
-    keep = jnp.where(ids_col[0] < ABSENT, 1.0, 0.0)
     gres = keep * g_v[...].astype(F32)
     summed(d, gres)
     gb_v[...] = gres.astype(BF)
-    pending.append(cout.either(core, gb_v, sent.at[:, side(0)], kept.at[:, side(0)]))
+    pending.append(cout.either(core, gb_v, sent.at[body_rows, side(0)], kept.at[body_rows, side(0)]))
     wa.wait()
     gat_v[...] = mm(a_v[...], gb_v[...], NT).astype(BF)
     for copy in heads:
@@ -253,7 +275,7 @@
         gup = gup.astype(BF)
         gj_v[c] = gup
         span = pl.ds(fc * c, fc)
-        pending.append(cout.either(core, gj_v.at[c], kept.at[:, span], sent.at[:, span]))
+        pending.append(cout.either(core, gj_v.at[c], kept.at[body_rows, span], sent.at[body_rows, span]))
         total = mm(gup, u_v[c], NT)
         if c == 0:
             acc_v[...] = total
@@ -282,14 +304,15 @@
                 gqt_v[at_rows, :] = mm(keys_t[64 * half : 64 * half + 64], gs) * 0.125
             gk_v[:, cols] = gk
             gv_b[:, cols] = gv.astype(BF)
-    pending.append(cout.either(core, gv_b, sent.at[:, side(1)], kept.at[:, side(1)]))
+    pending.append(cout.either(core, gv_b, sent.at[body_rows, side(1)], kept.at[body_rows, side(1)]))
     for copy in norms:
         copy.wait()
     for i, (grad, out) in enumerate(((gqt_v[...].T, gq_b), (gk_v[...], gk_b))):
         normal = n_v[:, d * i : d * i + d].astype(F32)
         summed(2 * d + d * i, grad * normal)
-        out[...] = norm_back(grad * gains[i], normal, r_v[:, d * i : d * i + d].astype(F32), spread[...]).astype(BF)
-        pending.append(cout.either(core, out, kept.at[:, side(i)], sent.at[:, side(i)]))
+        gain = gain_v[0:1, d * (2 + i) : d * (3 + i)]
+        out[...] = norm_back(grad * gain, normal, r_v[:, d * i : d * i + d].astype(F32), spread).astype(BF)
+        pending.append(cout.either(core, out, kept.at[body_rows, side(i)], sent.at[body_rows, side(i)]))
     for copy in wq:
         copy.wait()
     ghid = acc_v[...]
@@ -298,13 +321,16 @@
     rows_in.wait()
     xhat, rstd = row_norm(keep * x_v[...].astype(F32))
     summed(0, ghid * xhat)
-    pending.append(cout.start(sm_v, table))
-    gx = ghid * ngain[...]
+    top = sm_v[...].astype(BF).astype(F32)
+    sp_v[...] = jnp.concatenate([top, sm_v[...] - top, jnp.zeros((14, top.shape[1]), F32)], axis=0).astype(BF)
+    tail = pl.ds(rows, 16)
+    pending += [cout.start(sp_v, kept.at[tail]), cout.start(sp_v, sent.at[tail])]
+    gx = ghid * gain_v[0:1, :d]
     gmask = rstd * (gx - jnp.mean(gx, axis=-1, keepdims=True) - xhat * jnp.mean(gx * xhat, axis=-1, keepdims=True))
     out = keep * (keep * g_v[...].astype(F32) + gmask)
     out_v[...] = out
-    gbf[...] = out.astype(BF)
     ob_v[...] = out.astype(BF)
+    pending.append(cout.start(ob_v, gbf))
     result_out(home, out_v, gr_out.at[slot], ob_v, gr_send, cout)
     for copy in pending:
         copy.wait()
@@ -320,8 +346,13 @@
     return parts + pltpu.roll(parts, LANES - 8, 1)
 
 
-def small_table(d, ff, place, mine, theirs):
-    total = mine[...] + theirs[...]
+def small_table(d, ff, tables):
+    total = jnp.zeros((1, tables.shape[2]), F32)
+    for i in range(tables.shape[0]):
+        parts = tables[i].astype(F32)
+        total = total + parts[0:1] + parts[1:2]
+    lane = lax.broadcasted_iota(jnp.int32, (LANES, d), 0) % 64
+    place = jnp.where(lax.broadcasted_iota(jnp.int32, (LANES, d), 1) == lane // 2 * 24 + lane % 2, 1.0, 0.0)
     quarter = WIDE // 4
     ub = total[:, 4 * d :]
     up_rows = []
@@ -335,14 +366,14 @@
             lanes = lanes + total[:, d * i + LANES * p : d * i + LANES * (p + 1)]
         head_rows.append(lanes)
     both = jnp.concatenate(head_rows + [jnp.zeros((6, LANES), F32)], axis=0)
-    placed = lax.dot_general(both, place[...], NN, precision=lax.Precision.HIGHEST, preferred_element_type=F32)
+    placed = lax.dot_general(both, place, NN, precision=lax.Precision.HIGHEST, preferred_element_type=F32)
     rows = [total[:, :d], total[:, d : 2 * d]] + up_rows + [placed[0:1], placed[1:2], jnp.zeros((LANES - 8, d), F32)]
     return jnp.concatenate(rows, axis=0).T
 
 
-def weight_grad_kernel(d, ff, idx, place, mine, theirs, kept, got, *refs):
-    results, (big_v, a_v, b_v, c_v, out_v, ins, outs) = refs[:5], refs[5:]
-    rows = kept.shape[0]
+def weight_grad_kernel(d, ff, idx, kept, got, *refs):
+    results, (big_v, a_v, b_v, c_v, out_v, t_v, ins, outs) = refs[:5], refs[5:]
+    rows = kept.shape[0] - t_v.shape[1]
     tokens = 2 * rows
     quarter, half, third = WIDE // 4, ff // 2, ff // 3
     blocks = third // WIDE
@@ -351,7 +382,7 @@
     y, z, core = idx[0], idx[1], idx[2]
 
     def load(cin, at, width, to, to_at):
-        return [cin.start(src.at[:, pl.ds(at, width)], to.at[i, :, pl.ds(to_at, width)]) for i, src in enumerate((kept, got))]
+        return [cin.start(src.at[pl.ds(0, rows), pl.ds(at, width)], to.at[i, :, pl.ds(to_at, width)]) for i, src in enumerate((kept, got))]
 
     def wait(copies):
         for copy in copies:
@@ -394,6 +425,7 @@
         loads = [load(cin, third * k, third, big_v, third * k) for k in range(3)]
         attended = load(cin, ff + 3 * d, d, b_v, 0)
         hidden, values = load(cin, ff + 2 * d, d, c_v, 0), load(cin, ff + d, d, c_v, d)
+        smalls = [cin.start(src.at[pl.ds(rows, t_v.shape[1])], t_v.at[i]) for i, src in enumerate((kept, got))]
         wait(grads)
         gb = both(a_v)
         for k in range(3):
@@ -406,9 +438,9 @@
         pending = send_by_y(cout, 0, 4 * d)
         wait(attended)
         put(everything, slice(4 * d, 5 * d), lax.dot_general(both(b_v), gb, TN, preferred_element_type=F32))
-        wait(hidden + values)
+        wait(hidden + values + smalls)
         put(everything, slice(5 * d, 6 * d), lax.dot_general(both(c_v), both(c_v, d), TN, preferred_element_type=F32))
-        put(everything, slice(6 * d, 6 * d + LANES), split_small(small_table(d, ff, place, mine, theirs)))
+        put(everything, slice(6 * d, 6 * d + LANES), split_small(small_table(d, ff, t_v)))
         wait(pending + send_by_y(cout, 4 * d, 2 * d + LANES))
 
     @pl.when(core == 1)
@@ -446,42 +478,65 @@
     return jnp.concatenate([main.astype(BF), last], axis=1).reshape(shape)
 
 
-def relay_kernel(idx, up_in, down_in, up_got, down_got, up, down, up_v, down_v, ins, outs):
+def relay_kernel(idx, up_in, down_in, up_got, down_got, up, down, hold, ins, outs):
     half = up_got.shape[0]
+
     cin, cout = Copies(ins), Copies(outs)
+    parts = ((up_in, 0, up_got, up), (down_in, half, down_got, down))
+    loads = [[cin.start(block.at[pl.ds(at, half)], hold.at[2 * i]), cin.start(got, hold.at[2 * i + 1])]
+             for i, (block, at, got, _) in enumerate(parts)]
     pending = []
-    loads = [(cin.start(block.at[pl.ds(at, half)], hold), got, hold, out.at[pl.ds(at, half)])
-             for block, at, got, hold, out in ((up_in, 0, up_got, up_v, up), (down_in, half, down_got, down_v, down))]
-    for copy, got, hold, out in loads:
-        copy.wait()
-        hold[...] = added([hold, got])
-        pending.append(cout.start(hold, out))
+    for i, (_, at, _, out) in enumerate(parts):
+        for copy in loads[i]:
+            copy.wait()
+        hold[2 * i] = added([hold.at[2 * i], hold.at[2 * i + 1]])
+        pending.append(cout.start(hold.at[2 * i], out.at[pl.ds(at, half)]))
     for copy in pending:
         copy.wait()
 
 
 def mid_kernel(idx, *refs):
-    came, outs, hold = refs[:3], refs[3:7], refs[7]
-    hold[...] = added(came).reshape(hold.shape)
+    came, results, (in_v, out_v, ins, outs) = refs[:3], refs[3:7], refs[7:]
+    share = results[0].shape[0]
+
+    cin, cout = Copies(ins), Copies(outs)
     at = jnp.where(idx[2] == 0, idx[1], idx[0])
-    for s in range(4):
-        outs[s][...] = hold[lax.rem(at + s, 4)]
-
-
-def last_kernel(idx, *refs):
-    layers, (home_mine, home_other, away_mine, away_other), holds = (refs[:4], refs[4:8]), refs[8:12], refs[12:]
+    order = [2, 1, 3, 0]
+    blocks = [pl.multiple_of(lax.rem(at + s, 4) * share, 16) for s in order]
+    loads = [[cin.start(part.at[pl.ds(block, share)], in_v.at[i, p]) for p, part in enumerate(came)]
+             for i, block in enumerate(blocks)]
+    pending = []
+    for i, s in enumerate(order):
+        for copy in loads[i]:
+            copy.wait()
+        out_v[i] = added([in_v.at[i, p] for p in range(3)])
+        pending.append(cout.start(out_v.at[i], results[s]))
+    for copy in pending:
+        copy.wait()
+
+
+def last_pair_kernel(idx, *refs):
+    came, (home_mine, home_other, away_mine, away_other, in_v, hold, ins) = refs[:8], refs[8:]
+    share = home_mine.shape[0]
     core, odd = idx[2], idx[4]
-    for came, hold in zip(layers, holds):
-        hold[...] = added(came).astype(F32)
-    count = home_mine.shape[0]
-
-    def rows_of(hold, which):
-        return hold[pl.ds(pl.multiple_of(which * count, 8), count), :]
+
+    sum_of(came, in_v, hold, ins)
+
+    def rows_of(k, which):
+        return hold[k, pl.ds(pl.multiple_of(which * share, 8), share), :]
 
     for which, home, away in ((core, home_mine, away_mine), (1 - core, home_other, away_other)):
-        lower, upper = rows_of(holds[0], which), rows_of(holds[1], which)
-        home[...] = jnp.where(odd == 1, upper, lower).astype(home.dtype)
-        away[...] = jnp.where(odd == 1, lower, upper).astype(away.dtype)
+        home[...] = jnp.where(odd == 1, rows_of(1, which), rows_of(0, which)).astype(home.dtype)
+        away[...] = jnp.where(odd == 1, rows_of(0, which), rows_of(1, which)).astype(away.dtype)
+
+
+def sum_of(came, in_v, hold, sems):
+    copies = Copies(sems)
+    loads = [copies.start(part, in_v.at[i]) for i, part in enumerate(came)]
+    for k in range(len(came) // 4):
+        for copy in loads[4 * k : 4 * k + 4]:
+            copy.wait()
+        hold[k] = added([in_v.at[4 * k + i] for i in range(4)]).astype(F32)
 
 
 def place_kernel(idx, y_in, y_got, g_in, g_got, y_out, g_out, y_v, g_v, sems):
@@ -526,20 +581,17 @@
     out[:, at + 5 * d :] = table.astype(BF)
 
 
-def smalls_kernel(d, ff, base, stride, g, place, ngain, gains, ubias, obias, t_v, sems):
+def smalls_kernel(d, ff, base, stride, g, place, out, t_v, sems):
     copies = Copies(sems)
     loads = [copies.start(g.at[:, pl.ds(base + stride * layer, LANES)], t_v.at[layer]) for layer in range(2)]
     quarter = WIDE // 4
     for layer in range(2):
         loads[layer].wait()
         table = t_v[layer].astype(F32).T
-        ngain[layer] = table[0:1]
-        obias[layer] = table[1:2]
         pieces = [table[2 + j : 3 + j, quarter * b : quarter * (b + 1)] for b in range(ff // WIDE) for j in range(4)]
-        ubias[layer] = jnp.concatenate(pieces, axis=1)
         both = mm(table[0:8].astype(BF), place[...])
-        gains[layer, 0] = both[6:7]
-        gains[layer, 1] = both[7:8]
+        first = jnp.concatenate([table[0:1], table[1:2], both[6:7], both[7:8]], axis=1)
+        out[layer] = jnp.concatenate([first, jnp.concatenate(pieces, axis=1), jnp.zeros((6, ff), F32)], axis=0)
 
 
 def finish_kernel(d, ff, idx, own, a_in, b_in, c_in, shuffle, g_in, g_attn, g_down, g_ng, g_q, g_k, g_ub, g_ob):
@@ -592,7 +644,7 @@
             num_scalar_prefetch=1,
             grid=(1,),
             in_specs=[s for _, s in ins] + [ANY] * len(stashes),
-            out_specs=[whole(fresh[0])] + [ANY] * len(stashes),
+            out_specs=[ANY] * (1 + len(stashes)),
             scratch_shapes=scratch,
         ),
         out_shape=[jax.ShapeDtypeStruct(*fresh)] + [jax.ShapeDtypeStruct(a.shape, a.dtype) for a in stashes],
@@ -676,17 +728,11 @@
     g3 = g.reshape(ff // WIDE, WIDE // fshare, g.shape[1])
     element = jnp.arange(d, dtype=jnp.int32) % head
     spread_gain = (jnp.arange(d, dtype=jnp.int32)[:, None] == (element // hshare * dshare + element % hshare)[None, :]).astype(BF)
-    tables = [jax.ShapeDtypeStruct(s, F32) for s in ((2, 1, d), (2, 2, 1, d), (2, 1, ff), (2, 1, d))]
-    ngain, gains, ubias, obias = plain(
-        partial(smalls_kernel, d, ff, wide, stride), [g, spread_gain], [ANY, full(spread_gain)], tables,
-        [full(a) for a in tables], [pltpu.VMEM((2, d, LANES), BF), pltpu.SemaphoreType.DMA((2,))],
+    small = jax.ShapeDtypeStruct((2, 8, ff), F32)
+    smalls = plain(
+        partial(smalls_kernel, d, ff, wide, stride), [g, spread_gain], [ANY, full(spread_gain)], small, full(small),
+        [pltpu.VMEM((2, d, LANES), BF), pltpu.SemaphoreType.DMA((2,))],
     )
-
-    def of_layer(a, layer):
-        return (a, pl.BlockSpec((None,) + a.shape[1:], lambda i, idx: (layer,) + (0,) * (a.ndim - 1)))
-
-    column = jnp.arange(WIDE, dtype=jnp.int32) // head
-    spread = jnp.where(column[:, None] == column[None, :], 1.0 / head, 0.0).astype(BF)
 
     toks = tokens.reshape(slots, rows, d)
     seeds = cotangent.reshape(slots, rows, d)
@@ -694,7 +740,7 @@
     position = jnp.arange(rows, dtype=jnp.int32)
     image = jnp.sum((position[None, :, None] >= ends[:, None, :]).astype(jnp.int32), axis=-1)
     image = jnp.where(position[None, :] < ends[:, 2:3], image, ABSENT + position[None, :])
-    ids_col, ids_row = image[:, :, None], image[:, None, :]
+    ids = jnp.broadcast_to(image[:, None, :].astype(F32), (slots, 8, rows))
 
     def stash(*shape, dtype=BF):
         return pl.pallas_call(
@@ -711,7 +757,7 @@
     weights_v = [V((d, heads_part), BF), V((chunks, d, fc), BF), V((groups, fshare, WIDE // fshare, d), BF), V((d, d), BF)]
     sems = [pltpu.SemaphoreType.DMA((48,)), pltpu.SemaphoreType.DMA((48,))]
     stacked = ff + 4 * d
-    operands = [[stash(rows, stacked), stash(rows, stacked)] for _ in range(2)]
+    operands = [[stash(rows + 16, stacked), stash(rows + 16, stacked)] for _ in range(2)]
     kept = [[stash(rows, d) for _ in range(4)] + [stash(rows, 2 * d), stash(rows, 2 * d), stash(chunks, rows, fc),
              stash(heads, rows, rows), stash(16, rows, dtype=F32)] for _ in range(2)]
     results = [stash(slots, rows, d, dtype=F32), stash(rows, d)]
@@ -719,16 +765,14 @@
     for t in range(4):
         layer = t % 2
         ybf, done = call(
-            partial(forward_kernel, d, ff, chunks, stride * layer, t == 0),
+            partial(forward_kernel, d, ff, chunks, layer, stride * layer, t == 0),
             index_of(layer, t // 2),
-            [(here_x, ANY), (g, ANY), (g3, ANY), (ids_col, pick((rows, 1))), (ids_row, pick((1, rows))),
-             of_layer(ngain, layer), of_layer(gains, layer), of_layer(ubias, layer), of_layer(obias, layer),
-             (spread, whole((WIDE, WIDE)))],
+            [(a, ANY) for a in (here_x, g, g3, ids, smalls)],
             ((rows, d), BF),
             kept[layer][:9] + operands[layer] + results,
             [V((rows, d), BF), V((rows, d), BF)] + weights_v
             + [V((rows, d), BF)] * 3 + [V((rows, 2 * d), BF)] * 2 + [V((chunks, rows, fc), BF)] * 2
-            + [V((heads, rows, rows), BF), V((16, rows), F32), V((rows, d), BF), V((rows, d), F32), V((rows, d), F32), V((rows, d), BF)]
+            + [V((heads, rows, rows), BF), V((16, rows), F32), V((rows, d), BF), V((rows, d), F32), V((rows, d), F32), V((rows, d), BF), V((8, rows), F32), V((8, ff), F32)]
             + sems,
             1 << 10,
         )
@@ -738,11 +782,8 @@
     y_got = paired(y_send)
 
     results = [stash(slots, rows, d, dtype=F32), stash(rows, d)]
-    tables = [stash(1, stacked, dtype=F32) for _ in range(2)]
     width = 6 * d + LANES
     share = 2 * dshare
-    position = jnp.arange(LANES, dtype=jnp.int32)[:, None] % head
-    place = (position // hshare * dshare + position % hshare == jnp.arange(d, dtype=jnp.int32)[None, :]).astype(F32)
     here = jnp.stack([y, z, core, slot, odd]).astype(jnp.int32)
 
     def moved(x, leg, by):
@@ -753,14 +794,13 @@
 
         return lax.ppermute(x, "dp", [(i, to(i)) for i in range(ranks)])
 
-    def grads_by_place(layer, got, table_got):
+    def grads_by_place(layer, got):
         return simple(
             partial(weight_grad_kernel, d, ff), here,
-            [place, tables[layer], table_got, operands[layer][0], got],
-            [whole((LANES, d)), whole(table_got.shape), whole(table_got.shape), ANY, ANY],
+            [operands[layer][0], got], [ANY] * 2,
             [jax.ShapeDtypeStruct((side * share, width), BF)] * 3 + [jax.ShapeDtypeStruct((side // 2 * share, width), BF)] * 2,
             [ANY] * 5,
-            [V((2, rows, ff), BF), V((2, rows, d), BF), V((2, rows, d), BF), V((2, rows, 2 * d), BF), V((d, width), BF),
+            [V((2, rows, ff), BF), V((2, rows, d), BF), V((2, rows, d), BF), V((2, rows, 2 * d), BF), V((d, width), BF), V((2, 16, stacked), BF),
              pltpu.SemaphoreType.DMA((32,)), pltpu.SemaphoreType.DMA((32,))],
         )
 
@@ -773,8 +813,8 @@
         up, down = pl.pallas_call(
             relay_kernel,
             grid_spec=pltpu.PrefetchScalarGridSpec(
-                num_scalar_prefetch=1, grid=(1,), in_specs=[ANY, ANY, whole(part), whole(part)], out_specs=[ANY] * 2,
-                scratch_shapes=[V(part, BF), V(part, BF), pltpu.SemaphoreType.DMA((2,)), pltpu.SemaphoreType.DMA((2,))],
+                num_scalar_prefetch=1, grid=(1,), in_specs=[ANY] * 4, out_specs=[ANY] * 2,
+                scratch_shapes=[V((4,) + part, BF), pltpu.SemaphoreType.DMA((4,)), pltpu.SemaphoreType.DMA((2,))],
             ),
             out_shape=[jax.ShapeDtypeStruct(up.shape, BF)] * 2,
             input_output_aliases={1: 0, 2: 1},
@@ -789,8 +829,8 @@
 
     def by_second_axis(came):
         return simple(
-            mid_kernel, here, came, [whole(a.shape) for a in came],
-            [jax.ShapeDtypeStruct((share, width), BF)] * side, [whole((share, width))] * side, [V((side, share, width), BF)],
+            mid_kernel, here, came, [ANY] * 3, [jax.ShapeDtypeStruct((share, width), BF)] * side, [ANY] * side,
+            [V((side, 3, share, width), BF), V((side, share, width), BF), pltpu.SemaphoreType.DMA((12,)), pltpu.SemaphoreType.DMA((4,))],
         )
 
     here_g = seeds
@@ -798,32 +838,31 @@
     for t in range(4):
         layer = 1 - t % 2
         gbf, done = call(
-            partial(backward_kernel, d, ff, chunks, stride * layer, t == 0),
+            partial(backward_kernel, d, ff, chunks, layer, stride * layer, t == 0),
             index_of(layer, 1 - t // 2),
-            [(here_g, ANY), (g, ANY), (g3, ANY), (ids_col, pick((rows, 1))), of_layer(ngain, layer), of_layer(gains, layer),
-             (spread, whole((WIDE, WIDE)))] + [(a, ANY) for a in kept[layer]],
+            [(a, ANY) for a in [here_g, g, g3, ids, smalls] + kept[layer]],
             ((rows, d), BF),
-            operands[layer] + [tables[layer]] + results,
+            operands[layer] + results,
             [V((rows, d), BF), V((rows, d), BF)] + weights_v
             + [V((rows, d), BF)] * 4 + [V((rows, 2 * d), BF)] * 2
             + [V((chunks, rows, fc), BF), V((heads, rows, rows), BF), V((16, rows), F32)]
             + [V((d, rows), BF), V((d, rows), F32), V((rows, d), F32)]
-            + [V((rows, d), BF)] * 3 + [V((chunks, rows, fc), BF), V((rows, d), F32), V((rows, d), F32), V((rows, d), BF), V((1, stacked), F32)]
+            + [V((rows, d), BF)] * 3 + [V((chunks, rows, fc), BF), V((rows, d), F32), V((rows, d), F32), V((rows, d), BF), V((1, stacked), F32), V((16, stacked), BF), V((8, rows), F32), V((8, ff), F32)]
             + sems,
             1 << 10,
         )
-        operands[layer], tables[layer], results = done[:2], done[2], done[3:]
+        operands[layer], results = done[:2], done[2:]
         here_g = lax.ppermute(gbf, "section", [(3, 0), (2, 1)]) if t == 1 else gbf
         if t == 1:
             here_g, y_got = lax.optimization_barrier((here_g, y_got))
         if t == 3:
             operands[layer][1], swaps[0] = lax.optimization_barrier((operands[layer][1], swaps[0]))
         if t >= 2:
-            swaps.append((along(operands[layer][1], 1, 2, 1), along(tables[layer], 1, 2, 1)))
+            swaps.append(along(operands[layer][1], 1, 2, 1))
     gr_got = paired(results[1])
-    upper, gr_got = lax.optimization_barrier((grads_by_place(1, *swaps[0]), gr_got))
+    upper, gr_got = lax.optimization_barrier((grads_by_place(1, swaps[0]), gr_got))
     upper_came = halves(upper)
-    lower = grads_by_place(0, *swaps[1])
+    lower = grads_by_place(0, swaps[1])
     lower_came = halves(lower)
     legs = [first_leg(upper, upper_came), first_leg(lower, lower_came)]
     arrived = [second_leg(by_second_axis(came)) for came in legs]
@@ -840,9 +879,9 @@
 
     both = arrived[1] + arrived[0]
     home_mine, home_other, away_mine, away_other = simple(
-        last_kernel, here, both, [whole(a.shape) for a in both],
+        last_pair_kernel, here, both, [ANY] * 8,
         [jax.ShapeDtypeStruct((dshare, width), t) for t in (F32, BF, BF, BF)], [whole((dshare, width))] * 4,
-        [V((share, width), F32)] * 2,
+        [V((8, share, width), BF), V((2, share, width), F32), pltpu.SemaphoreType.DMA((8,))],
     )
     sections = lax.axis_size("section")
     cross = [(s * ranks + i, (s ^ 1) * ranks + (i ^ 1)) for s in range(sections) for i in range(ranks)]

time: 489 us -> 477 us (0.975); the launches traced: 486 us -> 468 us
  Pallas kernels: 188 us -> 173 us
    pallas_call x8, Pallas kernels: 119 us -> 112 us  [call(): pl.pallas_call(kernel, grid_spec=pltpu.PrefetchScalarGridSpec(num_scalar_...]
    pallas_call x6, Pallas kernels: 48.8 us -> 42.8 us  [simple(): pl.pallas_call(kernel, grid_spec=pltpu.PrefetchScalarGridSpec(num_scalar_...]
    unnamed x44 -> x38, local copies, waits for them, and re-layouts: 9.95 us -> 9.2 us
  transfers between devices with their start and end apart: 27 -> 25, of which waited for: 13 -> 11; matrix products, arithmetic and copies ran while one was open for 2% -> 1% of each run, Pallas kernels for 15% -> 14%
where the time goes in v9:
time: 477 us; the launch traced here: 468 us
  waiting for transfers between devices  228 us (48%)
  Pallas kernels  173 us (36%)
  starting transfers between devices  33.8 us (7%)
  between operations  15 us (3%)
  local copies, waits for them, and re-layouts  10.8 us (2%)
  other arithmetic  7.29 us (2%)
    pallas_call x8, Pallas kernels, call(): pl.pallas_call(kernel, grid_spec=pltpu.PrefetchScalarGridSpec(num_scalar_...  112 us
    all_gather x1, waiting for transfers between devices, body(): g = lax.all_gather(both, 'dp', axis=0, tiled=True)  101 us
    ppermute x1, waiting for transfers between devices, body(): here_g = lax.ppermute(gbf, 'section', [(3, 0), (2, 1)]) if t == 1 else gbf  53.7 us
    ppermute x14, waiting for transfers between devices, moved(): return lax.ppermute(x, 'dp', [(i, to(i)) for i in range(ranks)])  44.2 us
    pallas_call x6, Pallas kernels, simple(): pl.pallas_call(kernel, grid_spec=pltpu.PrefetchScalarGridSpec(num_scalar_...  42.8 us
    ppermute x14, starting transfers between devices, moved(): return lax.ppermute(x, 'dp', [(i, to(i)) for i in range(ranks)])  20.3 us
    ppermute x4, waiting for transfers between devices, paired(): return lax.ppermute(x, 'section', [(0, 1), (1, 0), (2, 3), (3, 2)])  11.8 us
    ppermute x1, waiting for transfers between devices, body(): here_x = lax.ppermute(ybf, 'section', [(0, 3), (1, 2)]) if t == 1 else ybf  11.8 us
  transfers between devices with their start and end apart: 25, of which 11 were waited for; matrix products, arithmetic and copies ran while one was open for 1% of the time, Pallas kernels for 14%

profile of v9, /device:TPU:1, one launch (start us, length us, event | category | flops | bytes accessed | tf_op | source)
XLA Modules:
  0.0 467.8 jit_solution(5860915660164057624)
XLA Ops:
  12.5 9.7 %collective-permute-done = bf16[24,9344]{1,0:T(8,128)(2,1)S(1)} collective-permute-done((bf16[24,9344]{1,0:T(8,128)(2,1)}, bf16[24,9344]{1,0:T(8,128)(2,1)S(1)}, u32[]{:S(2)}, u32[]{:S(2)}) %collective-permute-start) | collective-permute-done | bytes 448544 | tf_op jit(solution)/shard_map/ppermute | solution.py:689
  28.8 101.4 %all-gather.2.cloned.1.call-done.g.refs_1_ = bf16[768,18688]{1,0:T(8,128)(2,1)} async-done(((bf16[24,18688]{1,0:T(8,128)(2,1)}), bf16[768,18688]{1,0:T(8,128)(2,1)}) %all-gather.2.cloned.1.call-update) | async-done | bytes 28704784 | tf_op jit(solution)/shard_map/all_gather | solution.py:727
  134.4 16.6 %shard_map.201 = (bf16[384,768]{1,0:T(8,128)(2,1)}, bf16[384,768]{1,0:T(8,128)(2,1)}, bf16[384,768]{1,0:T(8,128)(2,1)}, bf16[384,768]{1,0:T(8,128)(2,1)}, bf16[3...) custom-call(s32[4]{0:T(128)} %get-tuple-element.250.idx, ...), custom_call_target="tpu_custom_call", output_to_operand_aliasing={{1}: (6, {}), {2}: (7, {}), {3}: (8, {}), {4}: (9, {}), {5}... | custom-call | flops 1024 | bytes 1024 | tf_op jit(solution)/shard_map/pallas_call | solution.py:641
  150.9 16.6 %shard_map.213 = (bf16[384,768]{1,0:T(8,128)(2,1)}, bf16[384,768]{1,0:T(8,128)(2,1)}, bf16[384,768]{1,0:T(8,128)(2,1)}, bf16[384,768]{1,0:T(8,128)(2,1)}, bf16[3...) custom-call(s32[4]{0:T(128)} %pad_add_fusion.idx, ...), custom_call_target="tpu_custom_call", output_to_operand_aliasing={{1}: (6, {}), {2}: (7, {}), {3}: (8, {}), {4}: (9, {}), {5}... | custom-call | flops 1024 | bytes 1024 | tf_op jit(solution)/shard_map/pallas_call | solution.py:641
  170.1 11.8 %collective-permute-done.1.refs_0_ = bf16[384,768]{1,0:T(8,128)(2,1)S(1)} collective-permute-done((bf16[384,768]{1,0:T(8,128)(2,1)}, bf16[384,768]{1,0:T(8,128)(2,1)S(1)}, u32[]{:S(2)}, u32[]{:S(2)}) %collective-permute-start.1) | collective-permute-done | bytes 589856 | tf_op jit(solution)/shard_map/ppermute | solution.py:780
  184.7 7.6 %shard_map.215 = (bf16[384,768]{1,0:T(8,128)(2,1)}, bf16[384,768]{1,0:T(8,128)(2,1)}, bf16[384,768]{1,0:T(8,128)(2,1)}, bf16[384,768]{1,0:T(8,128)(2,1)}, bf16[3...) custom-call(s32[4]{0:T(128)} %pad_add_fusion.1.idx, ...), custom_call_target="tpu_custom_call", output_to_operand_aliasing={{1}: (6, {}), {2}: (7, {}), {3}: (8, {}), {4}: (9, {}), {5}... | custom-call | flops 1024 | bytes 1024 | tf_op jit(solution)/shard_map/pallas_call | solution.py:641
  192.3 18.2 %shard_map.218 = (bf16[384,768]{1,0:T(8,128)(2,1)}, bf16[400,6144]{1,0:T(8,128)(2,1)}, bf16[400,6144]{1,0:T(8,128)(2,1)}, f32[2,384,768]{2,1,0:T(8,128)}, bf16[384,768]{1,0:T(8,128)(2,1)}) custom-call(s32[4]{0:T(128)} %pad_add_fusion.1.idx, ...), custom_call_target="tpu_custom_call", output_to_operand_aliasing={{1}: (15, {}), {2}: (16, {}), {3}: (17, {}), {4}: (18, {})} | custom-call | flops 1024 | bytes 1024 | tf_op jit(solution)/shard_map/pallas_call | solution.py:641
  210.6 9.6 %shard_map.219 = (bf16[384,768]{1,0:T(8,128)(2,1)}, bf16[400,6144]{1,0:T(8,128)(2,1)}, bf16[400,6144]{1,0:T(8,128)(2,1)}, f32[2,384,768]{2,1,0:T(8,128)}, bf16[384,768]{1,0:T(8,128)(2,1)}) custom-call(s32[4]{0:T(128)} %get-tuple-element.252.idx, ...), custom_call_target="tpu_custom_call", output_to_operand_aliasing={{1}: (15, {}), {2}: (16, {}), {3}: (17, {}), {4}: (18, {})} | custom-call | flops 1024 | bytes 1024 | tf_op jit(solution)/shard_map/pallas_call | solution.py:641
  222.7 53.7 %collective-permute-done.2.refs_0_ = bf16[384,768]{1,0:T(8,128)(2,1)S(1)} collective-permute-done((bf16[384,768]{1,0:T(8,128)(2,1)}, bf16[384,768]{1,0:T(8,128)(2,1)S(1)}, u32[]{:S(2)}, u32[]{:S(2)}) %collective-permute-start.2) | collective-permute-done | bytes 589856 | tf_op jit(solution)/shard_map/ppermute | solution.py:855
  277.5 20.6 %shard_map.220 = (bf16[384,768]{1,0:T(8,128)(2,1)}, bf16[400,6144]{1,0:T(8,128)(2,1)}, bf16[400,6144]{1,0:T(8,128)(2,1)}, f32[2,384,768]{2,1,0:T(8,128)}, bf16[384,768]{1,0:T(8,128)(2,1)}) custom-call(s32[4]{0:T(128)} %pad_add_fusion.idx, bf16[384,768]{1,0:T(8,128)(2,1)} %copy-done.10, ...), custom_call_target="tpu_custom_call", output_to_operand_aliasing={{1}: (15, {}), {2}: (16, {}), {3}: (17, {}), {4}: (18, {})} | custom-call | flops 1024 | bytes 1024 | tf_op jit(solution)/shard_map/pallas_call | solution.py:641
  299.4 21.0 %shard_map.221 = (bf16[384,768]{1,0:T(8,128)(2,1)}, bf16[400,6144]{1,0:T(8,128)(2,1)}, bf16[400,6144]{1,0:T(8,128)(2,1)}, f32[2,384,768]{2,1,0:T(8,128)}, bf16[384,768]{1,0:T(8,128)(2,1)}) custom-call(s32[4]{0:T(128)} %get-tuple-element.250.idx, ...), custom_call_target="tpu_custom_call", output_to_operand_aliasing={{1}: (15, {}), {2}: (16, {}), {3}: (17, {}), {4}: (18, {})} | custom-call | flops 1024 | bytes 1024 | tf_op jit(solution)/shard_map/pallas_call | solution.py:641
  321.4 11.9 %shard_map.222 = (bf16[192,4736]{1,0:T(8,128)(2,1)}, bf16[192,4736]{1,0:T(8,128)(2,1)}, bf16[192,4736]{1,0:T(8,128)(2,1)}, bf16[96,4736]{1,0:T(8,128)(2,1)}, bf16[96,4736]{1,0:T(8,128)(2,1)}) custom-call(s32[5]{0:T(128)} %stack.45.idx, bf16[400,6144]{1,0:T(8,128)(2,1)} %get-tuple-element.201.kept, bf16[400,6144]{1,0:T(8,128)(2,1)} %collective-permute-done.4.got), custom_call_target="tpu_custom_call" | custom-call | flops 1024 | bytes 1024 | tf_op jit(solution)/shard_map/pallas_call | solution.py:667
  338.2 11.9 %shard_map.224 = (bf16[192,4736]{1,0:T(8,128)(2,1)}, bf16[192,4736]{1,0:T(8,128)(2,1)}, bf16[192,4736]{1,0:T(8,128)(2,1)}, bf16[96,4736]{1,0:T(8,128)(2,1)}, bf16[96,4736]{1,0:T(8,128)(2,1)}) custom-call(s32[5]{0:T(128)} %stack.45.idx, bf16[400,6144]{1,0:T(8,128)(2,1)} %get-tuple-element.214.kept, bf16[400,6144]{1,0:T(8,128)(2,1)} %collective-permute-done.6.got), custom_call_target="tpu_custom_call" | custom-call | flops 1024 | bytes 1024 | tf_op jit(solution)/shard_map/pallas_call | solution.py:667
  365.5 4.3 shard_map.225
  372.5 11.3 %collective-permute-done.16.refs_1_ = bf16[192,4736]{1,0:T(8,128)(2,1)} collective-permute-done((bf16[192,4736]{1,0:T(8,128)(2,1)}, bf16[192,4736]{1,0:T(8,128)(2,1)}, u32[]{:S(2)}, u32[]{:S(2)}) %collective-permute-start.16) | collective-permute-done | bytes 1818656 | tf_op jit(solution)/shard_map/ppermute | solution.py:795
  383.8 4.5 shard_map.228
  392.8 20.1 %collective-permute-done.9.refs_1_ = bf16[192,4736]{1,0:T(8,128)(2,1)S(1)} collective-permute-done((bf16[192,4736]{1,0:T(8,128)(2,1)}, bf16[192,4736]{1,0:T(8,128)(2,1)S(1)}, u32[]{:S(2)}, u32[]{:S(2)}) %collective-permute-start.9) | collective-permute-done | bytes 1818656 | tf_op jit(solution)/shard_map/ppermute | solution.py:795
  414.8 4.4 shard_map.226
  423.8 4.5 collective-permute-done.11.refs_1_
  428.4 5.8 %collective-permute-done.12.refs_2_ = bf16[48,4736]{1,0:T(8,128)(2,1)S(1)} collective-permute-done((bf16[48,4736]{1,0:T(8,128)(2,1)}, bf16[48,4736]{1,0:T(8,128)(2,1)S(1)}, u32[]{:S(2)}, u32[]{:S(2)}) %collective-permute-start.12) | collective-permute-done | bytes 454688 | tf_op jit(solution)/shard_map/ppermute | solution.py:795
  435.1 4.3 shard_map.229
  439.6 4.5 collective-permute-start.22
  448.9 5.1 %collective-permute-done.23.c_in = bf16[24,4736]{1,0:T(8,128)(2,1)S(1)} collective-permute-done((bf16[24,4736]{1,0:T(8,128)(2,1)}, bf16[24,4736]{1,0:T(8,128)(2,1)S(1)}, u32[]{:S(2)}, u32[]{:S(2)}) %collective-permute-start.23) | collective-permute-done | bytes 227360 | tf_op jit(solution)/shard_map/ppermute | solution.py:888
  454.7 5.9 %shard_map.230 = (f32[24,5376]{1,0:T(8,128)}, f32[24,768]{1,0:T(8,128)}, f32[96,768]{1,0:T(8,128)}, f32[1,24]{1,0:T(1,128)}, f32[1,2]{1,0:T(1,128)}, /*index=5*/...) custom-call(s32[5]{0:T(128)} %stack.45.idx, f32[24,4736]{1,0:T(8,128)} %get-tuple-element.238.own, ...), custom_call_target="tpu_custom_call" | custom-call | flops 1024 | bytes 1024 | tf_op jit(solution)/shard_map/pallas_call | solution.py:667
  (127 shorter events, 67.5 us)
Async XLA Ops:
  7.2 123.0 %all-gather.2.cloned.1.call-start = ((), (), s32[]{:S(2)}) async-start(), calls=%async_computation | async-start | bytes 29601792 | tf_op jit(solution)/shard_map/all_gather | solution.py:727
  10.5 11.8 %collective-permute-start = (bf16[24,9344]{1,0:T(8,128)(2,1)}, bf16[24,9344]{1,0:T(8,128)(2,1)S(1)}, u32[]{:S(2)}, u32[]{:S(2)}) collective-permute-start(bf16[24,9344]{1,0:T(8,128)(2,1)} %shard_map.186), channel_id=1, source_target_pairs={{0,32},{32,0},{64,96},{96,64},{1,33},{33,1},{65,97},{97,65},{2,34}... | collective-permute-start | bytes 1345544 | tf_op jit(solution)/shard_map/ppermute | solution.py:689
  167.6 14.4 %collective-permute-start.1 = (bf16[384,768]{1,0:T(8,128)(2,1)}, bf16[384,768]{1,0:T(8,128)(2,1)S(1)}, u32[]{:S(2)}, u32[]{:S(2)}) collective-permute-start(bf16[384,768]{1,0:T(8,128)(2,1)} %get-tuple-element.133), channel_id=1, source_target_pairs={{0,96},{32,64},{1,97},{33,65},{2,98},{34,66},{3,99},{35,67},{4,100... | collective-permute-start | bytes 1769480 | tf_op jit(solution)/shard_map/ppermute | solution.py:780
  220.2 56.2 %collective-permute-start.2 = (bf16[384,768]{1,0:T(8,128)(2,1)}, bf16[384,768]{1,0:T(8,128)(2,1)S(1)}, u32[]{:S(2)}, u32[]{:S(2)}) collective-permute-start(bf16[384,768]{1,0:T(8,128)(2,1)} %get-tuple-element.187), channel_id=1, source_target_pairs={{96,0},{64,32},{97,1},{65,33},{98,2},{66,34},{99,3},{67,35},{100,4... | collective-permute-start | bytes 1769480 | tf_op jit(solution)/shard_map/ppermute | solution.py:855
  221.5 54.9 %collective-permute-start.3 = (bf16[384,768]{1,0:T(8,128)(2,1)S(1)}, bf16[384,768]{1,0:T(8,128)(2,1)S(1)}, u32[]{:S(2)}, u32[]{:S(2)}) collective-permute-start(bf16[384,768]{1,0:T(8,128)(2,1)S(1)} %copy-done), channel_id=1, source_target_pairs={{0,32},{32,0},{64,96},{96,64},{1,33},{33,1},{65,97},{97,65},{2,34}... | collective-permute-start | bytes 1769480 | tf_op jit(solution)/shard_map/ppermute | solution.py:689
  298.1 22.4 %collective-permute-start.4 = (bf16[400,6144]{1,0:T(8,128)(2,1)}, bf16[400,6144]{1,0:T(8,128)(2,1)}, u32[]{:S(2)}, u32[]{:S(2)}) collective-permute-start(bf16[400,6144]{1,0:T(8,128)(2,1)} %get-tuple-element.203), channel_id=1, source_target_pairs={{0,1},{1,0},{2,3},{3,2},{4,5},{5,4},{6,7},{7,6},{8,9},{9,8},{10,11... | collective-permute-start | bytes 14745608 | tf_op jit(solution)/shard_map/ppermute | solution.py:685
  320.5 17.7 %collective-permute-start.6 = (bf16[400,6144]{1,0:T(8,128)(2,1)}, bf16[400,6144]{1,0:T(8,128)(2,1)}, u32[]{:S(2)}, u32[]{:S(2)}) collective-permute-start(bf16[400,6144]{1,0:T(8,128)(2,1)} %get-tuple-element.215), channel_id=1, source_target_pairs={{0,1},{1,0},{2,3},{3,2},{4,5},{5,4},{6,7},{7,6},{8,9},{9,8},{10,11... | collective-permute-start | bytes 14745608 | tf_op jit(solution)/shard_map/ppermute | solution.py:685
  320.6 14.8 %collective-permute-start.5 = (bf16[384,768]{1,0:T(8,128)(2,1)}, bf16[384,768]{1,0:T(8,128)(2,1)S(1)}, u32[]{:S(2)}, u32[]{:S(2)}) collective-permute-start(bf16[384,768]{1,0:T(8,128)(2,1)} %get-tuple-element.210), channel_id=1, source_target_pairs={{0,32},{32,0},{64,96},{96,64},{1,33},{33,1},{65,97},{97,65},{2,34}... | collective-permute-start | bytes 1769480 | tf_op jit(solution)/shard_map/ppermute | solution.py:689
  335.4 17.7 %collective-permute-start.14 = (bf16[96,4736]{1,0:T(8,128)(2,1)}, bf16[96,4736]{1,0:T(8,128)(2,1)S(1)}, u32[]{:S(2)}, u32[]{:S(2)}) collective-permute-start(bf16[96,4736]{1,0:T(8,128)(2,1)} %get-tuple-element.230), channel_id=1, source_target_pairs={{0,8},{1,3},{2,10},{3,5},{4,12},{5,7},{6,14},{7,1},{8,16},{9,11},{... | collective-permute-start | bytes 2727944 | tf_op jit(solution)/shard_map/ppermute | solution.py:795
  335.9 17.1 %collective-permute-start.15 = (bf16[96,4736]{1,0:T(8,128)(2,1)}, bf16[96,4736]{1,0:T(8,128)(2,1)S(1)}, u32[]{:S(2)}, u32[]{:S(2)}) collective-permute-start(bf16[96,4736]{1,0:T(8,128)(2,1)} %get-tuple-element.231), channel_id=1, source_target_pairs={{0,24},{1,7},{2,26},{3,1},{4,28},{5,3},{6,30},{7,5},{8,0},{9,15},{... | collective-permute-start | bytes 2727944 | tf_op jit(solution)/shard_map/ppermute | solution.py:795
  350.1 14.2 %collective-permute-start.7 = (bf16[96,4736]{1,0:T(8,128)(2,1)}, bf16[96,4736]{1,0:T(8,128)(2,1)S(1)}, u32[]{:S(2)}, u32[]{:S(2)}) collective-permute-start(bf16[96,4736]{1,0:T(8,128)(2,1)} %get-tuple-element.219), channel_id=1, source_target_pairs={{0,8},{1,3},{2,10},{3,5},{4,12},{5,7},{6,14},{7,1},{8,16},{9,11},{... | collective-permute-start | bytes 2727944 | tf_op jit(solution)/shard_map/ppermute | solution.py:795
  350.4 13.9 %collective-permute-start.8 = (bf16[96,4736]{1,0:T(8,128)(2,1)}, bf16[96,4736]{1,0:T(8,128)(2,1)S(1)}, u32[]{:S(2)}, u32[]{:S(2)}) collective-permute-start(bf16[96,4736]{1,0:T(8,128)(2,1)} %get-tuple-element.220), channel_id=1, source_target_pairs={{0,24},{1,7},{2,26},{3,1},{4,28},{5,3},{6,30},{7,5},{8,0},{9,15},{... | collective-permute-start | bytes 2727944 | tf_op jit(solution)/shard_map/ppermute | solution.py:795
  359.1 24.7 %collective-permute-start.16 = (bf16[192,4736]{1,0:T(8,128)(2,1)}, bf16[192,4736]{1,0:T(8,128)(2,1)}, u32[]{:S(2)}, u32[]{:S(2)}) collective-permute-start(bf16[192,4736]{1,0:T(8,128)(2,1)} %get-tuple-element.232), channel_id=1, source_target_pairs={{0,8},{1,3},{2,10},{3,5},{4,12},{5,7},{6,14},{7,1},{8,16},{9,11},{... | collective-permute-start | bytes 5455880 | tf_op jit(solution)/shard_map/ppermute | solution.py:795
  359.2 24.6 %collective-permute-start.17 = (bf16[192,4736]{1,0:T(8,128)(2,1)}, bf16[192,4736]{1,0:T(8,128)(2,1)}, u32[]{:S(2)}, u32[]{:S(2)}) collective-permute-start(bf16[192,4736]{1,0:T(8,128)(2,1)} %get-tuple-element.233), channel_id=1, source_target_pairs={{0,24},{1,7},{2,26},{3,1},{4,28},{5,3},{6,30},{7,5},{8,0},{9,15},{... | collective-permute-start | bytes 5455880 | tf_op jit(solution)/shard_map/ppermute | solution.py:795
  369.8 43.2 %collective-permute-start.9 = (bf16[192,4736]{1,0:T(8,128)(2,1)}, bf16[192,4736]{1,0:T(8,128)(2,1)S(1)}, u32[]{:S(2)}, u32[]{:S(2)}) collective-permute-start(bf16[192,4736]{1,0:T(8,128)(2,1)} %get-tuple-element.221), channel_id=1, source_target_pairs={{0,8},{1,3},{2,10},{3,5},{4,12},{5,7},{6,14},{7,1},{8,16},{9,11},{... | collective-permute-start | bytes 5455880 | tf_op jit(solution)/shard_map/ppermute | solution.py:795
  369.8 43.1 %collective-permute-start.10 = (bf16[192,4736]{1,0:T(8,128)(2,1)}, bf16[192,4736]{1,0:T(8,128)(2,1)S(1)}, u32[]{:S(2)}, u32[]{:S(2)}) collective-permute-start(bf16[192,4736]{1,0:T(8,128)(2,1)} %get-tuple-element.222), channel_id=1, source_target_pairs={{0,24},{1,7},{2,26},{3,1},{4,28},{5,3},{6,30},{7,5},{8,0},{9,15},{... | collective-permute-start | bytes 5455880 | tf_op jit(solution)/shard_map/ppermute | solution.py:795
  388.3 34.7 %collective-permute-start.18 = (bf16[48,4736]{1,0:T(8,128)(2,1)}, bf16[48,4736]{1,0:T(8,128)(2,1)S(1)}, u32[]{:S(2)}, u32[]{:S(2)}) collective-permute-start(bf16[48,4736]{1,0:T(8,128)(2,1)} %get-tuple-element.235), channel_id=1, source_target_pairs={{0,2},{1,9},{2,4},{3,11},{4,6},{5,13},{6,0},{7,15},{8,10},{9,17},{... | collective-permute-start | bytes 1363976 | tf_op jit(solution)/shard_map/ppermute | solution.py:795
  389.2 34.6 %collective-permute-start.19 = (bf16[48,4736]{1,0:T(8,128)(2,1)}, bf16[48,4736]{1,0:T(8,128)(2,1)}, u32[]{:S(2)}, u32[]{:S(2)}) collective-permute-start(bf16[48,4736]{1,0:T(8,128)(2,1)} %get-tuple-element.236), channel_id=1, source_target_pairs={{0,4},{1,17},{2,6},{3,19},{4,0},{5,21},{6,2},{7,23},{8,12},{9,25},... | collective-permute-start | bytes 1363976 | tf_op jit(solution)/shard_map/ppermute | solution.py:795
  392.0 31.8 %collective-permute-start.20 = (bf16[48,4736]{1,0:T(8,128)(2,1)}, bf16[48,4736]{1,0:T(8,128)(2,1)}, u32[]{:S(2)}, u32[]{:S(2)}) collective-permute-start(bf16[48,4736]{1,0:T(8,128)(2,1)} %get-tuple-element.237), channel_id=1, source_target_pairs={{0,6},{1,25},{2,0},{3,27},{4,2},{5,29},{6,4},{7,31},{8,14},{9,1},{... | collective-permute-start | bytes 1363976 | tf_op jit(solution)/shard_map/ppermute | solution.py:795
  420.2 14.0 %collective-permute-start.12 = (bf16[48,4736]{1,0:T(8,128)(2,1)}, bf16[48,4736]{1,0:T(8,128)(2,1)S(1)}, u32[]{:S(2)}, u32[]{:S(2)}) collective-permute-start(bf16[48,4736]{1,0:T(8,128)(2,1)} %get-tuple-element.225), channel_id=1, source_target_pairs={{0,4},{1,17},{2,6},{3,19},{4,0},{5,21},{6,2},{7,23},{8,12},{9,25},... | collective-permute-start | bytes 1363976 | tf_op jit(solution)/shard_map/ppermute | solution.py:795
  423.0 11.2 %collective-permute-start.13 = (bf16[48,4736]{1,0:T(8,128)(2,1)}, bf16[48,4736]{1,0:T(8,128)(2,1)S(1)}, u32[]{:S(2)}, u32[]{:S(2)}) collective-permute-start(bf16[48,4736]{1,0:T(8,128)(2,1)} %get-tuple-element.226), channel_id=1, source_target_pairs={{0,6},{1,25},{2,0},{3,27},{4,2},{5,29},{6,4},{7,31},{8,14},{9,1},{... | collective-permute-start | bytes 1363976 | tf_op jit(solution)/shard_map/ppermute | solution.py:795
  439.4 9.4 %collective-permute-start.21 = (bf16[24,4736]{1,0:T(8,128)(2,1)}, bf16[24,4736]{1,0:T(8,128)(2,1)S(1)}, u32[]{:S(2)}, u32[]{:S(2)}) collective-permute-start(bf16[24,4736]{1,0:T(8,128)(2,1)} %get-tuple-element.239), channel_id=1, source_target_pairs={{0,32},{32,0},{64,96},{96,64},{1,33},{33,1},{65,97},{97,65},{2,34}... | collective-permute-start | bytes 681992 | tf_op jit(solution)/shard_map/ppermute | solution.py:689
  439.6 9.3 %collective-permute-start.22 = (bf16[24,4736]{1,0:T(8,128)(2,1)}, bf16[24,4736]{1,0:T(8,128)(2,1)S(1)}, u32[]{:S(2)}, u32[]{:S(2)}) collective-permute-start(bf16[24,4736]{1,0:T(8,128)(2,1)} %get-tuple-element.240), channel_id=1, source_target_pairs={{0,1},{1,0},{2,3},{3,2},{4,5},{5,4},{6,7},{7,6},{8,9},{9,8},{10,11... | collective-permute-start | bytes 681992 | tf_op jit(solution)/shard_map/ppermute | solution.py:685
  444.1 9.9 %collective-permute-start.23 = (bf16[24,4736]{1,0:T(8,128)(2,1)}, bf16[24,4736]{1,0:T(8,128)(2,1)S(1)}, u32[]{:S(2)}, u32[]{:S(2)}) collective-permute-start(bf16[24,4736]{1,0:T(8,128)(2,1)} %get-tuple-element.241), channel_id=1, source_target_pairs={{0,33},{1,32},{2,35},{3,34},{4,37},{5,36},{6,39},{7,38},{8,41},{9,... | collective-permute-start | bytes 681992 | tf_op jit(solution)/shard_map/ppermute | solution.py:888
  (20 other events, 75.1 us)
Sparse Core Ops, SparseCore 0:
  24.6 105.4 all-gather.1
